TPU v7x, 128 devices: a whole 4x4x4 slice. The times are simulated.
128 devices in a mesh: pool: 2 (over y_lo), tp: 4 (over x), dp: 16 (over y_hi, z, core).
Axes of the slice: x: 4, y: 4 (y_hi: 2, y_lo: 2; y = y_hi * 2 + y_lo), z: 4, core: 2. Of those that a mesh axis runs over, the one named last changes fastest.
Arguments:
- x_in: bfloat16 [2, 4096, 16384], P('pool', 'dp', 'tp'), may hold values from -6 to 6
- bc_in: bfloat16 [2, 4096, 2, 2048], P('pool', 'dp', None, 'tp'), may hold values from -1.5 to 1.5
- dt_raw: bfloat16 [2, 4096, 256], P('pool', 'dp', 'tp'), may hold values from -5 to 9
- conv_w_x: bfloat16 [4, 16384], P(None, 'tp'), may hold values from -3 to 3
- conv_b_x: float32 [16384], P('tp'), may hold values from -3 to 3
- conv_w_bc: bfloat16 [4, 2, 2048], P(None, None, 'tp'), may hold values from -3 to 3
- conv_b_bc: float32 [2, 2048], P(None, 'tp'), may hold values from -0.6 to 0.6
- dt_bias: float32 [256], P('tp'), may hold values from -1 to 1
- a_log: float32 [256], P('tp'), may hold values from -12 to 0
- d_skip: float32 [256], P('tp'), may hold values from 0.5 to 1.5
- lengths: int32 [2, 3], P('pool'), may hold values from 1 to 2048, 4096 in all within a row
- decode_prompt: int32 [2, 16, 4], P('pool', 'dp'), may hold values from 0 to 2
- dec_x: bfloat16 [2, 16, 4, 4, 16384], P('pool', 'dp', None, None, 'tp'), may hold values from -6 to 6
- dec_bc: bfloat16 [2, 16, 4, 4, 2, 2048], P('pool', 'dp', None, None, None, 'tp'), may hold values from -1.5 to 1.5
- dec_dt: bfloat16 [2, 16, 4, 4, 256], P('pool', 'dp', None, None, 'tp'), may hold values from -4 to 4
Outputs:
- prefill_out: bfloat16 [2, 4096, 16384], P('pool', 'dp', 'tp')
- decode_out: bfloat16 [2, 16, 4, 4, 16384], P('pool', 'dp', None, None, 'tp')
Inputs may be any that keep to these rules, and one draw needn't show every extreme that they name: `lengths`: the 3 prompts of a half fill its stream of 4096 tokens exactly; the longest has exactly 2048 tokens. `decode_prompt`: A prompt number of the other half; a prompt may be continued by several rows or by none.
All inputs are finite; a program needn't handle non-finite values.
Results may differ from a plain program's by a relative error of at most 0.0051.
Values may be sent and summed in bfloat16 or wider, within the bound.
No kernel may reach another device: no remote copies, remote signals or barrier semaphores. Data moves between devices by JAX's collectives and lax.ppermute only.
A program may use at most 256 MiB of HBM per device.

v0:
```python
import jax
import jax.numpy as jnp
from jax import lax
from jax.sharding import PartitionSpec as P

HEAD_DIM = 64
STATE = 256
CONV = 4
BLOCK_TOKENS = 128
PROMPTS = 3
STEPS = 4


HIGHEST_PRECISION = lax.Precision.HIGHEST


def from_behind(value, axis, steps):
    count = lax.axis_size(axis)
    first, last = (max(0, -steps), min(count, count - steps))
    return lax.ppermute(value, axis, [(source, source + steps) for source in range(first, last)])


def carried_in(value, axis, join, neutral):
    count, mine = (lax.axis_size(axis), lax.axis_index(axis))
    pieces = jax.tree.map(lambda part: lax.all_gather(part, axis), value)
    subtotal = jax.tree.map(
        lambda part, zero: jnp.full_like(part, 0) + jnp.asarray(zero, part.dtype), value, neutral
    )

    def lap(position, subtotal):
        longer = join(subtotal, jax.tree.map(lambda part: part[position], pieces))
        return jax.tree.map(lambda new, old: jnp.where(position < mine, new, old), longer, subtotal)

    return lax.fori_loop(0, count - 1, lap, subtotal)


def swapped(block, axis, bit):
    count = lax.axis_size(axis)
    route = []
    for low in range(count):
        high = low | 1 << bit
        if high != low and high < count:
            route += [(low, high), (high, low)]
    return lax.ppermute(block, axis, route)


def prompt_segments(lengths, positions):
    bounds = jnp.cumsum(lengths)
    segment = jnp.sum((positions[:, None] >= bounds[None, :]).astype(jnp.int32), axis=1)
    return jnp.where(positions < 0, -1, segment)


def conv_window(extended, segment, weight, offset):
    row_count = extended.shape[0] - (CONV - 1)
    own_segment = segment[CONV - 1 :]
    running = jnp.broadcast_to(offset[None, :], (row_count, extended.shape[1]))
    for tap_index in range(CONV):
        same_prompt = (segment[tap_index : tap_index + row_count] == own_segment)[:, None]
        term_value = weight[tap_index].astype(jnp.float32)[None, :] * extended[
            tap_index : tap_index + row_count
        ].astype(jnp.float32)
        running = running + jnp.where(same_prompt, term_value, 0.0)
    return jax.nn.silu(running).astype(jnp.bfloat16)


def span_outputs(
    mixed_rows, b_rows, c_rows, log_decay, step_size, segment, previous, carry_state, skip_gain
):
    span_len = mixed_rows.shape[0]
    cumulative = jnp.cumsum(log_decay, axis=0)
    positions = jnp.arange(span_len)
    causal = (positions[:, None] >= positions[None, :]) & (segment[:, None] == segment[None, :])
    across = jnp.moveaxis(cumulative, 0, -1)
    spread = across[:, :, :, None] - across[:, :, None, :]
    decay_mask = jnp.where(causal, jnp.exp(jnp.where(causal, spread, 0.0)), 0.0)
    scores = jnp.einsum("tgn,sgn->gts", c_rows, b_rows, preferred_element_type=jnp.float32)
    weights = (scores[:, None] * decay_mask * jnp.moveaxis(step_size, 0, -1)[:, :, None, :]).astype(
        jnp.bfloat16
    )
    inner_part = jnp.einsum(
        "gkts,sgkp->tgkp", weights, mixed_rows, preferred_element_type=jnp.float32
    )
    carried = jnp.einsum(
        "tgn,gkpn->tgkp", c_rows.astype(jnp.float32), carry_state, precision=HIGHEST_PRECISION
    )
    first_rows = (segment == previous)[:, None, None, None]
    outer_part = jnp.where(first_rows, jnp.exp(cumulative)[:, :, :, None] * carried, 0.0)
    return (
        inner_part + outer_part + skip_gain[None, :, :, None] * mixed_rows.astype(jnp.float32)
    ).astype(jnp.bfloat16)


def end_state(carry_state, mixed_rows, b_rows, log_decay, step_size, segment, previous, target):
    span_len = mixed_rows.shape[0]
    cumulative = jnp.cumsum(log_decay, axis=0)
    positions = jnp.arange(span_len)
    final_sum = lax.dynamic_index_in_dim(cumulative, target, 0, keepdims=False)
    own_segment = lax.dynamic_index_in_dim(segment, target, 0, keepdims=False)
    chosen = ((positions <= target) & (segment == own_segment))[:, None, None]
    row_weight = (
        jnp.where(chosen, jnp.exp(jnp.where(chosen, final_sum[None] - cumulative, 0.0)), 0.0)
        * step_size
    )
    scaled = (mixed_rows.astype(jnp.float32) * row_weight[:, :, :, None]).astype(jnp.bfloat16)
    fresh_part = jnp.einsum("sgkp,sgn->gkpn", scaled, b_rows, preferred_element_type=jnp.float32)
    keep_factor = jnp.where(own_segment == previous, jnp.exp(final_sum), 0.0)
    return keep_factor[:, :, None, None] * carry_state + fresh_part


def decode_conv(window_rows, weight, offset):
    running = jnp.broadcast_to(offset[None, :], (window_rows.shape[0], window_rows.shape[2]))
    for tap_index in range(CONV):
        running = running + weight[tap_index].astype(jnp.float32)[None, :] * window_rows[
            :, tap_index
        ].astype(jnp.float32)
    return jax.nn.silu(running).astype(jnp.bfloat16)


def decode_parts(
    carry_state,
    cache_x,
    cache_bc,
    new_x,
    new_bc,
    raw_step,
    conv_w_x,
    conv_b_x,
    weight_bc,
    offset_bc,
    dt_bias,
    group_rates,
    group_skip,
):
    row_total = carry_state.shape[0]
    group_count = carry_state.shape[1]
    per_group = carry_state.shape[2]
    fading = jnp.zeros((row_total, group_count, per_group), jnp.float32)
    readouts, skipped, readers, faded = ([], [], [], [])
    for step_index in range(STEPS):
        window_x = jnp.concatenate([cache_x, new_x[step_index][:, None]], axis=1)
        window_bc = jnp.concatenate([cache_bc, new_bc[step_index][:, None]], axis=1)
        mixed_rows = decode_conv(window_x, conv_w_x, conv_b_x)
        both_rows = decode_conv(window_bc, weight_bc, offset_bc).reshape(
            row_total, 2, group_count, STATE
        )
        step_size = jax.nn.softplus(
            raw_step[step_index].astype(jnp.float32) + dt_bias[None, :]
        ).reshape(row_total, group_count, per_group)
        values = mixed_rows.reshape(row_total, group_count, per_group, HEAD_DIM).astype(jnp.float32)
        b_rows = both_rows[:, 0].astype(jnp.float32)
        c_rows = both_rows[:, 1].astype(jnp.float32)
        fading = fading + step_size * group_rates[None]
        carry_state = (
            jnp.exp(step_size * group_rates[None])[:, :, :, None, None] * carry_state
            + (step_size[:, :, :, None] * values)[:, :, :, :, None] * b_rows[:, :, None, None, :]
        )
        readouts.append(
            jnp.einsum("rgn,rgkpn->rgkp", c_rows, carry_state, precision=HIGHEST_PRECISION)
        )
        skipped.append(group_skip[None, :, :, None] * values)
        readers.append(c_rows)
        faded.append(jnp.exp(fading))
        cache_x = window_x[:, 1:]
        cache_bc = window_bc[:, 1:]
    return (jnp.stack(readouts), jnp.stack(skipped), jnp.stack(readers), jnp.stack(faded))


def combine_states(earlier_part, later_part):
    return (
        earlier_part[0] * later_part[0],
        later_part[0][:, :, None, None] * earlier_part[1] + later_part[1],
    )


def on_device(
    x_in,
    bc_in,
    dt_raw,
    conv_w_x,
    conv_b_x,
    conv_w_bc,
    conv_b_bc,
    dt_bias,
    a_log,
    d_skip,
    lengths,
    decode_prompt,
    dec_x,
    dec_bc,
    dec_dt,
):
    tokens = x_in[0]
    row_count = tokens.shape[0]
    channels = tokens.shape[1]
    group_count = bc_in.shape[3] // STATE
    head_count = dt_raw.shape[2]
    per_group = head_count // group_count
    width_bc = 2 * bc_in.shape[3]
    rim_rows = CONV - 1
    block_count = row_count // BLOCK_TOKENS
    bc_rows = bc_in[0].reshape(row_count, width_bc)
    last_rows = jnp.concatenate(
        [tokens[row_count - rim_rows :], bc_rows[row_count - rim_rows :]], axis=1
    )
    prior_rows = from_behind(last_rows, "dp", 1)
    anchor = lax.axis_index("dp") * row_count
    segment_ext = prompt_segments(
        lengths[0], anchor + jnp.arange(-rim_rows, row_count, dtype=jnp.int32)
    )
    ext_x = jnp.concatenate([prior_rows[:, :channels], tokens], axis=0)
    ext_bc = jnp.concatenate([prior_rows[:, channels:], bc_rows], axis=0)
    weight_bc = conv_w_bc.reshape(CONV, width_bc)
    offset_bc = conv_b_bc.reshape(width_bc)
    mixed_all = conv_window(ext_x, segment_ext, conv_w_x, conv_b_x).reshape(
        block_count, BLOCK_TOKENS, group_count, per_group, HEAD_DIM
    )
    both_all = conv_window(ext_bc, segment_ext, weight_bc, offset_bc).reshape(
        block_count, BLOCK_TOKENS, 2, group_count, STATE
    )
    b_all = both_all[:, :, 0]
    c_all = both_all[:, :, 1]
    group_rates = (-jnp.exp(a_log)).reshape(group_count, per_group)
    group_skip = d_skip.reshape(group_count, per_group)
    step_all = jax.nn.softplus(dt_raw[0].astype(jnp.float32) + dt_bias[None, :]).reshape(
        block_count, BLOCK_TOKENS, group_count, per_group
    )
    decay_all = step_all * group_rates[None, None]
    segment_all = segment_ext[rim_rows:].reshape(block_count, BLOCK_TOKENS)
    previous_all = segment_ext[rim_rows - 1 : rim_rows - 1 + row_count : BLOCK_TOKENS]

    def local_pass(carry_state, inputs):
        mixed_rows, b_rows, log_decay, step_size, segment, previous = inputs
        return (
            end_state(
                carry_state,
                mixed_rows,
                b_rows,
                log_decay,
                step_size,
                segment,
                previous,
                BLOCK_TOKENS - 1,
            ),
            carry_state,
        )

    zero_state = jnp.zeros((group_count, per_group, HEAD_DIM, STATE), jnp.float32)
    device_state, local_starts = lax.scan(
        local_pass, zero_state, (mixed_all, b_all, decay_all, step_all, segment_all, previous_all)
    )
    totals = jnp.sum(decay_all, axis=1)
    exclusive = jnp.concatenate(
        [jnp.zeros_like(totals[:1]), jnp.cumsum(totals, axis=0)[:-1]], axis=0
    )
    lead_segment = segment_ext[rim_rows - 1]
    through = jnp.where(
        segment_ext[rim_rows + row_count - 1] == lead_segment, jnp.exp(jnp.sum(totals, axis=0)), 0.0
    )
    incoming = carried_in(
        (through, device_state), "dp", combine_states, (jnp.ones_like(through), zero_state)
    )[1]
    reach_factor = jnp.where((previous_all == lead_segment)[:, None, None], jnp.exp(exclusive), 0.0)
    starts_all = local_starts + reach_factor[:, :, :, None, None] * incoming[None]

    def block_output(inputs):
        return span_outputs(*inputs, group_skip)

    prefill_out = lax.map(
        block_output,
        (mixed_all, b_all, c_all, decay_all, step_all, segment_all, previous_all, starts_all),
    )
    bounds = jnp.cumsum(lengths[0])
    finals, caches = ([], [])
    for prompt in range(PROMPTS):
        local_pos = bounds[prompt] - 1 - anchor
        present = (local_pos >= 0) & (local_pos < row_count)
        clip_pos = jnp.clip(local_pos, 0, row_count - 1)
        block_index = clip_pos // BLOCK_TOKENS

        def select_block(array):
            return lax.dynamic_index_in_dim(array, block_index, 0, keepdims=False)

        prompt_state = end_state(
            select_block(starts_all),
            select_block(mixed_all),
            select_block(b_all),
            select_block(decay_all),
            select_block(step_all),
            select_block(segment_all),
            select_block(previous_all),
            clip_pos % BLOCK_TOKENS,
        )
        finals.append(jnp.where(present, prompt_state, 0.0))
        own_segment = lax.dynamic_index_in_dim(segment_ext, clip_pos + rim_rows, 0, keepdims=False)
        keep_rows = (
            lax.dynamic_slice_in_dim(segment_ext, clip_pos + 1, rim_rows, 0) == own_segment
        )[:, None]
        window_rows = jnp.concatenate(
            [
                lax.dynamic_slice_in_dim(ext_x, clip_pos + 1, rim_rows, 0),
                lax.dynamic_slice_in_dim(ext_bc, clip_pos + 1, rim_rows, 0),
            ],
            axis=1,
        )
        caches.append(jnp.where(keep_rows & present, window_rows.astype(jnp.float32), 0.0))
    finals = jnp.stack(finals)
    caches = jnp.stack(caches)
    row_total = decode_prompt.shape[2]
    selector = (
        decode_prompt[0, 0][:, None] == jnp.arange(PROMPTS, dtype=jnp.int32)[None, :]
    ).astype(jnp.float32)
    new_bc = dec_bc[0, 0].reshape(STEPS, row_total, width_bc)
    state_total, cache_total = lax.psum((finals, caches), "dp")
    state_other, cache_other = swapped((state_total, cache_total), "pool", 0)
    row_states = jnp.einsum("rq,qgkpn->rgkpn", selector, state_other, precision=HIGHEST_PRECISION)
    row_cache = jnp.einsum(
        "rq,qwc->rwc", selector, cache_other, precision=HIGHEST_PRECISION
    ).astype(jnp.bfloat16)
    readouts, skipped, readers, faded = decode_parts(
        row_states,
        row_cache[:, :, :channels],
        row_cache[:, :, channels:],
        dec_x[0, 0],
        new_bc,
        dec_dt[0, 0],
        conv_w_x,
        conv_b_x,
        weight_bc,
        offset_bc,
        dt_bias,
        group_rates,
        group_skip,
    )
    decoded = (readouts + skipped).astype(jnp.bfloat16).reshape(STEPS, row_total, channels)
    return (prefill_out.reshape(1, row_count, channels), decoded.reshape((1, 1) + decoded.shape))


def solution(mesh):
    in_specs = (
        P("pool", "dp", "tp"),
        P("pool", "dp", None, "tp"),
        P("pool", "dp", "tp"),
        P(None, "tp"),
        P("tp"),
        P(None, None, "tp"),
        P(None, "tp"),
        P("tp"),
        P("tp"),
        P("tp"),
        P("pool", None),
        P("pool", "dp", None),
        P("pool", "dp", None, None, "tp"),
        P("pool", "dp", None, None, None, "tp"),
        P("pool", "dp", None, None, "tp"),
    )
    out_specs = (P("pool", "dp", "tp"), P("pool", "dp", None, None, "tp"))
    return jax.shard_map(
        on_device, mesh=mesh, in_specs=in_specs, out_specs=out_specs, check_vma=False
    )
```

profile of v0, /device:TPU:1, one launch (start us, length us, event | category | flops | bytes accessed | tf_op | source)
XLA Modules:
  0.0 1143.3 jit_solution(1600034020373032613)
XLA Ops:
  8.8 4.9 collective-permute-start
  23.2 8.2 multiply_convert_fusion.2
  31.5 2.5 copy.199
  34.0 4.0 reshape.1599
  37.9 2.1 copy.205
  40.1 1.8 multiply_convert_fusion.9
  41.9 2.2 reshape.1600
  44.1 2.3 fusion.160
  46.4 24.1 %while.38 = (s32[]{:T(128)}, f32[2,32,64,256]{3,2,1,0:T(8,128)}, f32[2,2,32,64,256]{4,3,2,1,0:T(8,128)}, s32[2,128]{1,0:T(2,128)S(1)}, s32[2]{0:T(128)S(1)}, /*i...) while((s32[]{:T(128)}, f32[2,32,64,256]{3,2,1,0:T(8,128)}, ...), condition=%wide.region_4.5_spmd.clone, body=%wide.region_2.4_spmd.clone.sunk | while | flops 275276224 | bytes 18986140 | solution.py:248
  46.5 2.6 bitcast_dynamic-update-slice_fusion.2
  53.2 3.5 multiply_add_fusion.9
  56.7 4.8 bitcast_dynamic-update-slice_fusion.2
  65.5 5.0 multiply_add_fusion.9
  84.4 3.3 bitcast_and_fusion.3
  90.2 1.6 copy.228
  97.1 1.5 bitcast_multiply_fusion.6
  98.6 1.6 copy.224
  101.5 1.5 copy.218
  104.8 1.5 bitcast_multiply_fusion.7
  106.4 1.6 copy.220
  108.0 25.6 %all_gather.10 = f32[16,2,32]{2,1,0:T(2,128)} all-gather(f32[1,2,32]{2,1,0:T(2,128)} %select_n.415), channel_id=1, replica_groups=mesh['pool'=2,'tp'=4,'dp'=16] {'dp'}, dimensions={0}, use_global_device_ids=true | all-gather | bytes 4352 | tf_op jit(solution)/shard_map/all_gather | solution.py:25
  133.6 2.7 compare_and_fusion.2
  140.3 9.5 dynamic-slice_convert_fusion.2
  149.8 262.8 %all-gather.3.cloned.1.call-done = f32[32,32,64,256]{3,2,1,0:T(8,128)} async-done(((f32[2,32,64,256]{3,2,1,0:T(8,128)}), f32[32,32,64,256]{3,2,1,0:T(8,128)}) %all-gather.3.cloned.1.call-update) | async-done | bytes 67108880 | tf_op jit(solution)/shard_map/all_gather | solution.py:25
  412.5 102.3 %while.39 = (s32[]{:T(128)}, f32[2,32,64,256]{3,2,1,0:T(8,128)}, s32[]{:T(128)}, f32[16,2,32]{2,1,0:T(2,128)}, f32[16,2,32,64,256]{4,3,2,1,0:T(8,128)}, /*index=5*/s32[]{:T(128)}, s32[]{:T(128)}) while((s32[]{:T(128)}, f32[2,32,64,256]{3,2,1,0:T(8,128)}, s32[]{:T(128)}, f32[16,2,32]{2,1,0:T(2,128)}, ...), condition=%wide.region_9.10_spmd.clone, body=%wide.region_8.9_spmd.clone.sunk | while | flops 4194308 | bytes 12583793 | solution.py:34
  413.2 5.0 fusion.201
  418.8 6.3 fusion.201
  425.7 6.2 fusion.201
  432.6 6.2 fusion.201
  439.5 6.4 fusion.201
  446.6 6.3 fusion.201
  453.5 6.2 fusion.201
  460.3 6.2 fusion.201
  467.2 6.3 fusion.201
  474.2 6.2 fusion.201
  481.1 6.2 fusion.201
  488.0 6.2 fusion.201
  494.8 6.3 fusion.201
  501.8 6.2 fusion.201
  508.7 6.2 fusion.201
  514.9 5.3 multiply_add_fusion.5
  520.3 6.1 fusion.68
  526.4 2.8 fusion.71
  529.2 2.8 fusion.74
  532.1 11.4 %pad_maximum_fusion = f32[3,2,32,64,256]{4,3,2,1,0:T(8,128)} fusion(f32[1,2,32,64,256]{4,3,2,1,0:T(8,128)} %fusion.68, f32[1,2,32,64,256]{4,3,2,1,0:T(8,128)} %fusion.71, f32[1,2,32,64,256]{4,3,2,1,0:T(8,128)} %fusion.74), kind=kLoop, calls=%fused_computation.79 | loop fusion | flops 6291456 | bytes 25165824 | tf_op jit(solution)/shard_map/stack | solution.py:306
  543.7 173.8 %all-reduce.4.cloned.1.call-done = (f32[3,2,32,64,256]{4,3,2,1,0:T(8,128)}, f32[3,3,5120]{2,0,1:T(4,128)}) async-done(((f32[3,2,32,64,256]{4,3,2,1,0:T(8,128)}, f32[3,3,5120]{2,0,1:T(4,128)}), (f32[3,2,32,64,256]{4,3,2,1,0:T(8,128)}, f32[3,3,5120]{2,0,1:T(4,128)})) %all-reduce.4.cloned.1.call-update) | async-done | bytes 12767248 | tf_op jit(solution)/shard_map/psum | solution.py:313
  736.8 29.4 %while.37 = (s32[]{:T(128)}, bf16[2,128,2,32,64]{1,4,3,2,0:T(8,128)(2,1)}, bf16[2,128,2,32,64]{1,4,3,2,0:T(8,128)(2,1)S(1)}, bf16[2,128,2,256]{3,2,1,0:T(2,128)(...) while((s32[]{:T(128)}, ...), condition=%wide.region_12.13_spmd, body=%wide.region_10.12_spmd.sunk | while | flops 1772658816 | bytes 13537373 | solution.py:268
  739.6 1.9 broadcast_compare_fusion.3
  741.7 3.3 fusion.195
  745.8 6.0 fusion.196
  754.1 1.9 broadcast_compare_fusion.3
  756.1 3.3 fusion.195
  760.2 6.0 fusion.196
  766.2 7.5 copy.265
  773.9 6.8 reshape.1658
  780.8 210.9 %collective-permute-done.1 = f32[3,3,5120]{2,0,1:T(4,128)} collective-permute-done((f32[3,3,5120]{2,0,1:T(4,128)}, f32[3,3,5120]{2,0,1:T(4,128)}, u32[]{:S(2)}, u32[]{:S(2)}) %collective-permute-start.1) | collective-permute-done | bytes 184352 | tf_op jit(solution)/shard_map/ppermute | solution.py:44
  996.8 2.0 copy.240
  998.9 2.1 copy.236
  1001.0 2.0 copy.232
  1003.4 50.1 %multiply_add_fusion.1 = (f32[4,2,32,64,256]{4,0,3,2,1:T(4,128)S(1)}, f32[4,2,32,64,256]{4,0,3,2,1:T(4,128)}, f32[4,2,32,64,256]{4,0,3,2,1:T(4,128)}, f32[4,2,32,64,256]{4,0,3,2,1:T(4,128)}) fusion(f32[4,2,256]{2,0,1:T(4,128)S(1)} %copy-done.77, f32[4,2,32,64]{0,3,2,1:T(8,128)S(1)} %copy.244, f32[4,2,32]{0,2,1:T(8,128)S(1)} %copy-done.55, ...), kind=kOutput, calls=%fused_computation.75 | convolution fusion | flops 201326608 | bytes 79990800 | tf_op jit(solution)/shard_map/rq,qgkpn->rgkpn/dot_general | solution.py:315
  1053.5 11.0 fusion.54
  1064.6 23.4 %fusion.56 = f32[4,2,1,32,64]{4,2,3,1,0:T(1,128)S(1)} fusion(f32[4,2,32,64,256]{4,0,3,2,1:T(4,128)} %get-tuple-element.411, bf16[4,2,256,1,1]{2,1,0,3,4:T(2,128)(2,1)S(1)} %get-tuple-element.486), kind=kOutput, calls=%fused_computation.67 | convolution fusion | flops 50331648 | bytes 16846848 | tf_op jit(solution)/shard_map/rgn,rgkpn->rgkp/dot_general | solution.py:158
  1088.2 23.4 %fusion.58 = f32[4,2,1,32,64]{4,2,3,1,0:T(1,128)S(1)} fusion(f32[4,2,32,64,256]{4,0,3,2,1:T(4,128)} %get-tuple-element.412, bf16[4,2,256,1,1]{2,1,0,3,4:T(2,128)(2,1)S(1)} %get-tuple-element.484), kind=kOutput, calls=%fused_computation.69 | convolution fusion | flops 50331648 | bytes 16846848 | tf_op jit(solution)/shard_map/rgn,rgkpn->rgkp/dot_general | solution.py:158
  1111.6 23.4 %fusion.60 = f32[4,2,1,32,64]{4,2,3,1,0:T(1,128)S(1)} fusion(f32[4,2,32,64,256]{4,0,3,2,1:T(4,128)} %get-tuple-element.531, bf16[4,2,256,1,1]{2,1,0,3,4:T(2,128)(2,1)S(1)} %get-tuple-element.482), kind=kOutput, calls=%fused_computation.71 | convolution fusion | flops 50331648 | bytes 16846848 | tf_op jit(solution)/shard_map/rgn,rgkpn->rgkp/dot_general | solution.py:158
  (392 shorter events, 80.3 us)
Async XLA Ops:
  7.2 405.4 %all-gather.3.cloned.1.call-start = ((), (), s32[]{:S(2)}) async-start(), calls=%async_computation | async-start | bytes 71303168 | tf_op jit(solution)/shard_map/all_gather | solution.py:25
  8.8 14.4 %collective-permute-start = (bf16[3,5120]{1,0:T(4,128)(2,1)S(1)}, bf16[3,5120]{1,0:T(4,128)(2,1)S(1)}, u32[]{:S(2)}, u32[]{:S(2)}) collective-permute-start(bf16[3,5120]{1,0:T(4,128)(2,1)S(1)} %pad_maximum_fusion.2), channel_id=1, source_target_pairs={{0,1},{1,2},{2,3},{3,4},{4,5},{5,6},{6,7},{7,8},{8,9},{9,10},{10,1... | collective-permute-start | bytes 92168 | tf_op jit(solution)/shard_map/ppermute | solution.py:20
  14.7 19.2 %copy-start.22 = (f32[1,4096]{1,0:T(1,128)}, f32[1,4096]{1,0:T(1,128)S(1)}, u32[]{:S(2)}) copy-start(f32[1,4096]{1,0:T(1,128)S(1)} %get-tuple-element.479) | copy-start | bytes 49156
  14.7 19.2 %copy-start.24 = (f32[1,4096]{1,0:T(1,128)}, f32[1,4096]{1,0:T(1,128)S(1)}, u32[]{:S(2)}) copy-start(f32[1,4096]{1,0:T(1,128)S(1)} %get-tuple-element.480) | copy-start | bytes 49156
  14.7 19.2 %copy-start.26 = (f32[1,4096]{1,0:T(1,128)}, f32[1,4096]{1,0:T(1,128)S(1)}, u32[]{:S(2)}) copy-start(f32[1,4096]{1,0:T(1,128)S(1)} %get-tuple-element.481) | copy-start | bytes 49156
  16.3 17.6 %copy-start.48 = (s32[259]{0:T(512)}, s32[259]{0:T(512)S(1)}, u32[]{:S(2)}) copy-start(s32[259]{0:T(512)S(1)} %compare_select_fusion.6) | copy-start | bytes 3112
  20.0 13.9 %copy-start.84 = (f32[2,32]{1,0:T(2,128)}, f32[2,32]{1,0:T(2,128)S(1)}, u32[]{:S(2)}) copy-start(f32[2,32]{1,0:T(2,128)S(1)} %add.816) | copy-start | bytes 772
  21.0 13.0 %copy-start.12 = (f32[2,128,2,32]{1,0,3,2:T(2,128)}, f32[2,128,2,32]{1,0,3,2:T(2,128)S(1)}, u32[]{:S(2)}) copy-start(f32[2,128,2,32]{1,0,3,2:T(2,128)S(1)} %get-tuple-element.428) | copy-start | bytes 196612
  23.2 10.7 copy-start.19
  56.7 7.8 copy-start.6
  56.7 8.0 copy-start.40
  70.5 9.6 copy-start.42
  70.5 9.6 copy-start.81
  70.5 35.8 %copy-start.1 = (bf16[2,128,2,32,64]{1,4,3,2,0:T(8,128)(2,1)}, bf16[2,128,2,32,64]{1,4,3,2,0:T(8,128)(2,1)S(1)}, u32[]{:S(2)}) copy-start(bf16[2,128,2,32,64]{1,4,3,2,0:T(8,128)(2,1)S(1)} %get-tuple-element.795) | copy-start | bytes 6291460
  70.6 7.9 copy-start.13
  70.6 65.7 %copy-start.20 = (bf16[3,4096]{1,0:T(4,128)(2,1)S(1)}, bf16[3,4096]{1,0:T(4,128)(2,1)}, u32[]{:S(2)}) copy-start(bf16[3,4096]{1,0:T(4,128)(2,1)} %copy-done.19) | copy-start | bytes 73732
  70.7 646.8 %all-reduce.4.cloned.1.call-start = ((), (), s32[]{:S(2)}) async-start(), calls=%async_computation.1 | async-start | bytes 25657344 | tf_op jit(solution)/shard_map/psum | solution.py:313
  108.0 32.3 %copy-start.3 = (bf16[2,128,2,32,64]{1,0,4,3,2:T(2,128)(2,1)S(1)}, bf16[2,128,2,32,64]{1,0,4,3,2:T(2,128)(2,1)}, u32[]{:S(2)}) copy-start(bf16[2,128,2,32,64]{1,0,4,3,2:T(2,128)(2,1)} %reshape.1599) | copy-start | bytes 6291460
  412.5 102.3 %copy-start.78 = (f32[2,2,32]{2,1,0:T(2,128)S(1)}, f32[2,2,32]{2,1,0:T(2,128)}, u32[]{:S(2)}) copy-start(f32[2,2,32]{2,1,0:T(2,128)} %copy.204) | copy-start | bytes 1540
  520.2 9.0 copy-start
  543.5 174.2 %copy-start.66 = (f32[2,512]{1,0:T(2,128)S(1)}, f32[2,512]{1,0:T(2,128)}, u32[]{:S(2)}) copy-start(f32[2,512]{1,0:T(2,128)} %param.27) | copy-start | bytes 12292
  543.5 174.9 %copy-start.21 = (f32[4096]{0:T(1024)S(1)}, f32[4096]{0:T(1024)}, u32[]{:S(2)}) copy-start(f32[4096]{0:T(1024)} %param.25) | copy-start | bytes 49156
  543.5 175.5 %copy-start.51 = (bf16[1,1,4,4,2,512]{5,4,3,2,1,0:T(2,128)(2,1)S(1)}, bf16[1,1,4,4,2,512]{5,4,3,2,1,0:T(2,128)(2,1)}, u32[]{:S(2)}) copy-start(bf16[1,1,4,4,2,512]{5,4,3,2,1,0:T(2,128)(2,1)} %param.34) | copy-start | bytes 98308
  543.5 176.2 %copy-start.65 = (f32[1,2,512]{2,1,0:T(2,128)S(1)}, f32[1,2,512]{2,1,0:T(2,128)}, u32[]{:S(2)}) copy-start(f32[1,2,512]{2,1,0:T(2,128)} %get-tuple-element.496) | copy-start | bytes 12292
  543.5 176.8 %copy-start.64 = (f32[1,2,512]{2,1,0:T(2,128)S(1)}, f32[1,2,512]{2,1,0:T(2,128)}, u32[]{:S(2)}) copy-start(f32[1,2,512]{2,1,0:T(2,128)} %get-tuple-element.497) | copy-start | bytes 12292
  543.5 177.4 %copy-start.63 = (f32[1,2,512]{2,1,0:T(2,128)S(1)}, f32[1,2,512]{2,1,0:T(2,128)}, u32[]{:S(2)}) copy-start(f32[1,2,512]{2,1,0:T(2,128)} %get-tuple-element.495) | copy-start | bytes 12292
  543.5 178.0 %copy-start.62 = (f32[1,2,512]{2,1,0:T(2,128)S(1)}, f32[1,2,512]{2,1,0:T(2,128)}, u32[]{:S(2)}) copy-start(f32[1,2,512]{2,1,0:T(2,128)} %get-tuple-element.490) | copy-start | bytes 12292
  543.6 180.5 %copy-start.86 = (bf16[1,1,4,4,64]{4,3,2,1,0:T(4,128)(2,1)S(1)}, bf16[1,1,4,4,64]{4,3,2,1,0:T(4,128)(2,1)}, u32[]{:S(2)}) copy-start(bf16[1,1,4,4,64]{4,3,2,1,0:T(4,128)(2,1)} %param.35) | copy-start | bytes 6148
  543.6 180.8 %copy-start.83 = (f32[2,32]{1,0:T(2,128)S(1)}, f32[2,32]{1,0:T(2,128)}, u32[]{:S(2)}) copy-start(f32[2,32]{1,0:T(2,128)} %copy-done.82) | copy-start | bytes 772
  543.6 180.8 %copy-start.85 = (f32[2,32]{1,0:T(2,128)S(1)}, f32[2,32]{1,0:T(2,128)}, u32[]{:S(2)}) copy-start(f32[2,32]{1,0:T(2,128)} %copy-done.84) | copy-start | bytes 772
  543.6 182.3 %copy-start.11 = (bf16[1,1,4,4,4096]{4,3,2,1,0:T(4,128)(2,1)S(1)}, bf16[1,1,4,4,4096]{4,3,2,1,0:T(4,128)(2,1)}, u32[]{:S(2)}) copy-start(bf16[1,1,4,4,4096]{4,3,2,1,0:T(4,128)(2,1)} %param.33) | copy-start | bytes 393220
  543.6 183.1 %copy-start.18 = (bf16[4,4096]{1,0:T(4,128)(2,1)S(1)}, bf16[4,4096]{1,0:T(4,128)(2,1)}, u32[]{:S(2)}) copy-start(bf16[4,4096]{1,0:T(4,128)(2,1)} %param.24) | copy-start | bytes 98308
  543.6 191.2 %copy-start.23 = (f32[1,4096]{1,0:T(1,128)S(1)}, f32[1,4096]{1,0:T(1,128)}, u32[]{:S(2)}) copy-start(f32[1,4096]{1,0:T(1,128)} %copy-done.22) | copy-start | bytes 49156
  543.6 191.2 %copy-start.25 = (f32[1,4096]{1,0:T(1,128)S(1)}, f32[1,4096]{1,0:T(1,128)}, u32[]{:S(2)}) copy-start(f32[1,4096]{1,0:T(1,128)} %copy-done.24) | copy-start | bytes 49156
  543.6 191.2 %copy-start.27 = (f32[1,4096]{1,0:T(1,128)S(1)}, f32[1,4096]{1,0:T(1,128)}, u32[]{:S(2)}) copy-start(f32[1,4096]{1,0:T(1,128)} %copy-done.26) | copy-start | bytes 49156
  543.6 193.1 %copy-start.2 = (bf16[2,128,2,32,64]{1,4,3,2,0:T(8,128)(2,1)S(1)}, bf16[2,128,2,32,64]{1,4,3,2,0:T(8,128)(2,1)}, u32[]{:S(2)}) copy-start(bf16[2,128,2,32,64]{1,4,3,2,0:T(8,128)(2,1)} %copy-done.1) | copy-start | bytes 6291460
  543.7 193.1 %copy-start.10 = (bf16[2,128,2,256]{3,2,1,0:T(2,128)(2,1)S(1)}, bf16[2,128,2,256]{3,2,1,0:T(2,128)(2,1)}, u32[]{:S(2)}) copy-start(bf16[2,128,2,256]{3,2,1,0:T(2,128)(2,1)} %get-tuple-element.755) | copy-start | bytes 786436
  717.5 285.8 %collective-permute-start.2 = (f32[3,2,32,64,256]{4,3,2,1,0:T(8,128)}, f32[3,2,32,64,256]{4,3,2,1,0:T(8,128)}, u32[]{:S(2)}, u32[]{:S(2)}) collective-permute-start(f32[3,2,32,64,256]{4,3,2,1,0:T(8,128)} %get-tuple-element.406), channel_id=1, source_target_pairs={{0,64},{64,0},{1,65},{65,1},{2,66},{66,2},{3,67},{67,3},{4,68},{68... | collective-permute-start | bytes 37748744 | tf_op jit(solution)/shard_map/ppermute | solution.py:44
  735.6 256.0 %collective-permute-start.1 = (f32[3,3,5120]{2,0,1:T(4,128)}, f32[3,3,5120]{2,0,1:T(4,128)}, u32[]{:S(2)}, u32[]{:S(2)}) collective-permute-start(f32[3,3,5120]{2,0,1:T(4,128)} %get-tuple-element.407), channel_id=1, source_target_pairs={{0,64},{64,0},{1,65},{65,1},{2,66},{66,2},{3,67},{67,3},{4,68},{68... | collective-permute-start | bytes 552968 | tf_op jit(solution)/shard_map/ppermute | solution.py:44
  773.7 217.9 %copy-start.87 = (s32[1,1,4]{2,1,0:T(1,128)S(1)}, s32[1,1,4]{2,1,0:T(1,128)}, u32[]{:S(2)}) copy-start(s32[1,1,4]{2,1,0:T(1,128)} %param.32) | copy-start | bytes 52
  773.7 219.3 %copy-start.44 = (f32[4,2,2,256]{3,2,1,0:T(2,128)S(1)}, f32[4,2,2,256]{3,2,1,0:T(2,128)}, u32[]{:S(2)}) copy-start(f32[4,2,2,256]{3,2,1,0:T(2,128)} %reshape.1616) | copy-start | bytes 49156
  773.7 219.4 %copy-start.45 = (f32[4,2,2,256]{3,2,1,0:T(2,128)S(1)}, f32[4,2,2,256]{3,2,1,0:T(2,128)}, u32[]{:S(2)}) copy-start(f32[4,2,2,256]{3,2,1,0:T(2,128)} %reshape.1626) | copy-start | bytes 49156
  773.7 219.4 %copy-start.46 = (f32[4,2,2,256]{3,2,1,0:T(2,128)S(1)}, f32[4,2,2,256]{3,2,1,0:T(2,128)}, u32[]{:S(2)}) copy-start(f32[4,2,2,256]{3,2,1,0:T(2,128)} %reshape.1630) | copy-start | bytes 49156
  773.7 219.4 %copy-start.47 = (f32[4,2,2,256]{3,2,1,0:T(2,128)S(1)}, f32[4,2,2,256]{3,2,1,0:T(2,128)}, u32[]{:S(2)}) copy-start(f32[4,2,2,256]{3,2,1,0:T(2,128)} %reshape.1634) | copy-start | bytes 49156
  773.8 219.4 %copy-start.67 = (f32[2,2,256]{2,1,0:T(2,128)S(1)}, f32[2,2,256]{2,1,0:T(2,128)}, u32[]{:S(2)}) copy-start(f32[2,2,256]{2,1,0:T(2,128)} %broadcast_in_dim.369) | copy-start | bytes 12292
  773.8 219.4 %copy-start.68 = (f32[2,2,256]{2,1,0:T(2,128)S(1)}, f32[2,2,256]{2,1,0:T(2,128)}, u32[]{:S(2)}) copy-start(f32[2,2,256]{2,1,0:T(2,128)} %reshape.1615) | copy-start | bytes 12292
  773.8 219.4 %copy-start.69 = (f32[2,2,256]{2,1,0:T(2,128)S(1)}, f32[2,2,256]{2,1,0:T(2,128)}, u32[]{:S(2)}) copy-start(f32[2,2,256]{2,1,0:T(2,128)} %reshape.1613) | copy-start | bytes 12292
  773.8 219.4 %copy-start.70 = (f32[2,2,256]{2,1,0:T(2,128)S(1)}, f32[2,2,256]{2,1,0:T(2,128)}, u32[]{:S(2)}) copy-start(f32[2,2,256]{2,1,0:T(2,128)} %reshape.1611) | copy-start | bytes 12292
  773.8 219.4 %copy-start.71 = (f32[2,2,256]{2,1,0:T(2,128)S(1)}, f32[2,2,256]{2,1,0:T(2,128)}, u32[]{:S(2)}) copy-start(f32[2,2,256]{2,1,0:T(2,128)} %reshape.1609) | copy-start | bytes 12292
  773.8 221.1 %copy-start.14 = (f32[4,2,32,64]{3,2,1,0:T(8,128)S(1)}, f32[4,2,32,64]{3,2,1,0:T(8,128)}, u32[]{:S(2)}) copy-start(f32[4,2,32,64]{3,2,1,0:T(8,128)} %reshape.1624) | copy-start | bytes 196612
  773.8 221.1 %copy-start.15 = (f32[4,2,32,64]{3,2,1,0:T(8,128)S(1)}, f32[4,2,32,64]{3,2,1,0:T(8,128)}, u32[]{:S(2)}) copy-start(f32[4,2,32,64]{3,2,1,0:T(8,128)} %reshape.1628) | copy-start | bytes 196612
  773.8 221.1 %copy-start.16 = (f32[4,2,32,64]{3,2,1,0:T(8,128)S(1)}, f32[4,2,32,64]{3,2,1,0:T(8,128)}, u32[]{:S(2)}) copy-start(f32[4,2,32,64]{3,2,1,0:T(8,128)} %reshape.1632) | copy-start | bytes 196612
  773.8 221.1 %copy-start.17 = (f32[4,2,32,64]{3,2,1,0:T(8,128)S(1)}, f32[4,2,32,64]{3,2,1,0:T(8,128)}, u32[]{:S(2)}) copy-start(f32[4,2,32,64]{3,2,1,0:T(8,128)} %reshape.1636) | copy-start | bytes 196612
  773.8 221.1 %copy-start.35 = (f32[2,32,64]{2,1,0:T(8,128)S(1)}, f32[2,32,64]{2,1,0:T(8,128)}, u32[]{:S(2)}) copy-start(f32[2,32,64]{2,1,0:T(8,128)} %broadcast_in_dim.380) | copy-start | bytes 49156
  773.9 221.1 %copy-start.36 = (f32[2,32,64]{2,1,0:T(8,128)S(1)}, f32[2,32,64]{2,1,0:T(8,128)}, u32[]{:S(2)}) copy-start(f32[2,32,64]{2,1,0:T(8,128)} %mul.1070) | copy-start | bytes 49156
  773.9 221.1 %copy-start.37 = (f32[2,32,64]{2,1,0:T(8,128)S(1)}, f32[2,32,64]{2,1,0:T(8,128)}, u32[]{:S(2)}) copy-start(f32[2,32,64]{2,1,0:T(8,128)} %mul.1067) | copy-start | bytes 49156
  773.9 221.1 %copy-start.38 = (f32[2,32,64]{2,1,0:T(8,128)S(1)}, f32[2,32,64]{2,1,0:T(8,128)}, u32[]{:S(2)}) copy-start(f32[2,32,64]{2,1,0:T(8,128)} %mul.1064) | copy-start | bytes 49156
  773.9 221.1 %copy-start.39 = (f32[2,32,64]{2,1,0:T(8,128)S(1)}, f32[2,32,64]{2,1,0:T(8,128)}, u32[]{:S(2)}) copy-start(f32[2,32,64]{2,1,0:T(8,128)} %mul.1061) | copy-start | bytes 49156
  773.9 221.1 %copy-start.58 = (f32[4,2,32]{2,1,0:T(2,128)S(1)}, f32[4,2,32]{2,1,0:T(2,128)}, u32[]{:S(2)}) copy-start(f32[4,2,32]{2,1,0:T(2,128)} %copy.231) | copy-start | bytes 3076
  773.9 221.1 %copy-start.59 = (f32[4,2,32]{2,1,0:T(2,128)S(1)}, f32[4,2,32]{2,1,0:T(2,128)}, u32[]{:S(2)}) copy-start(f32[4,2,32]{2,1,0:T(2,128)} %copy.235) | copy-start | bytes 3076
  773.9 221.1 %copy-start.60 = (f32[4,2,32]{2,1,0:T(2,128)S(1)}, f32[4,2,32]{2,1,0:T(2,128)}, u32[]{:S(2)}) copy-start(f32[4,2,32]{2,1,0:T(2,128)} %copy.239) | copy-start | bytes 3076
  773.9 221.1 %copy-start.61 = (f32[4,2,32]{2,1,0:T(2,128)S(1)}, f32[4,2,32]{2,1,0:T(2,128)}, u32[]{:S(2)}) copy-start(f32[4,2,32]{2,1,0:T(2,128)} %copy.243) | copy-start | bytes 3076
  995.3 7.8 copy-start.30
  1111.6 23.5 %copy-start.28 = (f32[1,1,1,4,4096]{4,3,2,1,0:T(4,128)S(1)}, f32[1,1,1,4,4096]{4,3,2,1,0:T(4,128)}, u32[]{:S(2)}) copy-start(f32[1,1,1,4,4096]{4,3,2,1,0:T(4,128)} %convert_multiply_fusion.9) | copy-start | bytes 196612
  (41 other events, 189.4 us)
Sparse Core Ops, SparseCore 0:
  70.8 341.7 all-gather.2
  543.8 173.5 all-reduce.3
where the time goes:
time: 1160 us; the launch traced here: 1140 us
  waiting for transfers between devices  647 us (56%)
  other arithmetic  172 us (15%)
  matrix products  172 us (15%)
  local copies, waits for them, and re-layouts  94.4 us (8%)
  blocking collectives  25.6 us (2%)
  between operations  23 us (2%)
    all_gather x1, waiting for transfers between devices, carried_in(): pieces = jax.tree.map(lambda part: lax.all_gather(part, axis), value)  263 us
    ppermute x2, waiting for transfers between devices, swapped(): return lax.ppermute(block, axis, route)  211 us
    psum x1, waiting for transfers between devices, on_device(): state_total, cache_total = lax.psum((finals, caches), 'dp')  174 us
    select_n x15, other arithmetic, lap(): jnp.where(position < mine, new, old)  92.5 us
    dot_general x4, matrix products, decode_parts(): jnp.einsum('rgn,rgkpn->rgkp', c_rows, carry_state, precision=HIGHEST_PREC...  81.2 us
    dot_general x1, matrix products, on_device(): jnp.einsum('rq,qgkpn->rgkpn', selector, state_other, precision=HIGHEST_PR...  50.1 us
    all_gather x1, blocking collectives, carried_in(): pieces = jax.tree.map(lambda part: lax.all_gather(part, axis), value)  25.6 us
  transfers between devices with their start and end apart: 5, of which 3 were waited for; matrix products, arithmetic and copies ran while one was open for 11% of the time, Pallas kernels for 0%

commit v1 on v0

v1 whole, which is shorter than its diff:
```python
import functools

import jax
import jax.numpy as jnp
from jax import lax
from jax.experimental import pallas as pl
from jax.experimental.pallas import tpu as pltpu
from jax.sharding import PartitionSpec as P

HEAD_DIM = 64
STATE = 256
CONV = 4
BLOCK = 128
PROMPTS = 3
STEPS = 4
ROWS = 4
CORES = 2
RING = 4
LANES = 128
REP = 32
CHIP_TOKENS = 512
BLOCKS = CHIP_TOKENS // BLOCK
GROUP_CH = 2048
CHUNK = GROUP_CH // RING
WIDE = GROUP_CH + 1024
LOG2E = 1.4426950408889634
F32 = jnp.float32
BF16 = jnp.bfloat16
VMEM = 56 * 1024 * 1024


def split3(value):
    high = value.astype(BF16).astype(F32)
    rest = value - high
    middle = rest.astype(BF16).astype(F32)
    return high, middle, rest - middle


def pack3(value):
    high, middle, low = split3(value)
    lane = lax.broadcasted_iota(jnp.int32, value.shape, 1)
    return jnp.where(lane < REP, high, jnp.where(lane < 2 * REP, middle, low)).astype(BF16)


def spread_matrix(chunk):
    lane = lax.broadcasted_iota(jnp.int32, (LANES, CHUNK), 0)
    head = lax.broadcasted_iota(jnp.int32, (LANES, CHUNK), 1) // HEAD_DIM + chunk * (CHUNK // HEAD_DIM)
    hit = ((lane & (REP - 1)) == head) & (lane < 3 * REP)
    return jnp.where(hit, 1.0, 0.0).astype(BF16)


def mm(a, b):
    return jnp.dot(a, b, preferred_element_type=F32)


def silu(value):
    half = 0.5 * value
    return half + half * jnp.tanh(half)


def softplus(value):
    return jnp.maximum(value, 0.0) + jnp.log1p(jnp.exp(-jnp.abs(value)))


def seg_vec(s_ref, pos):
    anchor, lo0, lo1 = s_ref[3], s_ref[4], s_ref[5]
    seg = (pos >= lo0).astype(jnp.int32) + (pos >= lo1).astype(jnp.int32)
    return jnp.where(pos < -anchor, -1, seg)


def seg_at(s_ref, pos):
    anchor, lo0, lo1 = s_ref[3], s_ref[4], s_ref[5]
    seg = jnp.where(pos >= lo0, 1, 0) + jnp.where(pos >= lo1, 1, 0)
    return jnp.where(pos + anchor < 0, -1, seg)


def rows_of(parts, count, width):
    row = lax.broadcasted_iota(jnp.int32, (count, width), 0)
    out = jnp.zeros((count, width), F32)
    for index, part in enumerate(parts):
        out = jnp.where(row == index, part, out)
    return out


def conv_rows(src, start, weight, offset, mask):
    lanes = offset.shape[1]
    running = jnp.broadcast_to(offset, (BLOCK, lanes))
    for tap in range(CONV):
        term = weight[tap : tap + 1] * src[pl.ds(5 + tap + start, BLOCK), :]
        if tap < CONV - 1:
            keep = mask[tap, pl.ds(start, BLOCK), :]
            term = term * jnp.concatenate([keep] * (lanes // LANES), axis=1)
        running = running + term
    return silu(running)


def cache_rows(s_ref, src, out):
    out[...] = jnp.zeros_like(out)
    for prompt in range(PROMPTS):
        last = (s_ref[4] - 1, s_ref[5] - 1, RING * CORES * CHIP_TOKENS - 1 - s_ref[3])[prompt]

        @pl.when((last >= 0) & (last < CHIP_TOKENS))
        def _():
            for tap in range(CONV - 1):
                row = last - (CONV - 2) + tap
                same = jnp.where(seg_at(s_ref, row) == seg_at(s_ref, last), 1.0, 0.0)
                value = src[pl.ds(row + 8, 1), :]
                out[pl.ds(prompt * 3 + tap, 1), :] = jnp.where(same > 0.5, value, 0.0)


def cut_of(s_ref):
    first, second = s_ref[4] - 1, s_ref[5] - 1
    limit = CHIP_TOKENS - 1
    one = jnp.where((second >= 0) & (second < limit), second, -1)
    return jnp.where((first >= 0) & (first < limit), first, one)


def kernel_a(
    s_ref, x_own, x_rec, halo_x, wx, bx, g_own, g_rec, halo_g, wg, bg, vecs,
    l0, l1, l2, l3, xc_out, bcc_out, dtc_out, wc3_out, cx_out, cg_out,
    xs, gs, mask, wp3, keep3, bt, cache,
):
    m = pl.program_id(0)
    core = s_ref[0]
    chunk = s_ref[1] ^ m
    first = core == 0
    half = CHIP_TOKENS // 2

    @pl.when(m == 0)
    def _():
        pos = lax.broadcasted_iota(jnp.int32, (CHIP_TOKENS, LANES), 0)
        own_seg = seg_vec(s_ref, pos)
        for tap in range(CONV - 1):
            mask[tap] = jnp.where(seg_vec(s_ref, pos - 3 + tap) == own_seg, 1.0, 0.0)
        gs[0:8] = halo_g[:, 0:512].astype(F32)
        gs[8 : 8 + half] = jnp.where(first, g_own[:, 0:512], g_rec[:, 0:512]).astype(F32)
        gs[8 + half :] = jnp.where(first, g_rec[:, 0:512], g_own[:, 0:512]).astype(F32)
        weight = wg[...].astype(F32)
        for j in range(BLOCKS):
            both = conv_rows(gs, j * BLOCK, weight, bg[...], mask).astype(BF16)
            bcc_out[pl.ds(j * BLOCK, BLOCK), :] = both
            bt[j] = both[:, 0:STATE].astype(F32).T.astype(BF16)
        cache_rows(s_ref, gs, cache)
        cg_out[...] = cache[...].astype(BF16)
        raw_a = jnp.where(first, g_own[:, 512:640], g_rec[:, 512:640]).astype(F32)
        raw_b = jnp.where(first, g_rec[:, 512:640], g_own[:, 512:640]).astype(F32)
        dt = softplus(jnp.concatenate([raw_a, raw_b], axis=0) + vecs[0:1])
        decay = dt * vecs[1:2]
        row = lax.broadcasted_iota(jnp.int32, (BLOCK, BLOCK), 0)
        col = lax.broadcasted_iota(jnp.int32, (BLOCK, BLOCK), 1)
        lower = jnp.where(row >= col, 1.0, 0.0).astype(BF16)
        dtc_out[0:CHIP_TOKENS] = dt
        total = jnp.zeros((1, LANES), F32)
        before = seg_at(s_ref, -1)
        keeps = []
        for j in range(BLOCKS):
            rows = slice(j * BLOCK, (j + 1) * BLOCK)
            high, middle, low = split3(decay[rows])
            cum = mm(lower, high.astype(BF16)) + mm(lower, middle.astype(BF16)) + mm(lower, low.astype(BF16))
            dtc_out[CHIP_TOKENS + j * BLOCK : CHIP_TOKENS + (j + 1) * BLOCK] = cum
            end = cum[BLOCK - 1 :]
            end_seg = seg_at(s_ref, (j + 1) * BLOCK - 1)
            weight_p = jnp.where(own_seg[rows] == end_seg, jnp.exp2(end - cum) * dt[rows], 0.0)
            wp3[pl.ds(j * BLOCK, BLOCK), :] = pack3(weight_p)
            reach = jnp.where(own_seg[rows] == before, jnp.exp2(total + cum), 0.0)
            wc3_out[pl.ds(j * BLOCK, BLOCK), :] = pack3(reach)
            keeps.append(jnp.where(seg_at(s_ref, j * BLOCK - 1) == end_seg, jnp.exp2(end), 0.0))
            total = total + end
        keeps.append(jnp.where(before == seg_at(s_ref, CHIP_TOKENS - 1), jnp.exp2(total), 0.0))
        keep3[...] = pack3(rows_of(keeps, 16, LANES))

    xs[0:8] = halo_x[...].astype(F32)
    xs[8 : 8 + half] = jnp.where(first, x_own[...], x_rec[...]).astype(F32)
    xs[8 + half :] = jnp.where(first, x_rec[...], x_own[...]).astype(F32)
    weight = wx[...].astype(F32)
    spread = spread_matrix(chunk)
    keep = mm(keep3[...], spread)
    state = None
    for j in range(BLOCKS):
        xc = conv_rows(xs, j * BLOCK, weight, bx[...], mask).astype(BF16)
        xc_out[pl.ds(j * BLOCK, BLOCK), :] = xc
        scaled = (xc.astype(F32) * mm(wp3[pl.ds(j * BLOCK, BLOCK), :], spread)).astype(BF16)
        fresh = mm(bt[j], scaled)
        state = fresh if j == 0 else keep[j : j + 1] * state + fresh
    cache_rows(s_ref, xs, cache)
    cx_out[...] = cache[...].astype(BF16)
    tail = rows_of(split3(keep[BLOCKS : BLOCKS + 1]), 16, CHUNK).astype(BF16)
    for index, out in enumerate((l0, l1, l2, l3)):

        @pl.when(m == index)
        def _():
            out[0:STATE] = state.astype(BF16)
            out[STATE:] = tail


def run_a(scalars, x_in, recv, halo, wx, bx, g_own, wg, bg, vecs):
    def fixed(shape):
        return pl.BlockSpec(shape, lambda m, s: (0,) * len(shape))

    def chunked(rows, per_core=0):
        return pl.BlockSpec((rows, CHUNK), lambda m, s: (0, s[0] * per_core + (s[1] ^ m)))

    half = CHIP_TOKENS // 2
    side = pl.BlockSpec((half, 1024), lambda m, s: (0, 2))
    return pl.pallas_call(
        kernel_a,
        grid_spec=pltpu.PrefetchScalarGridSpec(
            num_scalar_prefetch=1,
            grid=(RING,),
            in_specs=[
                chunked(half, RING), chunked(half), chunked(8), chunked(CONV, RING), chunked(1, RING),
                fixed((half, 1024)), side, pl.BlockSpec((8, 1024), lambda m, s: (0, 2)),
                fixed((CONV, 512)), fixed((1, 512)), fixed((8, LANES)),
            ],
            out_specs=[fixed((STATE + 16, CHUNK))] * RING + [
                chunked(CHIP_TOKENS), fixed((CHIP_TOKENS, 512)), fixed((2 * CHIP_TOKENS, LANES)),
                fixed((CHIP_TOKENS, LANES)), chunked(16), fixed((16, 512)),
            ],
            scratch_shapes=[
                pltpu.VMEM((CHIP_TOKENS + 8, CHUNK), F32),
                pltpu.VMEM((CHIP_TOKENS + 8, 512), F32),
                pltpu.VMEM((CONV - 1, CHIP_TOKENS, LANES), F32),
                pltpu.VMEM((CHIP_TOKENS, LANES), BF16),
                pltpu.VMEM((16, LANES), BF16),
                pltpu.VMEM((BLOCKS, STATE, BLOCK), BF16),
                pltpu.VMEM((16, CHUNK), F32),
            ],
        ),
        out_shape=[jax.ShapeDtypeStruct((STATE + 16, CHUNK), BF16)] * RING + [
            jax.ShapeDtypeStruct((CHIP_TOKENS, GROUP_CH), BF16),
            jax.ShapeDtypeStruct((CHIP_TOKENS, 512), BF16),
            jax.ShapeDtypeStruct((2 * CHIP_TOKENS, LANES), F32),
            jax.ShapeDtypeStruct((CHIP_TOKENS, LANES), BF16),
            jax.ShapeDtypeStruct((16, GROUP_CH), BF16),
            jax.ShapeDtypeStruct((16, 512), BF16),
        ],
        compiler_params=pltpu.CompilerParams(vmem_limit_bytes=VMEM),
        cost_estimate=pl.CostEstimate(flops=6 * 10**9, bytes_accessed=8 * 10**6, transcendentals=10**6),
        name="conv_and_states",
    )(scalars, x_in, recv, halo, wx, bx, g_own, recv, halo, wg, bg, vecs)


def kernel_b(
    s_ref, xc_ref, bcc, dtc, skip, cx, cg,
    f0, f1, f2, f3, local_out,
    wp3, wb3, keep3, bt, gm, cum_t, dt_t, wf3,
):
    m = pl.program_id(0)
    chunk = s_ref[1] ^ m
    cut = cut_of(s_ref)
    cut_block = cut // BLOCK

    @pl.when(m == 0)
    def _():
        pos = lax.broadcasted_iota(jnp.int32, (BLOCK, LANES), 0)
        row = lax.broadcasted_iota(jnp.int32, (BLOCK, BLOCK), 0)
        col = lax.broadcasted_iota(jnp.int32, (BLOCK, BLOCK), 1)
        total = jnp.zeros((1, LANES), F32)
        before = seg_at(s_ref, -1)
        keeps = []
        cut_keep = jnp.zeros((1, LANES), F32)
        cut_reach = jnp.zeros((1, LANES), F32)
        cut_row = dtc[pl.ds(CHIP_TOKENS + jnp.maximum(cut, 0), 1), :]
        cut_seg = seg_at(s_ref, cut)
        wf3[...] = jnp.zeros_like(wf3)
        for j in range(BLOCKS):
            dt = dtc[j * BLOCK : (j + 1) * BLOCK]
            cum = dtc[CHIP_TOKENS + j * BLOCK : CHIP_TOKENS + (j + 1) * BLOCK]
            end = cum[BLOCK - 1 :]
            seg = seg_vec(s_ref, pos + j * BLOCK)
            end_seg = seg_at(s_ref, (j + 1) * BLOCK - 1)
            prev_seg = seg_at(s_ref, j * BLOCK - 1)
            wp3[pl.ds(j * BLOCK, BLOCK), :] = pack3(jnp.where(seg == end_seg, jnp.exp2(end - cum) * dt, 0.0))
            wb3[pl.ds(j * BLOCK, BLOCK), :] = pack3(jnp.where(seg == prev_seg, jnp.exp2(cum), 0.0))
            keeps.append(jnp.where(prev_seg == end_seg, jnp.exp2(end), 0.0))
            b_rows = bcc[pl.ds(j * BLOCK, BLOCK), 0:STATE]
            c_rows = bcc[pl.ds(j * BLOCK, BLOCK), STATE : 2 * STATE]
            b_t = b_rows.astype(F32).T.astype(BF16)
            bt[j] = b_t
            scores = mm(c_rows, b_t)
            same = seg_vec(s_ref, row + j * BLOCK) == seg_vec(s_ref, col + j * BLOCK)
            gm[j] = jnp.where((row >= col) & same, scores, 0.0)
            cum_t[j] = cum.T
            dt_t[j] = dt.T
            here = cut_block == j
            cut_keep = jnp.where(here & (cut_seg == prev_seg), jnp.exp2(cut_row), cut_keep)
            cut_reach = jnp.where(here & (cut_seg == before), jnp.exp2(total + cut_row), cut_reach)

            @pl.when((cut >= 0) & here)
            def _():
                chosen = (seg == cut_seg) & (pos + j * BLOCK <= cut)
                wf3[...] = pack3(jnp.where(chosen, jnp.exp2(jnp.minimum(cut_row - cum, 0.0)) * dt, 0.0))

            total = total + end
        keep3[...] = pack3(rows_of(keeps + [cut_keep, cut_reach], 16, LANES))

    spread = spread_matrix(chunk)
    keep = mm(keep3[...], spread)
    half_lane = lax.broadcasted_iota(jnp.int32, (BLOCK, LANES), 1) < HEAD_DIM
    outs = (f0, f1, f2, f3)
    for index, out in enumerate(outs):

        @pl.when(m == index)
        def _():
            out[0:STATE] = jnp.zeros((STATE, CHUNK), BF16)
            out[STATE : STATE + 16] = rows_of(split3(keep[BLOCKS + 1 : BLOCKS + 2]), 16, CHUNK).astype(BF16)
            out[STATE + 16 : STATE + 32] = cx[...]
            out[STATE + 32 : STATE + 48] = cg[...]

    state = None
    pairs = CHUNK // LANES
    for j in range(BLOCKS):
        rows = slice(j * BLOCK, (j + 1) * BLOCK)
        xc = xc_ref[rows]
        xf = xc.astype(F32)
        base = skip[...] * xf
        if j > 0:
            high = state.astype(BF16)
            low = (state - high.astype(F32)).astype(BF16)
            c_rows = bcc[rows, STATE : 2 * STATE]
            base = base + mm(wb3[rows], spread) * (mm(c_rows, high) + mm(c_rows, low))

        def cut_state(state, xf):
            scaled = (xf * mm(wf3[...], spread)).astype(BF16)
            fresh = mm(bt[j], scaled)
            if j > 0:
                fresh = keep[BLOCKS : BLOCKS + 1] * state + fresh
            for index, out in enumerate(outs):

                @pl.when(m == index)
                def _():
                    out[0:STATE] = fresh.astype(BF16)

        @pl.when((cut >= 0) & (cut_block == j))
        def _():
            cut_state(state, xf)

        if j < BLOCKS - 1:
            scaled = (xf * mm(wp3[rows], spread)).astype(BF16)
            fresh = mm(bt[j], scaled)
            state = fresh if j == 0 else keep[j : j + 1] * state + fresh
        cum = dtc[CHIP_TOKENS + j * BLOCK : CHIP_TOKENS + (j + 1) * BLOCK]
        heads = chunk * (CHUNK // HEAD_DIM)
        turned = pltpu.roll(cum, LANES - heads, 1)
        cum_rows = cum_t[j, pl.ds(pl.multiple_of(heads, 8), 8), :]
        dt_rows = dt_t[j, pl.ds(pl.multiple_of(heads, 8), 8), :]
        score = gm[j]
        for pair in range(pairs):
            weights = []
            for head in (2 * pair, 2 * pair + 1):
                gap = jnp.minimum(turned[:, head : head + 1] - cum_rows[head : head + 1], 0.0)
                weights.append((jnp.exp2(gap) * (score * dt_rows[head : head + 1])).astype(BF16))
            lanes = slice(pair * LANES, (pair + 1) * LANES)
            two = xc[:, lanes]
            zero = jnp.zeros_like(two)
            stacked = jnp.concatenate([jnp.where(half_lane, two, zero), jnp.where(half_lane, zero, two)], axis=0)
            inner = mm(jnp.concatenate(weights, axis=1), stacked)
            local_out[rows, lanes] = inner + base[:, lanes]


def run_b(scalars, xc, bcc, dtc, skip, cx, cg):
    def fixed(shape):
        return pl.BlockSpec(shape, lambda m, s: (0,) * len(shape))

    def chunked(rows, per_core=0):
        return pl.BlockSpec((rows, CHUNK), lambda m, s: (0, s[0] * per_core + (s[1] ^ m)))

    return pl.pallas_call(
        kernel_b,
        grid_spec=pltpu.PrefetchScalarGridSpec(
            num_scalar_prefetch=1,
            grid=(RING,),
            in_specs=[
                chunked(CHIP_TOKENS), fixed((CHIP_TOKENS, 512)), fixed((2 * CHIP_TOKENS, LANES)),
                chunked(1, RING), chunked(16), fixed((16, 512)),
            ],
            out_specs=[fixed((STATE + 48, CHUNK))] * RING + [chunked(CHIP_TOKENS)],
            scratch_shapes=[
                pltpu.VMEM((CHIP_TOKENS, LANES), BF16),
                pltpu.VMEM((CHIP_TOKENS, LANES), BF16),
                pltpu.VMEM((16, LANES), BF16),
                pltpu.VMEM((BLOCKS, STATE, BLOCK), BF16),
                pltpu.VMEM((BLOCKS, BLOCK, BLOCK), F32),
                pltpu.VMEM((BLOCKS, LANES, BLOCK), F32),
                pltpu.VMEM((BLOCKS, LANES, BLOCK), F32),
                pltpu.VMEM((BLOCK, LANES), BF16),
            ],
        ),
        out_shape=[jax.ShapeDtypeStruct((STATE + 48, CHUNK), BF16)] * RING
        + [jax.ShapeDtypeStruct((CHIP_TOKENS, GROUP_CH), F32)],
        compiler_params=pltpu.CompilerParams(vmem_limit_bytes=VMEM),
        cost_estimate=pl.CostEstimate(flops=12 * 10**9, bytes_accessed=8 * 10**6, transcendentals=2 * 10**6),
        name="output_within_chip",
    )(scalars, xc, bcc, dtc, skip, cx, cg)


def pick(refs, which, rows):
    out = refs[0][rows]
    for index in range(1, len(refs)):
        out = jnp.where(which == index, refs[index][rows], out)
    return out.astype(F32)


def decay_rows(tile):
    return tile[0:1] + tile[1:2] + tile[2:3]


def kernel_total(s_ref, l0, l1, l2, l3, total_out):
    state = jnp.zeros((STATE, CHUNK), F32)
    for chip in range(RING):
        which = s_ref[1] ^ chip
        part = pick((l0, l1, l2, l3), which, slice(0, STATE))
        factor = decay_rows(pick((l0, l1, l2, l3), which, slice(STATE, STATE + 16)))
        state = factor * state + part
    total_out[...] = state.astype(BF16)


def kernel_starts(s_ref, l0, l1, l2, l3, start, r0, r1, r2, r3):
    state = start[...].astype(F32)
    for chip in range(RING):
        which = s_ref[1] ^ chip
        for index, out in enumerate((r0, r1, r2, r3)):

            @pl.when(which == index)
            def _():
                out[...] = state.astype(BF16)

        if chip < RING - 1:
            part = pick((l0, l1, l2, l3), which, slice(0, STATE))
            factor = decay_rows(pick((l0, l1, l2, l3), which, slice(STATE, STATE + 16)))
            state = factor * state + part


def whole_call(kernel, out_shape, name, flops, scratch=()):
    def run(scalars, *args):
        return pl.pallas_call(
            kernel,
            in_specs=[pl.BlockSpec(memory_space=pltpu.SMEM)] + [pl.BlockSpec(memory_space=pltpu.VMEM)] * len(args),
            out_specs=jax.tree.map(lambda _: pl.BlockSpec(memory_space=pltpu.VMEM), out_shape),
            out_shape=out_shape,
            scratch_shapes=list(scratch),
            compiler_params=pltpu.CompilerParams(vmem_limit_bytes=VMEM),
            cost_estimate=pl.CostEstimate(flops=flops, bytes_accessed=3 * 10**6, transcendentals=0),
            name=name,
        )(scalars, *args)

    return run


def kernel_decode(
    s_ref, l0, l1, l2, l3, start, f0, f1, f2, f3, d0, d1, d2, d3,
    wx, bx, wg, bg, vecs, skip, bounds,
    keep_out, send_out,
    final, rows_f32, result,
):
    z, upper = s_ref[1], s_ref[2]
    ls, fs, ds = (l0, l1, l2, l3), (f0, f1, f2, f3), (d0, d1, d2, d3)
    lasts = [bounds[q] - 1 for q in range(PROMPTS)]
    final[...] = jnp.zeros_like(final)
    state = start[...].astype(F32)
    for chip in range(RING):
        which = z ^ chip
        origin = (upper * RING + chip) * CHIP_TOKENS
        part = pick(ls, which, slice(0, STATE))
        factor = decay_rows(pick(ls, which, slice(STATE, STATE + 16)))
        after = factor * state + part
        for q in range(PROMPTS):
            local = lasts[q] - origin

            @pl.when(local == CHIP_TOKENS - 1)
            def _():
                final[q] = after

            @pl.when((local >= 0) & (local < CHIP_TOKENS - 1))
            def _():
                fresh = pick(fs, which, slice(0, STATE))
                reach = decay_rows(pick(fs, which, slice(STATE, STATE + 16)))
                final[q] = fresh + reach * state

        state = after
    cache_x = sum(f[STATE + 16 : STATE + 32].astype(F32) for f in fs)
    cache_g = sum(f[STATE + 32 : STATE + 48].astype(F32) for f in fs)
    spread = spread_matrix(z)
    for index, d in enumerate(ds):
        rows_f32[index] = d[...].astype(F32)

    def step_rows(step, lanes):
        tiles = [
            rows_f32[index, 32 * side + 8 * step : 32 * side + 8 * step + 8, lanes]
            for index in range(RING)
            for side in range(2)
        ]
        return jnp.concatenate(tiles, axis=0)

    prompt = step_rows(0, slice(1024, 1152))[:, 96:97]
    chosen = [prompt == float(q) for q in range(PROMPTS)]
    mine = jnp.zeros_like(prompt)
    for q in range(PROMPTS):
        inside = jnp.where(lasts[q] // (RING * CHIP_TOKENS) == upper, 1.0, 0.0)
        mine = jnp.where(chosen[q], inside, mine)

    def window(cache, lanes):
        rows = []
        for tap in range(CONV - 1):
            row = jnp.zeros((STEPS * 16, CHUNK), F32)
            for q in range(PROMPTS):
                row = jnp.where(chosen[q], cache[3 * q + tap : 3 * q + tap + 1], row)
            rows.append(row)
        return rows + [step_rows(step, lanes) for step in range(STEPS)]

    def convolved(rows, weight, offset):
        out = []
        for step in range(STEPS):
            running = jnp.broadcast_to(offset, rows[0].shape)
            for tap in range(CONV):
                running = running + weight[tap : tap + 1] * rows[step + tap]
            out.append(silu(running).astype(BF16))
        return out

    mixed = convolved(window(cache_x, slice(0, 512)), wx[...].astype(F32), bx[...])
    both = convolved(window(cache_g, slice(512, 1024)), wg[...].astype(F32), bg[...])
    steps, fades = [], []
    fade = jnp.zeros((STEPS * 16, LANES), F32)
    for step in range(STEPS):
        dt = softplus(step_rows(step, slice(1024, 1152)) + vecs[0:1])
        fade = fade + dt * vecs[1:2]
        steps.append(dt)
        fades.append(fade)
    readers = jnp.concatenate([rows[:, STATE:] for rows in both], axis=0)
    readout = jnp.zeros((STEPS * STEPS * 16, CHUNK), F32)
    for q in range(PROMPTS):
        high = final[q].astype(BF16)
        low = (final[q] - high.astype(F32)).astype(BF16)
        value = mm(readers, high) + mm(readers, low)
        readout = jnp.where(jnp.concatenate([chosen[q]] * STEPS, axis=0), value, readout)
    for step in range(STEPS):
        mixed_now = mixed[step].astype(F32)
        total = readout[64 * step : 64 * step + 64] * mm(pack3(jnp.exp2(fades[step])), spread)
        total = total + skip[...] * mixed_now
        reader = both[step][:, STATE:].astype(F32)
        for past in range(step + 1):
            weight = steps[past]
            if past < step:
                weight = weight * jnp.exp2(fades[step] - fades[past])
            product = jnp.sum(reader * both[past][:, 0:STATE].astype(F32), axis=1, keepdims=True)
            total = total + mm(pack3(weight), spread) * (product * mixed[past].astype(F32))
        total = jnp.where(mine > 0.5, total, 0.0)
        for index in range(RING):
            for side in range(2):
                tile = total[8 * (2 * index + side) : 8 * (2 * index + side) + 8]
                result[index, 32 * side + 8 * step : 32 * side + 8 * step + 8, :] = tile
    for index in range(RING):
        keep_out[index] = result[index, pl.ds(pl.multiple_of(32 * upper, 32), 32), :].astype(BF16)
        send_out[index] = result[index, pl.ds(pl.multiple_of(32 * (1 - upper), 32), 32), :].astype(BF16)


def kernel_d(s_ref, local, c_rows, wc3, r0, r1, r2, r3, out):
    m = pl.program_id(0)
    spread = spread_matrix(s_ref[1] ^ m)
    factor = mm(wc3[...], spread)
    for index, r in enumerate((r0, r1, r2, r3)):

        @pl.when(m == index)
        def _():
            out[...] = (local[...] + factor * mm(c_rows[...], r[...])).astype(BF16)


def run_d(scalars, local, bcc, wc3, starts, own):
    half = CHIP_TOKENS // 2

    def row(s):
        return s[0] if own else 1 - s[0]

    return pl.pallas_call(
        kernel_d,
        grid_spec=pltpu.PrefetchScalarGridSpec(
            num_scalar_prefetch=1,
            grid=(RING,),
            in_specs=[
                pl.BlockSpec((half, CHUNK), lambda m, s: (row(s), s[1] ^ m)),
                pl.BlockSpec((half, STATE), lambda m, s: (row(s), 1)),
                pl.BlockSpec((half, LANES), lambda m, s: (row(s), 0)),
            ] + [pl.BlockSpec((STATE, CHUNK), lambda m, s: (0, 0))] * RING,
            out_specs=pl.BlockSpec((half, CHUNK), lambda m, s: (0, s[1] ^ m)),
        ),
        out_shape=jax.ShapeDtypeStruct((half, GROUP_CH), BF16),
        compiler_params=pltpu.CompilerParams(vmem_limit_bytes=VMEM),
        cost_estimate=pl.CostEstimate(flops=10**9, bytes_accessed=4 * 10**6, transcendentals=0),
        name="carried_own" if own else "carried_other",
    )(scalars, local, bcc, wc3, *starts)


def on_device(
    x_in, bc_in, dt_raw, conv_w_x, conv_b_x, conv_w_bc, conv_b_bc, dt_bias, a_log, d_skip,
    lengths, decode_prompt, dec_x, dec_bc, dec_dt,
):
    count = lax.axis_size("dp")
    place = lax.axis_index("dp")
    core = place % CORES
    z = (place // CORES) % RING
    upper = place // (CORES * RING)
    anchor = (place // CORES) * CHIP_TOKENS
    bounds = jnp.cumsum(lengths[0]).astype(jnp.int32)
    zero = jnp.int32(0)
    scalars = jnp.stack([core, z, upper, anchor, bounds[0] - anchor, bounds[1] - anchor, zero, zero]).astype(jnp.int32)
    both = ("pool", "dp")

    def group_part(x, bc, dt, group, extra=None):
        rows = x.shape[0]
        channels = lax.dynamic_slice_in_dim(x, group * GROUP_CH, GROUP_CH, 1)
        return jnp.concatenate([channels, group_side(bc, dt, group, extra)], axis=1).reshape(rows, WIDE)

    def group_side(bc, dt, group, extra=None):
        rows = bc.shape[0]
        b_c = lax.dynamic_slice_in_dim(bc, group * STATE, STATE, 2).reshape(rows, 2 * STATE)
        steps = lax.dynamic_slice_in_dim(dt, group * REP, REP, 1)
        last = jnp.zeros((rows, REP), BF16) if extra is None else jnp.broadcast_to(extra, (rows, REP))
        return jnp.concatenate([b_c, steps, steps, steps, last, jnp.zeros((rows, 384), BF16)], axis=1)

    tokens, bc_rows, dt_rows = x_in[0], bc_in[0], dt_raw[0]
    recv = lax.ppermute(
        group_part(tokens, bc_rows, dt_rows, 1 - core), "dp", [(i, i ^ 1) for i in range(count)]
    )
    rim = CONV - 1
    halo = None
    for group in range(CORES):
        rows = group_part(tokens[-rim:], bc_rows[-rim:], dt_rows[-rim:], group)
        rows = jnp.pad(rows, ((8 - rim, 0), (0, 0)))
        part = lax.ppermute(rows, "dp", [(i, i + 1 + group) for i in range(1, count - 1, 2)])
        halo = part if halo is None else halo + part

    dec_rows = STEPS * ROWS
    d_x = dec_x[0, 0].reshape(dec_rows, -1)
    d_bc = dec_bc[0, 0].reshape(dec_rows, 2, -1)
    d_dt = dec_dt[0, 0].reshape(dec_rows, -1)
    d_prompt = jnp.tile(decode_prompt[0, 0].astype(BF16), STEPS)[:, None]
    total = 2 * count
    same = lax.ppermute(
        group_part(d_x, d_bc, d_dt, core, d_prompt), both, [(i, (i + count) % total) for i in range(total)]
    )
    cross = lax.ppermute(
        group_part(d_x, d_bc, d_dt, 1 - core, d_prompt), both, [(i, ((i + count) % total) ^ 1) for i in range(total)]
    )
    pair = jnp.where(core == 0, jnp.stack([same, cross]), jnp.stack([cross, same]))
    pair = pair.reshape(CORES, STEPS, ROWS, WIDE).swapaxes(0, 1).reshape(CORES * dec_rows, WIDE)
    far = lax.ppermute(pair, "dp", [(i, i ^ (CORES * RING)) for i in range(count)])
    queries = jnp.where(upper == 0, jnp.concatenate([pair, far]), jnp.concatenate([far, pair]))

    def z_swap(value, m):
        if m == 0:
            return value
        return lax.ppermute(value, "dp", [(i, i ^ (CORES * m)) for i in range(count)])

    dec_parts = []
    for m in range(RING):
        channels = lax.dynamic_slice_in_dim(queries, (z ^ m) * CHUNK, CHUNK, 1)
        dec_parts.append(z_swap(jnp.concatenate([channels, queries[:, GROUP_CH : GROUP_CH + 640]], axis=1), m))

    w_group = lax.dynamic_slice_in_dim(conv_w_bc, core * STATE, STATE, 2).reshape(CONV, 2 * STATE)
    b_group = lax.dynamic_slice_in_dim(conv_b_bc, core * STATE, STATE, 1).reshape(1, 2 * STATE)
    rates = -LOG2E * jnp.exp(a_log)
    heads = jnp.stack([dt_bias, rates])
    heads = lax.dynamic_slice_in_dim(heads, core * REP, REP, 1)
    vecs = jnp.pad(jnp.tile(heads, (1, 3)), ((0, 6), (0, LANES - 3 * REP)))
    skip = jnp.repeat(d_skip, HEAD_DIM)[None]
    b_x = conv_b_x[None]
    g_own = group_side(bc_rows, dt_rows, core)

    *ls, xc, bcc, dtc, wc3, cx, cg = run_a(scalars, tokens, recv, halo, conv_w_x, b_x, g_own, w_group, b_group, vecs)
    ls = [z_swap(part, m) for m, part in enumerate(ls)]
    *fs, local = run_b(scalars, xc, bcc, dtc, skip, cx, cg)
    fs = [z_swap(part, m) for m, part in enumerate(fs)]

    state_shape = jax.ShapeDtypeStruct((STATE, CHUNK), BF16)
    half_total = whole_call(kernel_total, state_shape, "half_total", 10**6)(scalars, *ls)
    start = lax.ppermute(half_total, "dp", [(i, i + CORES * RING) for i in range(CORES * RING)])
    starts = whole_call(kernel_starts, [state_shape] * RING, "chip_starts", 10**6)(scalars, *ls, start)
    starts = [z_swap(part, m) for m, part in enumerate(starts)]

    def own_columns(value):
        return lax.dynamic_slice_in_dim(value, core * GROUP_CH + z * CHUNK, CHUNK, 1)

    def decode(bounds_ref_args):
        shape = jax.ShapeDtypeStruct((RING, 32, CHUNK), BF16)
        args = [*ls, start, *fs, *dec_parts, own_columns(conv_w_x), own_columns(b_x), w_group, b_group, vecs, own_columns(skip)]
        return pl.pallas_call(
            kernel_decode,
            in_specs=[pl.BlockSpec(memory_space=pltpu.SMEM)]
            + [pl.BlockSpec(memory_space=pltpu.VMEM)] * len(args)
            + [pl.BlockSpec(memory_space=pltpu.SMEM)],
            out_specs=[pl.BlockSpec(memory_space=pltpu.VMEM)] * 2,
            out_shape=[shape, shape],
            scratch_shapes=[
                pltpu.VMEM((PROMPTS, STATE, CHUNK), F32),
                pltpu.VMEM((RING, 64, 1152), F32),
                pltpu.VMEM((RING, 64, CHUNK), F32),
            ],
            compiler_params=pltpu.CompilerParams(vmem_limit_bytes=VMEM),
            cost_estimate=pl.CostEstimate(flops=4 * 10**9, bytes_accessed=6 * 10**6, transcendentals=0),
            name="decode_rows",
        )(scalars, *args, bounds_ref_args)

    kept, sent = decode(bounds)
    answers = kept + lax.ppermute(sent, "dp", [(i, i ^ (CORES * RING)) for i in range(count)])
    answers = jnp.stack([z_swap(answers[m], m) for m in range(RING)])
    answers = jnp.concatenate(
        [lax.dynamic_index_in_dim(answers, z ^ j, 0, keepdims=False) for j in range(RING)], axis=1
    )
    answers = answers.reshape(STEPS, CORES, ROWS, GROUP_CH)

    def answers_of(source):
        return lax.dynamic_index_in_dim(answers, source, 1, keepdims=False).reshape(dec_rows, GROUP_CH)

    same = lax.ppermute(answers_of(core), both, [(i, (i + count) % total) for i in range(total)])
    cross = lax.ppermute(answers_of(1 - core), both, [(i, ((i + count) % total) ^ 1) for i in range(total)])
    decoded = jnp.where(core == 0, jnp.concatenate([same, cross], axis=1), jnp.concatenate([cross, same], axis=1))

    other_rows = run_d(scalars, local, bcc, wc3, starts, False)
    other_group = lax.ppermute(other_rows, "dp", [(i, i ^ 1) for i in range(count)])
    own_group = run_d(scalars, local, bcc, wc3, starts, True)
    out = jnp.where(
        core == 0,
        jnp.concatenate([own_group, other_group], axis=1),
        jnp.concatenate([other_group, own_group], axis=1),
    )
    return out[None], decoded.reshape(dec_x.shape)


def solution(mesh):
    in_specs = (
        P("pool", "dp", "tp"),
        P("pool", "dp", None, "tp"),
        P("pool", "dp", "tp"),
        P(None, "tp"),
        P("tp"),
        P(None, None, "tp"),
        P(None, "tp"),
        P("tp"),
        P("tp"),
        P("tp"),
        P("pool", None),
        P("pool", "dp", None),
        P("pool", "dp", None, None, "tp"),
        P("pool", "dp", None, None, None, "tp"),
        P("pool", "dp", None, None, "tp"),
    )
    out_specs = (P("pool", "dp", "tp"), P("pool", "dp", None, None, "tp"))
    return jax.shard_map(on_device, mesh=mesh, in_specs=in_specs, out_specs=out_specs, check_vma=False)
```

time: 1160 us -> 152 us (0.13); the launches traced: 1140 us -> 151 us
  waiting for transfers between devices: 647 us -> 24.4 us
  matrix products: 172 us -> 0 us
  other arithmetic: 172 us -> 7.11 us
  local copies, waits for them, and re-layouts: 94.4 us -> 19.6 us
  Pallas kernels: 0 us -> 53.7 us
  starting transfers between devices: 6.48 us -> 43.9 us
  blocking collectives: 25.6 us -> 0 us
  between operations: 23 us -> 2.47 us
    all_gather x1 -> x0, waiting for transfers between devices: 263 us -> none  [carried_in(): pieces = jax.tree.map(lambda part: lax.all_gather(part, axis), value)]
    ppermute x3 -> x26, waiting for transfers between devices: 211 us -> 24.4 us  [the longest x15 13.6 us: z_swap(): return lax.ppermute(value, 'dp', [(i, i ^ CORES * m) for i in range(count)])]
    psum x1 -> x0, waiting for transfers between devices: 174 us -> none  [on_device(): state_total, cache_total = lax.psum((finals, caches), 'dp')]
    dot_general x17 -> x0, matrix products: 172 us -> none  [the longest x4 81.2 us: decode_parts(): jnp.einsum('rgn,rgkpn->rgkp', c_rows, carry_state, precision=HIGHEST_PREC...]
    select_n x25 -> x3, other arithmetic: 95.9 us -> 4.47 us  [the longest x1 3.65 us: on_device(): jnp.where(core == 0, jnp.concatenate([own_group, other_group], axis=1), j...]
    pallas_call x0 -> x7, Pallas kernels: none -> 53.7 us  [the longest x1 16.6 us: run_b(): pl.pallas_call(kernel_b, grid_spec=pltpu.PrefetchScalarGridSpec(num_scala...]
    ppermute x3 -> x26, starting transfers between devices: 6.4 us -> 43.9 us  [the longest x15 17.5 us: z_swap(): return lax.ppermute(value, 'dp', [(i, i ^ CORES * m) for i in range(count)])]
    mul x34 -> x0, local copies, waits for them, and re-layouts: 26.7 us -> none  [the longest x15 9.78 us: combine_states(): later_part[0][:, :, None, None] * earlier_part[1] + later_part[1]]
  transfers between devices with their start and end apart: 5 -> 26, of which waited for: 3 -> 9; matrix products, arithmetic and copies ran while one was open for 11% -> 11% of each run, Pallas kernels for 0% -> 28%
where the time goes in v1:
time: 152 us; the launch traced here: 151 us
  Pallas kernels  53.7 us (35%)
  starting transfers between devices  43.9 us (29%)
  waiting for transfers between devices  24.4 us (16%)
  local copies, waits for them, and re-layouts  19.6 us (13%)
  other arithmetic  7.11 us (5%)
  between operations  2.47 us (2%)
    ppermute x15, starting transfers between devices, z_swap(): return lax.ppermute(value, 'dp', [(i, i ^ CORES * m) for i in range(count)])  17.5 us
    pallas_call x1, Pallas kernels, run_b(): pl.pallas_call(kernel_b, grid_spec=pltpu.PrefetchScalarGridSpec(num_scala...  16.6 us
    pallas_call x1, Pallas kernels, run_a(): pl.pallas_call(kernel_a, grid_spec=pltpu.PrefetchScalarGridSpec(num_scala...  15.6 us
    ppermute x15, waiting for transfers between devices, z_swap(): return lax.ppermute(value, 'dp', [(i, i ^ CORES * m) for i in range(count)])  13.6 us
    pallas_call x2, Pallas kernels, run_d(): pl.pallas_call(kernel_d, grid_spec=pltpu.PrefetchScalarGridSpec(num_scala...  11.1 us
    ppermute x2, starting transfers between devices, on_device(): lax.ppermute(rows, 'dp', [(i, i + 1 + group) for i in range(1, count - 1,...  7.07 us
    ppermute x1, starting transfers between devices, on_device(): lax.ppermute(other_rows, 'dp', [(i, i ^ 1) for i in range(count)])  6.4 us
    pallas_call x2, Pallas kernels, run(): pl.pallas_call(kernel, in_specs=[pl.BlockSpec(memory_space=pltpu.SMEM)] +...  5.18 us
  transfers between devices with their start and end apart: 26, of which 9 were waited for; matrix products, arithmetic and copies ran while one was open for 11% of the time, Pallas kernels for 28%

profile of v1, /device:TPU:1, one launch (start us, length us, event | category | flops | bytes accessed | tf_op | source)
XLA Modules:
  0.0 151.2 jit_solution(1598456995278678997)
XLA Ops:
  0.7 1.4 constant_dynamic-slice_fusion.22
  2.1 0.7 constant_dynamic-slice_fusion.21
  3.0 1.3 dynamic-slice_bitcast_fusion
  4.4 0.6 concatenate.98
  5.0 1.5 collective-permute-start
  6.5 0.9 slice_bitcast_fusion.3
  7.4 0.7 slice_bitcast_fusion.4
  8.5 3.5 %collective-permute-start.1 = (bf16[8,3072]{1,0:T(8,128)(2,1)S(1)}, bf16[8,3072]{1,0:T(8,128)(2,1)S(1)}, u32[]{:S(2)}, u32[]{:S(2)}) collective-permute-start(bf16[8,3072]{1,0:T(8,128)(2,1)S(1)} %pad.11), channel_id=1, source_target_pairs={{1,2},{3,4},{5,6},{7,8},{9,10},{11,12},{13,14},{17,18},{19,20},{21... | collective-permute-start | bytes 147464 | tf_op jit(solution)/shard_map/ppermute | solution.py:629
  12.2 3.5 %collective-permute-start.2 = (bf16[8,3072]{1,0:T(8,128)(2,1)S(1)}, bf16[8,3072]{1,0:T(8,128)(2,1)S(1)}, u32[]{:S(2)}, u32[]{:S(2)}) collective-permute-start(bf16[8,3072]{1,0:T(8,128)(2,1)S(1)} %pad.12), channel_id=1, source_target_pairs={{1,3},{3,5},{5,7},{7,9},{9,11},{11,13},{13,15},{17,19},{19,21},{21... | collective-permute-start | bytes 147464 | tf_op jit(solution)/shard_map/ppermute | solution.py:629
  15.7 0.9 reshape_squeeze.9
  16.7 0.8 constant_dynamic-slice_fusion.16
  18.0 1.3 collective-permute-start.14
  19.3 0.2 reduce-window.4
  19.5 0.6 fusion.6
  20.1 2.8 %collective-permute-done.15 = bf16[16,3072]{1,0:T(8,128)(2,1)S(1)} collective-permute-done((bf16[16,3072]{1,0:T(8,128)(2,1)S(1)}, bf16[16,3072]{1,0:T(8,128)(2,1)S(1)}, u32[]{:S(2)}, u32[]{:S(2)}) %collective-permute-start.15) | collective-permute-done | bytes 98336 | tf_op jit(solution)/shard_map/ppermute | solution.py:641
  23.0 1.0 collective-permute-done.14
  24.2 2.4 %collective-permute-start.16 = (bf16[32,3072]{1,0:T(8,128)(2,1)S(1)}, bf16[32,3072]{1,0:T(8,128)(2,1)S(1)}, u32[]{:S(2)}, u32[]{:S(2)}) collective-permute-start(bf16[32,3072]{1,0:T(8,128)(2,1)S(1)} %reshape.210), channel_id=1, source_target_pairs={{0,8},{1,9},{2,10},{3,11},{4,12},{5,13},{6,14},{7,15},{8,0},{9,1},... | collective-permute-start | bytes 589832 | tf_op jit(solution)/shard_map/ppermute | solution.py:646
  28.0 0.6 copy.28
  28.6 0.6 copy.29
  29.3 0.7 broadcast_in_dim_reshape.3.skip
  30.0 1.0 concatenate.101.g_own
  31.1 0.6 pad.13.vecs
  31.7 0.6 stack.62.s_ref
  32.3 0.6 add.95.halo_x.halo_g
  33.1 0.7 pad_maximum_fusion
  33.8 1.3 collective-permute-start.17
  35.1 0.3 collective-permute-start.18
  35.4 15.6 %conv_and_states.1 = (bf16[272,512]{1,0:T(8,128)(2,1)}, bf16[272,512]{1,0:T(8,128)(2,1)}, bf16[272,512]{1,0:T(8,128)(2,1)}, bf16[272,512]{1,0:T(8,128)(2,1)}, bf...) custom-call(s32[8]{0:T(128)} %stack.62.s_ref, ...), custom_call_target="tpu_custom_call" | custom-call | flops 6000000000 | bytes 8000000 | tf_op jit(solution)/shard_map/conv_and_states/pallas_call | solution.py:205
  51.1 0.9 collective-permute-start.3
  51.9 2.5 %collective-permute-start.4 = (bf16[272,512]{1,0:T(8,128)(2,1)}, bf16[272,512]{1,0:T(8,128)(2,1)S(1)}, u32[]{:S(2)}, u32[]{:S(2)}) collective-permute-start(bf16[272,512]{1,0:T(8,128)(2,1)} %get-tuple-element.32), channel_id=1, source_target_pairs={{0,4},{1,5},{2,6},{3,7},{4,0},{5,1},{6,2},{7,3},{8,12},{9,13},{10,... | collective-permute-start | bytes 835592 | tf_op jit(solution)/shard_map/ppermute | solution.py:652
  54.4 0.6 collective-permute-start.5
  55.0 16.6 %output_within_chip.1 = (bf16[304,512]{1,0:T(8,128)(2,1)}, bf16[304,512]{1,0:T(8,128)(2,1)}, bf16[304,512]{1,0:T(8,128)(2,1)}, bf16[304,512]{1,0:T(8,128)(2,1)}, f32[512,2048]{1,0:T(8,128)}) custom-call(s32[8]{0:T(128)} %stack.62.s_ref, bf16[512,2048]{1,0:T(8,128)(2,1)} %get-tuple-element.23.xc_ref, bf16[512,512]{1,0:T(8,128)(2,1)} %get-tuple-element.24.bcc.c_rows, ...), custom_call_target="tpu_custom_call" | custom-call | flops 12000000000 | bytes 8000000 | tf_op jit(solution)/shard_map/output_within_chip/pallas_call | solution.py:368
  71.8 1.7 %collective-permute-start.12 = (bf16[304,512]{1,0:T(8,128)(2,1)}, bf16[304,512]{1,0:T(8,128)(2,1)S(1)}, u32[]{:S(2)}, u32[]{:S(2)}) collective-permute-start(bf16[304,512]{1,0:T(8,128)(2,1)} %get-tuple-element.40), channel_id=1, source_target_pairs={{0,4},{1,5},{2,6},{3,7},{4,0},{5,1},{6,2},{7,3},{8,12},{9,13},{10,... | collective-permute-start | bytes 933896 | tf_op jit(solution)/shard_map/ppermute | solution.py:652
  73.4 2.2 %collective-permute-start.13 = (bf16[304,512]{1,0:T(8,128)(2,1)}, bf16[304,512]{1,0:T(8,128)(2,1)S(1)}, u32[]{:S(2)}, u32[]{:S(2)}) collective-permute-start(bf16[304,512]{1,0:T(8,128)(2,1)} %get-tuple-element.41), channel_id=1, source_target_pairs={{0,6},{1,7},{2,4},{3,5},{4,2},{5,3},{6,0},{7,1},{8,14},{9,15},{10,... | collective-permute-start | bytes 933896 | tf_op jit(solution)/shard_map/ppermute | solution.py:652
  75.6 2.3 %half_total.1 = bf16[256,512]{1,0:T(8,128)(2,1)} custom-call(s32[8]{0:T(128)} %stack.62.s_ref, bf16[272,512]{1,0:T(8,128)(2,1)} %get-tuple-element.30.l0, bf16[272,512]{1,0:T(8,128)(2,1)} %copy-done.1, bf16[272,512]{1,0:T(8,128)(2,1)} %copy-done.2, bf16[272,512]{1,0:T(8,128)(2,1)} %copy-done.3), custom_call_target="tpu_custom_call" | custom-call | flops 1000000 | bytes 3000000 | tf_op jit(solution)/shard_map/half_total/pallas_call | solution.py:436
  77.9 4.4 %collective-permute-start.6 = (bf16[256,512]{1,0:T(8,128)(2,1)}, bf16[256,512]{1,0:T(8,128)(2,1)S(1)}, u32[]{:S(2)}, u32[]{:S(2)}) collective-permute-start(bf16[256,512]{1,0:T(8,128)(2,1)} %half_total.1), channel_id=1, source_target_pairs={{0,8},{1,9},{2,10},{3,11},{4,12},{5,13},{6,14},{7,15},{16,24},{17,... | collective-permute-start | bytes 786440 | tf_op jit(solution)/shard_map/ppermute | solution.py:676
  82.4 0.8 collective-permute-start.19
  83.1 1.2 constant_dynamic-slice_fusion.6.skip
  84.4 1.3 dynamic-slice.8
  85.7 1.3 constant_dynamic-slice_fusion.7.wx
  87.0 4.8 %collective-permute-done.19.d3 = bf16[64,1152]{1,0:T(8,128)(2,1)S(1)} collective-permute-done((bf16[64,1152]{1,0:T(8,128)(2,1)S(1)}, bf16[64,1152]{1,0:T(8,128)(2,1)S(1)}, u32[]{:S(2)}, u32[]{:S(2)}) %collective-permute-start.19) | collective-permute-done | bytes 147488 | tf_op jit(solution)/shard_map/ppermute | solution.py:652
  91.8 0.6 copy-done.19
  92.8 5.2 %decode_rows.1 = (bf16[4,32,512]{2,1,0:T(8,128)(2,1)}, bf16[4,32,512]{2,1,0:T(8,128)(2,1)}) custom-call(s32[8]{0:T(128)} %stack.62.s_ref, bf16[272,512]{1,0:T(8,128)(2,1)} %get-tuple-element.30.l0, bf16[272,512]{1,0:T(8,128)(2,1)} %copy-done.1, bf16[272,512]{1,0:T(8,128)(2,1)} %copy-done.2, bf16[272,512]{1,0:T(8,128)(2,1)} %copy-done.3, ...), custom_call_target="tpu_custom_call" | custom-call | flops 4000000000 | bytes 6000000 | tf_op jit(solution)/shard_map/decode_rows/pallas_call | solution.py:686
  98.0 1.8 %collective-permute-start.20 = (bf16[4,32,512]{2,1,0:T(8,128)(2,1)}, bf16[4,32,512]{2,1,0:T(8,128)(2,1)S(1)}, u32[]{:S(2)}, u32[]{:S(2)}) collective-permute-start(bf16[4,32,512]{2,1,0:T(8,128)(2,1)} %get-tuple-element.43), channel_id=1, source_target_pairs={{0,8},{1,9},{2,10},{3,11},{4,12},{5,13},{6,14},{7,15},{8,0},{9,1},... | collective-permute-start | bytes 393224 | tf_op jit(solution)/shard_map/ppermute | solution.py:704
  99.8 3.8 %collective-permute-done.20 = bf16[4,32,512]{2,1,0:T(8,128)(2,1)S(1)} collective-permute-done((bf16[4,32,512]{2,1,0:T(8,128)(2,1)}, bf16[4,32,512]{2,1,0:T(8,128)(2,1)S(1)}, u32[]{:S(2)}, u32[]{:S(2)}) %collective-permute-start.20) | collective-permute-done | bytes 131104 | tf_op jit(solution)/shard_map/ppermute | solution.py:704
  103.6 0.9 add.105
  104.5 2.2 %collective-permute-start.23 = (bf16[32,512]{1,0:T(8,128)(2,1)S(1)}, bf16[32,512]{1,0:T(8,128)(2,1)S(1)}, u32[]{:S(2)}, u32[]{:S(2)}) collective-permute-start(bf16[32,512]{1,0:T(8,128)(2,1)S(1)} %get-tuple-element.57), channel_id=1, source_target_pairs={{0,6},{1,7},{2,4},{3,5},{4,2},{5,3},{6,0},{7,1},{8,14},{9,15},{10,... | collective-permute-start | bytes 98312 | tf_op jit(solution)/shard_map/ppermute | solution.py:652
  106.8 1.1 collective-permute-start.21
  107.9 2.9 %chip_starts.1 = (bf16[256,512]{1,0:T(8,128)(2,1)}, bf16[256,512]{1,0:T(8,128)(2,1)}, bf16[256,512]{1,0:T(8,128)(2,1)}, bf16[256,512]{1,0:T(8,128)(2,1)}) custom-call(s32[8]{0:T(128)} %stack.62.s_ref, bf16[272,512]{1,0:T(8,128)(2,1)} %get-tuple-element.30.l0, bf16[272,512]{1,0:T(8,128)(2,1)} %copy-done.1, bf16[272,512]{1,0:T(8,128)(2,1)} %copy-done.2, ...), custom_call_target="tpu_custom_call" | custom-call | flops 1000000 | bytes 3000000 | tf_op jit(solution)/shard_map/chip_starts/pallas_call | solution.py:436
  110.8 0.4 collective-permute-start.7
  111.1 3.0 %collective-permute-start.8 = (bf16[256,512]{1,0:T(8,128)(2,1)}, bf16[256,512]{1,0:T(8,128)(2,1)S(1)}, u32[]{:S(2)}, u32[]{:S(2)}) collective-permute-start(bf16[256,512]{1,0:T(8,128)(2,1)} %get-tuple-element.36), channel_id=1, source_target_pairs={{0,4},{1,5},{2,6},{3,7},{4,0},{5,1},{6,2},{7,3},{8,12},{9,13},{10,... | collective-permute-start | bytes 786440 | tf_op jit(solution)/shard_map/ppermute | solution.py:652
  114.1 0.5 collective-permute-start.9
  114.8 2.1 %collective-permute-done.7.r1 = bf16[256,512]{1,0:T(8,128)(2,1)S(1)} collective-permute-done((bf16[256,512]{1,0:T(8,128)(2,1)}, bf16[256,512]{1,0:T(8,128)(2,1)S(1)}, u32[]{:S(2)}, u32[]{:S(2)}) %collective-permute-start.7) | collective-permute-done | bytes 262176 | tf_op jit(solution)/shard_map/ppermute | solution.py:652
  116.9 5.9 %collective-permute-done.8.r2 = bf16[256,512]{1,0:T(8,128)(2,1)S(1)} collective-permute-done((bf16[256,512]{1,0:T(8,128)(2,1)}, bf16[256,512]{1,0:T(8,128)(2,1)S(1)}, u32[]{:S(2)}, u32[]{:S(2)}) %collective-permute-start.8) | collective-permute-done | bytes 262176 | tf_op jit(solution)/shard_map/ppermute | solution.py:652
  122.8 0.8 collective-permute-done.9.r3
  123.6 0.7 copy-done.6
  124.3 5.5 %carried_other.1 = bf16[256,2048]{1,0:T(8,128)(2,1)} custom-call(s32[8]{0:T(128)} %stack.62.s_ref, f32[512,2048]{1,0:T(8,128)} %get-tuple-element.28.local, bf16[512,512]{1,0:T(8,128)(2,1)} %get-tuple-element.24.bcc.c_rows, bf16[512,128]{1,0:T(8,128)(2,1)} %get-tuple-element.29.wc3, bf16[256,512]{1,0:T(8,128)(2,1)} %get-tuple-element.34.r0, ...), custom_call_target="tpu_custom_call" | custom-call | flops 1000000000 | bytes 4000000 | tf_op jit(solution)/shard_map/carried_other/pallas_call | solution.py:574
  129.8 6.4 %collective-permute-start.10 = (bf16[256,2048]{1,0:T(8,128)(2,1)}, bf16[256,2048]{1,0:T(8,128)(2,1)S(1)}, u32[]{:S(2)}, u32[]{:S(2)}) collective-permute-start(bf16[256,2048]{1,0:T(8,128)(2,1)} %carried_other.1), channel_id=1, source_target_pairs={{0,1},{1,0},{2,3},{3,2},{4,5},{5,4},{6,7},{7,6},{8,9},{9,8},{10,11... | collective-permute-start | bytes 3145736 | tf_op jit(solution)/shard_map/ppermute | solution.py:719
  136.4 1.4 collective-permute-start.24
  137.8 2.9 %collective-permute-done.25 = bf16[16,2048]{1,0:T(8,128)(2,1)S(1)} collective-permute-done((bf16[16,2048]{1,0:T(8,128)(2,1)S(1)}, bf16[16,2048]{1,0:T(8,128)(2,1)S(1)}, u32[]{:S(2)}, u32[]{:S(2)}) %collective-permute-start.25) | collective-permute-done | bytes 65568 | tf_op jit(solution)/shard_map/ppermute | solution.py:715
  140.8 0.4 collective-permute-done.24
  141.2 0.8 maximum_select_fusion.3
  141.9 5.6 %carried_own.1 = bf16[256,2048]{1,0:T(8,128)(2,1)} custom-call(s32[8]{0:T(128)} %stack.62.s_ref, f32[512,2048]{1,0:T(8,128)} %get-tuple-element.28.local, bf16[512,512]{1,0:T(8,128)(2,1)} %get-tuple-element.24.bcc.c_rows, bf16[512,128]{1,0:T(8,128)(2,1)} %get-tuple-element.29.wc3, bf16[256,512]{1,0:T(8,128)(2,1)} %get-tuple-element.34.r0, ...), custom_call_target="tpu_custom_call" | custom-call | flops 1000000000 | bytes 4000000 | tf_op jit(solution)/shard_map/carried_own/pallas_call | solution.py:574
  147.5 3.6 %maximum_select_fusion = bf16[1,256,4096]{2,1,0:T(8,128)(2,1)} fusion(bf16[1,256,2048]{2,1,0:T(8,128)(2,1)S(1)} %bitcast.66, bf16[1,256,2048]{2,1,0:T(8,128)(2,1)} %bitcast.65, pred[]{:T(512)S(6)} %eq.11), kind=kLoop, calls=%fused_computation | loop fusion | flops 9437184 | bytes 4194305 | tf_op jit(solution)/shard_map/jit(_where)/select_n | solution.py:721
  (127 shorter events, 3.0 us)
Async XLA Ops:
  0.6 19.4 %copy-start = (bf16[4,2,512]{2,1,0:T(2,128)(2,1)S(1)}, bf16[4,2,512]{2,1,0:T(2,128)(2,1)}, u32[]{:S(2)}) copy-start(bf16[4,2,512]{2,1,0:T(2,128)(2,1)} %param.20) | copy-start | bytes 24580
  4.3 3.8 %copy-start.8 = (bf16[1,256,64]{1,2,0:T(8,128)(2,1)S(1)}, bf16[1,256,64]{1,2,0:T(8,128)(2,1)}, u32[]{:S(2)}) copy-start(bf16[1,256,64]{1,2,0:T(8,128)(2,1)} %param.17) | copy-start | bytes 98308
  4.4 13.1 %copy-start.9 = (bf16[1,1,4,4,64]{4,3,2,1,0:T(4,128)(2,1)S(1)}, bf16[1,1,4,4,64]{4,3,2,1,0:T(4,128)(2,1)}, u32[]{:S(2)}) copy-start(bf16[1,1,4,4,64]{4,3,2,1,0:T(4,128)(2,1)} %param.29) | copy-start | bytes 6148
  4.4 13.2 %copy-start.20 = (s32[1,1,4]{2,1,0:T(1,128)S(1)}, s32[1,1,4]{2,1,0:T(1,128)}, u32[]{:S(2)}) copy-start(s32[1,1,4]{2,1,0:T(1,128)} %param.26) | copy-start | bytes 52
  4.4 14.9 %copy-start.21 = (s32[1,3]{1,0:T(1,128)S(1)}, s32[1,3]{1,0:T(1,128)}, u32[]{:S(2)}) copy-start(s32[1,3]{1,0:T(1,128)} %param.25) | copy-start | bytes 40
  4.4 15.7 %copy-start.22 = (f32[64]{0:T(128)S(1)}, f32[64]{0:T(128)}, u32[]{:S(2)}) copy-start(f32[64]{0:T(128)} %param.23) | copy-start | bytes 772
  4.4 15.7 %copy-start.11 = (f32[2,512]{1,0:T(2,128)S(1)}, f32[2,512]{1,0:T(2,128)}, u32[]{:S(2)}) copy-start(f32[2,512]{1,0:T(2,128)} %param.21) | copy-start | bytes 12292
  5.0 21.6 %copy-start.13 = (f32[64]{0:T(128)S(1)}, f32[64]{0:T(128)}, u32[]{:S(2)}) copy-start(f32[64]{0:T(128)} %param.22) | copy-start | bytes 772
  5.0 24.3 %copy-start.12 = (f32[64]{0:T(128)S(1)}, f32[64]{0:T(128)}, u32[]{:S(2)}) copy-start(f32[64]{0:T(128)} %param.24) | copy-start | bytes 772
  5.0 30.4 %collective-permute-start = (bf16[256,3072]{1,0:T(8,128)(2,1)S(1)}, bf16[256,3072]{1,0:T(8,128)(2,1)}, u32[]{:S(2)}, u32[]{:S(2)}) collective-permute-start(bf16[256,3072]{1,0:T(8,128)(2,1)S(1)} %concatenate.98), channel_id=1, source_target_pairs={{0,1},{1,0},{2,3},{3,2},{4,5},{5,4},{6,7},{7,6},{8,9},{9,8},{10,11... | collective-permute-start | bytes 4718600 | tf_op jit(solution)/shard_map/ppermute | solution.py:621
  8.5 23.8 %collective-permute-start.1 = (bf16[8,3072]{1,0:T(8,128)(2,1)S(1)}, bf16[8,3072]{1,0:T(8,128)(2,1)S(1)}, u32[]{:S(2)}, u32[]{:S(2)}) collective-permute-start(bf16[8,3072]{1,0:T(8,128)(2,1)S(1)} %pad.11), channel_id=1, source_target_pairs={{1,2},{3,4},{5,6},{7,8},{9,10},{11,12},{13,14},{17,18},{19,20},{21... | collective-permute-start | bytes 147464 | tf_op jit(solution)/shard_map/ppermute | solution.py:629
  12.2 20.1 %collective-permute-start.2 = (bf16[8,3072]{1,0:T(8,128)(2,1)S(1)}, bf16[8,3072]{1,0:T(8,128)(2,1)S(1)}, u32[]{:S(2)}, u32[]{:S(2)}) collective-permute-start(bf16[8,3072]{1,0:T(8,128)(2,1)S(1)} %pad.12), channel_id=1, source_target_pairs={{1,3},{3,5},{5,7},{7,9},{9,11},{11,13},{13,15},{17,19},{19,21},{21... | collective-permute-start | bytes 147464 | tf_op jit(solution)/shard_map/ppermute | solution.py:629
  17.8 5.1 %collective-permute-start.15 = (bf16[16,3072]{1,0:T(8,128)(2,1)S(1)}, bf16[16,3072]{1,0:T(8,128)(2,1)S(1)}, u32[]{:S(2)}, u32[]{:S(2)}) collective-permute-start(bf16[16,3072]{1,0:T(8,128)(2,1)S(1)} %concatenate.107), channel_id=1, source_target_pairs={{0,65},{1,64},{2,67},{3,66},{4,69},{5,68},{6,71},{7,70},{8,73},{9,... | collective-permute-start | bytes 294920 | tf_op jit(solution)/shard_map/ppermute | solution.py:641
  18.0 5.9 %collective-permute-start.14 = (bf16[16,3072]{1,0:T(8,128)(2,1)S(1)}, bf16[16,3072]{1,0:T(8,128)(2,1)S(1)}, u32[]{:S(2)}, u32[]{:S(2)}) collective-permute-start(bf16[16,3072]{1,0:T(8,128)(2,1)S(1)} %concatenate.106), channel_id=1, source_target_pairs={{0,64},{1,65},{2,66},{3,67},{4,68},{5,69},{6,70},{7,71},{8,72},{9,... | collective-permute-start | bytes 294920 | tf_op jit(solution)/shard_map/ppermute | solution.py:638
  19.5 13.5 %copy-start.10 = (s32[3,1]{0,1:T(1,128)}, s32[3,1]{0,1:T(1,128)S(1)}, u32[]{:S(2)}) copy-start(s32[3,1]{0,1:T(1,128)S(1)} %reduce-window.4) | copy-start | bytes 40
  24.2 8.7 %collective-permute-start.16 = (bf16[32,3072]{1,0:T(8,128)(2,1)S(1)}, bf16[32,3072]{1,0:T(8,128)(2,1)S(1)}, u32[]{:S(2)}, u32[]{:S(2)}) collective-permute-start(bf16[32,3072]{1,0:T(8,128)(2,1)S(1)} %reshape.210), channel_id=1, source_target_pairs={{0,8},{1,9},{2,10},{3,11},{4,12},{5,13},{6,14},{7,15},{8,0},{9,1},... | collective-permute-start | bytes 589832 | tf_op jit(solution)/shard_map/ppermute | solution.py:646
  33.8 44.1 %collective-permute-start.17 = (bf16[64,1152]{1,0:T(8,128)(2,1)S(1)}, bf16[64,1152]{1,0:T(8,128)(2,1)S(1)}, u32[]{:S(2)}, u32[]{:S(2)}) collective-permute-start(bf16[64,1152]{1,0:T(8,128)(2,1)S(1)} %get-tuple-element.63), channel_id=1, source_target_pairs={{0,2},{1,3},{2,0},{3,1},{4,6},{5,7},{6,4},{7,5},{8,10},{9,11},{10,... | collective-permute-start | bytes 442376 | tf_op jit(solution)/shard_map/ppermute | solution.py:652
  35.1 47.2 %collective-permute-start.18 = (bf16[64,1152]{1,0:T(8,128)(2,1)S(1)}, bf16[64,1152]{1,0:T(8,128)(2,1)S(1)}, u32[]{:S(2)}, u32[]{:S(2)}) collective-permute-start(bf16[64,1152]{1,0:T(8,128)(2,1)S(1)} %get-tuple-element.64), channel_id=1, source_target_pairs={{0,4},{1,5},{2,6},{3,7},{4,0},{5,1},{6,2},{7,3},{8,12},{9,13},{10,... | collective-permute-start | bytes 442376 | tf_op jit(solution)/shard_map/ppermute | solution.py:652
  51.1 20.6 %collective-permute-start.3 = (bf16[272,512]{1,0:T(8,128)(2,1)}, bf16[272,512]{1,0:T(8,128)(2,1)S(1)}, u32[]{:S(2)}, u32[]{:S(2)}) collective-permute-start(bf16[272,512]{1,0:T(8,128)(2,1)} %get-tuple-element.31), channel_id=1, source_target_pairs={{0,2},{1,3},{2,0},{3,1},{4,6},{5,7},{6,4},{7,5},{8,10},{9,11},{10,... | collective-permute-start | bytes 835592 | tf_op jit(solution)/shard_map/ppermute | solution.py:652
  51.9 19.8 %collective-permute-start.4 = (bf16[272,512]{1,0:T(8,128)(2,1)}, bf16[272,512]{1,0:T(8,128)(2,1)S(1)}, u32[]{:S(2)}, u32[]{:S(2)}) collective-permute-start(bf16[272,512]{1,0:T(8,128)(2,1)} %get-tuple-element.32), channel_id=1, source_target_pairs={{0,4},{1,5},{2,6},{3,7},{4,0},{5,1},{6,2},{7,3},{8,12},{9,13},{10,... | collective-permute-start | bytes 835592 | tf_op jit(solution)/shard_map/ppermute | solution.py:652
  54.4 19.0 %collective-permute-start.5 = (bf16[272,512]{1,0:T(8,128)(2,1)}, bf16[272,512]{1,0:T(8,128)(2,1)S(1)}, u32[]{:S(2)}, u32[]{:S(2)}) collective-permute-start(bf16[272,512]{1,0:T(8,128)(2,1)} %get-tuple-element.33), channel_id=1, source_target_pairs={{0,6},{1,7},{2,4},{3,5},{4,2},{5,3},{6,0},{7,1},{8,14},{9,15},{10,... | collective-permute-start | bytes 835592 | tf_op jit(solution)/shard_map/ppermute | solution.py:652
  71.6 4.0 %copy-start.1 = (bf16[272,512]{1,0:T(8,128)(2,1)}, bf16[272,512]{1,0:T(8,128)(2,1)S(1)}, u32[]{:S(2)}) copy-start(bf16[272,512]{1,0:T(8,128)(2,1)S(1)} %collective-permute-done.3.l1) | copy-start | bytes 835588
  71.6 20.1 %collective-permute-start.11 = (bf16[304,512]{1,0:T(8,128)(2,1)}, bf16[304,512]{1,0:T(8,128)(2,1)S(1)}, u32[]{:S(2)}, u32[]{:S(2)}) collective-permute-start(bf16[304,512]{1,0:T(8,128)(2,1)} %get-tuple-element.39), channel_id=1, source_target_pairs={{0,2},{1,3},{2,0},{3,1},{4,6},{5,7},{6,4},{7,5},{8,10},{9,11},{10,... | collective-permute-start | bytes 933896 | tf_op jit(solution)/shard_map/ppermute | solution.py:652
  71.8 3.9 %copy-start.2 = (bf16[272,512]{1,0:T(8,128)(2,1)}, bf16[272,512]{1,0:T(8,128)(2,1)S(1)}, u32[]{:S(2)}) copy-start(bf16[272,512]{1,0:T(8,128)(2,1)S(1)} %collective-permute-done.4.l2) | copy-start | bytes 835588
  71.8 20.0 %collective-permute-start.12 = (bf16[304,512]{1,0:T(8,128)(2,1)}, bf16[304,512]{1,0:T(8,128)(2,1)S(1)}, u32[]{:S(2)}, u32[]{:S(2)}) collective-permute-start(bf16[304,512]{1,0:T(8,128)(2,1)} %get-tuple-element.40), channel_id=1, source_target_pairs={{0,4},{1,5},{2,6},{3,7},{4,0},{5,1},{6,2},{7,3},{8,12},{9,13},{10,... | collective-permute-start | bytes 933896 | tf_op jit(solution)/shard_map/ppermute | solution.py:652
  73.4 2.2 %copy-start.3 = (bf16[272,512]{1,0:T(8,128)(2,1)}, bf16[272,512]{1,0:T(8,128)(2,1)S(1)}, u32[]{:S(2)}) copy-start(bf16[272,512]{1,0:T(8,128)(2,1)S(1)} %collective-permute-done.5.l3) | copy-start | bytes 835588
  73.4 18.4 %collective-permute-start.13 = (bf16[304,512]{1,0:T(8,128)(2,1)}, bf16[304,512]{1,0:T(8,128)(2,1)S(1)}, u32[]{:S(2)}, u32[]{:S(2)}) collective-permute-start(bf16[304,512]{1,0:T(8,128)(2,1)} %get-tuple-element.41), channel_id=1, source_target_pairs={{0,6},{1,7},{2,4},{3,5},{4,2},{5,3},{6,0},{7,1},{8,14},{9,15},{10,... | collective-permute-start | bytes 933896 | tf_op jit(solution)/shard_map/ppermute | solution.py:652
  77.9 13.9 %copy-start.17 = (bf16[64,1152]{1,0:T(8,128)(2,1)}, bf16[64,1152]{1,0:T(8,128)(2,1)S(1)}, u32[]{:S(2)}) copy-start(bf16[64,1152]{1,0:T(8,128)(2,1)S(1)} %collective-permute-done.17.d1) | copy-start | bytes 442372
  77.9 13.9 %collective-permute-start.6 = (bf16[256,512]{1,0:T(8,128)(2,1)}, bf16[256,512]{1,0:T(8,128)(2,1)S(1)}, u32[]{:S(2)}, u32[]{:S(2)}) collective-permute-start(bf16[256,512]{1,0:T(8,128)(2,1)} %half_total.1), channel_id=1, source_target_pairs={{0,8},{1,9},{2,10},{3,11},{4,12},{5,13},{6,14},{7,15},{16,24},{17,... | collective-permute-start | bytes 786440 | tf_op jit(solution)/shard_map/ppermute | solution.py:676
  82.3 9.5 %copy-start.18 = (bf16[64,1152]{1,0:T(8,128)(2,1)}, bf16[64,1152]{1,0:T(8,128)(2,1)S(1)}, u32[]{:S(2)}) copy-start(bf16[64,1152]{1,0:T(8,128)(2,1)S(1)} %collective-permute-done.18.d2) | copy-start | bytes 442372
  82.4 9.4 %collective-permute-start.19 = (bf16[64,1152]{1,0:T(8,128)(2,1)S(1)}, bf16[64,1152]{1,0:T(8,128)(2,1)S(1)}, u32[]{:S(2)}, u32[]{:S(2)}) collective-permute-start(bf16[64,1152]{1,0:T(8,128)(2,1)S(1)} %get-tuple-element.62), channel_id=1, source_target_pairs={{0,6},{1,7},{2,4},{3,5},{4,2},{5,3},{6,0},{7,1},{8,14},{9,15},{10,... | collective-permute-start | bytes 442376 | tf_op jit(solution)/shard_map/ppermute | solution.py:652
  91.8 0.7 copy-start.19
  91.8 0.8 copy-start.14
  91.8 0.9 copy-start.15
  91.8 1.0 copy-start.16
  91.8 1.0 copy-start.7
  98.0 5.6 %collective-permute-start.20 = (bf16[4,32,512]{2,1,0:T(8,128)(2,1)}, bf16[4,32,512]{2,1,0:T(8,128)(2,1)S(1)}, u32[]{:S(2)}, u32[]{:S(2)}) collective-permute-start(bf16[4,32,512]{2,1,0:T(8,128)(2,1)} %get-tuple-element.43), channel_id=1, source_target_pairs={{0,8},{1,9},{2,10},{3,11},{4,12},{5,13},{6,14},{7,15},{8,0},{9,1},... | collective-permute-start | bytes 393224 | tf_op jit(solution)/shard_map/ppermute | solution.py:704
  104.5 9.6 %collective-permute-start.23 = (bf16[32,512]{1,0:T(8,128)(2,1)S(1)}, bf16[32,512]{1,0:T(8,128)(2,1)S(1)}, u32[]{:S(2)}, u32[]{:S(2)}) collective-permute-start(bf16[32,512]{1,0:T(8,128)(2,1)S(1)} %get-tuple-element.57), channel_id=1, source_target_pairs={{0,6},{1,7},{2,4},{3,5},{4,2},{5,3},{6,0},{7,1},{8,14},{9,15},{10,... | collective-permute-start | bytes 98312 | tf_op jit(solution)/shard_map/ppermute | solution.py:652
  106.8 7.9 %collective-permute-start.22 = (bf16[32,512]{1,0:T(8,128)(2,1)S(1)}, bf16[32,512]{1,0:T(8,128)(2,1)S(1)}, u32[]{:S(2)}, u32[]{:S(2)}) collective-permute-start(bf16[32,512]{1,0:T(8,128)(2,1)S(1)} %get-tuple-element.58), channel_id=1, source_target_pairs={{0,4},{1,5},{2,6},{3,7},{4,0},{5,1},{6,2},{7,3},{8,12},{9,13},{10,... | collective-permute-start | bytes 98312 | tf_op jit(solution)/shard_map/ppermute | solution.py:652
  106.8 7.9 %collective-permute-start.21 = (bf16[32,512]{1,0:T(8,128)(2,1)S(1)}, bf16[32,512]{1,0:T(8,128)(2,1)S(1)}, u32[]{:S(2)}, u32[]{:S(2)}) collective-permute-start(bf16[32,512]{1,0:T(8,128)(2,1)S(1)} %get-tuple-element.59), channel_id=1, source_target_pairs={{0,2},{1,3},{2,0},{3,1},{4,6},{5,7},{6,4},{7,5},{8,10},{9,11},{10,... | collective-permute-start | bytes 98312 | tf_op jit(solution)/shard_map/ppermute | solution.py:652
  110.8 6.1 %collective-permute-start.7 = (bf16[256,512]{1,0:T(8,128)(2,1)}, bf16[256,512]{1,0:T(8,128)(2,1)S(1)}, u32[]{:S(2)}, u32[]{:S(2)}) collective-permute-start(bf16[256,512]{1,0:T(8,128)(2,1)} %get-tuple-element.35), channel_id=1, source_target_pairs={{0,2},{1,3},{2,0},{3,1},{4,6},{5,7},{6,4},{7,5},{8,10},{9,11},{10,... | collective-permute-start | bytes 786440 | tf_op jit(solution)/shard_map/ppermute | solution.py:652
  111.1 11.6 %collective-permute-start.8 = (bf16[256,512]{1,0:T(8,128)(2,1)}, bf16[256,512]{1,0:T(8,128)(2,1)S(1)}, u32[]{:S(2)}, u32[]{:S(2)}) collective-permute-start(bf16[256,512]{1,0:T(8,128)(2,1)} %get-tuple-element.36), channel_id=1, source_target_pairs={{0,4},{1,5},{2,6},{3,7},{4,0},{5,1},{6,2},{7,3},{8,12},{9,13},{10,... | collective-permute-start | bytes 786440 | tf_op jit(solution)/shard_map/ppermute | solution.py:652
  114.1 9.5 %collective-permute-start.9 = (bf16[256,512]{1,0:T(8,128)(2,1)}, bf16[256,512]{1,0:T(8,128)(2,1)S(1)}, u32[]{:S(2)}, u32[]{:S(2)}) collective-permute-start(bf16[256,512]{1,0:T(8,128)(2,1)} %get-tuple-element.37), channel_id=1, source_target_pairs={{0,6},{1,7},{2,4},{3,5},{4,2},{5,3},{6,0},{7,1},{8,14},{9,15},{10,... | collective-permute-start | bytes 786440 | tf_op jit(solution)/shard_map/ppermute | solution.py:652
  116.9 6.7 %copy-start.4 = (bf16[256,512]{1,0:T(8,128)(2,1)}, bf16[256,512]{1,0:T(8,128)(2,1)S(1)}, u32[]{:S(2)}) copy-start(bf16[256,512]{1,0:T(8,128)(2,1)S(1)} %collective-permute-done.7.r1) | copy-start | bytes 786436
  122.8 0.8 copy-start.5
  123.6 0.7 copy-start.6
  129.8 17.7 %collective-permute-start.10 = (bf16[256,2048]{1,0:T(8,128)(2,1)}, bf16[256,2048]{1,0:T(8,128)(2,1)S(1)}, u32[]{:S(2)}, u32[]{:S(2)}) collective-permute-start(bf16[256,2048]{1,0:T(8,128)(2,1)} %carried_other.1), channel_id=1, source_target_pairs={{0,1},{1,0},{2,3},{3,2},{4,5},{5,4},{6,7},{7,6},{8,9},{9,8},{10,11... | collective-permute-start | bytes 3145736 | tf_op jit(solution)/shard_map/ppermute | solution.py:719
  136.3 4.4 %collective-permute-start.25 = (bf16[16,2048]{1,0:T(8,128)(2,1)S(1)}, bf16[16,2048]{1,0:T(8,128)(2,1)S(1)}, u32[]{:S(2)}, u32[]{:S(2)}) collective-permute-start(bf16[16,2048]{1,0:T(8,128)(2,1)S(1)} %reshape.213), channel_id=1, source_target_pairs={{0,65},{1,64},{2,67},{3,66},{4,69},{5,68},{6,71},{7,70},{8,73},{9,... | collective-permute-start | bytes 196616 | tf_op jit(solution)/shard_map/ppermute | solution.py:715
  136.4 4.7 %collective-permute-start.24 = (bf16[16,2048]{1,0:T(8,128)(2,1)S(1)}, bf16[16,2048]{1,0:T(8,128)(2,1)S(1)}, u32[]{:S(2)}, u32[]{:S(2)}) collective-permute-start(bf16[16,2048]{1,0:T(8,128)(2,1)S(1)} %reshape.212), channel_id=1, source_target_pairs={{0,64},{1,65},{2,66},{3,67},{4,68},{5,69},{6,70},{7,71},{8,72},{9,... | collective-permute-start | bytes 196616 | tf_op jit(solution)/shard_map/ppermute | solution.py:714

commit v2 on v1

--- a/solution.py
+++ b/solution.py
@@ -17,6 +17,8 @@
 CORES = 2
 RING = 4
 LANES = 128
+DEC = STATE + 48
+MSG = DEC + 144
 REP = 32
 CHIP_TOKENS = 512
 BLOCKS = CHIP_TOKENS // BLOCK
@@ -26,7 +28,7 @@
 LOG2E = 1.4426950408889634
 F32 = jnp.float32
 BF16 = jnp.bfloat16
-VMEM = 56 * 1024 * 1024
+MIB = 1024 * 1024
 
 
 def split3(value):
@@ -44,9 +46,13 @@
 
 def spread_matrix(chunk):
     lane = lax.broadcasted_iota(jnp.int32, (LANES, CHUNK), 0)
-    head = lax.broadcasted_iota(jnp.int32, (LANES, CHUNK), 1) // HEAD_DIM + chunk * (CHUNK // HEAD_DIM)
+    head = (lax.broadcasted_iota(jnp.int32, (LANES, CHUNK), 1) >> 6) + chunk * (CHUNK // HEAD_DIM)
     hit = ((lane & (REP - 1)) == head) & (lane < 3 * REP)
     return jnp.where(hit, 1.0, 0.0).astype(BF16)
+
+
+def in_hbm(value):
+    return pltpu.with_memory_space_constraint(value, pltpu.HBM)
 
 
 def mm(a, b):
@@ -82,16 +88,13 @@
     return out
 
 
-def conv_rows(src, start, weight, offset, mask):
-    lanes = offset.shape[1]
-    running = jnp.broadcast_to(offset, (BLOCK, lanes))
-    for tap in range(CONV):
-        term = weight[tap : tap + 1] * src[pl.ds(5 + tap + start, BLOCK), :]
-        if tap < CONV - 1:
-            keep = mask[tap, pl.ds(start, BLOCK), :]
-            term = term * jnp.concatenate([keep] * (lanes // LANES), axis=1)
-        running = running + term
-    return silu(running)
+def conv_tile(src, start, lanes, weight, offset, mask):
+    tile = src[pl.ds(start, BLOCK + 8), lanes]
+    running = jnp.broadcast_to(offset[:, lanes], (BLOCK, LANES))
+    for tap in range(CONV - 1):
+        moved = pltpu.roll(tile, CONV - 1 - tap, 0)[8:]
+        running = running + weight[tap : tap + 1, lanes] * (moved * mask[tap, pl.ds(start, BLOCK), :])
+    return silu(running + weight[CONV - 1 : CONV, lanes] * tile[8:])
 
 
 def cache_rows(s_ref, src, out):
@@ -118,7 +121,7 @@
 def kernel_a(
     s_ref, x_own, x_rec, halo_x, wx, bx, g_own, g_rec, halo_g, wg, bg, vecs,
     l0, l1, l2, l3, xc_out, bcc_out, dtc_out, wc3_out, cx_out, cg_out,
-    xs, gs, mask, wp3, keep3, bt, cache,
+    xs, gs, mask, wp3, keep3, bt, cache, wide, scaled,
 ):
     m = pl.program_id(0)
     core = s_ref[0]
@@ -132,14 +135,17 @@
         own_seg = seg_vec(s_ref, pos)
         for tap in range(CONV - 1):
             mask[tap] = jnp.where(seg_vec(s_ref, pos - 3 + tap) == own_seg, 1.0, 0.0)
-        gs[0:8] = halo_g[:, 0:512].astype(F32)
+        gs[0:8] = halo_g[:, 0:512].astype(F32)[8:]
         gs[8 : 8 + half] = jnp.where(first, g_own[:, 0:512], g_rec[:, 0:512]).astype(F32)
         gs[8 + half :] = jnp.where(first, g_rec[:, 0:512], g_own[:, 0:512]).astype(F32)
         weight = wg[...].astype(F32)
         for j in range(BLOCKS):
-            both = conv_rows(gs, j * BLOCK, weight, bg[...], mask).astype(BF16)
-            bcc_out[pl.ds(j * BLOCK, BLOCK), :] = both
-            bt[j] = both[:, 0:STATE].astype(F32).T.astype(BF16)
+            for strip in range(4):
+                lanes = slice(strip * LANES, (strip + 1) * LANES)
+                tile = conv_tile(gs, j * BLOCK, lanes, weight, bg, mask).astype(BF16)
+                bcc_out[pl.ds(j * BLOCK, BLOCK), lanes] = tile
+                if strip < 2:
+                    bt[j, lanes, :] = tile.astype(F32).T.astype(BF16)
         cache_rows(s_ref, gs, cache)
         cg_out[...] = cache[...].astype(BF16)
         raw_a = jnp.where(first, g_own[:, 512:640], g_rec[:, 512:640]).astype(F32)
@@ -169,19 +175,23 @@
         keeps.append(jnp.where(before == seg_at(s_ref, CHIP_TOKENS - 1), jnp.exp2(total), 0.0))
         keep3[...] = pack3(rows_of(keeps, 16, LANES))
 
-    xs[0:8] = halo_x[...].astype(F32)
+    xs[0:8] = halo_x[...].astype(F32)[8:]
     xs[8 : 8 + half] = jnp.where(first, x_own[...], x_rec[...]).astype(F32)
     xs[8 + half :] = jnp.where(first, x_rec[...], x_own[...]).astype(F32)
     weight = wx[...].astype(F32)
     spread = spread_matrix(chunk)
     keep = mm(keep3[...], spread)
-    state = None
     for j in range(BLOCKS):
-        xc = conv_rows(xs, j * BLOCK, weight, bx[...], mask).astype(BF16)
-        xc_out[pl.ds(j * BLOCK, BLOCK), :] = xc
-        scaled = (xc.astype(F32) * mm(wp3[pl.ds(j * BLOCK, BLOCK), :], spread)).astype(BF16)
-        fresh = mm(bt[j], scaled)
-        state = fresh if j == 0 else keep[j : j + 1] * state + fresh
+        rows = pl.ds(j * BLOCK, BLOCK)
+        wide[...] = mm(wp3[rows, :], spread)
+        for strip in range(CHUNK // LANES):
+            lanes = slice(strip * LANES, (strip + 1) * LANES)
+            xc = conv_tile(xs, j * BLOCK, lanes, weight, bx, mask).astype(BF16)
+            xc_out[rows, lanes] = xc
+            scaled[rows, lanes] = (xc.astype(F32) * wide[:, lanes]).astype(BF16)
+    state = mm(bt[0], scaled[0:BLOCK, :])
+    for j in range(1, BLOCKS):
+        state = keep[j : j + 1] * state + mm(bt[j], scaled[pl.ds(j * BLOCK, BLOCK), :])
     cache_rows(s_ref, xs, cache)
     cx_out[...] = cache[...].astype(BF16)
     tail = rows_of(split3(keep[BLOCKS : BLOCKS + 1]), 16, CHUNK).astype(BF16)
@@ -208,8 +218,8 @@
             num_scalar_prefetch=1,
             grid=(RING,),
             in_specs=[
-                chunked(half, RING), chunked(half), chunked(8), chunked(CONV, RING), chunked(1, RING),
-                fixed((half, 1024)), side, pl.BlockSpec((8, 1024), lambda m, s: (0, 2)),
+                chunked(half, RING), chunked(half), chunked(16), chunked(CONV, RING), chunked(1, RING),
+                fixed((half, 1024)), side, pl.BlockSpec((16, 1024), lambda m, s: (0, 2)),
                 fixed((CONV, 512)), fixed((1, 512)), fixed((8, LANES)),
             ],
             out_specs=[fixed((STATE + 16, CHUNK))] * RING + [
@@ -224,6 +234,8 @@
                 pltpu.VMEM((16, LANES), BF16),
                 pltpu.VMEM((BLOCKS, STATE, BLOCK), BF16),
                 pltpu.VMEM((16, CHUNK), F32),
+                pltpu.VMEM((BLOCK, CHUNK), F32),
+                pltpu.VMEM((CHIP_TOKENS, CHUNK), BF16),
             ],
         ),
         out_shape=[jax.ShapeDtypeStruct((STATE + 16, CHUNK), BF16)] * RING + [
@@ -234,16 +246,16 @@
             jax.ShapeDtypeStruct((16, GROUP_CH), BF16),
             jax.ShapeDtypeStruct((16, 512), BF16),
         ],
-        compiler_params=pltpu.CompilerParams(vmem_limit_bytes=VMEM),
+        compiler_params=pltpu.CompilerParams(vmem_limit_bytes=16 * MIB),
         cost_estimate=pl.CostEstimate(flops=6 * 10**9, bytes_accessed=8 * 10**6, transcendentals=10**6),
         name="conv_and_states",
     )(scalars, x_in, recv, halo, wx, bx, g_own, recv, halo, wg, bg, vecs)
 
 
 def kernel_b(
-    s_ref, xc_ref, bcc, dtc, skip, cx, cg,
+    s_ref, xc_ref, bcc, dtc, skip, cx, cg, near_same, near_cross, far_same, far_cross,
     f0, f1, f2, f3, local_out,
-    wp3, wb3, keep3, bt, gm, cum_t, dt_t, wf3,
+    wp3, wb3, keep3, bt, gm, cum_t, dt_t, wf3, wide, reach, carried, scaled, parts, dec_rows,
 ):
     m = pl.program_id(0)
     chunk = s_ref[1] ^ m
@@ -293,6 +305,15 @@
 
             total = total + end
         keep3[...] = pack3(rows_of(keeps + [cut_keep, cut_reach], 16, LANES))
+        core, upper = s_ref[0], s_ref[2]
+        for top in range(2):
+            for source in range(CORES):
+                near = jnp.where(core == source, near_same[...], near_cross[...])
+                far = jnp.where(core == source, far_same[...], far_cross[...])
+                value = jnp.where(upper == top, near, far).astype(F32)
+                for step in range(STEPS):
+                    at = 32 * top + 8 * step + ROWS * source
+                    dec_rows[at : at + ROWS, :] = value[ROWS * step : ROWS * step + ROWS, :]
 
     spread = spread_matrix(chunk)
     keep = mm(keep3[...], spread)
@@ -306,23 +327,31 @@
             out[STATE : STATE + 16] = rows_of(split3(keep[BLOCKS + 1 : BLOCKS + 2]), 16, CHUNK).astype(BF16)
             out[STATE + 16 : STATE + 32] = cx[...]
             out[STATE + 32 : STATE + 48] = cg[...]
+            at = pl.multiple_of(chunk * CHUNK, CHUNK)
+            out[DEC : DEC + 64] = dec_rows[:, pl.ds(at, CHUNK)].astype(BF16)
+            out[DEC + 64 : DEC + 128] = dec_rows[:, GROUP_CH : GROUP_CH + 512].astype(BF16)
+            for part in range(4):
+                steps = dec_rows[16 * part : 16 * part + 16, GROUP_CH + 512 : GROUP_CH + 640]
+                out[DEC + 128 : DEC + 144, part * LANES : (part + 1) * LANES] = steps.astype(BF16)
 
     state = None
     pairs = CHUNK // LANES
+    heads = chunk * (CHUNK // HEAD_DIM)
+    heads_tile = pl.ds(pl.multiple_of(heads, 8), 8)
     for j in range(BLOCKS):
         rows = slice(j * BLOCK, (j + 1) * BLOCK)
-        xc = xc_ref[rows]
-        xf = xc.astype(F32)
-        base = skip[...] * xf
         if j > 0:
             high = state.astype(BF16)
-            low = (state - high.astype(F32)).astype(BF16)
+            parts[0:STATE] = high
+            parts[STATE:] = (state - high.astype(F32)).astype(BF16)
             c_rows = bcc[rows, STATE : 2 * STATE]
-            base = base + mm(wb3[rows], spread) * (mm(c_rows, high) + mm(c_rows, low))
-
-        def cut_state(state, xf):
-            scaled = (xf * mm(wf3[...], spread)).astype(BF16)
-            fresh = mm(bt[j], scaled)
+            carried[...] = mm(jnp.concatenate([c_rows, c_rows], axis=1), parts[...])
+            reach[...] = mm(wb3[rows], spread)
+
+        @pl.when((cut >= 0) & (cut_block == j))
+        def _():
+            wide[...] = mm(wf3[...], spread)
+            fresh = mm(bt[j], (xc_ref[rows].astype(F32) * wide[...]).astype(BF16))
             if j > 0:
                 fresh = keep[BLOCKS : BLOCKS + 1] * state + fresh
             for index, out in enumerate(outs):
@@ -331,34 +360,33 @@
                 def _():
                     out[0:STATE] = fresh.astype(BF16)
 
-        @pl.when((cut >= 0) & (cut_block == j))
-        def _():
-            cut_state(state, xf)
-
         if j < BLOCKS - 1:
-            scaled = (xf * mm(wp3[rows], spread)).astype(BF16)
-            fresh = mm(bt[j], scaled)
+            wide[...] = mm(wp3[rows], spread)
+            for pair in range(pairs):
+                lanes = slice(pair * LANES, (pair + 1) * LANES)
+                scaled[:, lanes] = (xc_ref[rows, lanes].astype(F32) * wide[:, lanes]).astype(BF16)
+            fresh = mm(bt[j], scaled[...])
             state = fresh if j == 0 else keep[j : j + 1] * state + fresh
         cum = dtc[CHIP_TOKENS + j * BLOCK : CHIP_TOKENS + (j + 1) * BLOCK]
-        heads = chunk * (CHUNK // HEAD_DIM)
         turned = pltpu.roll(cum, LANES - heads, 1)
-        cum_rows = cum_t[j, pl.ds(pl.multiple_of(heads, 8), 8), :]
-        dt_rows = dt_t[j, pl.ds(pl.multiple_of(heads, 8), 8), :]
-        score = gm[j]
+        cum_rows = cum_t[j, heads_tile, :]
+        dt_rows = dt_t[j, heads_tile, :]
         for pair in range(pairs):
             weights = []
             for head in (2 * pair, 2 * pair + 1):
                 gap = jnp.minimum(turned[:, head : head + 1] - cum_rows[head : head + 1], 0.0)
-                weights.append((jnp.exp2(gap) * (score * dt_rows[head : head + 1])).astype(BF16))
+                weights.append((jnp.exp2(gap) * (gm[j] * dt_rows[head : head + 1])).astype(BF16))
             lanes = slice(pair * LANES, (pair + 1) * LANES)
-            two = xc[:, lanes]
+            two = xc_ref[rows, lanes]
             zero = jnp.zeros_like(two)
             stacked = jnp.concatenate([jnp.where(half_lane, two, zero), jnp.where(half_lane, zero, two)], axis=0)
-            inner = mm(jnp.concatenate(weights, axis=1), stacked)
-            local_out[rows, lanes] = inner + base[:, lanes]
-
-
-def run_b(scalars, xc, bcc, dtc, skip, cx, cg):
+            value = mm(jnp.concatenate(weights, axis=1), stacked) + skip[:, lanes] * two.astype(F32)
+            if j > 0:
+                value = value + reach[:, lanes] * carried[:, lanes]
+            local_out[rows, lanes] = value
+
+
+def run_b(scalars, xc, bcc, dtc, skip, cx, cg, dec_hops):
     def fixed(shape):
         return pl.BlockSpec(shape, lambda m, s: (0,) * len(shape))
 
@@ -373,8 +401,8 @@
             in_specs=[
                 chunked(CHIP_TOKENS), fixed((CHIP_TOKENS, 512)), fixed((2 * CHIP_TOKENS, LANES)),
                 chunked(1, RING), chunked(16), fixed((16, 512)),
-            ],
-            out_specs=[fixed((STATE + 48, CHUNK))] * RING + [chunked(CHIP_TOKENS)],
+            ] + [fixed((16, WIDE))] * 4,
+            out_specs=[fixed((MSG, CHUNK))] * RING + [chunked(CHIP_TOKENS)],
             scratch_shapes=[
                 pltpu.VMEM((CHIP_TOKENS, LANES), BF16),
                 pltpu.VMEM((CHIP_TOKENS, LANES), BF16),
@@ -384,14 +412,20 @@
                 pltpu.VMEM((BLOCKS, LANES, BLOCK), F32),
                 pltpu.VMEM((BLOCKS, LANES, BLOCK), F32),
                 pltpu.VMEM((BLOCK, LANES), BF16),
+                pltpu.VMEM((BLOCK, CHUNK), F32),
+                pltpu.VMEM((BLOCK, CHUNK), F32),
+                pltpu.VMEM((BLOCK, CHUNK), F32),
+                pltpu.VMEM((BLOCK, CHUNK), BF16),
+                pltpu.VMEM((2 * STATE, CHUNK), BF16),
+                pltpu.VMEM((64, WIDE), F32),
             ],
         ),
-        out_shape=[jax.ShapeDtypeStruct((STATE + 48, CHUNK), BF16)] * RING
-        + [jax.ShapeDtypeStruct((CHIP_TOKENS, GROUP_CH), F32)],
-        compiler_params=pltpu.CompilerParams(vmem_limit_bytes=VMEM),
+        out_shape=[jax.ShapeDtypeStruct((MSG, CHUNK), BF16)] * RING
+        + [pltpu.HBM((CHIP_TOKENS, GROUP_CH), F32)],
+        compiler_params=pltpu.CompilerParams(vmem_limit_bytes=14 * MIB),
         cost_estimate=pl.CostEstimate(flops=12 * 10**9, bytes_accessed=8 * 10**6, transcendentals=2 * 10**6),
         name="output_within_chip",
-    )(scalars, xc, bcc, dtc, skip, cx, cg)
+    )(scalars, xc, bcc, dtc, skip, cx, cg, *dec_hops)
 
 
 def pick(refs, which, rows):
@@ -439,7 +473,7 @@
             out_specs=jax.tree.map(lambda _: pl.BlockSpec(memory_space=pltpu.VMEM), out_shape),
             out_shape=out_shape,
             scratch_shapes=list(scratch),
-            compiler_params=pltpu.CompilerParams(vmem_limit_bytes=VMEM),
+            compiler_params=pltpu.CompilerParams(vmem_limit_bytes=8 * MIB),
             cost_estimate=pl.CostEstimate(flops=flops, bytes_accessed=3 * 10**6, transcendentals=0),
             name=name,
         )(scalars, *args)
@@ -448,13 +482,13 @@
 
 
 def kernel_decode(
-    s_ref, l0, l1, l2, l3, start, f0, f1, f2, f3, d0, d1, d2, d3,
+    s_ref, l0, l1, l2, l3, start, f0, f1, f2, f3,
     wx, bx, wg, bg, vecs, skip, bounds,
     keep_out, send_out,
     final, rows_f32, result,
 ):
     z, upper = s_ref[1], s_ref[2]
-    ls, fs, ds = (l0, l1, l2, l3), (f0, f1, f2, f3), (d0, d1, d2, d3)
+    ls, fs = (l0, l1, l2, l3), (f0, f1, f2, f3)
     lasts = [bounds[q] - 1 for q in range(PROMPTS)]
     final[...] = jnp.zeros_like(final)
     state = start[...].astype(F32)
@@ -481,8 +515,12 @@
     cache_x = sum(f[STATE + 16 : STATE + 32].astype(F32) for f in fs)
     cache_g = sum(f[STATE + 32 : STATE + 48].astype(F32) for f in fs)
     spread = spread_matrix(z)
-    for index, d in enumerate(ds):
-        rows_f32[index] = d[...].astype(F32)
+    for index, f in enumerate(fs):
+        rows_f32[index, :, 0:CHUNK] = f[DEC : DEC + 64].astype(F32)
+        rows_f32[index, :, CHUNK : CHUNK + 512] = f[DEC + 64 : DEC + 128].astype(F32)
+        for part in range(4):
+            steps = f[DEC + 128 : DEC + 144, part * LANES : (part + 1) * LANES].astype(F32)
+            rows_f32[index, 16 * part : 16 * part + 16, CHUNK + 512 :] = steps
 
     def step_rows(step, lanes):
         tiles = [
@@ -557,12 +595,13 @@
 def kernel_d(s_ref, local, c_rows, wc3, r0, r1, r2, r3, out):
     m = pl.program_id(0)
     spread = spread_matrix(s_ref[1] ^ m)
-    factor = mm(wc3[...], spread)
     for index, r in enumerate((r0, r1, r2, r3)):
 
         @pl.when(m == index)
         def _():
-            out[...] = (local[...] + factor * mm(c_rows[...], r[...])).astype(BF16)
+            for lanes in (slice(0, 256), slice(256, 512)):
+                factor = mm(wc3[...], spread[:, lanes])
+                out[:, lanes] = (local[:, lanes] + factor * mm(c_rows[...], r[:, lanes])).astype(BF16)
 
 
 def run_d(scalars, local, bcc, wc3, starts, own):
@@ -571,6 +610,7 @@
     def row(s):
         return s[0] if own else 1 - s[0]
 
+    width = CORES * GROUP_CH if own else GROUP_CH
     return pl.pallas_call(
         kernel_d,
         grid_spec=pltpu.PrefetchScalarGridSpec(
@@ -581,13 +621,102 @@
                 pl.BlockSpec((half, STATE), lambda m, s: (row(s), 1)),
                 pl.BlockSpec((half, LANES), lambda m, s: (row(s), 0)),
             ] + [pl.BlockSpec((STATE, CHUNK), lambda m, s: (0, 0))] * RING,
-            out_specs=pl.BlockSpec((half, CHUNK), lambda m, s: (0, s[1] ^ m)),
+            out_specs=pl.BlockSpec((half, CHUNK), lambda m, s: (0, (s[0] * RING if own else 0) + (s[1] ^ m))),
         ),
-        out_shape=jax.ShapeDtypeStruct((half, GROUP_CH), BF16),
-        compiler_params=pltpu.CompilerParams(vmem_limit_bytes=VMEM),
+        out_shape=jax.ShapeDtypeStruct((half, width), BF16),
+        compiler_params=pltpu.CompilerParams(vmem_limit_bytes=8 * MIB),
         cost_estimate=pl.CostEstimate(flops=10**9, bytes_accessed=4 * 10**6, transcendentals=0),
         name="carried_own" if own else "carried_other",
     )(scalars, local, bcc, wc3, *starts)
+
+
+def kernel_put(s_ref, part, whole, out):
+    out[...] = part[...]
+
+
+def put_group(scalars, whole, part):
+    half = CHIP_TOKENS // 2
+    return pl.pallas_call(
+        kernel_put,
+        grid_spec=pltpu.PrefetchScalarGridSpec(
+            num_scalar_prefetch=1,
+            grid=(2,),
+            in_specs=[
+                pl.BlockSpec((half, GROUP_CH // 2), lambda m, s: (0, m)),
+                pl.BlockSpec(memory_space=pl.ANY),
+            ],
+            out_specs=pl.BlockSpec((half, GROUP_CH // 2), lambda m, s: (0, (1 - s[0]) * 2 + m)),
+        ),
+        out_shape=jax.ShapeDtypeStruct(whole.shape, BF16),
+        input_output_aliases={2: 0},
+        compiler_params=pltpu.CompilerParams(vmem_limit_bytes=4 * MIB),
+        cost_estimate=pl.CostEstimate(flops=0, bytes_accessed=2 * 10**6, transcendentals=0),
+        name="put_group",
+    )(scalars, part, whole)
+
+
+def side_tiles(bc, dt, group):
+    lane = lax.broadcasted_iota(jnp.int32, (64, LANES), 1)
+    head = lax.broadcasted_iota(jnp.int32, (64, LANES), 0)
+    copies = jnp.where(((lane & (REP - 1)) + group * REP == head) & (lane < 3 * REP), 1.0, 0.0).astype(BF16)
+    first = group == 0
+    return [
+        jnp.where(first, bc[:, 0, 0:STATE], bc[:, 0, STATE : 2 * STATE]),
+        jnp.where(first, bc[:, 1, 0:STATE], bc[:, 1, STATE : 2 * STATE]),
+        mm(dt[...], copies).astype(BF16),
+    ]
+
+
+def kernel_pack(s_ref, x, bc, dt, x_last, bc_last, dt_last, send, halo0, halo1, side):
+    core = s_ref[0]
+    rows = x.shape[0]
+    send[:, 0:GROUP_CH] = x[...]
+    for target, group, offset in ((send, 1 - core, GROUP_CH), (side, core, 0)):
+        b_tile, c_tile, steps = side_tiles(bc, dt, group)
+        target[:, offset : offset + STATE] = b_tile
+        target[:, offset + STATE : offset + 2 * STATE] = c_tile
+        target[:, offset + 2 * STATE : offset + 2 * STATE + LANES] = steps
+        target[:, offset + 2 * STATE + LANES : offset + 1024] = jnp.zeros((rows, 384), BF16)
+
+    @pl.when(pl.program_id(0) == 0)
+    def _():
+        for group, halo in ((0, halo0), (1, halo1)):
+            b_tile, c_tile, _ = side_tiles(bc_last, dt_last, jnp.int32(group))
+            halo[:, 0:GROUP_CH] = x_last[:, group * GROUP_CH : (group + 1) * GROUP_CH]
+            halo[:, GROUP_CH : GROUP_CH + STATE] = b_tile
+            halo[:, GROUP_CH + STATE : GROUP_CH + 2 * STATE] = c_tile
+            halo[:, GROUP_CH + 2 * STATE :] = jnp.zeros((16, 512), BF16)
+
+
+def run_pack(core, x, bc, dt):
+    rows = x.shape[0]
+    tile = rows // RING
+    last = rows // 16 - 1
+    return pl.pallas_call(
+        kernel_pack,
+        grid_spec=pltpu.PrefetchScalarGridSpec(
+            num_scalar_prefetch=1,
+            grid=(RING,),
+            in_specs=[
+                pl.BlockSpec((tile, GROUP_CH), lambda i, s: (i, 1 - s[0])),
+                pl.BlockSpec((tile, 2, 512), lambda i, s: (i, 0, 0)),
+                pl.BlockSpec((tile, 64), lambda i, s: (i, 0)),
+                pl.BlockSpec((16, CORES * GROUP_CH), lambda i, s: (last, 0)),
+                pl.BlockSpec((16, 2, 512), lambda i, s: (last, 0, 0)),
+                pl.BlockSpec((16, 64), lambda i, s: (last, 0)),
+            ],
+            out_specs=[
+                pl.BlockSpec((tile, WIDE), lambda i, s: (i, 0)),
+                pl.BlockSpec((16, WIDE), lambda i, s: (0, 0)),
+                pl.BlockSpec((16, WIDE), lambda i, s: (0, 0)),
+                pl.BlockSpec((tile, 1024), lambda i, s: (i, 0)),
+            ],
+        ),
+        out_shape=[jax.ShapeDtypeStruct(shape, BF16) for shape in ((rows, WIDE), (16, WIDE), (16, WIDE), (rows, 1024))],
+        compiler_params=pltpu.CompilerParams(vmem_limit_bytes=8 * MIB),
+        cost_estimate=pl.CostEstimate(flops=10**6, bytes_accessed=4 * 10**6, transcendentals=0),
+        name="pack",
+    )(core[None], x, bc, dt, x, bc, dt)
 
 
 def on_device(
@@ -600,7 +729,7 @@
     z = (place // CORES) % RING
     upper = place // (CORES * RING)
     anchor = (place // CORES) * CHIP_TOKENS
-    bounds = jnp.cumsum(lengths[0]).astype(jnp.int32)
+    bounds = jnp.stack([lengths[0, 0], lengths[0, 0] + lengths[0, 1], jnp.sum(lengths[0])]).astype(jnp.int32)
     zero = jnp.int32(0)
     scalars = jnp.stack([core, z, upper, anchor, bounds[0] - anchor, bounds[1] - anchor, zero, zero]).astype(jnp.int32)
     both = ("pool", "dp")
@@ -617,44 +746,34 @@
         last = jnp.zeros((rows, REP), BF16) if extra is None else jnp.broadcast_to(extra, (rows, REP))
         return jnp.concatenate([b_c, steps, steps, steps, last, jnp.zeros((rows, 384), BF16)], axis=1)
 
-    tokens, bc_rows, dt_rows = x_in[0], bc_in[0], dt_raw[0]
-    recv = lax.ppermute(
-        group_part(tokens, bc_rows, dt_rows, 1 - core), "dp", [(i, i ^ 1) for i in range(count)]
-    )
-    rim = CONV - 1
-    halo = None
-    for group in range(CORES):
-        rows = group_part(tokens[-rim:], bc_rows[-rim:], dt_rows[-rim:], group)
-        rows = jnp.pad(rows, ((8 - rim, 0), (0, 0)))
-        part = lax.ppermute(rows, "dp", [(i, i + 1 + group) for i in range(1, count - 1, 2)])
-        halo = part if halo is None else halo + part
+    x_rows, bc_rows, dt_rows = (in_hbm(value[0]) for value in (x_in, bc_in, dt_raw))
+    packed, halo0, halo1, g_own = run_pack(core.astype(jnp.int32), x_rows, bc_rows, dt_rows)
+    recv = lax.ppermute(packed, "dp", [(i, i ^ 1) for i in range(count)])
+    halo = lax.ppermute(halo0, "dp", [(i, i + 1) for i in range(1, count - 1, 2)])
+    halo = halo + lax.ppermute(halo1, "dp", [(i, i + 2) for i in range(1, count - 1, 2)])
+
+    def after(value, other):
+        return lax.optimization_barrier((value, other))[0]
 
     dec_rows = STEPS * ROWS
-    d_x = dec_x[0, 0].reshape(dec_rows, -1)
-    d_bc = dec_bc[0, 0].reshape(dec_rows, 2, -1)
-    d_dt = dec_dt[0, 0].reshape(dec_rows, -1)
+    d_x, d_bc, d_dt = after((dec_x, dec_bc, dec_dt), halo1)
+    d_x = d_x[0, 0].reshape(dec_rows, -1)
+    d_bc = d_bc[0, 0].reshape(dec_rows, 2, -1)
+    d_dt = d_dt[0, 0].reshape(dec_rows, -1)
     d_prompt = jnp.tile(decode_prompt[0, 0].astype(BF16), STEPS)[:, None]
     total = 2 * count
-    same = lax.ppermute(
-        group_part(d_x, d_bc, d_dt, core, d_prompt), both, [(i, (i + count) % total) for i in range(total)]
-    )
-    cross = lax.ppermute(
-        group_part(d_x, d_bc, d_dt, 1 - core, d_prompt), both, [(i, ((i + count) % total) ^ 1) for i in range(total)]
-    )
-    pair = jnp.where(core == 0, jnp.stack([same, cross]), jnp.stack([cross, same]))
-    pair = pair.reshape(CORES, STEPS, ROWS, WIDE).swapaxes(0, 1).reshape(CORES * dec_rows, WIDE)
-    far = lax.ppermute(pair, "dp", [(i, i ^ (CORES * RING)) for i in range(count)])
-    queries = jnp.where(upper == 0, jnp.concatenate([pair, far]), jnp.concatenate([far, pair]))
+    d_same = group_part(d_x, d_bc, d_dt, core, d_prompt)
+    d_cross = group_part(d_x, d_bc, d_dt, 1 - core, d_prompt)
+
+    def hop(value, flip):
+        return lax.ppermute(value, both, [(i, ((i + count) % total) ^ flip) for i in range(total)])
+
+    dec_hops = [hop(d_same, 0), hop(d_cross, 1), hop(d_same, CORES * RING), hop(d_cross, CORES * RING + 1)]
 
     def z_swap(value, m):
         if m == 0:
             return value
         return lax.ppermute(value, "dp", [(i, i ^ (CORES * m)) for i in range(count)])
-
-    dec_parts = []
-    for m in range(RING):
-        channels = lax.dynamic_slice_in_dim(queries, (z ^ m) * CHUNK, CHUNK, 1)
-        dec_parts.append(z_swap(jnp.concatenate([channels, queries[:, GROUP_CH : GROUP_CH + 640]], axis=1), m))
 
     w_group = lax.dynamic_slice_in_dim(conv_w_bc, core * STATE, STATE, 2).reshape(CONV, 2 * STATE)
     b_group = lax.dynamic_slice_in_dim(conv_b_bc, core * STATE, STATE, 1).reshape(1, 2 * STATE)
@@ -664,11 +783,12 @@
     vecs = jnp.pad(jnp.tile(heads, (1, 3)), ((0, 6), (0, LANES - 3 * REP)))
     skip = jnp.repeat(d_skip, HEAD_DIM)[None]
     b_x = conv_b_x[None]
-    g_own = group_side(bc_rows, dt_rows, core)
-
-    *ls, xc, bcc, dtc, wc3, cx, cg = run_a(scalars, tokens, recv, halo, conv_w_x, b_x, g_own, w_group, b_group, vecs)
-    ls = [z_swap(part, m) for m, part in enumerate(ls)]
-    *fs, local = run_b(scalars, xc, bcc, dtc, skip, cx, cg)
+
+    *ls, xc, bcc, dtc, wc3, cx, cg = run_a(scalars, x_rows, recv, halo, conv_w_x, b_x, g_own, w_group, b_group, vecs)
+    sent_ls = [z_swap(part, m) for m, part in enumerate(ls)]
+    *fs, local = run_b(scalars, xc, bcc, dtc, skip, cx, cg, dec_hops)
+    local = in_hbm(local)
+    ls = after(tuple(sent_ls), fs[0])
     fs = [z_swap(part, m) for m, part in enumerate(fs)]
 
     state_shape = jax.ShapeDtypeStruct((STATE, CHUNK), BF16)
@@ -682,7 +802,7 @@
 
     def decode(bounds_ref_args):
         shape = jax.ShapeDtypeStruct((RING, 32, CHUNK), BF16)
-        args = [*ls, start, *fs, *dec_parts, own_columns(conv_w_x), own_columns(b_x), w_group, b_group, vecs, own_columns(skip)]
+        args = [*ls, start, *fs, own_columns(conv_w_x), own_columns(b_x), w_group, b_group, vecs, own_columns(skip)]
         return pl.pallas_call(
             kernel_decode,
             in_specs=[pl.BlockSpec(memory_space=pltpu.SMEM)]
@@ -695,34 +815,29 @@
                 pltpu.VMEM((RING, 64, 1152), F32),
                 pltpu.VMEM((RING, 64, CHUNK), F32),
             ],
-            compiler_params=pltpu.CompilerParams(vmem_limit_bytes=VMEM),
-            cost_estimate=pl.CostEstimate(flops=4 * 10**9, bytes_accessed=6 * 10**6, transcendentals=0),
+            compiler_params=pltpu.CompilerParams(vmem_limit_bytes=14 * MIB),
+            cost_estimate=pl.CostEstimate(flops=20 * 10**9, bytes_accessed=6 * 10**6, transcendentals=0),
             name="decode_rows",
         )(scalars, *args, bounds_ref_args)
 
-    kept, sent = decode(bounds)
-    answers = kept + lax.ppermute(sent, "dp", [(i, i ^ (CORES * RING)) for i in range(count)])
-    answers = jnp.stack([z_swap(answers[m], m) for m in range(RING)])
-    answers = jnp.concatenate(
-        [lax.dynamic_index_in_dim(answers, z ^ j, 0, keepdims=False) for j in range(RING)], axis=1
-    )
-    answers = answers.reshape(STEPS, CORES, ROWS, GROUP_CH)
-
-    def answers_of(source):
-        return lax.dynamic_index_in_dim(answers, source, 1, keepdims=False).reshape(dec_rows, GROUP_CH)
-
-    same = lax.ppermute(answers_of(core), both, [(i, (i + count) % total) for i in range(total)])
-    cross = lax.ppermute(answers_of(1 - core), both, [(i, ((i + count) % total) ^ 1) for i in range(total)])
-    decoded = jnp.where(core == 0, jnp.concatenate([same, cross], axis=1), jnp.concatenate([cross, same], axis=1))
-
+    kept, sent = after(tuple(decode(bounds)), starts[1])
     other_rows = run_d(scalars, local, bcc, wc3, starts, False)
     other_group = lax.ppermute(other_rows, "dp", [(i, i ^ 1) for i in range(count)])
+    straight = lax.ppermute(kept, both, [(i, (i + count) % total) for i in range(total)])
+    crossed = lax.ppermute(sent, both, [(i, ((i + count) % total) ^ (CORES * RING)) for i in range(total)])
+    answers = after(straight + crossed, other_rows)
+    answers = [z_swap(answers[m], m) for m in range(RING)]
+    columns = [
+        functools.reduce(lambda a, m: jnp.where(z == j ^ m, answers[m], a), range(1, RING), answers[0])
+        for j in range(RING)
+    ]
+    answers = jnp.concatenate(columns, axis=1).reshape(STEPS, CORES, ROWS, GROUP_CH)
+    first, second = (answers[:, i].reshape(dec_rows, GROUP_CH) for i in range(CORES))
+    mine = jnp.where(core == 0, first, second)
+    theirs = lax.ppermute(jnp.where(core == 0, second, first), "dp", [(i, i ^ 1) for i in range(count)])
+    decoded = jnp.where(core == 0, jnp.concatenate([mine, theirs], axis=1), jnp.concatenate([theirs, mine], axis=1))
     own_group = run_d(scalars, local, bcc, wc3, starts, True)
-    out = jnp.where(
-        core == 0,
-        jnp.concatenate([own_group, other_group], axis=1),
-        jnp.concatenate([other_group, own_group], axis=1),
-    )
+    out = put_group(scalars, own_group, other_group)
     return out[None], decoded.reshape(dec_x.shape)
 
 

time: 152 us -> 112 us (0.74)
  local copies, waits for them, and re-layouts: 19.6 us -> 6.87 us
  waiting for transfers between devices: 24.4 us -> 13.5 us
  Pallas kernels: 53.7 us -> 46.6 us
  starting transfers between devices: 43.9 us -> 38.9 us
  other arithmetic: 7.11 us -> 2.89 us
    ppermute x9 -> x10, waiting for transfers between devices: 10.8 us -> 0.03 us  [the longest x4 0.01 us: hop(): lax.ppermute(value, both, [(i, (i + count) % total ^ flip) for i in range...]
    pallas_call x0 -> x2, Pallas kernels: none -> 7.23 us  [the longest x1 4.64 us: run_pack(): pl.pallas_call(kernel_pack, grid_spec=pltpu.PrefetchScalarGridSpec(num_sc...]
    pallas_call x1, Pallas kernels: 15.6 us -> 10.5 us  [run_a(): pl.pallas_call(kernel_a, grid_spec=pltpu.PrefetchScalarGridSpec(num_scala...]
    ppermute x1, starting transfers between devices: 6.4 us -> 2.07 us  [on_device(): lax.ppermute(other_rows, 'dp', [(i, i ^ 1) for i in range(count)])]
    select_n x3 -> x2, other arithmetic: 4.47 us -> 0.78 us  [the longest x1 0.76 us: on_device(): jnp.where(core == 0, jnp.concatenate([mine, theirs], axis=1), jnp.concate...]
    pallas_call x2, Pallas kernels: 5.18 us -> 2.09 us  [run(): pl.pallas_call(kernel, in_specs=[pl.BlockSpec(memory_space=pltpu.SMEM)] +...]
    ppermute x15 -> x12, waiting for transfers between devices: 13.6 us -> 10.9 us  [z_swap(): return lax.ppermute(value, 'dp', [(i, i ^ CORES * m) for i in range(count)])]
    pallas_call x2, Pallas kernels: 11.1 us -> 8.44 us  [run_d(): pl.pallas_call(kernel_d, grid_spec=pltpu.PrefetchScalarGridSpec(num_scala...]
  transfers between devices with their start and end apart: 26 -> 24, of which waited for: 9 -> 6; matrix products, arithmetic and copies ran while one was open for 11% -> 4% of each run, Pallas kernels for 28% -> 35%
where the time goes in v2:
time: 112 us
  Pallas kernels  46.6 us (42%)
  starting transfers between devices  38.9 us (35%)
  waiting for transfers between devices  13.5 us (12%)
  local copies, waits for them, and re-layouts  6.87 us (6%)
  between operations  3.16 us (3%)
  other arithmetic  2.89 us (3%)
    ppermute x12, starting transfers between devices, z_swap(): return lax.ppermute(value, 'dp', [(i, i ^ CORES * m) for i in range(count)])  16.4 us
    pallas_call x1, Pallas kernels, run_b(): pl.pallas_call(kernel_b, grid_spec=pltpu.PrefetchScalarGridSpec(num_scala...  14.4 us
    ppermute x12, waiting for transfers between devices, z_swap(): return lax.ppermute(value, 'dp', [(i, i ^ CORES * m) for i in range(count)])  10.9 us
    pallas_call x1, Pallas kernels, run_a(): pl.pallas_call(kernel_a, grid_spec=pltpu.PrefetchScalarGridSpec(num_scala...  10.5 us
    pallas_call x2, Pallas kernels, run_d(): pl.pallas_call(kernel_d, grid_spec=pltpu.PrefetchScalarGridSpec(num_scala...  8.44 us
    ppermute x4, starting transfers between devices, hop(): lax.ppermute(value, both, [(i, (i + count) % total ^ flip) for i in range...  6.59 us
    unnamed x39, local copies, waits for them, and re-layouts  5.16 us
    pallas_call x1, Pallas kernels, run_pack(): pl.pallas_call(kernel_pack, grid_spec=pltpu.PrefetchScalarGridSpec(num_sc...  4.64 us
  transfers between devices with their start and end apart: 24, of which 6 were waited for; matrix products, arithmetic and copies ran while one was open for 4% of the time, Pallas kernels for 35%

profile of v2, /device:TPU:1, one launch (start us, length us, event | category | flops | bytes accessed | tf_op | source)
XLA Modules:
  0.0 111.9 jit_solution(550194431986309934)
XLA Ops:
  0.6 0.0 copy-start
  0.7 1.5 %copy.21 = bf16[1,256,64]{2,1,0:T(8,128)(2,1)} copy(bf16[1,256,64]{1,2,0:T(8,128)(2,1)} %param.17) | data formatting | bytes 65536 | tf_op args[2]
  2.2 0.0 copy-start.15
  2.2 0.0 copy-start.13
  2.2 0.0 copy-start.11
  2.2 0.0 copy-start.10
  2.2 0.0 copy-start.1
  2.2 0.0 copy-start.2
  2.2 4.6 %pack.1 = (bf16[256,3072]{1,0:T(8,128)(2,1)}, bf16[16,3072]{1,0:T(8,128)(2,1)S(1)}, bf16[16,3072]{1,0:T(8,128)(2,1)S(1)}, bf16[256,1024]{1,0:T(8,128)(2,1)S(1)}) custom-call(s32[1]{0:T(128)} %bitcast.s_ref, bf16[256,4096]{1,0:T(8,128)(2,1)} %bitcast.84, bf16[256,2,512]{2,1,0:T(2,128)(2,1)} %bitcast.88, bf16[256,64]{1,0:T(8,128)(2,1)} %bitcast.90, ...), custom_call_target="tpu_custom_call" | custom-call | flops 1000000 | bytes 4000000 | tf_op jit(solution)/shard_map/pack/pallas_call | solution.py:695
  6.9 1.4 %collective-permute-start = (bf16[256,3072]{1,0:T(8,128)(2,1)}, bf16[256,3072]{1,0:T(8,128)(2,1)S(1)}, u32[]{:S(2)}, u32[]{:S(2)}) collective-permute-start(bf16[256,3072]{1,0:T(8,128)(2,1)} %get-tuple-element.37), channel_id=1, source_target_pairs={{0,1},{1,0},{2,3},{3,2},{4,5},{5,4},{6,7},{7,6},{8,9},{9,8},{10,11... | collective-permute-start | bytes 4718600 | tf_op jit(solution)/shard_map/ppermute | solution.py:751
  8.3 3.6 %collective-permute-start.2 = (bf16[16,3072]{1,0:T(8,128)(2,1)S(1)}, bf16[16,3072]{1,0:T(8,128)(2,1)S(1)}, u32[]{:S(2)}, u32[]{:S(2)}) collective-permute-start(bf16[16,3072]{1,0:T(8,128)(2,1)S(1)} %get-tuple-element.39), channel_id=1, source_target_pairs={{1,3},{3,5},{5,7},{7,9},{9,11},{11,13},{13,15},{17,19},{19,21},{21... | collective-permute-start | bytes 294920 | tf_op jit(solution)/shard_map/ppermute | solution.py:753
  12.1 0.1 broadcast_in_dim.22
  12.2 0.1 constant_dynamic-slice_fusion.2
  12.3 0.1 broadcast_in_dim.23
  12.4 0.1 concatenate.33
  12.5 1.3 %collective-permute-start.3 = (bf16[16,3072]{1,0:T(8,128)(2,1)S(1)}, bf16[16,3072]{1,0:T(8,128)(2,1)S(1)}, u32[]{:S(2)}, u32[]{:S(2)}) collective-permute-start(bf16[16,3072]{1,0:T(8,128)(2,1)S(1)} %concatenate.33), channel_id=1, source_target_pairs={{0,64},{1,65},{2,66},{3,67},{4,68},{5,69},{6,70},{7,71},{8,72},{9,... | collective-permute-start | bytes 294920 | tf_op jit(solution)/shard_map/ppermute | solution.py:769
  13.8 1.9 %collective-permute-start.5 = (bf16[16,3072]{1,0:T(8,128)(2,1)S(1)}, bf16[16,3072]{1,0:T(8,128)(2,1)S(1)}, u32[]{:S(2)}, u32[]{:S(2)}) collective-permute-start(bf16[16,3072]{1,0:T(8,128)(2,1)S(1)} %concatenate.33), channel_id=1, source_target_pairs={{0,72},{1,73},{2,74},{3,75},{4,76},{5,77},{6,78},{7,79},{8,64},{9,... | collective-permute-start | bytes 294920 | tf_op jit(solution)/shard_map/ppermute | solution.py:769
  15.7 1.3 %collective-permute-start.1 = (bf16[16,3072]{1,0:T(8,128)(2,1)S(1)}, bf16[16,3072]{1,0:T(8,128)(2,1)S(1)}, u32[]{:S(2)}, u32[]{:S(2)}) collective-permute-start(bf16[16,3072]{1,0:T(8,128)(2,1)S(1)} %get-tuple-element.38), channel_id=1, source_target_pairs={{1,2},{3,4},{5,6},{7,8},{9,10},{11,12},{13,14},{17,18},{19,20},{21... | collective-permute-start | bytes 294920 | tf_op jit(solution)/shard_map/ppermute | solution.py:752
  17.0 0.1 constant_dynamic-slice_fusion.8
  17.1 0.1 tile.7
  17.3 0.6 fusion.9
  19.9 0.1 broadcast_in_dim.21
  20.0 0.1 broadcast_in_dim_reshape.3.skip
  20.1 0.1 concatenate.34
  20.2 0.1 stack.45.s_ref
  20.3 0.1 collective-permute-start.4
  20.4 3.3 %collective-permute-start.6 = (bf16[16,3072]{1,0:T(8,128)(2,1)S(1)}, bf16[16,3072]{1,0:T(8,128)(2,1)S(1)}, u32[]{:S(2)}, u32[]{:S(2)}) collective-permute-start(bf16[16,3072]{1,0:T(8,128)(2,1)S(1)} %concatenate.34), channel_id=1, source_target_pairs={{0,73},{1,72},{2,75},{3,74},{4,77},{5,76},{6,79},{7,78},{8,65},{9,... | collective-permute-start | bytes 294920 | tf_op jit(solution)/shard_map/ppermute | solution.py:769
  23.7 0.0 copy-start.3
  23.7 1.1 %copy-done.3 = bf16[256,3072]{1,0:T(8,128)(2,1)} copy-done((bf16[256,3072]{1,0:T(8,128)(2,1)}, bf16[256,3072]{1,0:T(8,128)(2,1)S(1)}, u32[]{:S(2)}) %copy-start.3) | copy-done | bytes 1572888
  24.9 1.4 %copy-done.4 = bf16[256,3072]{1,0:T(8,128)(2,1)S(1)} copy-done((bf16[256,3072]{1,0:T(8,128)(2,1)S(1)}, bf16[256,3072]{1,0:T(8,128)(2,1)}, u32[]{:S(2)}) %copy-start.4) | copy-done | bytes 1572888
  26.3 10.5 %conv_and_states.1 = (bf16[272,512]{1,0:T(8,128)(2,1)S(1)}, bf16[272,512]{1,0:T(8,128)(2,1)S(1)}, bf16[272,512]{1,0:T(8,128)(2,1)}, bf16[272,512]{1,0:T(8,128)(2...) custom-call(s32[8]{0:T(128)S(1)} %stack.45.s_ref, ...), custom_call_target="tpu_custom_call" | custom-call | flops 6000000000 | bytes 8000000 | tf_op jit(solution)/shard_map/conv_and_states/pallas_call | solution.py:215
  36.8 1.6 %collective-permute-start.8 = (bf16[272,512]{1,0:T(8,128)(2,1)}, bf16[272,512]{1,0:T(8,128)(2,1)S(1)}, u32[]{:S(2)}, u32[]{:S(2)}) collective-permute-start(bf16[272,512]{1,0:T(8,128)(2,1)} %get-tuple-element.53), channel_id=1, source_target_pairs={{0,4},{1,5},{2,6},{3,7},{4,0},{5,1},{6,2},{7,3},{8,12},{9,13},{10,... | collective-permute-start | bytes 835592 | tf_op jit(solution)/shard_map/ppermute | solution.py:776
  38.4 2.3 %collective-permute-start.9 = (bf16[272,512]{1,0:T(8,128)(2,1)S(1)}, bf16[272,512]{1,0:T(8,128)(2,1)S(1)}, u32[]{:S(2)}, u32[]{:S(2)}) collective-permute-start(bf16[272,512]{1,0:T(8,128)(2,1)S(1)} %get-tuple-element.54), channel_id=1, source_target_pairs={{0,6},{1,7},{2,4},{3,5},{4,2},{5,3},{6,0},{7,1},{8,14},{9,15},{10,... | collective-permute-start | bytes 835592 | tf_op jit(solution)/shard_map/ppermute | solution.py:776
  40.7 14.4 %output_within_chip.1 = (bf16[448,512]{1,0:T(8,128)(2,1)S(1)}, bf16[448,512]{1,0:T(8,128)(2,1)}, bf16[448,512]{1,0:T(8,128)(2,1)}, bf16[448,512]{1,0:T(8,128)(2,1)}, f32[512,2048]{1,0:T(8,128)}) custom-call(s32[8]{0:T(128)S(1)} %stack.45.s_ref, bf16[512,2048]{1,0:T(8,128)(2,1)S(1)} %get-tuple-element.41.xc_ref, ...), custom_call_target="tpu_custom_call" | custom-call | flops 12000000000 | bytes 8000000 | tf_op jit(solution)/shard_map/output_within_chip/pallas_call | solution.py:396
  55.0 1.5 %collective-permute-start.16 = (bf16[448,512]{1,0:T(8,128)(2,1)}, bf16[448,512]{1,0:T(8,128)(2,1)}, u32[]{:S(2)}, u32[]{:S(2)}) collective-permute-start(bf16[448,512]{1,0:T(8,128)(2,1)} %get-tuple-element.65), channel_id=1, source_target_pairs={{0,4},{1,5},{2,6},{3,7},{4,0},{5,1},{6,2},{7,3},{8,12},{9,13},{10,... | collective-permute-start | bytes 1376264 | tf_op jit(solution)/shard_map/ppermute | solution.py:776
  56.6 2.3 %collective-permute-start.17 = (bf16[448,512]{1,0:T(8,128)(2,1)}, bf16[448,512]{1,0:T(8,128)(2,1)}, u32[]{:S(2)}, u32[]{:S(2)}) collective-permute-start(bf16[448,512]{1,0:T(8,128)(2,1)} %get-tuple-element.66), channel_id=1, source_target_pairs={{0,6},{1,7},{2,4},{3,5},{4,2},{5,3},{6,0},{7,1},{8,14},{9,15},{10,... | collective-permute-start | bytes 1376264 | tf_op jit(solution)/shard_map/ppermute | solution.py:776
  58.9 0.6 reduce_sum.9
  59.5 0.9 half_total.1
  60.4 2.3 %collective-permute-start.10 = (bf16[256,512]{1,0:T(8,128)(2,1)S(1)}, bf16[256,512]{1,0:T(8,128)(2,1)S(1)}, u32[]{:S(2)}, u32[]{:S(2)}) collective-permute-start(bf16[256,512]{1,0:T(8,128)(2,1)S(1)} %half_total.1), channel_id=1, source_target_pairs={{0,8},{1,9},{2,10},{3,11},{4,12},{5,13},{6,14},{7,15},{16,24},{17,... | collective-permute-start | bytes 786440 | tf_op jit(solution)/shard_map/ppermute | solution.py:796
  62.7 1.3 %pad_add_fusion.bounds = s32[3]{0:T(128)S(1)} fusion(s32[1]{0:T(128)} %bitcast.21, s32[1]{0:T(128)} %bitcast.20, s32[1]{0:T(128)} %bitcast.19), kind=kLoop, calls=%fused_computation.34 | loop fusion | flops 6 | bytes 24 | tf_op jit(solution)/shard_map/stack | solution.py:732
  64.0 0.1 dynamic-slice.3
  64.1 2.6 %collective-permute-done.10.start = bf16[256,512]{1,0:T(8,128)(2,1)S(1)} collective-permute-done((bf16[256,512]{1,0:T(8,128)(2,1)S(1)}, bf16[256,512]{1,0:T(8,128)(2,1)S(1)}, u32[]{:S(2)}, u32[]{:S(2)}) %collective-permute-start.10) | collective-permute-done | bytes 262176 | tf_op jit(solution)/shard_map/ppermute | solution.py:796
  66.7 1.2 %chip_starts.1 = (bf16[256,512]{1,0:T(8,128)(2,1)S(1)}, bf16[256,512]{1,0:T(8,128)(2,1)S(1)}, bf16[256,512]{1,0:T(8,128)(2,1)S(1)}, bf16[256,512]{1,0:T(8,128)(2,1)S(1)}) custom-call(s32[8]{0:T(128)S(1)} %stack.45.s_ref, bf16[272,512]{1,0:T(8,128)(2,1)S(1)} %get-tuple-element.56.l0, bf16[272,512]{1,0:T(8,128)(2,1)S(1)} %collective-permute-done.7.l1, ...), custom_call_target="tpu_custom_call" | custom-call | flops 1000000 | bytes 3000000 | tf_op jit(solution)/shard_map/chip_starts/pallas_call | solution.py:470
  68.0 1.7 %collective-permute-start.11 = (bf16[256,512]{1,0:T(8,128)(2,1)S(1)}, bf16[256,512]{1,0:T(8,128)(2,1)S(1)}, u32[]{:S(2)}, u32[]{:S(2)}) collective-permute-start(bf16[256,512]{1,0:T(8,128)(2,1)S(1)} %get-tuple-element.61), channel_id=1, source_target_pairs={{0,2},{1,3},{2,0},{3,1},{4,6},{5,7},{6,4},{7,5},{8,10},{9,11},{10,... | collective-permute-start | bytes 786440 | tf_op jit(solution)/shard_map/ppermute | solution.py:776
  69.7 3.0 %collective-permute-start.12 = (bf16[256,512]{1,0:T(8,128)(2,1)S(1)}, bf16[256,512]{1,0:T(8,128)(2,1)S(1)}, u32[]{:S(2)}, u32[]{:S(2)}) collective-permute-start(bf16[256,512]{1,0:T(8,128)(2,1)S(1)} %get-tuple-element.62), channel_id=1, source_target_pairs={{0,4},{1,5},{2,6},{3,7},{4,0},{5,1},{6,2},{7,3},{8,12},{9,13},{10,... | collective-permute-start | bytes 786440 | tf_op jit(solution)/shard_map/ppermute | solution.py:776
  72.7 4.1 %collective-permute-done.16.f2 = bf16[448,512]{1,0:T(8,128)(2,1)} collective-permute-done((bf16[448,512]{1,0:T(8,128)(2,1)}, bf16[448,512]{1,0:T(8,128)(2,1)}, u32[]{:S(2)}, u32[]{:S(2)}) %collective-permute-start.16) | collective-permute-done | bytes 458784 | tf_op jit(solution)/shard_map/ppermute | solution.py:776
  76.8 2.6 %collective-permute-done.17.f3 = bf16[448,512]{1,0:T(8,128)(2,1)} collective-permute-done((bf16[448,512]{1,0:T(8,128)(2,1)}, bf16[448,512]{1,0:T(8,128)(2,1)}, u32[]{:S(2)}, u32[]{:S(2)}) %collective-permute-start.17) | collective-permute-done | bytes 458784 | tf_op jit(solution)/shard_map/ppermute | solution.py:776
  79.4 1.0 copy-done.6
  80.4 3.9 %decode_rows.1 = (bf16[4,32,512]{2,1,0:T(8,128)(2,1)S(1)}, bf16[4,32,512]{2,1,0:T(8,128)(2,1)S(1)}) custom-call(s32[8]{0:T(128)S(1)} %stack.45.s_ref, bf16[272,512]{1,0:T(8,128)(2,1)S(1)} %get-tuple-element.56.l0, bf16[272,512]{1,0:T(8,128)(2,1)S(1)} %collective-permute-done.7.l1, bf16[272,512]{1,0:T(8,128)(2,1)S(1)} %collective-permute-done.8.l2, ...), custom_call_target="tpu_custom_call" | custom-call | flops 20000000000 | bytes 6000000 | tf_op jit(solution)/shard_map/decode_rows/pallas_call | solution.py:806
  84.3 1.9 %collective-permute-start.18 = (bf16[4,32,512]{2,1,0:T(8,128)(2,1)S(1)}, bf16[4,32,512]{2,1,0:T(8,128)(2,1)S(1)}, u32[]{:S(2)}, u32[]{:S(2)}) collective-permute-start(bf16[4,32,512]{2,1,0:T(8,128)(2,1)S(1)} %get-tuple-element.69), channel_id=1, source_target_pairs={{0,64},{1,65},{2,66},{3,67},{4,68},{5,69},{6,70},{7,71},{8,72},{9,... | collective-permute-start | bytes 393224 | tf_op jit(solution)/shard_map/ppermute | solution.py:826
  86.3 1.4 %collective-permute-start.19 = (bf16[4,32,512]{2,1,0:T(8,128)(2,1)S(1)}, bf16[4,32,512]{2,1,0:T(8,128)(2,1)S(1)}, u32[]{:S(2)}, u32[]{:S(2)}) collective-permute-start(bf16[4,32,512]{2,1,0:T(8,128)(2,1)S(1)} %get-tuple-element.70), channel_id=1, source_target_pairs={{0,72},{1,73},{2,74},{3,75},{4,76},{5,77},{6,78},{7,79},{8,64},{9,... | collective-permute-start | bytes 393224 | tf_op jit(solution)/shard_map/ppermute | solution.py:827
  87.6 0.4 collective-permute-done.12.r2
  88.0 2.3 %collective-permute-done.13.r3 = bf16[256,512]{1,0:T(8,128)(2,1)S(1)} collective-permute-done((bf16[256,512]{1,0:T(8,128)(2,1)S(1)}, bf16[256,512]{1,0:T(8,128)(2,1)S(1)}, u32[]{:S(2)}, u32[]{:S(2)}) %collective-permute-start.13) | collective-permute-done | bytes 262176 | tf_op jit(solution)/shard_map/ppermute | solution.py:776
  90.3 3.7 %carried_other.1 = bf16[256,2048]{1,0:T(8,128)(2,1)S(1)} custom-call(s32[8]{0:T(128)S(1)} %stack.45.s_ref, f32[512,2048]{1,0:T(8,128)} %get-tuple-element.49.local, bf16[512,512]{1,0:T(8,128)(2,1)S(1)} %get-tuple-element.42.bcc.c_rows, bf16[512,128]{1,0:T(8,128)(2,1)S(1)} %get-tuple-element.50.wc3, bf16[256,512]{1,0:T(8,128)(2,1)S(1)} %get-tuple-element.60.r0, ...), custom_call_target="tpu_custom_call" | custom-call | flops 1000000000 | bytes 4000000 | tf_op jit(solution)/shard_map/carried_other/pallas_call | solution.py:614
  94.1 3.3 %collective-permute-start.20 = (bf16[32,512]{1,0:T(8,128)(2,1)S(1)}, bf16[32,512]{1,0:T(8,128)(2,1)S(1)}, u32[]{:S(2)}, u32[]{:S(2)}) collective-permute-start(bf16[32,512]{1,0:T(8,128)(2,1)S(1)} %get-tuple-element.80), channel_id=1, source_target_pairs={{0,6},{1,7},{2,4},{3,5},{4,2},{5,3},{6,0},{7,1},{8,14},{9,15},{10,... | collective-permute-start | bytes 98312 | tf_op jit(solution)/shard_map/ppermute | solution.py:776
  97.4 0.7 collective-permute-start.22
  98.1 2.1 %collective-permute-start.14 = (bf16[256,2048]{1,0:T(8,128)(2,1)S(1)}, bf16[256,2048]{1,0:T(8,128)(2,1)}, u32[]{:S(2)}, u32[]{:S(2)}) collective-permute-start(bf16[256,2048]{1,0:T(8,128)(2,1)S(1)} %carried_other.1), channel_id=1, source_target_pairs={{0,1},{1,0},{2,3},{3,2},{4,5},{5,4},{6,7},{7,6},{8,9},{9,8},{10,11... | collective-permute-start | bytes 3145736 | tf_op jit(solution)/shard_map/ppermute | solution.py:825
  100.1 1.5 %collective-permute-done.21 = bf16[32,512]{1,0:T(8,128)(2,1)S(1)} collective-permute-done((bf16[32,512]{1,0:T(8,128)(2,1)S(1)}, bf16[32,512]{1,0:T(8,128)(2,1)S(1)}, u32[]{:S(2)}, u32[]{:S(2)}) %collective-permute-start.21) | collective-permute-done | bytes 32800 | tf_op jit(solution)/shard_map/ppermute | solution.py:776
  101.7 0.1 reshape.102
  101.8 0.1 select_bitcast_fusion
  101.9 1.9 %collective-permute-start.23 = (bf16[16,2048]{1,0:T(8,128)(2,1)S(1)}, bf16[16,2048]{1,0:T(8,128)(2,1)S(1)}, u32[]{:S(2)}, u32[]{:S(2)}) collective-permute-start(bf16[16,2048]{1,0:T(8,128)(2,1)S(1)} %select_n.174), channel_id=1, source_target_pairs={{0,1},{1,0},{2,3},{3,2},{4,5},{5,4},{6,7},{7,6},{8,9},{9,8},{10,11... | collective-permute-start | bytes 196616 | tf_op jit(solution)/shard_map/ppermute | solution.py:837
  103.8 4.7 %carried_own.1.whole = bf16[256,4096]{1,0:T(8,128)(2,1)} custom-call(s32[8]{0:T(128)S(1)} %stack.45.s_ref, f32[512,2048]{1,0:T(8,128)} %get-tuple-element.49.local, bf16[512,512]{1,0:T(8,128)(2,1)S(1)} %get-tuple-element.42.bcc.c_rows, bf16[512,128]{1,0:T(8,128)(2,1)S(1)} %get-tuple-element.50.wc3, bf16[256,512]{1,0:T(8,128)(2,1)S(1)} %get-tuple-element.60.r0, ...), custom_call_target="tpu_custom_call" | custom-call | flops 1000000000 | bytes 4000000 | tf_op jit(solution)/shard_map/carried_own/pallas_call | solution.py:614
  108.5 0.8 maximum_select_fusion
  109.3 2.6 %put_group.1 = bf16[256,4096]{1,0:T(8,128)(2,1)} custom-call(s32[8]{0:T(128)S(1)} %stack.45.s_ref, bf16[256,2048]{1,0:T(8,128)(2,1)} %collective-permute-done.14.part, bf16[256,4096]{1,0:T(8,128)(2,1)} %carried_own.1.whole), custom_call_target="tpu_custom_call", output_to_operand_aliasing={{}: (2, {})} | custom-call | bytes 2000000 | tf_op jit(solution)/shard_map/put_group/pallas_call | solution.py:639
  (69 shorter events, 0.4 us)
Async XLA Ops:
  0.6 16.6 %copy-start = (bf16[4,2,512]{2,1,0:T(2,128)(2,1)S(1)}, bf16[4,2,512]{2,1,0:T(2,128)(2,1)}, u32[]{:S(2)}) copy-start(bf16[4,2,512]{2,1,0:T(2,128)(2,1)} %param.20) | copy-start | bytes 24580
  2.1 9.8 %copy-start.7 = (bf16[1,1,4,4,4096]{4,3,2,1,0:T(4,128)(2,1)S(1)}, bf16[1,1,4,4,4096]{4,3,2,1,0:T(4,128)(2,1)}, u32[]{:S(2)}) copy-start(bf16[1,1,4,4,4096]{4,3,2,1,0:T(4,128)(2,1)} %param.27) | copy-start | bytes 393220
  2.1 9.9 %copy-start.8 = (bf16[1,1,4,4,2,512]{5,4,3,2,1,0:T(2,128)(2,1)S(1)}, bf16[1,1,4,4,2,512]{5,4,3,2,1,0:T(2,128)(2,1)}, u32[]{:S(2)}) copy-start(bf16[1,1,4,4,2,512]{5,4,3,2,1,0:T(2,128)(2,1)} %param.28) | copy-start | bytes 98308
  2.1 9.9 %copy-start.14 = (s32[1,1,4]{2,1,0:T(1,128)S(1)}, s32[1,1,4]{2,1,0:T(1,128)}, u32[]{:S(2)}) copy-start(s32[1,1,4]{2,1,0:T(1,128)} %param.26) | copy-start | bytes 52
  2.2 10.0 %copy-start.9 = (bf16[1,1,4,4,64]{4,3,2,1,0:T(4,128)(2,1)S(1)}, bf16[1,1,4,4,64]{4,3,2,1,0:T(4,128)(2,1)}, u32[]{:S(2)}) copy-start(bf16[1,1,4,4,64]{4,3,2,1,0:T(4,128)(2,1)} %param.29) | copy-start | bytes 6148
  2.2 14.8 %copy-start.15 = (f32[64]{0:T(128)S(1)}, f32[64]{0:T(128)}, u32[]{:S(2)}) copy-start(f32[64]{0:T(128)} %param.23) | copy-start | bytes 772
  2.2 14.8 %copy-start.13 = (f32[64]{0:T(128)S(1)}, f32[64]{0:T(128)}, u32[]{:S(2)}) copy-start(f32[64]{0:T(128)} %param.22) | copy-start | bytes 772
  2.2 15.1 %copy-start.11 = (f32[2,512]{1,0:T(2,128)S(1)}, f32[2,512]{1,0:T(2,128)}, u32[]{:S(2)}) copy-start(f32[2,512]{1,0:T(2,128)} %param.21) | copy-start | bytes 12292
  2.2 15.1 %copy-start.10 = (s32[1,3]{1,0:T(1,128)S(1)}, s32[1,3]{1,0:T(1,128)}, u32[]{:S(2)}) copy-start(s32[1,3]{1,0:T(1,128)} %param.25) | copy-start | bytes 40
  2.2 17.7 %copy-start.12 = (f32[64]{0:T(128)S(1)}, f32[64]{0:T(128)}, u32[]{:S(2)}) copy-start(f32[64]{0:T(128)} %param.24) | copy-start | bytes 772
  2.2 22.6 %copy-start.1 = (bf16[4,4096]{1,0:T(4,128)(2,1)S(1)}, bf16[4,4096]{1,0:T(4,128)(2,1)}, u32[]{:S(2)}) copy-start(bf16[4,4096]{1,0:T(4,128)(2,1)} %wx.1) | copy-start | bytes 98308
  2.2 22.6 %copy-start.2 = (f32[4096]{0:T(1024)S(1)}, f32[4096]{0:T(1024)}, u32[]{:S(2)}) copy-start(f32[4096]{0:T(1024)} %param.19) | copy-start | bytes 49156
  6.9 16.8 %collective-permute-start = (bf16[256,3072]{1,0:T(8,128)(2,1)}, bf16[256,3072]{1,0:T(8,128)(2,1)S(1)}, u32[]{:S(2)}, u32[]{:S(2)}) collective-permute-start(bf16[256,3072]{1,0:T(8,128)(2,1)} %get-tuple-element.37), channel_id=1, source_target_pairs={{0,1},{1,0},{2,3},{3,2},{4,5},{5,4},{6,7},{7,6},{8,9},{9,8},{10,11... | collective-permute-start | bytes 4718600 | tf_op jit(solution)/shard_map/ppermute | solution.py:751
  8.3 12.0 %collective-permute-start.2 = (bf16[16,3072]{1,0:T(8,128)(2,1)S(1)}, bf16[16,3072]{1,0:T(8,128)(2,1)S(1)}, u32[]{:S(2)}, u32[]{:S(2)}) collective-permute-start(bf16[16,3072]{1,0:T(8,128)(2,1)S(1)} %get-tuple-element.39), channel_id=1, source_target_pairs={{1,3},{3,5},{5,7},{7,9},{9,11},{11,13},{13,15},{17,19},{19,21},{21... | collective-permute-start | bytes 294920 | tf_op jit(solution)/shard_map/ppermute | solution.py:753
  12.5 24.4 %collective-permute-start.3 = (bf16[16,3072]{1,0:T(8,128)(2,1)S(1)}, bf16[16,3072]{1,0:T(8,128)(2,1)S(1)}, u32[]{:S(2)}, u32[]{:S(2)}) collective-permute-start(bf16[16,3072]{1,0:T(8,128)(2,1)S(1)} %concatenate.33), channel_id=1, source_target_pairs={{0,64},{1,65},{2,66},{3,67},{4,68},{5,69},{6,70},{7,71},{8,72},{9,... | collective-permute-start | bytes 294920 | tf_op jit(solution)/shard_map/ppermute | solution.py:769
  13.8 26.9 %collective-permute-start.5 = (bf16[16,3072]{1,0:T(8,128)(2,1)S(1)}, bf16[16,3072]{1,0:T(8,128)(2,1)S(1)}, u32[]{:S(2)}, u32[]{:S(2)}) collective-permute-start(bf16[16,3072]{1,0:T(8,128)(2,1)S(1)} %concatenate.33), channel_id=1, source_target_pairs={{0,72},{1,73},{2,74},{3,75},{4,76},{5,77},{6,78},{7,79},{8,64},{9,... | collective-permute-start | bytes 294920 | tf_op jit(solution)/shard_map/ppermute | solution.py:769
  15.7 4.7 %collective-permute-start.1 = (bf16[16,3072]{1,0:T(8,128)(2,1)S(1)}, bf16[16,3072]{1,0:T(8,128)(2,1)S(1)}, u32[]{:S(2)}, u32[]{:S(2)}) collective-permute-start(bf16[16,3072]{1,0:T(8,128)(2,1)S(1)} %get-tuple-element.38), channel_id=1, source_target_pairs={{1,2},{3,4},{5,6},{7,8},{9,10},{11,12},{13,14},{17,18},{19,20},{21... | collective-permute-start | bytes 294920 | tf_op jit(solution)/shard_map/ppermute | solution.py:752
  20.3 18.1 %collective-permute-start.4 = (bf16[16,3072]{1,0:T(8,128)(2,1)S(1)}, bf16[16,3072]{1,0:T(8,128)(2,1)S(1)}, u32[]{:S(2)}, u32[]{:S(2)}) collective-permute-start(bf16[16,3072]{1,0:T(8,128)(2,1)S(1)} %concatenate.34), channel_id=1, source_target_pairs={{0,65},{1,64},{2,67},{3,66},{4,69},{5,68},{6,71},{7,70},{8,73},{9,... | collective-permute-start | bytes 294920 | tf_op jit(solution)/shard_map/ppermute | solution.py:769
  20.4 20.3 %collective-permute-start.6 = (bf16[16,3072]{1,0:T(8,128)(2,1)S(1)}, bf16[16,3072]{1,0:T(8,128)(2,1)S(1)}, u32[]{:S(2)}, u32[]{:S(2)}) collective-permute-start(bf16[16,3072]{1,0:T(8,128)(2,1)S(1)} %concatenate.34), channel_id=1, source_target_pairs={{0,73},{1,72},{2,75},{3,74},{4,77},{5,76},{6,79},{7,78},{8,65},{9,... | collective-permute-start | bytes 294920 | tf_op jit(solution)/shard_map/ppermute | solution.py:769
  23.7 1.1 %copy-start.3 = (bf16[256,3072]{1,0:T(8,128)(2,1)}, bf16[256,3072]{1,0:T(8,128)(2,1)S(1)}, u32[]{:S(2)}) copy-start(bf16[256,3072]{1,0:T(8,128)(2,1)S(1)} %collective-permute-done.x_rec.g_rec) | copy-start | bytes 4718596
  24.9 1.4 %copy-start.4 = (bf16[256,3072]{1,0:T(8,128)(2,1)S(1)}, bf16[256,3072]{1,0:T(8,128)(2,1)}, u32[]{:S(2)}) copy-start(bf16[256,3072]{1,0:T(8,128)(2,1)} %copy-done.3) | copy-start | bytes 4718596
  36.8 19.8 %collective-permute-start.7 = (bf16[272,512]{1,0:T(8,128)(2,1)S(1)}, bf16[272,512]{1,0:T(8,128)(2,1)S(1)}, u32[]{:S(2)}, u32[]{:S(2)}) collective-permute-start(bf16[272,512]{1,0:T(8,128)(2,1)S(1)} %get-tuple-element.52), channel_id=1, source_target_pairs={{0,2},{1,3},{2,0},{3,1},{4,6},{5,7},{6,4},{7,5},{8,10},{9,11},{10,... | collective-permute-start | bytes 835592 | tf_op jit(solution)/shard_map/ppermute | solution.py:776
  36.8 22.7 %collective-permute-start.8 = (bf16[272,512]{1,0:T(8,128)(2,1)}, bf16[272,512]{1,0:T(8,128)(2,1)S(1)}, u32[]{:S(2)}, u32[]{:S(2)}) collective-permute-start(bf16[272,512]{1,0:T(8,128)(2,1)} %get-tuple-element.53), channel_id=1, source_target_pairs={{0,4},{1,5},{2,6},{3,7},{4,0},{5,1},{6,2},{7,3},{8,12},{9,13},{10,... | collective-permute-start | bytes 835592 | tf_op jit(solution)/shard_map/ppermute | solution.py:776
  38.4 21.2 %collective-permute-start.9 = (bf16[272,512]{1,0:T(8,128)(2,1)S(1)}, bf16[272,512]{1,0:T(8,128)(2,1)S(1)}, u32[]{:S(2)}, u32[]{:S(2)}) collective-permute-start(bf16[272,512]{1,0:T(8,128)(2,1)S(1)} %get-tuple-element.54), channel_id=1, source_target_pairs={{0,6},{1,7},{2,4},{3,5},{4,2},{5,3},{6,0},{7,1},{8,14},{9,15},{10,... | collective-permute-start | bytes 835592 | tf_op jit(solution)/shard_map/ppermute | solution.py:776
  55.0 12.9 %copy-start.5 = (bf16[448,512]{1,0:T(8,128)(2,1)}, bf16[448,512]{1,0:T(8,128)(2,1)S(1)}, u32[]{:S(2)}) copy-start(bf16[448,512]{1,0:T(8,128)(2,1)S(1)} %get-tuple-element.55.f0) | copy-start | bytes 1376260
  55.0 17.7 %collective-permute-start.15 = (bf16[448,512]{1,0:T(8,128)(2,1)}, bf16[448,512]{1,0:T(8,128)(2,1)}, u32[]{:S(2)}, u32[]{:S(2)}) collective-permute-start(bf16[448,512]{1,0:T(8,128)(2,1)} %get-tuple-element.64), channel_id=1, source_target_pairs={{0,2},{1,3},{2,0},{3,1},{4,6},{5,7},{6,4},{7,5},{8,10},{9,11},{10,... | collective-permute-start | bytes 1376264 | tf_op jit(solution)/shard_map/ppermute | solution.py:776
  55.0 21.8 %collective-permute-start.16 = (bf16[448,512]{1,0:T(8,128)(2,1)}, bf16[448,512]{1,0:T(8,128)(2,1)}, u32[]{:S(2)}, u32[]{:S(2)}) collective-permute-start(bf16[448,512]{1,0:T(8,128)(2,1)} %get-tuple-element.65), channel_id=1, source_target_pairs={{0,4},{1,5},{2,6},{3,7},{4,0},{5,1},{6,2},{7,3},{8,12},{9,13},{10,... | collective-permute-start | bytes 1376264 | tf_op jit(solution)/shard_map/ppermute | solution.py:776
  56.6 22.8 %collective-permute-start.17 = (bf16[448,512]{1,0:T(8,128)(2,1)}, bf16[448,512]{1,0:T(8,128)(2,1)}, u32[]{:S(2)}, u32[]{:S(2)}) collective-permute-start(bf16[448,512]{1,0:T(8,128)(2,1)} %get-tuple-element.66), channel_id=1, source_target_pairs={{0,6},{1,7},{2,4},{3,5},{4,2},{5,3},{6,0},{7,1},{8,14},{9,15},{10,... | collective-permute-start | bytes 1376264 | tf_op jit(solution)/shard_map/ppermute | solution.py:776
  60.4 6.3 %collective-permute-start.10 = (bf16[256,512]{1,0:T(8,128)(2,1)S(1)}, bf16[256,512]{1,0:T(8,128)(2,1)S(1)}, u32[]{:S(2)}, u32[]{:S(2)}) collective-permute-start(bf16[256,512]{1,0:T(8,128)(2,1)S(1)} %half_total.1), channel_id=1, source_target_pairs={{0,8},{1,9},{2,10},{3,11},{4,12},{5,13},{6,14},{7,15},{16,24},{17,... | collective-permute-start | bytes 786440 | tf_op jit(solution)/shard_map/ppermute | solution.py:796
  68.0 16.4 %collective-permute-start.11 = (bf16[256,512]{1,0:T(8,128)(2,1)S(1)}, bf16[256,512]{1,0:T(8,128)(2,1)S(1)}, u32[]{:S(2)}, u32[]{:S(2)}) collective-permute-start(bf16[256,512]{1,0:T(8,128)(2,1)S(1)} %get-tuple-element.61), channel_id=1, source_target_pairs={{0,2},{1,3},{2,0},{3,1},{4,6},{5,7},{6,4},{7,5},{8,10},{9,11},{10,... | collective-permute-start | bytes 786440 | tf_op jit(solution)/shard_map/ppermute | solution.py:776
  69.7 18.3 %collective-permute-start.12 = (bf16[256,512]{1,0:T(8,128)(2,1)S(1)}, bf16[256,512]{1,0:T(8,128)(2,1)S(1)}, u32[]{:S(2)}, u32[]{:S(2)}) collective-permute-start(bf16[256,512]{1,0:T(8,128)(2,1)S(1)} %get-tuple-element.62), channel_id=1, source_target_pairs={{0,4},{1,5},{2,6},{3,7},{4,0},{5,1},{6,2},{7,3},{8,12},{9,13},{10,... | collective-permute-start | bytes 786440 | tf_op jit(solution)/shard_map/ppermute | solution.py:776
  72.7 17.6 %collective-permute-start.13 = (bf16[256,512]{1,0:T(8,128)(2,1)S(1)}, bf16[256,512]{1,0:T(8,128)(2,1)S(1)}, u32[]{:S(2)}, u32[]{:S(2)}) collective-permute-start(bf16[256,512]{1,0:T(8,128)(2,1)S(1)} %get-tuple-element.63), channel_id=1, source_target_pairs={{0,6},{1,7},{2,4},{3,5},{4,2},{5,3},{6,0},{7,1},{8,14},{9,15},{10,... | collective-permute-start | bytes 786440 | tf_op jit(solution)/shard_map/ppermute | solution.py:776
  79.4 1.0 copy-start.6
  84.3 9.7 %collective-permute-start.18 = (bf16[4,32,512]{2,1,0:T(8,128)(2,1)S(1)}, bf16[4,32,512]{2,1,0:T(8,128)(2,1)S(1)}, u32[]{:S(2)}, u32[]{:S(2)}) collective-permute-start(bf16[4,32,512]{2,1,0:T(8,128)(2,1)S(1)} %get-tuple-element.69), channel_id=1, source_target_pairs={{0,64},{1,65},{2,66},{3,67},{4,68},{5,69},{6,70},{7,71},{8,72},{9,... | collective-permute-start | bytes 393224 | tf_op jit(solution)/shard_map/ppermute | solution.py:826
  86.3 7.8 %collective-permute-start.19 = (bf16[4,32,512]{2,1,0:T(8,128)(2,1)S(1)}, bf16[4,32,512]{2,1,0:T(8,128)(2,1)S(1)}, u32[]{:S(2)}, u32[]{:S(2)}) collective-permute-start(bf16[4,32,512]{2,1,0:T(8,128)(2,1)S(1)} %get-tuple-element.70), channel_id=1, source_target_pairs={{0,72},{1,73},{2,74},{3,75},{4,76},{5,77},{6,78},{7,79},{8,64},{9,... | collective-permute-start | bytes 393224 | tf_op jit(solution)/shard_map/ppermute | solution.py:827
  94.1 6.0 %collective-permute-start.20 = (bf16[32,512]{1,0:T(8,128)(2,1)S(1)}, bf16[32,512]{1,0:T(8,128)(2,1)S(1)}, u32[]{:S(2)}, u32[]{:S(2)}) collective-permute-start(bf16[32,512]{1,0:T(8,128)(2,1)S(1)} %get-tuple-element.80), channel_id=1, source_target_pairs={{0,6},{1,7},{2,4},{3,5},{4,2},{5,3},{6,0},{7,1},{8,14},{9,15},{10,... | collective-permute-start | bytes 98312 | tf_op jit(solution)/shard_map/ppermute | solution.py:776
  97.4 4.3 %collective-permute-start.21 = (bf16[32,512]{1,0:T(8,128)(2,1)S(1)}, bf16[32,512]{1,0:T(8,128)(2,1)S(1)}, u32[]{:S(2)}, u32[]{:S(2)}) collective-permute-start(bf16[32,512]{1,0:T(8,128)(2,1)S(1)} %get-tuple-element.79), channel_id=1, source_target_pairs={{0,4},{1,5},{2,6},{3,7},{4,0},{5,1},{6,2},{7,3},{8,12},{9,13},{10,... | collective-permute-start | bytes 98312 | tf_op jit(solution)/shard_map/ppermute | solution.py:776
  97.4 4.3 %collective-permute-start.22 = (bf16[32,512]{1,0:T(8,128)(2,1)S(1)}, bf16[32,512]{1,0:T(8,128)(2,1)S(1)}, u32[]{:S(2)}, u32[]{:S(2)}) collective-permute-start(bf16[32,512]{1,0:T(8,128)(2,1)S(1)} %get-tuple-element.78), channel_id=1, source_target_pairs={{0,2},{1,3},{2,0},{3,1},{4,6},{5,7},{6,4},{7,5},{8,10},{9,11},{10,... | collective-permute-start | bytes 98312 | tf_op jit(solution)/shard_map/ppermute | solution.py:776
  98.1 11.2 %collective-permute-start.14 = (bf16[256,2048]{1,0:T(8,128)(2,1)S(1)}, bf16[256,2048]{1,0:T(8,128)(2,1)}, u32[]{:S(2)}, u32[]{:S(2)}) collective-permute-start(bf16[256,2048]{1,0:T(8,128)(2,1)S(1)} %carried_other.1), channel_id=1, source_target_pairs={{0,1},{1,0},{2,3},{3,2},{4,5},{5,4},{6,7},{7,6},{8,9},{9,8},{10,11... | collective-permute-start | bytes 3145736 | tf_op jit(solution)/shard_map/ppermute | solution.py:825
  101.9 6.6 %collective-permute-start.23 = (bf16[16,2048]{1,0:T(8,128)(2,1)S(1)}, bf16[16,2048]{1,0:T(8,128)(2,1)S(1)}, u32[]{:S(2)}, u32[]{:S(2)}) collective-permute-start(bf16[16,2048]{1,0:T(8,128)(2,1)S(1)} %select_n.174), channel_id=1, source_target_pairs={{0,1},{1,0},{2,3},{3,2},{4,5},{5,4},{6,7},{7,6},{8,9},{9,8},{10,11... | collective-permute-start | bytes 196616 | tf_op jit(solution)/shard_map/ppermute | solution.py:837

commit v3 on v2

--- a/solution.py
+++ b/solution.py
@@ -19,6 +19,7 @@
 LANES = 128
 DEC = STATE + 48
 MSG = DEC + 144
+SCRATCH_B = 14
 REP = 32
 CHIP_TOKENS = 512
 BLOCKS = CHIP_TOKENS // BLOCK
@@ -253,16 +254,16 @@
 
 
 def kernel_b(
-    s_ref, xc_ref, bcc, dtc, skip, cx, cg, near_same, near_cross, far_same, far_cross,
-    f0, f1, f2, f3, local_out,
-    wp3, wb3, keep3, bt, gm, cum_t, dt_t, wf3, wide, reach, carried, scaled, parts, dec_rows,
+    base, count, s_ref, xc_ref, bcc, dtc, skip, cx, cg, near_same, near_cross, far_same, far_cross, *rest
 ):
-    m = pl.program_id(0)
+    *outs, local_out = rest[-SCRATCH_B - count - 1 : -SCRATCH_B]
+    (wp3, wb3, keep3, bt, gm, cum_t, dt_t, wf3, wide, reach, carried, scaled, parts, dec_rows) = rest[-SCRATCH_B:]
+    m = pl.program_id(0) + base
     chunk = s_ref[1] ^ m
     cut = cut_of(s_ref)
     cut_block = cut // BLOCK
 
-    @pl.when(m == 0)
+    @pl.when(m == base)
     def _():
         pos = lax.broadcasted_iota(jnp.int32, (BLOCK, LANES), 0)
         row = lax.broadcasted_iota(jnp.int32, (BLOCK, BLOCK), 0)
@@ -318,10 +319,9 @@
     spread = spread_matrix(chunk)
     keep = mm(keep3[...], spread)
     half_lane = lax.broadcasted_iota(jnp.int32, (BLOCK, LANES), 1) < HEAD_DIM
-    outs = (f0, f1, f2, f3)
     for index, out in enumerate(outs):
 
-        @pl.when(m == index)
+        @pl.when(m == base + index)
         def _():
             out[0:STATE] = jnp.zeros((STATE, CHUNK), BF16)
             out[STATE : STATE + 16] = rows_of(split3(keep[BLOCKS + 1 : BLOCKS + 2]), 16, CHUNK).astype(BF16)
@@ -356,7 +356,7 @@
                 fresh = keep[BLOCKS : BLOCKS + 1] * state + fresh
             for index, out in enumerate(outs):
 
-                @pl.when(m == index)
+                @pl.when(m == base + index)
                 def _():
                     out[0:STATE] = fresh.astype(BF16)
 
@@ -386,46 +386,57 @@
             local_out[rows, lanes] = value
 
 
-def run_b(scalars, xc, bcc, dtc, skip, cx, cg, dec_hops):
+def run_b(scalars, xc, bcc, dtc, skip, cx, cg, dec_hops, base, count, local=None):
     def fixed(shape):
         return pl.BlockSpec(shape, lambda m, s: (0,) * len(shape))
 
     def chunked(rows, per_core=0):
-        return pl.BlockSpec((rows, CHUNK), lambda m, s: (0, s[0] * per_core + (s[1] ^ m)))
-
+        return pl.BlockSpec((rows, CHUNK), lambda m, s: (0, s[0] * per_core + (s[1] ^ (m + base))))
+
+    args = [scalars, xc, bcc, dtc, skip, cx, cg, *dec_hops]
+    in_specs = [
+        chunked(CHIP_TOKENS), fixed((CHIP_TOKENS, 512)), fixed((2 * CHIP_TOKENS, LANES)),
+        chunked(1, RING), chunked(16), fixed((16, 512)),
+    ] + [fixed((16, WIDE))] * 4
+    aliases = {}
+    if local is not None:
+        aliases = {len(args): count}
+        args.append(local)
+        in_specs.append(pl.BlockSpec(memory_space=pl.ANY))
+    scratch = [
+        pltpu.VMEM((CHIP_TOKENS, LANES), BF16),
+        pltpu.VMEM((CHIP_TOKENS, LANES), BF16),
+        pltpu.VMEM((16, LANES), BF16),
+        pltpu.VMEM((BLOCKS, STATE, BLOCK), BF16),
+        pltpu.VMEM((BLOCKS, BLOCK, BLOCK), F32),
+        pltpu.VMEM((BLOCKS, LANES, BLOCK), F32),
+        pltpu.VMEM((BLOCKS, LANES, BLOCK), F32),
+        pltpu.VMEM((BLOCK, LANES), BF16),
+        pltpu.VMEM((BLOCK, CHUNK), F32),
+        pltpu.VMEM((BLOCK, CHUNK), F32),
+        pltpu.VMEM((BLOCK, CHUNK), F32),
+        pltpu.VMEM((BLOCK, CHUNK), BF16),
+        pltpu.VMEM((2 * STATE, CHUNK), BF16),
+        pltpu.VMEM((64, WIDE), F32),
+    ]
+    assert len(scratch) == SCRATCH_B
     return pl.pallas_call(
-        kernel_b,
+        functools.partial(kernel_b, base, count),
         grid_spec=pltpu.PrefetchScalarGridSpec(
             num_scalar_prefetch=1,
-            grid=(RING,),
-            in_specs=[
-                chunked(CHIP_TOKENS), fixed((CHIP_TOKENS, 512)), fixed((2 * CHIP_TOKENS, LANES)),
-                chunked(1, RING), chunked(16), fixed((16, 512)),
-            ] + [fixed((16, WIDE))] * 4,
-            out_specs=[fixed((MSG, CHUNK))] * RING + [chunked(CHIP_TOKENS)],
-            scratch_shapes=[
-                pltpu.VMEM((CHIP_TOKENS, LANES), BF16),
-                pltpu.VMEM((CHIP_TOKENS, LANES), BF16),
-                pltpu.VMEM((16, LANES), BF16),
-                pltpu.VMEM((BLOCKS, STATE, BLOCK), BF16),
-                pltpu.VMEM((BLOCKS, BLOCK, BLOCK), F32),
-                pltpu.VMEM((BLOCKS, LANES, BLOCK), F32),
-                pltpu.VMEM((BLOCKS, LANES, BLOCK), F32),
-                pltpu.VMEM((BLOCK, LANES), BF16),
-                pltpu.VMEM((BLOCK, CHUNK), F32),
-                pltpu.VMEM((BLOCK, CHUNK), F32),
-                pltpu.VMEM((BLOCK, CHUNK), F32),
-                pltpu.VMEM((BLOCK, CHUNK), BF16),
-                pltpu.VMEM((2 * STATE, CHUNK), BF16),
-                pltpu.VMEM((64, WIDE), F32),
-            ],
+            grid=(count,),
+            in_specs=in_specs,
+            out_specs=[fixed((MSG, CHUNK))] * count + [chunked(CHIP_TOKENS)],
+            scratch_shapes=scratch,
         ),
-        out_shape=[jax.ShapeDtypeStruct((MSG, CHUNK), BF16)] * RING
-        + [pltpu.HBM((CHIP_TOKENS, GROUP_CH), F32)],
+        out_shape=[jax.ShapeDtypeStruct((MSG, CHUNK), BF16)] * count + [pltpu.HBM((CHIP_TOKENS, GROUP_CH), F32)],
+        input_output_aliases=aliases,
         compiler_params=pltpu.CompilerParams(vmem_limit_bytes=14 * MIB),
-        cost_estimate=pl.CostEstimate(flops=12 * 10**9, bytes_accessed=8 * 10**6, transcendentals=2 * 10**6),
-        name="output_within_chip",
-    )(scalars, xc, bcc, dtc, skip, cx, cg, *dec_hops)
+        cost_estimate=pl.CostEstimate(
+            flops=3 * count * 10**9, bytes_accessed=2 * count * 10**6, transcendentals=count * 10**5
+        ),
+        name=f"output_within_chip_{base}",
+    )(*args)
 
 
 def pick(refs, which, rows):
@@ -655,68 +666,96 @@
     )(scalars, part, whole)
 
 
-def side_tiles(bc, dt, group):
+def head_copies(group):
     lane = lax.broadcasted_iota(jnp.int32, (64, LANES), 1)
     head = lax.broadcasted_iota(jnp.int32, (64, LANES), 0)
-    copies = jnp.where(((lane & (REP - 1)) + group * REP == head) & (lane < 3 * REP), 1.0, 0.0).astype(BF16)
-    first = group == 0
-    return [
-        jnp.where(first, bc[:, 0, 0:STATE], bc[:, 0, STATE : 2 * STATE]),
-        jnp.where(first, bc[:, 1, 0:STATE], bc[:, 1, STATE : 2 * STATE]),
-        mm(dt[...], copies).astype(BF16),
-    ]
-
-
-def kernel_pack(s_ref, x, bc, dt, x_last, bc_last, dt_last, send, halo0, halo1, side):
+    hit = ((lane & (REP - 1)) + group * REP == head) & (lane < 3 * REP)
+    return jnp.where(hit, 1.0, 0.0).astype(BF16)
+
+
+def kernel_pack(s_ref, x, bc, dt_t, x_last, bc_last, dx, dbc, ddt, send, halo0, halo1, side, d_own, d_other, rows_f32):
     core = s_ref[0]
+    first = core == 0
     rows = x.shape[0]
+    start = pl.multiple_of(pl.program_id(0) * rows, rows)
+    dt = dt_t[:, pl.ds(start, rows)].astype(F32).T.astype(BF16)
+    b_rows, c_rows = bc[:, 0, :], bc[:, 1, :]
     send[:, 0:GROUP_CH] = x[...]
     for target, group, offset in ((send, 1 - core, GROUP_CH), (side, core, 0)):
-        b_tile, c_tile, steps = side_tiles(bc, dt, group)
-        target[:, offset : offset + STATE] = b_tile
-        target[:, offset + STATE : offset + 2 * STATE] = c_tile
-        target[:, offset + 2 * STATE : offset + 2 * STATE + LANES] = steps
-        target[:, offset + 2 * STATE + LANES : offset + 1024] = jnp.zeros((rows, 384), BF16)
+        low = group == 0
+        target[:, offset : offset + STATE] = jnp.where(low, b_rows[:, 0:STATE], b_rows[:, STATE:])
+        target[:, offset + STATE : offset + 2 * STATE] = jnp.where(low, c_rows[:, 0:STATE], c_rows[:, STATE:])
+        target[:, offset + 512 : offset + 640] = mm(dt, head_copies(group)).astype(BF16)
+        target[:, offset + 640 : offset + 1024] = jnp.zeros((rows, 384), BF16)
 
     @pl.when(pl.program_id(0) == 0)
     def _():
+        b_last, c_last = bc_last[:, 0, :], bc_last[:, 1, :]
         for group, halo in ((0, halo0), (1, halo1)):
-            b_tile, c_tile, _ = side_tiles(bc_last, dt_last, jnp.int32(group))
             halo[:, 0:GROUP_CH] = x_last[:, group * GROUP_CH : (group + 1) * GROUP_CH]
-            halo[:, GROUP_CH : GROUP_CH + STATE] = b_tile
-            halo[:, GROUP_CH + STATE : GROUP_CH + 2 * STATE] = c_tile
-            halo[:, GROUP_CH + 2 * STATE :] = jnp.zeros((16, 512), BF16)
-
-
-def run_pack(core, x, bc, dt):
+            halo[:, GROUP_CH : GROUP_CH + STATE] = b_last[:, group * STATE : (group + 1) * STATE]
+            halo[:, GROUP_CH + STATE : GROUP_CH + 512] = c_last[:, group * STATE : (group + 1) * STATE]
+            halo[:, GROUP_CH + 512 :] = jnp.zeros((16, 512), BF16)
+        lane = lax.broadcasted_iota(jnp.int32, (ROWS, LANES), 1)
+        row = lax.broadcasted_iota(jnp.int32, (ROWS, LANES), 0)
+        prompt = jnp.zeros((ROWS, LANES), F32)
+        for r in range(ROWS):
+            prompt = jnp.where(row == r, s_ref[1 + r].astype(F32), prompt)
+        for out, group in ((d_own, core), (d_other, 1 - core)):
+            low = group == 0
+            rows_f32[...] = jnp.zeros_like(rows_f32)
+            for step in range(STEPS):
+                at = slice(ROWS * step, ROWS * step + ROWS)
+                value = dx[step].astype(F32)
+                rows_f32[at, 0:GROUP_CH] = jnp.where(low, value[:, 0:GROUP_CH], value[:, GROUP_CH:])
+                for part in range(2):
+                    value = dbc[step, :, part, :].astype(F32)
+                    to = GROUP_CH + part * STATE
+                    rows_f32[at, to : to + STATE] = jnp.where(low, value[:, 0:STATE], value[:, STATE:])
+                steps = mm(ddt[step], head_copies(group))
+                rows_f32[at, GROUP_CH + 512 : GROUP_CH + 640] = jnp.where(lane < 3 * REP, steps, prompt)
+            out[...] = rows_f32[...].astype(BF16)
+
+
+def run_pack(scalars, x, bc, dt_t, dx, dbc, ddt):
     rows = x.shape[0]
-    tile = rows // RING
+    tile = rows // 2
     last = rows // 16 - 1
+    small = (16, WIDE)
+
+    def fixed(shape):
+        return pl.BlockSpec(shape, lambda i, s: (0,) * len(shape))
+
     return pl.pallas_call(
         kernel_pack,
         grid_spec=pltpu.PrefetchScalarGridSpec(
             num_scalar_prefetch=1,
-            grid=(RING,),
+            grid=(2,),
             in_specs=[
                 pl.BlockSpec((tile, GROUP_CH), lambda i, s: (i, 1 - s[0])),
                 pl.BlockSpec((tile, 2, 512), lambda i, s: (i, 0, 0)),
-                pl.BlockSpec((tile, 64), lambda i, s: (i, 0)),
+                fixed(dt_t.shape),
                 pl.BlockSpec((16, CORES * GROUP_CH), lambda i, s: (last, 0)),
                 pl.BlockSpec((16, 2, 512), lambda i, s: (last, 0, 0)),
-                pl.BlockSpec((16, 64), lambda i, s: (last, 0)),
+                fixed(dx.shape),
+                fixed(dbc.shape),
+                fixed(ddt.shape),
             ],
             out_specs=[
                 pl.BlockSpec((tile, WIDE), lambda i, s: (i, 0)),
-                pl.BlockSpec((16, WIDE), lambda i, s: (0, 0)),
-                pl.BlockSpec((16, WIDE), lambda i, s: (0, 0)),
+                fixed(small),
+                fixed(small),
                 pl.BlockSpec((tile, 1024), lambda i, s: (i, 0)),
+                fixed(small),
+                fixed(small),
             ],
+            scratch_shapes=[pltpu.VMEM(small, F32)],
         ),
-        out_shape=[jax.ShapeDtypeStruct(shape, BF16) for shape in ((rows, WIDE), (16, WIDE), (16, WIDE), (rows, 1024))],
-        compiler_params=pltpu.CompilerParams(vmem_limit_bytes=8 * MIB),
+        out_shape=[pltpu.HBM(shape, BF16) for shape in ((rows, WIDE), small, small, (rows, 1024), small, small)],
+        compiler_params=pltpu.CompilerParams(vmem_limit_bytes=12 * MIB),
         cost_estimate=pl.CostEstimate(flops=10**6, bytes_accessed=4 * 10**6, transcendentals=0),
         name="pack",
-    )(core[None], x, bc, dt, x, bc, dt)
+    )(scalars, x, bc, dt_t, x, bc, dx, dbc, ddt)
 
 
 def on_device(
@@ -734,21 +773,13 @@
     scalars = jnp.stack([core, z, upper, anchor, bounds[0] - anchor, bounds[1] - anchor, zero, zero]).astype(jnp.int32)
     both = ("pool", "dp")
 
-    def group_part(x, bc, dt, group, extra=None):
-        rows = x.shape[0]
-        channels = lax.dynamic_slice_in_dim(x, group * GROUP_CH, GROUP_CH, 1)
-        return jnp.concatenate([channels, group_side(bc, dt, group, extra)], axis=1).reshape(rows, WIDE)
-
-    def group_side(bc, dt, group, extra=None):
-        rows = bc.shape[0]
-        b_c = lax.dynamic_slice_in_dim(bc, group * STATE, STATE, 2).reshape(rows, 2 * STATE)
-        steps = lax.dynamic_slice_in_dim(dt, group * REP, REP, 1)
-        last = jnp.zeros((rows, REP), BF16) if extra is None else jnp.broadcast_to(extra, (rows, REP))
-        return jnp.concatenate([b_c, steps, steps, steps, last, jnp.zeros((rows, 384), BF16)], axis=1)
-
-    x_rows, bc_rows, dt_rows = (in_hbm(value[0]) for value in (x_in, bc_in, dt_raw))
-    packed, halo0, halo1, g_own = run_pack(core.astype(jnp.int32), x_rows, bc_rows, dt_rows)
-    recv = lax.ppermute(packed, "dp", [(i, i ^ 1) for i in range(count)])
+    x_rows, bc_rows = in_hbm(x_in[0]), in_hbm(bc_in[0])
+    own = jnp.concatenate([core[None], decode_prompt[0, 0]]).astype(jnp.int32)
+    packed, halo0, halo1, g_own, d_own, d_other = run_pack(
+        own, x_rows, bc_rows, in_hbm(dt_raw[0].T), in_hbm(dec_x[0, 0]), in_hbm(dec_bc[0, 0]), in_hbm(dec_dt[0, 0])
+    )
+    recv = in_hbm(lax.ppermute(packed, "dp", [(i, i ^ 1) for i in range(count)]))
+    g_own = in_hbm(g_own)
     halo = lax.ppermute(halo0, "dp", [(i, i + 1) for i in range(1, count - 1, 2)])
     halo = halo + lax.ppermute(halo1, "dp", [(i, i + 2) for i in range(1, count - 1, 2)])
 
@@ -756,19 +787,12 @@
         return lax.optimization_barrier((value, other))[0]
 
     dec_rows = STEPS * ROWS
-    d_x, d_bc, d_dt = after((dec_x, dec_bc, dec_dt), halo1)
-    d_x = d_x[0, 0].reshape(dec_rows, -1)
-    d_bc = d_bc[0, 0].reshape(dec_rows, 2, -1)
-    d_dt = d_dt[0, 0].reshape(dec_rows, -1)
-    d_prompt = jnp.tile(decode_prompt[0, 0].astype(BF16), STEPS)[:, None]
     total = 2 * count
-    d_same = group_part(d_x, d_bc, d_dt, core, d_prompt)
-    d_cross = group_part(d_x, d_bc, d_dt, 1 - core, d_prompt)
 
     def hop(value, flip):
         return lax.ppermute(value, both, [(i, ((i + count) % total) ^ flip) for i in range(total)])
 
-    dec_hops = [hop(d_same, 0), hop(d_cross, 1), hop(d_same, CORES * RING), hop(d_cross, CORES * RING + 1)]
+    dec_hops = [hop(d_own, 0), hop(d_other, 1), hop(d_own, CORES * RING), hop(d_other, CORES * RING + 1)]
 
     def z_swap(value, m):
         if m == 0:
@@ -786,13 +810,13 @@
 
     *ls, xc, bcc, dtc, wc3, cx, cg = run_a(scalars, x_rows, recv, halo, conv_w_x, b_x, g_own, w_group, b_group, vecs)
     sent_ls = [z_swap(part, m) for m, part in enumerate(ls)]
-    *fs, local = run_b(scalars, xc, bcc, dtc, skip, cx, cg, dec_hops)
-    local = in_hbm(local)
+    *fs, local = run_b(scalars, xc, bcc, dtc, skip, cx, cg, dec_hops, 1, 3)
     ls = after(tuple(sent_ls), fs[0])
-    fs = [z_swap(part, m) for m, part in enumerate(fs)]
-
     state_shape = jax.ShapeDtypeStruct((STATE, CHUNK), BF16)
     half_total = whole_call(kernel_total, state_shape, "half_total", 10**6)(scalars, *ls)
+    own_end, local = run_b(scalars, xc, bcc, dtc, skip, cx, cg, after(tuple(dec_hops), half_total), 0, 1, in_hbm(local))
+    fs = [z_swap(part, m) for m, part in enumerate([own_end, *fs])]
+    local = in_hbm(local)
     start = lax.ppermute(half_total, "dp", [(i, i + CORES * RING) for i in range(CORES * RING)])
     starts = whole_call(kernel_starts, [state_shape] * RING, "chip_starts", 10**6)(scalars, *ls, start)
     starts = [z_swap(part, m) for m, part in enumerate(starts)]
@@ -827,6 +851,8 @@
     crossed = lax.ppermute(sent, both, [(i, ((i + count) % total) ^ (CORES * RING)) for i in range(total)])
     answers = after(straight + crossed, other_rows)
     answers = [z_swap(answers[m], m) for m in range(RING)]
+    own_group = run_d(scalars, local, bcc, wc3, starts, True)
+    answers = after(tuple(answers), own_group)
     columns = [
         functools.reduce(lambda a, m: jnp.where(z == j ^ m, answers[m], a), range(1, RING), answers[0])
         for j in range(RING)
@@ -836,7 +862,6 @@
     mine = jnp.where(core == 0, first, second)
     theirs = lax.ppermute(jnp.where(core == 0, second, first), "dp", [(i, i ^ 1) for i in range(count)])
     decoded = jnp.where(core == 0, jnp.concatenate([mine, theirs], axis=1), jnp.concatenate([theirs, mine], axis=1))
-    own_group = run_d(scalars, local, bcc, wc3, starts, True)
     out = put_group(scalars, own_group, other_group)
     return out[None], decoded.reshape(dec_x.shape)
 

time: 112 us -> 106 us (0.946)
  waiting for transfers between devices: 13.5 us -> 6.69 us
  local copies, waits for them, and re-layouts: 6.87 us -> 1.36 us
  starting transfers between devices: 38.9 us -> 41.5 us
  other arithmetic: 2.89 us -> 4.53 us
  Pallas kernels: 46.6 us -> 48.2 us
    ppermute x12, waiting for transfers between devices: 10.9 us -> 5.76 us  [z_swap(): return lax.ppermute(value, 'dp', [(i, i ^ CORES * m) for i in range(count)])]
    unnamed x39 -> x20, local copies, waits for them, and re-layouts: 5.16 us -> 0.07 us
    ppermute x1, starting transfers between devices: 1.28 us -> 4.06 us  [on_device(): lax.ppermute(halo0, 'dp', [(i, i + 1) for i in range(1, count - 1, 2)])]
    ppermute x1, waiting for transfers between devices: 2.62 us -> 0.01 us  [on_device(): lax.ppermute(half_total, 'dp', [(i, i + CORES * RING) for i in range(CORE...]
    pallas_call x1 -> x2, Pallas kernels: 14.4 us -> 16.8 us  [run_b(): pl.pallas_call(functools.partial(kernel_b, base, count), grid_spec=pltpu....]
    ppermute x4, starting transfers between devices: 6.59 us -> 4.36 us  [hop(): lax.ppermute(value, both, [(i, (i + count) % total ^ flip) for i in range...]
    ppermute x1, starting transfers between devices: 2.28 us -> 4.5 us  [on_device(): lax.ppermute(half_total, 'dp', [(i, i + CORES * RING) for i in range(CORE...]
    ppermute x1, starting transfers between devices: 1.37 us -> 3.43 us  [on_device(): lax.ppermute(sent, both, [(i, (i + count) % total ^ CORES * RING) for i i...]
  transfers between devices with their start and end apart: 24 -> 24, of which waited for: 6 -> 4; matrix products, arithmetic and copies ran while one was open for 4% -> 5% of each run, Pallas kernels for 35% -> 40%
where the time goes in v3:
time: 106 us; the launch traced here: 105 us
  Pallas kernels  48.2 us (45%)
  starting transfers between devices  41.5 us (39%)
  waiting for transfers between devices  6.69 us (6%)
  other arithmetic  4.53 us (4%)
  between operations  3.09 us (3%)
  local copies, waits for them, and re-layouts  1.36 us (1%)
    pallas_call x2, Pallas kernels, run_b(): pl.pallas_call(functools.partial(kernel_b, base, count), grid_spec=pltpu....  16.8 us
    ppermute x12, starting transfers between devices, z_swap(): return lax.ppermute(value, 'dp', [(i, i ^ CORES * m) for i in range(count)])  15.7 us
    pallas_call x1, Pallas kernels, run_a(): pl.pallas_call(kernel_a, grid_spec=pltpu.PrefetchScalarGridSpec(num_scala...  10.3 us
    pallas_call x2, Pallas kernels, run_d(): pl.pallas_call(kernel_d, grid_spec=pltpu.PrefetchScalarGridSpec(num_scala...  9.42 us
    ppermute x12, waiting for transfers between devices, z_swap(): return lax.ppermute(value, 'dp', [(i, i ^ CORES * m) for i in range(count)])  5.76 us
    pallas_call x1, Pallas kernels, run_pack(): pl.pallas_call(kernel_pack, grid_spec=pltpu.PrefetchScalarGridSpec(num_sc...  4.84 us
    ppermute x1, starting transfers between devices, on_device(): lax.ppermute(half_total, 'dp', [(i, i + CORES * RING) for i in range(CORE...  4.5 us
    ppermute x4, starting transfers between devices, hop(): lax.ppermute(value, both, [(i, (i + count) % total ^ flip) for i in range...  4.36 us
  transfers between devices with their start and end apart: 24, of which 4 were waited for; matrix products, arithmetic and copies ran while one was open for 5% of the time, Pallas kernels for 40%

profile of v3, /device:TPU:1, one launch (start us, length us, event | category | flops | bytes accessed | tf_op | source)
XLA Modules:
  0.0 105.3 jit_solution(15167433181860047725)
XLA Ops:
  0.6 0.0 copy-start
  0.7 0.7 pad_add_fusion.s_ref
  1.4 0.0 copy-start.5
  1.4 0.0 copy-start.2
  1.4 0.0 copy-start.1
  1.4 4.8 %pack.1 = (bf16[256,3072]{1,0:T(8,128)(2,1)}, bf16[16,3072]{1,0:T(8,128)(2,1)}, bf16[16,3072]{1,0:T(8,128)(2,1)}, bf16[256,1024]{1,0:T(8,128)(2,1)}, bf16[16,3072]{1,0:T(8,128)(2,1)}, /*index=5*/bf16[16,3072]{1,0:T(8,128)(2,1)}) custom-call(s32[5]{0:T(128)S(1)} %pad_add_fusion.s_ref, bf16[256,4096]{1,0:T(8,128)(2,1)} %bitcast.63, ...), custom_call_target="tpu_custom_call" | custom-call | flops 1000000 | bytes 4000000 | tf_op jit(solution)/shard_map/pack/pallas_call | solution.py:729
  6.3 1.5 %collective-permute-start = (bf16[256,3072]{1,0:T(8,128)(2,1)}, bf16[256,3072]{1,0:T(8,128)(2,1)}, u32[]{:S(2)}, u32[]{:S(2)}) collective-permute-start(bf16[256,3072]{1,0:T(8,128)(2,1)} %get-tuple-element.45), channel_id=1, source_target_pairs={{0,1},{1,0},{2,3},{3,2},{4,5},{5,4},{6,7},{7,6},{8,9},{9,8},{10,11... | collective-permute-start | bytes 4718600 | tf_op jit(solution)/shard_map/ppermute | solution.py:781
  7.8 1.4 %collective-permute-start.3 = (bf16[16,3072]{1,0:T(8,128)(2,1)}, bf16[16,3072]{1,0:T(8,128)(2,1)S(1)}, u32[]{:S(2)}, u32[]{:S(2)}) collective-permute-start(bf16[16,3072]{1,0:T(8,128)(2,1)} %get-tuple-element.54), channel_id=1, source_target_pairs={{0,64},{1,65},{2,66},{3,67},{4,68},{5,69},{6,70},{7,71},{8,72},{9,... | collective-permute-start | bytes 294920 | tf_op jit(solution)/shard_map/ppermute | solution.py:793
  9.2 1.9 %collective-permute-start.5 = (bf16[16,3072]{1,0:T(8,128)(2,1)}, bf16[16,3072]{1,0:T(8,128)(2,1)S(1)}, u32[]{:S(2)}, u32[]{:S(2)}) collective-permute-start(bf16[16,3072]{1,0:T(8,128)(2,1)} %get-tuple-element.54), channel_id=1, source_target_pairs={{0,72},{1,73},{2,74},{3,75},{4,76},{5,77},{6,78},{7,79},{8,64},{9,... | collective-permute-start | bytes 294920 | tf_op jit(solution)/shard_map/ppermute | solution.py:793
  11.1 4.1 %collective-permute-start.1 = (bf16[16,3072]{1,0:T(8,128)(2,1)}, bf16[16,3072]{1,0:T(8,128)(2,1)S(1)}, u32[]{:S(2)}, u32[]{:S(2)}) collective-permute-start(bf16[16,3072]{1,0:T(8,128)(2,1)} %get-tuple-element.46), channel_id=1, source_target_pairs={{1,2},{3,4},{5,6},{7,8},{9,10},{11,12},{13,14},{17,18},{19,20},{21... | collective-permute-start | bytes 294920 | tf_op jit(solution)/shard_map/ppermute | solution.py:783
  15.1 3.5 %collective-permute-start.2 = (bf16[16,3072]{1,0:T(8,128)(2,1)}, bf16[16,3072]{1,0:T(8,128)(2,1)S(1)}, u32[]{:S(2)}, u32[]{:S(2)}) collective-permute-start(bf16[16,3072]{1,0:T(8,128)(2,1)} %get-tuple-element.47), channel_id=1, source_target_pairs={{1,3},{3,5},{5,7},{7,9},{9,11},{11,13},{13,15},{17,19},{19,21},{21... | collective-permute-start | bytes 294920 | tf_op jit(solution)/shard_map/ppermute | solution.py:784
  18.8 0.6 reduce_sum.9
  19.4 0.7 fusion
  22.2 0.1 constant_dynamic-slice_fusion.2
  22.3 0.1 tile.10
  22.4 0.1 broadcast_in_dim.11
  22.4 0.1 broadcast_in_dim_reshape.3.skip
  22.6 0.1 dynamic-slice.3
  22.7 0.1 stack.45.s_ref
  22.8 0.1 collective-permute-start.4
  22.9 1.0 collective-permute-start.6
  23.9 10.3 %conv_and_states.1 = (bf16[272,512]{1,0:T(8,128)(2,1)S(1)}, bf16[272,512]{1,0:T(8,128)(2,1)S(1)}, bf16[272,512]{1,0:T(8,128)(2,1)S(1)}, bf16[272,512]{1,0:T(8,12...) custom-call(s32[8]{0:T(128)S(1)} %stack.45.s_ref, ...), custom_call_target="tpu_custom_call" | custom-call | flops 6000000000 | bytes 8000000 | tf_op jit(solution)/shard_map/conv_and_states/pallas_call | solution.py:216
  34.2 1.4 %collective-permute-start.7 = (bf16[272,512]{1,0:T(8,128)(2,1)S(1)}, bf16[272,512]{1,0:T(8,128)(2,1)S(1)}, u32[]{:S(2)}, u32[]{:S(2)}) collective-permute-start(bf16[272,512]{1,0:T(8,128)(2,1)S(1)} %get-tuple-element.57), channel_id=1, source_target_pairs={{0,2},{1,3},{2,0},{3,1},{4,6},{5,7},{6,4},{7,5},{8,10},{9,11},{10,... | collective-permute-start | bytes 835592 | tf_op jit(solution)/shard_map/ppermute | solution.py:800
  35.7 0.4 collective-permute-start.8
  36.1 0.0 collective-permute-done.4.near_cross
  36.1 2.1 %collective-permute-start.9 = (bf16[272,512]{1,0:T(8,128)(2,1)S(1)}, bf16[272,512]{1,0:T(8,128)(2,1)S(1)}, u32[]{:S(2)}, u32[]{:S(2)}) collective-permute-start(bf16[272,512]{1,0:T(8,128)(2,1)S(1)} %get-tuple-element.59), channel_id=1, source_target_pairs={{0,6},{1,7},{2,4},{3,5},{4,2},{5,3},{6,0},{7,1},{8,14},{9,15},{10,... | collective-permute-start | bytes 835592 | tf_op jit(solution)/shard_map/ppermute | solution.py:800
  38.2 11.2 %output_within_chip_1.1 = (bf16[448,512]{1,0:T(8,128)(2,1)S(1)}, bf16[448,512]{1,0:T(8,128)(2,1)S(1)}, bf16[448,512]{1,0:T(8,128)(2,1)S(1)}, f32[512,2048]{1,0:T(8,128)}) custom-call(s32[8]{0:T(128)S(1)} %stack.45.s_ref, bf16[512,2048]{1,0:T(8,128)(2,1)S(1)} %get-tuple-element.49.xc_ref, bf16[512,512]{1,0:T(8,128)(2,1)S(1)} %get-tuple-element.50.bcc.c_rows, ...), custom_call_target="tpu_custom_call" | custom-call | flops 8999999488 | bytes 6000000 | tf_op jit(solution)/shard_map/output_within_chip_1/pallas_call | solution.py:423
  49.4 0.1 collective-permute-start.15
  49.5 1.7 %collective-permute-start.16 = (bf16[448,512]{1,0:T(8,128)(2,1)S(1)}, bf16[448,512]{1,0:T(8,128)(2,1)S(1)}, u32[]{:S(2)}, u32[]{:S(2)}) collective-permute-start(bf16[448,512]{1,0:T(8,128)(2,1)S(1)} %get-tuple-element.77), channel_id=1, source_target_pairs={{0,4},{1,5},{2,6},{3,7},{4,0},{5,1},{6,2},{7,3},{8,12},{9,13},{10,... | collective-permute-start | bytes 1376264 | tf_op jit(solution)/shard_map/ppermute | solution.py:800
  51.2 0.0 collective-permute-done.7.l1
  51.2 2.1 %collective-permute-start.17 = (bf16[448,512]{1,0:T(8,128)(2,1)S(1)}, bf16[448,512]{1,0:T(8,128)(2,1)S(1)}, u32[]{:S(2)}, u32[]{:S(2)}) collective-permute-start(bf16[448,512]{1,0:T(8,128)(2,1)S(1)} %get-tuple-element.78), channel_id=1, source_target_pairs={{0,6},{1,7},{2,4},{3,5},{4,2},{5,3},{6,0},{7,1},{8,14},{9,15},{10,... | collective-permute-start | bytes 1376264 | tf_op jit(solution)/shard_map/ppermute | solution.py:800
  53.3 1.3 %pad_add_fusion.1.bounds = s32[3]{0:T(128)S(1)} fusion(s32[1]{0:T(128)} %bitcast.23, s32[1]{0:T(128)} %bitcast.22, s32[1]{0:T(128)} %bitcast.21), kind=kLoop, calls=%fused_computation.21 | loop fusion | flops 6 | bytes 24 | tf_op jit(solution)/shard_map/stack | solution.py:771
  54.6 0.0 collective-permute-done.8.l2
  54.6 0.9 half_total.1
  55.5 4.5 %collective-permute-start.10 = (bf16[256,512]{1,0:T(8,128)(2,1)S(1)}, bf16[256,512]{1,0:T(8,128)(2,1)S(1)}, u32[]{:S(2)}, u32[]{:S(2)}) collective-permute-start(bf16[256,512]{1,0:T(8,128)(2,1)S(1)} %half_total.1), channel_id=1, source_target_pairs={{0,8},{1,9},{2,10},{3,11},{4,12},{5,13},{6,14},{7,15},{16,24},{17,... | collective-permute-start | bytes 786440 | tf_op jit(solution)/shard_map/ppermute | solution.py:820
  60.0 5.5 %output_within_chip_0.1 = (bf16[448,512]{1,0:T(8,128)(2,1)S(1)}, f32[512,2048]{1,0:T(8,128)}) custom-call(s32[8]{0:T(128)S(1)} %stack.45.s_ref, bf16[512,2048]{1,0:T(8,128)(2,1)S(1)} %get-tuple-element.49.xc_ref, bf16[512,512]{1,0:T(8,128)(2,1)S(1)} %get-tuple-element.50.bcc.c_rows, ...), custom_call_target="tpu_custom_call", output_to_operand_aliasing={{1}: (11, {})} | custom-call | flops 3000000000 | bytes 2000000 | tf_op jit(solution)/shard_map/output_within_chip_0/pallas_call | solution.py:423
  65.5 0.0 collective-permute-done.10.start
  65.5 1.2 %chip_starts.1 = (bf16[256,512]{1,0:T(8,128)(2,1)S(1)}, bf16[256,512]{1,0:T(8,128)(2,1)S(1)}, bf16[256,512]{1,0:T(8,128)(2,1)S(1)}, bf16[256,512]{1,0:T(8,128)(2,1)S(1)}) custom-call(s32[8]{0:T(128)S(1)} %stack.45.s_ref, bf16[272,512]{1,0:T(8,128)(2,1)S(1)} %get-tuple-element.61.l0, bf16[272,512]{1,0:T(8,128)(2,1)S(1)} %collective-permute-done.7.l1, ...), custom_call_target="tpu_custom_call" | custom-call | flops 1000000 | bytes 3000000 | tf_op jit(solution)/shard_map/chip_starts/pallas_call | solution.py:481
  66.7 0.3 collective-permute-start.11
  67.0 2.2 %collective-permute-start.12 = (bf16[256,512]{1,0:T(8,128)(2,1)S(1)}, bf16[256,512]{1,0:T(8,128)(2,1)S(1)}, u32[]{:S(2)}, u32[]{:S(2)}) collective-permute-start(bf16[256,512]{1,0:T(8,128)(2,1)S(1)} %get-tuple-element.74), channel_id=1, source_target_pairs={{0,4},{1,5},{2,6},{3,7},{4,0},{5,1},{6,2},{7,3},{8,12},{9,13},{10,... | collective-permute-start | bytes 786440 | tf_op jit(solution)/shard_map/ppermute | solution.py:800
  69.2 0.0 collective-permute-done.15.f1
  69.2 1.5 %collective-permute-start.13 = (bf16[256,512]{1,0:T(8,128)(2,1)S(1)}, bf16[256,512]{1,0:T(8,128)(2,1)S(1)}, u32[]{:S(2)}, u32[]{:S(2)}) collective-permute-start(bf16[256,512]{1,0:T(8,128)(2,1)S(1)} %get-tuple-element.75), channel_id=1, source_target_pairs={{0,6},{1,7},{2,4},{3,5},{4,2},{5,3},{6,0},{7,1},{8,14},{9,15},{10,... | collective-permute-start | bytes 786440 | tf_op jit(solution)/shard_map/ppermute | solution.py:800
  70.7 3.1 %decode_rows.1 = (bf16[4,32,512]{2,1,0:T(8,128)(2,1)S(1)}, bf16[4,32,512]{2,1,0:T(8,128)(2,1)S(1)}) custom-call(s32[8]{0:T(128)S(1)} %stack.45.s_ref, bf16[272,512]{1,0:T(8,128)(2,1)S(1)} %get-tuple-element.61.l0, bf16[272,512]{1,0:T(8,128)(2,1)S(1)} %collective-permute-done.7.l1, bf16[272,512]{1,0:T(8,128)(2,1)S(1)} %collective-permute-done.8.l2, ...), custom_call_target="tpu_custom_call" | custom-call | flops 20000000000 | bytes 6000000 | tf_op jit(solution)/shard_map/decode_rows/pallas_call | solution.py:830
  73.8 1.4 %collective-permute-done.11.r1 = bf16[256,512]{1,0:T(8,128)(2,1)S(1)} collective-permute-done((bf16[256,512]{1,0:T(8,128)(2,1)S(1)}, bf16[256,512]{1,0:T(8,128)(2,1)S(1)}, u32[]{:S(2)}, u32[]{:S(2)}) %collective-permute-start.11) | collective-permute-done | bytes 262176 | tf_op jit(solution)/shard_map/ppermute | solution.py:800
  75.2 1.8 %collective-permute-start.18 = (bf16[4,32,512]{2,1,0:T(8,128)(2,1)S(1)}, bf16[4,32,512]{2,1,0:T(8,128)(2,1)}, u32[]{:S(2)}, u32[]{:S(2)}) collective-permute-start(bf16[4,32,512]{2,1,0:T(8,128)(2,1)S(1)} %get-tuple-element.81), channel_id=1, source_target_pairs={{0,64},{1,65},{2,66},{3,67},{4,68},{5,69},{6,70},{7,71},{8,72},{9,... | collective-permute-start | bytes 393224 | tf_op jit(solution)/shard_map/ppermute | solution.py:850
  77.0 3.4 %collective-permute-start.19 = (bf16[4,32,512]{2,1,0:T(8,128)(2,1)S(1)}, bf16[4,32,512]{2,1,0:T(8,128)(2,1)}, u32[]{:S(2)}, u32[]{:S(2)}) collective-permute-start(bf16[4,32,512]{2,1,0:T(8,128)(2,1)S(1)} %get-tuple-element.82), channel_id=1, source_target_pairs={{0,72},{1,73},{2,74},{3,75},{4,76},{5,77},{6,78},{7,79},{8,64},{9,... | collective-permute-start | bytes 393224 | tf_op jit(solution)/shard_map/ppermute | solution.py:851
  80.4 1.3 %collective-permute-done.12.r2 = bf16[256,512]{1,0:T(8,128)(2,1)S(1)} collective-permute-done((bf16[256,512]{1,0:T(8,128)(2,1)S(1)}, bf16[256,512]{1,0:T(8,128)(2,1)S(1)}, u32[]{:S(2)}, u32[]{:S(2)}) %collective-permute-start.12) | collective-permute-done | bytes 262176 | tf_op jit(solution)/shard_map/ppermute | solution.py:800
  81.7 3.0 %collective-permute-done.13.r3 = bf16[256,512]{1,0:T(8,128)(2,1)S(1)} collective-permute-done((bf16[256,512]{1,0:T(8,128)(2,1)S(1)}, bf16[256,512]{1,0:T(8,128)(2,1)S(1)}, u32[]{:S(2)}, u32[]{:S(2)}) %collective-permute-start.13) | collective-permute-done | bytes 262176 | tf_op jit(solution)/shard_map/ppermute | solution.py:800
  84.8 4.7 %carried_other.1 = bf16[256,2048]{1,0:T(8,128)(2,1)} custom-call(s32[8]{0:T(128)S(1)} %stack.45.s_ref, f32[512,2048]{1,0:T(8,128)} %get-tuple-element.70.local, bf16[512,512]{1,0:T(8,128)(2,1)S(1)} %get-tuple-element.50.bcc.c_rows, bf16[512,128]{1,0:T(8,128)(2,1)S(1)} %get-tuple-element.71.wc3, bf16[256,512]{1,0:T(8,128)(2,1)S(1)} %get-tuple-element.72.r0, ...), custom_call_target="tpu_custom_call" | custom-call | flops 1000000000 | bytes 4000000 | tf_op jit(solution)/shard_map/carried_other/pallas_call | solution.py:625
  89.5 1.7 %collective-permute-start.14 = (bf16[256,2048]{1,0:T(8,128)(2,1)}, bf16[256,2048]{1,0:T(8,128)(2,1)S(1)}, u32[]{:S(2)}, u32[]{:S(2)}) collective-permute-start(bf16[256,2048]{1,0:T(8,128)(2,1)} %carried_other.1), channel_id=1, source_target_pairs={{0,1},{1,0},{2,3},{3,2},{4,5},{5,4},{6,7},{7,6},{8,9},{9,8},{10,11... | collective-permute-start | bytes 3145736 | tf_op jit(solution)/shard_map/ppermute | solution.py:849
  91.1 0.0 collective-permute-done.18
  91.1 0.0 collective-permute-done.19
  91.1 1.0 add.45
  92.2 0.1 collective-permute-start.20
  92.3 3.2 %collective-permute-start.21 = (bf16[32,512]{1,0:T(8,128)(2,1)S(1)}, bf16[32,512]{1,0:T(8,128)(2,1)S(1)}, u32[]{:S(2)}, u32[]{:S(2)}) collective-permute-start(bf16[32,512]{1,0:T(8,128)(2,1)S(1)} %get-tuple-element.95), channel_id=1, source_target_pairs={{0,4},{1,5},{2,6},{3,7},{4,0},{5,1},{6,2},{7,3},{8,12},{9,13},{10,... | collective-permute-start | bytes 98312 | tf_op jit(solution)/shard_map/ppermute | solution.py:800
  95.5 0.6 collective-permute-start.22
  96.1 4.7 %carried_own.1.whole = bf16[256,4096]{1,0:T(8,128)(2,1)} custom-call(s32[8]{0:T(128)S(1)} %stack.45.s_ref, f32[512,2048]{1,0:T(8,128)} %get-tuple-element.70.local, bf16[512,512]{1,0:T(8,128)(2,1)S(1)} %get-tuple-element.50.bcc.c_rows, bf16[512,128]{1,0:T(8,128)(2,1)S(1)} %get-tuple-element.71.wc3, bf16[256,512]{1,0:T(8,128)(2,1)S(1)} %get-tuple-element.72.r0, ...), custom_call_target="tpu_custom_call" | custom-call | flops 1000000000 | bytes 4000000 | tf_op jit(solution)/shard_map/carried_own/pallas_call | solution.py:625
  100.9 0.1 reshape.87
  100.9 0.1 select_bitcast_fusion
  101.0 0.9 collective-permute-start.23
  102.0 0.9 collective-permute-done.23
  102.9 0.8 maximum_select_fusion
  103.7 0.0 collective-permute-done.14.part
  103.7 1.6 %put_group.1 = bf16[256,4096]{1,0:T(8,128)(2,1)} custom-call(s32[8]{0:T(128)S(1)} %stack.45.s_ref, bf16[256,2048]{1,0:T(8,128)(2,1)S(1)} %collective-permute-done.14.part, bf16[256,4096]{1,0:T(8,128)(2,1)} %carried_own.1.whole), custom_call_target="tpu_custom_call", output_to_operand_aliasing={{}: (2, {})} | custom-call | bytes 2000000 | tf_op jit(solution)/shard_map/put_group/pallas_call | solution.py:650
  (41 shorter events, 0.2 us)
Async XLA Ops:
  0.6 21.4 %copy-start = (bf16[4,2,512]{2,1,0:T(2,128)(2,1)S(1)}, bf16[4,2,512]{2,1,0:T(2,128)(2,1)}, u32[]{:S(2)}) copy-start(bf16[4,2,512]{2,1,0:T(2,128)(2,1)} %param.20) | copy-start | bytes 24580
  1.4 17.4 %copy-start.3 = (s32[1,3]{1,0:T(1,128)S(1)}, s32[1,3]{1,0:T(1,128)}, u32[]{:S(2)}) copy-start(s32[1,3]{1,0:T(1,128)} %param.25) | copy-start | bytes 40
  1.4 20.7 %copy-start.4 = (f32[2,512]{1,0:T(2,128)S(1)}, f32[2,512]{1,0:T(2,128)}, u32[]{:S(2)}) copy-start(f32[2,512]{1,0:T(2,128)} %param.21) | copy-start | bytes 12292
  1.4 20.8 %copy-start.7 = (f32[64]{0:T(128)S(1)}, f32[64]{0:T(128)}, u32[]{:S(2)}) copy-start(f32[64]{0:T(128)} %param.23) | copy-start | bytes 772
  1.4 20.8 %copy-start.6 = (f32[64]{0:T(128)S(1)}, f32[64]{0:T(128)}, u32[]{:S(2)}) copy-start(f32[64]{0:T(128)} %param.22) | copy-start | bytes 772
  1.4 21.0 %copy-start.5 = (f32[64]{0:T(128)S(1)}, f32[64]{0:T(128)}, u32[]{:S(2)}) copy-start(f32[64]{0:T(128)} %param.24) | copy-start | bytes 772
  1.4 21.2 %copy-start.2 = (f32[4096]{0:T(1024)S(1)}, f32[4096]{0:T(1024)}, u32[]{:S(2)}) copy-start(f32[4096]{0:T(1024)} %param.19) | copy-start | bytes 49156
  1.4 22.5 %copy-start.1 = (bf16[4,4096]{1,0:T(4,128)(2,1)S(1)}, bf16[4,4096]{1,0:T(4,128)(2,1)}, u32[]{:S(2)}) copy-start(bf16[4,4096]{1,0:T(4,128)(2,1)} %wx.1) | copy-start | bytes 98308
  6.3 17.6 %collective-permute-start = (bf16[256,3072]{1,0:T(8,128)(2,1)}, bf16[256,3072]{1,0:T(8,128)(2,1)}, u32[]{:S(2)}, u32[]{:S(2)}) collective-permute-start(bf16[256,3072]{1,0:T(8,128)(2,1)} %get-tuple-element.45), channel_id=1, source_target_pairs={{0,1},{1,0},{2,3},{3,2},{4,5},{5,4},{6,7},{7,6},{8,9},{9,8},{10,11... | collective-permute-start | bytes 4718600 | tf_op jit(solution)/shard_map/ppermute | solution.py:781
  7.8 27.9 %collective-permute-start.3 = (bf16[16,3072]{1,0:T(8,128)(2,1)}, bf16[16,3072]{1,0:T(8,128)(2,1)S(1)}, u32[]{:S(2)}, u32[]{:S(2)}) collective-permute-start(bf16[16,3072]{1,0:T(8,128)(2,1)} %get-tuple-element.54), channel_id=1, source_target_pairs={{0,64},{1,65},{2,66},{3,67},{4,68},{5,69},{6,70},{7,71},{8,72},{9,... | collective-permute-start | bytes 294920 | tf_op jit(solution)/shard_map/ppermute | solution.py:793
  9.2 29.0 %collective-permute-start.5 = (bf16[16,3072]{1,0:T(8,128)(2,1)}, bf16[16,3072]{1,0:T(8,128)(2,1)S(1)}, u32[]{:S(2)}, u32[]{:S(2)}) collective-permute-start(bf16[16,3072]{1,0:T(8,128)(2,1)} %get-tuple-element.54), channel_id=1, source_target_pairs={{0,72},{1,73},{2,74},{3,75},{4,76},{5,77},{6,78},{7,79},{8,64},{9,... | collective-permute-start | bytes 294920 | tf_op jit(solution)/shard_map/ppermute | solution.py:793
  11.1 11.7 %collective-permute-start.1 = (bf16[16,3072]{1,0:T(8,128)(2,1)}, bf16[16,3072]{1,0:T(8,128)(2,1)S(1)}, u32[]{:S(2)}, u32[]{:S(2)}) collective-permute-start(bf16[16,3072]{1,0:T(8,128)(2,1)} %get-tuple-element.46), channel_id=1, source_target_pairs={{1,2},{3,4},{5,6},{7,8},{9,10},{11,12},{13,14},{17,18},{19,20},{21... | collective-permute-start | bytes 294920 | tf_op jit(solution)/shard_map/ppermute | solution.py:783
  15.1 7.7 %collective-permute-start.2 = (bf16[16,3072]{1,0:T(8,128)(2,1)}, bf16[16,3072]{1,0:T(8,128)(2,1)S(1)}, u32[]{:S(2)}, u32[]{:S(2)}) collective-permute-start(bf16[16,3072]{1,0:T(8,128)(2,1)} %get-tuple-element.47), channel_id=1, source_target_pairs={{1,3},{3,5},{5,7},{7,9},{9,11},{11,13},{13,15},{17,19},{19,21},{21... | collective-permute-start | bytes 294920 | tf_op jit(solution)/shard_map/ppermute | solution.py:784
  22.8 13.3 %collective-permute-start.4 = (bf16[16,3072]{1,0:T(8,128)(2,1)}, bf16[16,3072]{1,0:T(8,128)(2,1)S(1)}, u32[]{:S(2)}, u32[]{:S(2)}) collective-permute-start(bf16[16,3072]{1,0:T(8,128)(2,1)} %get-tuple-element.55), channel_id=1, source_target_pairs={{0,65},{1,64},{2,67},{3,66},{4,69},{5,68},{6,71},{7,70},{8,73},{9,... | collective-permute-start | bytes 294920 | tf_op jit(solution)/shard_map/ppermute | solution.py:793
  22.9 15.3 %collective-permute-start.6 = (bf16[16,3072]{1,0:T(8,128)(2,1)}, bf16[16,3072]{1,0:T(8,128)(2,1)S(1)}, u32[]{:S(2)}, u32[]{:S(2)}) collective-permute-start(bf16[16,3072]{1,0:T(8,128)(2,1)} %get-tuple-element.55), channel_id=1, source_target_pairs={{0,73},{1,72},{2,75},{3,74},{4,77},{5,76},{6,79},{7,78},{8,65},{9,... | collective-permute-start | bytes 294920 | tf_op jit(solution)/shard_map/ppermute | solution.py:793
  34.2 17.0 %collective-permute-start.7 = (bf16[272,512]{1,0:T(8,128)(2,1)S(1)}, bf16[272,512]{1,0:T(8,128)(2,1)S(1)}, u32[]{:S(2)}, u32[]{:S(2)}) collective-permute-start(bf16[272,512]{1,0:T(8,128)(2,1)S(1)} %get-tuple-element.57), channel_id=1, source_target_pairs={{0,2},{1,3},{2,0},{3,1},{4,6},{5,7},{6,4},{7,5},{8,10},{9,11},{10,... | collective-permute-start | bytes 835592 | tf_op jit(solution)/shard_map/ppermute | solution.py:800
  35.7 18.9 %collective-permute-start.8 = (bf16[272,512]{1,0:T(8,128)(2,1)S(1)}, bf16[272,512]{1,0:T(8,128)(2,1)S(1)}, u32[]{:S(2)}, u32[]{:S(2)}) collective-permute-start(bf16[272,512]{1,0:T(8,128)(2,1)S(1)} %get-tuple-element.58), channel_id=1, source_target_pairs={{0,4},{1,5},{2,6},{3,7},{4,0},{5,1},{6,2},{7,3},{8,12},{9,13},{10,... | collective-permute-start | bytes 835592 | tf_op jit(solution)/shard_map/ppermute | solution.py:800
  36.1 18.5 %collective-permute-start.9 = (bf16[272,512]{1,0:T(8,128)(2,1)S(1)}, bf16[272,512]{1,0:T(8,128)(2,1)S(1)}, u32[]{:S(2)}, u32[]{:S(2)}) collective-permute-start(bf16[272,512]{1,0:T(8,128)(2,1)S(1)} %get-tuple-element.59), channel_id=1, source_target_pairs={{0,6},{1,7},{2,4},{3,5},{4,2},{5,3},{6,0},{7,1},{8,14},{9,15},{10,... | collective-permute-start | bytes 835592 | tf_op jit(solution)/shard_map/ppermute | solution.py:800
  49.4 19.8 %collective-permute-start.15 = (bf16[448,512]{1,0:T(8,128)(2,1)S(1)}, bf16[448,512]{1,0:T(8,128)(2,1)S(1)}, u32[]{:S(2)}, u32[]{:S(2)}) collective-permute-start(bf16[448,512]{1,0:T(8,128)(2,1)S(1)} %get-tuple-element.60), channel_id=1, source_target_pairs={{0,2},{1,3},{2,0},{3,1},{4,6},{5,7},{6,4},{7,5},{8,10},{9,11},{10,... | collective-permute-start | bytes 1376264 | tf_op jit(solution)/shard_map/ppermute | solution.py:800
  49.5 21.1 %collective-permute-start.16 = (bf16[448,512]{1,0:T(8,128)(2,1)S(1)}, bf16[448,512]{1,0:T(8,128)(2,1)S(1)}, u32[]{:S(2)}, u32[]{:S(2)}) collective-permute-start(bf16[448,512]{1,0:T(8,128)(2,1)S(1)} %get-tuple-element.77), channel_id=1, source_target_pairs={{0,4},{1,5},{2,6},{3,7},{4,0},{5,1},{6,2},{7,3},{8,12},{9,13},{10,... | collective-permute-start | bytes 1376264 | tf_op jit(solution)/shard_map/ppermute | solution.py:800
  51.2 19.4 %collective-permute-start.17 = (bf16[448,512]{1,0:T(8,128)(2,1)S(1)}, bf16[448,512]{1,0:T(8,128)(2,1)S(1)}, u32[]{:S(2)}, u32[]{:S(2)}) collective-permute-start(bf16[448,512]{1,0:T(8,128)(2,1)S(1)} %get-tuple-element.78), channel_id=1, source_target_pairs={{0,6},{1,7},{2,4},{3,5},{4,2},{5,3},{6,0},{7,1},{8,14},{9,15},{10,... | collective-permute-start | bytes 1376264 | tf_op jit(solution)/shard_map/ppermute | solution.py:800
  55.5 10.1 %collective-permute-start.10 = (bf16[256,512]{1,0:T(8,128)(2,1)S(1)}, bf16[256,512]{1,0:T(8,128)(2,1)S(1)}, u32[]{:S(2)}, u32[]{:S(2)}) collective-permute-start(bf16[256,512]{1,0:T(8,128)(2,1)S(1)} %half_total.1), channel_id=1, source_target_pairs={{0,8},{1,9},{2,10},{3,11},{4,12},{5,13},{6,14},{7,15},{16,24},{17,... | collective-permute-start | bytes 786440 | tf_op jit(solution)/shard_map/ppermute | solution.py:820
  66.7 8.5 %collective-permute-start.11 = (bf16[256,512]{1,0:T(8,128)(2,1)S(1)}, bf16[256,512]{1,0:T(8,128)(2,1)S(1)}, u32[]{:S(2)}, u32[]{:S(2)}) collective-permute-start(bf16[256,512]{1,0:T(8,128)(2,1)S(1)} %get-tuple-element.73), channel_id=1, source_target_pairs={{0,2},{1,3},{2,0},{3,1},{4,6},{5,7},{6,4},{7,5},{8,10},{9,11},{10,... | collective-permute-start | bytes 786440 | tf_op jit(solution)/shard_map/ppermute | solution.py:800
  67.0 14.8 %collective-permute-start.12 = (bf16[256,512]{1,0:T(8,128)(2,1)S(1)}, bf16[256,512]{1,0:T(8,128)(2,1)S(1)}, u32[]{:S(2)}, u32[]{:S(2)}) collective-permute-start(bf16[256,512]{1,0:T(8,128)(2,1)S(1)} %get-tuple-element.74), channel_id=1, source_target_pairs={{0,4},{1,5},{2,6},{3,7},{4,0},{5,1},{6,2},{7,3},{8,12},{9,13},{10,... | collective-permute-start | bytes 786440 | tf_op jit(solution)/shard_map/ppermute | solution.py:800
  69.2 15.6 %collective-permute-start.13 = (bf16[256,512]{1,0:T(8,128)(2,1)S(1)}, bf16[256,512]{1,0:T(8,128)(2,1)S(1)}, u32[]{:S(2)}, u32[]{:S(2)}) collective-permute-start(bf16[256,512]{1,0:T(8,128)(2,1)S(1)} %get-tuple-element.75), channel_id=1, source_target_pairs={{0,6},{1,7},{2,4},{3,5},{4,2},{5,3},{6,0},{7,1},{8,14},{9,15},{10,... | collective-permute-start | bytes 786440 | tf_op jit(solution)/shard_map/ppermute | solution.py:800
  75.2 16.0 %collective-permute-start.18 = (bf16[4,32,512]{2,1,0:T(8,128)(2,1)S(1)}, bf16[4,32,512]{2,1,0:T(8,128)(2,1)}, u32[]{:S(2)}, u32[]{:S(2)}) collective-permute-start(bf16[4,32,512]{2,1,0:T(8,128)(2,1)S(1)} %get-tuple-element.81), channel_id=1, source_target_pairs={{0,64},{1,65},{2,66},{3,67},{4,68},{5,69},{6,70},{7,71},{8,72},{9,... | collective-permute-start | bytes 393224 | tf_op jit(solution)/shard_map/ppermute | solution.py:850
  77.0 14.2 %collective-permute-start.19 = (bf16[4,32,512]{2,1,0:T(8,128)(2,1)S(1)}, bf16[4,32,512]{2,1,0:T(8,128)(2,1)}, u32[]{:S(2)}, u32[]{:S(2)}) collective-permute-start(bf16[4,32,512]{2,1,0:T(8,128)(2,1)S(1)} %get-tuple-element.82), channel_id=1, source_target_pairs={{0,72},{1,73},{2,74},{3,75},{4,76},{5,77},{6,78},{7,79},{8,64},{9,... | collective-permute-start | bytes 393224 | tf_op jit(solution)/shard_map/ppermute | solution.py:851
  89.5 14.2 %collective-permute-start.14 = (bf16[256,2048]{1,0:T(8,128)(2,1)}, bf16[256,2048]{1,0:T(8,128)(2,1)S(1)}, u32[]{:S(2)}, u32[]{:S(2)}) collective-permute-start(bf16[256,2048]{1,0:T(8,128)(2,1)} %carried_other.1), channel_id=1, source_target_pairs={{0,1},{1,0},{2,3},{3,2},{4,5},{5,4},{6,7},{7,6},{8,9},{9,8},{10,11... | collective-permute-start | bytes 3145736 | tf_op jit(solution)/shard_map/ppermute | solution.py:849
  92.2 8.6 %collective-permute-start.20 = (bf16[32,512]{1,0:T(8,128)(2,1)S(1)}, bf16[32,512]{1,0:T(8,128)(2,1)S(1)}, u32[]{:S(2)}, u32[]{:S(2)}) collective-permute-start(bf16[32,512]{1,0:T(8,128)(2,1)S(1)} %get-tuple-element.96), channel_id=1, source_target_pairs={{0,2},{1,3},{2,0},{3,1},{4,6},{5,7},{6,4},{7,5},{8,10},{9,11},{10,... | collective-permute-start | bytes 98312 | tf_op jit(solution)/shard_map/ppermute | solution.py:800
  92.3 8.5 %collective-permute-start.21 = (bf16[32,512]{1,0:T(8,128)(2,1)S(1)}, bf16[32,512]{1,0:T(8,128)(2,1)S(1)}, u32[]{:S(2)}, u32[]{:S(2)}) collective-permute-start(bf16[32,512]{1,0:T(8,128)(2,1)S(1)} %get-tuple-element.95), channel_id=1, source_target_pairs={{0,4},{1,5},{2,6},{3,7},{4,0},{5,1},{6,2},{7,3},{8,12},{9,13},{10,... | collective-permute-start | bytes 98312 | tf_op jit(solution)/shard_map/ppermute | solution.py:800
  95.5 5.3 %collective-permute-start.22 = (bf16[32,512]{1,0:T(8,128)(2,1)S(1)}, bf16[32,512]{1,0:T(8,128)(2,1)S(1)}, u32[]{:S(2)}, u32[]{:S(2)}) collective-permute-start(bf16[32,512]{1,0:T(8,128)(2,1)S(1)} %get-tuple-element.94), channel_id=1, source_target_pairs={{0,6},{1,7},{2,4},{3,5},{4,2},{5,3},{6,0},{7,1},{8,14},{9,15},{10,... | collective-permute-start | bytes 98312 | tf_op jit(solution)/shard_map/ppermute | solution.py:800
  101.0 1.8 %collective-permute-start.23 = (bf16[16,2048]{1,0:T(8,128)(2,1)S(1)}, bf16[16,2048]{1,0:T(8,128)(2,1)S(1)}, u32[]{:S(2)}, u32[]{:S(2)}) collective-permute-start(bf16[16,2048]{1,0:T(8,128)(2,1)S(1)} %select_n.156), channel_id=1, source_target_pairs={{0,1},{1,0},{2,3},{3,2},{4,5},{5,4},{6,7},{7,6},{8,9},{9,8},{10,11... | collective-permute-start | bytes 196616 | tf_op jit(solution)/shard_map/ppermute | solution.py:863

commit v4 on v3

--- a/solution.py
+++ b/solution.py
@@ -500,7 +500,8 @@
 ):
     z, upper = s_ref[1], s_ref[2]
     ls, fs = (l0, l1, l2, l3), (f0, f1, f2, f3)
-    lasts = [bounds[q] - 1 for q in range(PROMPTS)]
+    first, second = bounds[0, 0], bounds[0, 0] + bounds[0, 1]
+    lasts = [first - 1, second - 1, second + bounds[0, 2] - 1]
     final[...] = jnp.zeros_like(final)
     state = start[...].astype(F32)
     for chip in range(RING):
@@ -604,15 +605,20 @@
 
 
 def kernel_d(s_ref, local, c_rows, wc3, r0, r1, r2, r3, out):
-    m = pl.program_id(0)
-    spread = spread_matrix(s_ref[1] ^ m)
-    for index, r in enumerate((r0, r1, r2, r3)):
-
-        @pl.when(m == index)
-        def _():
-            for lanes in (slice(0, 256), slice(256, 512)):
-                factor = mm(wc3[...], spread[:, lanes])
-                out[:, lanes] = (local[:, lanes] + factor * mm(c_rows[...], r[:, lanes])).astype(BF16)
+    z = s_ref[1]
+    block = (z >> 1) ^ pl.program_id(0)
+    for side in range(2):
+        chunk = 2 * block + side
+        spread = spread_matrix(chunk)
+        for index, r in enumerate((r0, r1, r2, r3)):
+
+            @pl.when((chunk ^ z) == index)
+            def _():
+                for part in range(2):
+                    lanes = slice(part * 256, (part + 1) * 256)
+                    to = slice(side * CHUNK + part * 256, side * CHUNK + (part + 1) * 256)
+                    factor = mm(wc3[...], spread[:, lanes])
+                    out[:, to] = (local[:, to] + factor * mm(c_rows[...], r[:, lanes])).astype(BF16)
 
 
 def run_d(scalars, local, bcc, wc3, starts, own):
@@ -626,16 +632,16 @@
         kernel_d,
         grid_spec=pltpu.PrefetchScalarGridSpec(
             num_scalar_prefetch=1,
-            grid=(RING,),
+            grid=(2,),
             in_specs=[
-                pl.BlockSpec((half, CHUNK), lambda m, s: (row(s), s[1] ^ m)),
+                pl.BlockSpec((half, 2 * CHUNK), lambda m, s: (row(s), (s[1] >> 1) ^ m)),
                 pl.BlockSpec((half, STATE), lambda m, s: (row(s), 1)),
                 pl.BlockSpec((half, LANES), lambda m, s: (row(s), 0)),
             ] + [pl.BlockSpec((STATE, CHUNK), lambda m, s: (0, 0))] * RING,
-            out_specs=pl.BlockSpec((half, CHUNK), lambda m, s: (0, (s[0] * RING if own else 0) + (s[1] ^ m))),
+            out_specs=pl.BlockSpec((half, 2 * CHUNK), lambda m, s: (0, (s[0] * 2 if own else 0) + ((s[1] >> 1) ^ m))),
         ),
         out_shape=jax.ShapeDtypeStruct((half, width), BF16),
-        compiler_params=pltpu.CompilerParams(vmem_limit_bytes=8 * MIB),
+        compiler_params=pltpu.CompilerParams(vmem_limit_bytes=12 * MIB),
         cost_estimate=pl.CostEstimate(flops=10**9, bytes_accessed=4 * 10**6, transcendentals=0),
         name="carried_own" if own else "carried_other",
     )(scalars, local, bcc, wc3, *starts)
@@ -768,7 +774,7 @@
     z = (place // CORES) % RING
     upper = place // (CORES * RING)
     anchor = (place // CORES) * CHIP_TOKENS
-    bounds = jnp.stack([lengths[0, 0], lengths[0, 0] + lengths[0, 1], jnp.sum(lengths[0])]).astype(jnp.int32)
+    bounds = (lengths[0, 0], lengths[0, 0] + lengths[0, 1])
     zero = jnp.int32(0)
     scalars = jnp.stack([core, z, upper, anchor, bounds[0] - anchor, bounds[1] - anchor, zero, zero]).astype(jnp.int32)
     both = ("pool", "dp")
@@ -844,7 +850,7 @@
             name="decode_rows",
         )(scalars, *args, bounds_ref_args)
 
-    kept, sent = after(tuple(decode(bounds)), starts[1])
+    kept, sent = after(tuple(decode(lengths.astype(jnp.int32))), starts[1])
     other_rows = run_d(scalars, local, bcc, wc3, starts, False)
     other_group = lax.ppermute(other_rows, "dp", [(i, i ^ 1) for i in range(count)])
     straight = lax.ppermute(kept, both, [(i, (i + count) % total) for i in range(total)])
@@ -861,8 +867,9 @@
     first, second = (answers[:, i].reshape(dec_rows, GROUP_CH) for i in range(CORES))
     mine = jnp.where(core == 0, first, second)
     theirs = lax.ppermute(jnp.where(core == 0, second, first), "dp", [(i, i ^ 1) for i in range(count)])
+    out = put_group(scalars, own_group, other_group)
+    theirs = after(theirs, out)
     decoded = jnp.where(core == 0, jnp.concatenate([mine, theirs], axis=1), jnp.concatenate([theirs, mine], axis=1))
-    out = put_group(scalars, own_group, other_group)
     return out[None], decoded.reshape(dec_x.shape)
 
 

time: 106 us -> 104 us (0.981)
  starting transfers between devices: 41.5 us -> 43.7 us
  other arithmetic: 4.53 us -> 2.63 us
  Pallas kernels: 48.2 us -> 46.6 us
    ppermute x1, starting transfers between devices: 1.79 us -> 3.68 us  [on_device(): lax.ppermute(kept, both, [(i, (i + count) % total) for i in range(total)])]
    pallas_call x2, Pallas kernels: 9.42 us -> 7.73 us  [run_d(): pl.pallas_call(kernel_d, grid_spec=pltpu.PrefetchScalarGridSpec(num_scala...]
    another operation x1 -> x0, other arithmetic: 1.29 us -> none  [on_device(): jnp.stack([lengths[0, 0], lengths[0, 0] + lengths[0, 1], jnp.sum(lengths[...]
  transfers between devices with their start and end apart: 24 -> 24, of which waited for: 4 -> 4; matrix products, arithmetic and copies ran while one was open for 5% -> 2% of each run, Pallas kernels for 40% -> 40%
where the time goes in v4:
time: 104 us; the launch traced here: 103 us
  Pallas kernels  46.6 us (45%)
  starting transfers between devices  43.7 us (42%)
  waiting for transfers between devices  5.84 us (6%)
  between operations  3.14 us (3%)
  other arithmetic  2.63 us (3%)
  local copies, waits for them, and re-layouts  1.36 us (1%)
    pallas_call x2, Pallas kernels, run_b(): pl.pallas_call(functools.partial(kernel_b, base, count), grid_spec=pltpu....  16.8 us
    ppermute x12, starting transfers between devices, z_swap(): return lax.ppermute(value, 'dp', [(i, i ^ CORES * m) for i in range(count)])  15.9 us
    pallas_call x1, Pallas kernels, run_a(): pl.pallas_call(kernel_a, grid_spec=pltpu.PrefetchScalarGridSpec(num_scala...  10.3 us
    pallas_call x2, Pallas kernels, run_d(): pl.pallas_call(kernel_d, grid_spec=pltpu.PrefetchScalarGridSpec(num_scala...  7.73 us
    ppermute x12, waiting for transfers between devices, z_swap(): return lax.ppermute(value, 'dp', [(i, i ^ CORES * m) for i in range(count)])  5.81 us
    pallas_call x1, Pallas kernels, run_pack(): pl.pallas_call(kernel_pack, grid_spec=pltpu.PrefetchScalarGridSpec(num_sc...  4.84 us
    ppermute x1, starting transfers between devices, on_device(): lax.ppermute(half_total, 'dp', [(i, i + CORES * RING) for i in range(CORE...  4.45 us
    ppermute x4, starting transfers between devices, hop(): lax.ppermute(value, both, [(i, (i + count) % total ^ flip) for i in range...  4.34 us
  transfers between devices with their start and end apart: 24, of which 4 were waited for; matrix products, arithmetic and copies ran while one was open for 2% of the time, Pallas kernels for 40%

profile of v4, /device:TPU:1, one launch (start us, length us, event | category | flops | bytes accessed | tf_op | source)
XLA Modules:
  0.0 103.3 jit_solution(15133693610346240219)
XLA Ops:
  0.6 0.0 copy-start
  0.7 0.7 pad_add_fusion.s_ref
  1.4 0.0 copy-start.5
  1.4 0.0 copy-start.3
  1.4 0.0 copy-start.2
  1.4 4.8 %pack.1 = (bf16[256,3072]{1,0:T(8,128)(2,1)}, bf16[16,3072]{1,0:T(8,128)(2,1)}, bf16[16,3072]{1,0:T(8,128)(2,1)}, bf16[256,1024]{1,0:T(8,128)(2,1)}, bf16[16,3072]{1,0:T(8,128)(2,1)}, /*index=5*/bf16[16,3072]{1,0:T(8,128)(2,1)}) custom-call(s32[5]{0:T(128)S(1)} %pad_add_fusion.s_ref, bf16[256,4096]{1,0:T(8,128)(2,1)} %bitcast.60, ...), custom_call_target="tpu_custom_call" | custom-call | flops 1000000 | bytes 4000000 | tf_op jit(solution)/shard_map/pack/pallas_call | solution.py:735
  6.3 1.5 %collective-permute-start = (bf16[256,3072]{1,0:T(8,128)(2,1)}, bf16[256,3072]{1,0:T(8,128)(2,1)}, u32[]{:S(2)}, u32[]{:S(2)}) collective-permute-start(bf16[256,3072]{1,0:T(8,128)(2,1)} %get-tuple-element.46), channel_id=1, source_target_pairs={{0,1},{1,0},{2,3},{3,2},{4,5},{5,4},{6,7},{7,6},{8,9},{9,8},{10,11... | collective-permute-start | bytes 4718600 | tf_op jit(solution)/shard_map/ppermute | solution.py:787
  7.8 1.4 %collective-permute-start.3 = (bf16[16,3072]{1,0:T(8,128)(2,1)}, bf16[16,3072]{1,0:T(8,128)(2,1)S(1)}, u32[]{:S(2)}, u32[]{:S(2)}) collective-permute-start(bf16[16,3072]{1,0:T(8,128)(2,1)} %get-tuple-element.55), channel_id=1, source_target_pairs={{0,64},{1,65},{2,66},{3,67},{4,68},{5,69},{6,70},{7,71},{8,72},{9,... | collective-permute-start | bytes 294920 | tf_op jit(solution)/shard_map/ppermute | solution.py:799
  9.2 1.9 %collective-permute-start.5 = (bf16[16,3072]{1,0:T(8,128)(2,1)}, bf16[16,3072]{1,0:T(8,128)(2,1)S(1)}, u32[]{:S(2)}, u32[]{:S(2)}) collective-permute-start(bf16[16,3072]{1,0:T(8,128)(2,1)} %get-tuple-element.55), channel_id=1, source_target_pairs={{0,72},{1,73},{2,74},{3,75},{4,76},{5,77},{6,78},{7,79},{8,64},{9,... | collective-permute-start | bytes 294920 | tf_op jit(solution)/shard_map/ppermute | solution.py:799
  11.1 4.1 %collective-permute-start.1 = (bf16[16,3072]{1,0:T(8,128)(2,1)}, bf16[16,3072]{1,0:T(8,128)(2,1)S(1)}, u32[]{:S(2)}, u32[]{:S(2)}) collective-permute-start(bf16[16,3072]{1,0:T(8,128)(2,1)} %get-tuple-element.47), channel_id=1, source_target_pairs={{1,2},{3,4},{5,6},{7,8},{9,10},{11,12},{13,14},{17,18},{19,20},{21... | collective-permute-start | bytes 294920 | tf_op jit(solution)/shard_map/ppermute | solution.py:789
  15.1 3.5 %collective-permute-start.2 = (bf16[16,3072]{1,0:T(8,128)(2,1)}, bf16[16,3072]{1,0:T(8,128)(2,1)S(1)}, u32[]{:S(2)}, u32[]{:S(2)}) collective-permute-start(bf16[16,3072]{1,0:T(8,128)(2,1)} %get-tuple-element.48), channel_id=1, source_target_pairs={{1,3},{3,5},{5,7},{7,9},{9,11},{11,13},{13,15},{17,19},{19,21},{21... | collective-permute-start | bytes 294920 | tf_op jit(solution)/shard_map/ppermute | solution.py:790
  18.8 0.7 fusion
  21.6 0.1 constant_dynamic-slice_fusion.2
  21.7 0.1 tile.10
  21.8 0.1 broadcast_in_dim.11
  21.9 0.1 broadcast_in_dim_reshape.3.skip
  22.0 0.1 dynamic-slice.3
  22.1 0.1 stack.36.s_ref
  22.2 0.0 collective-permute-done.1
  22.2 0.1 collective-permute-start.4
  22.3 0.0 collective-permute-done.2
  22.3 1.0 collective-permute-start.6
  23.3 0.0 collective-permute-done.x_rec.g_rec
  23.3 10.3 %conv_and_states.1 = (bf16[272,512]{1,0:T(8,128)(2,1)S(1)}, bf16[272,512]{1,0:T(8,128)(2,1)S(1)}, bf16[272,512]{1,0:T(8,128)(2,1)S(1)}, bf16[272,512]{1,0:T(8,12...) custom-call(s32[8]{0:T(128)S(1)} %stack.36.s_ref, ...), custom_call_target="tpu_custom_call" | custom-call | flops 6000000000 | bytes 8000000 | tf_op jit(solution)/shard_map/conv_and_states/pallas_call | solution.py:216
  33.7 1.4 %collective-permute-start.7 = (bf16[272,512]{1,0:T(8,128)(2,1)S(1)}, bf16[272,512]{1,0:T(8,128)(2,1)S(1)}, u32[]{:S(2)}, u32[]{:S(2)}) collective-permute-start(bf16[272,512]{1,0:T(8,128)(2,1)S(1)} %get-tuple-element.58), channel_id=1, source_target_pairs={{0,2},{1,3},{2,0},{3,1},{4,6},{5,7},{6,4},{7,5},{8,10},{9,11},{10,... | collective-permute-start | bytes 835592 | tf_op jit(solution)/shard_map/ppermute | solution.py:806
  35.1 0.0 collective-permute-done.3.near_same
  35.1 0.4 collective-permute-start.8
  35.5 2.1 %collective-permute-start.9 = (bf16[272,512]{1,0:T(8,128)(2,1)S(1)}, bf16[272,512]{1,0:T(8,128)(2,1)S(1)}, u32[]{:S(2)}, u32[]{:S(2)}) collective-permute-start(bf16[272,512]{1,0:T(8,128)(2,1)S(1)} %get-tuple-element.60), channel_id=1, source_target_pairs={{0,6},{1,7},{2,4},{3,5},{4,2},{5,3},{6,0},{7,1},{8,14},{9,15},{10,... | collective-permute-start | bytes 835592 | tf_op jit(solution)/shard_map/ppermute | solution.py:806
  37.6 0.0 collective-permute-done.5.far_same
  37.6 0.0 collective-permute-done.6.far_cross
  37.6 11.3 %output_within_chip_1.1 = (bf16[448,512]{1,0:T(8,128)(2,1)S(1)}, bf16[448,512]{1,0:T(8,128)(2,1)S(1)}, bf16[448,512]{1,0:T(8,128)(2,1)S(1)}, f32[512,2048]{1,0:T(8,128)}) custom-call(s32[8]{0:T(128)S(1)} %stack.36.s_ref, bf16[512,2048]{1,0:T(8,128)(2,1)S(1)} %get-tuple-element.50.xc_ref, bf16[512,512]{1,0:T(8,128)(2,1)S(1)} %get-tuple-element.51.bcc.c_rows, ...), custom_call_target="tpu_custom_call" | custom-call | flops 8999999488 | bytes 6000000 | tf_op jit(solution)/shard_map/output_within_chip_1/pallas_call | solution.py:423
  48.9 0.1 collective-permute-start.15
  49.0 2.8 %collective-permute-start.16 = (bf16[448,512]{1,0:T(8,128)(2,1)S(1)}, bf16[448,512]{1,0:T(8,128)(2,1)S(1)}, u32[]{:S(2)}, u32[]{:S(2)}) collective-permute-start(bf16[448,512]{1,0:T(8,128)(2,1)S(1)} %get-tuple-element.78), channel_id=1, source_target_pairs={{0,4},{1,5},{2,6},{3,7},{4,0},{5,1},{6,2},{7,3},{8,12},{9,13},{10,... | collective-permute-start | bytes 1376264 | tf_op jit(solution)/shard_map/ppermute | solution.py:806
  51.8 0.0 collective-permute-done.7.l1
  51.8 1.0 collective-permute-start.17
  52.8 0.0 collective-permute-done.9.l3
  52.8 0.9 half_total.1
  53.7 4.4 %collective-permute-start.10 = (bf16[256,512]{1,0:T(8,128)(2,1)S(1)}, bf16[256,512]{1,0:T(8,128)(2,1)S(1)}, u32[]{:S(2)}, u32[]{:S(2)}) collective-permute-start(bf16[256,512]{1,0:T(8,128)(2,1)S(1)} %half_total.1), channel_id=1, source_target_pairs={{0,8},{1,9},{2,10},{3,11},{4,12},{5,13},{6,14},{7,15},{16,24},{17,... | collective-permute-start | bytes 786440 | tf_op jit(solution)/shard_map/ppermute | solution.py:826
  58.1 5.5 %output_within_chip_0.1 = (bf16[448,512]{1,0:T(8,128)(2,1)S(1)}, f32[512,2048]{1,0:T(8,128)}) custom-call(s32[8]{0:T(128)S(1)} %stack.36.s_ref, bf16[512,2048]{1,0:T(8,128)(2,1)S(1)} %get-tuple-element.50.xc_ref, bf16[512,512]{1,0:T(8,128)(2,1)S(1)} %get-tuple-element.51.bcc.c_rows, ...), custom_call_target="tpu_custom_call", output_to_operand_aliasing={{1}: (11, {})} | custom-call | flops 3000000000 | bytes 2000000 | tf_op jit(solution)/shard_map/output_within_chip_0/pallas_call | solution.py:423
  63.6 1.2 %chip_starts.1 = (bf16[256,512]{1,0:T(8,128)(2,1)S(1)}, bf16[256,512]{1,0:T(8,128)(2,1)S(1)}, bf16[256,512]{1,0:T(8,128)(2,1)S(1)}, bf16[256,512]{1,0:T(8,128)(2,1)S(1)}) custom-call(s32[8]{0:T(128)S(1)} %stack.36.s_ref, bf16[272,512]{1,0:T(8,128)(2,1)S(1)} %get-tuple-element.62.l0, bf16[272,512]{1,0:T(8,128)(2,1)S(1)} %collective-permute-done.7.l1, ...), custom_call_target="tpu_custom_call" | custom-call | flops 1000000 | bytes 3000000 | tf_op jit(solution)/shard_map/chip_starts/pallas_call | solution.py:481
  64.8 0.1 collective-permute-start.11
  64.9 4.1 %collective-permute-start.12 = (bf16[256,512]{1,0:T(8,128)(2,1)S(1)}, bf16[256,512]{1,0:T(8,128)(2,1)S(1)}, u32[]{:S(2)}, u32[]{:S(2)}) collective-permute-start(bf16[256,512]{1,0:T(8,128)(2,1)S(1)} %get-tuple-element.75), channel_id=1, source_target_pairs={{0,4},{1,5},{2,6},{3,7},{4,0},{5,1},{6,2},{7,3},{8,12},{9,13},{10,... | collective-permute-start | bytes 786440 | tf_op jit(solution)/shard_map/ppermute | solution.py:806
  69.0 0.9 collective-permute-done.16.f2
  70.0 0.0 collective-permute-done.17.f3
  70.0 3.2 %decode_rows.1 = (bf16[4,32,512]{2,1,0:T(8,128)(2,1)S(1)}, bf16[4,32,512]{2,1,0:T(8,128)(2,1)S(1)}) custom-call(s32[8]{0:T(128)S(1)} %stack.36.s_ref, bf16[272,512]{1,0:T(8,128)(2,1)S(1)} %get-tuple-element.62.l0, bf16[272,512]{1,0:T(8,128)(2,1)S(1)} %collective-permute-done.7.l1, bf16[272,512]{1,0:T(8,128)(2,1)S(1)} %collective-permute-done.8.l2, ...), custom_call_target="tpu_custom_call" | custom-call | flops 20000000000 | bytes 6000000 | tf_op jit(solution)/shard_map/decode_rows/pallas_call | solution.py:836
  73.2 0.2 collective-permute-done.11.r1
  73.4 3.7 %collective-permute-start.18 = (bf16[4,32,512]{2,1,0:T(8,128)(2,1)S(1)}, bf16[4,32,512]{2,1,0:T(8,128)(2,1)}, u32[]{:S(2)}, u32[]{:S(2)}) collective-permute-start(bf16[4,32,512]{2,1,0:T(8,128)(2,1)S(1)} %get-tuple-element.82), channel_id=1, source_target_pairs={{0,64},{1,65},{2,66},{3,67},{4,68},{5,69},{6,70},{7,71},{8,72},{9,... | collective-permute-start | bytes 393224 | tf_op jit(solution)/shard_map/ppermute | solution.py:856
  77.1 3.6 %collective-permute-start.19 = (bf16[4,32,512]{2,1,0:T(8,128)(2,1)S(1)}, bf16[4,32,512]{2,1,0:T(8,128)(2,1)}, u32[]{:S(2)}, u32[]{:S(2)}) collective-permute-start(bf16[4,32,512]{2,1,0:T(8,128)(2,1)S(1)} %get-tuple-element.83), channel_id=1, source_target_pairs={{0,72},{1,73},{2,74},{3,75},{4,76},{5,77},{6,78},{7,79},{8,64},{9,... | collective-permute-start | bytes 393224 | tf_op jit(solution)/shard_map/ppermute | solution.py:857
  80.7 0.8 collective-permute-done.12.r2
  81.5 3.8 %collective-permute-done.13.r3 = bf16[256,512]{1,0:T(8,128)(2,1)S(1)} collective-permute-done((bf16[256,512]{1,0:T(8,128)(2,1)S(1)}, bf16[256,512]{1,0:T(8,128)(2,1)S(1)}, u32[]{:S(2)}, u32[]{:S(2)}) %collective-permute-start.13) | collective-permute-done | bytes 262176 | tf_op jit(solution)/shard_map/ppermute | solution.py:806
  85.3 3.9 %carried_other.1 = bf16[256,2048]{1,0:T(8,128)(2,1)} custom-call(s32[8]{0:T(128)S(1)} %stack.36.s_ref, f32[512,2048]{1,0:T(8,128)} %get-tuple-element.71.local, bf16[512,512]{1,0:T(8,128)(2,1)S(1)} %get-tuple-element.51.bcc.c_rows, bf16[512,128]{1,0:T(8,128)(2,1)S(1)} %get-tuple-element.72.wc3, bf16[256,512]{1,0:T(8,128)(2,1)S(1)} %get-tuple-element.73.r0, ...), custom_call_target="tpu_custom_call" | custom-call | flops 1000000000 | bytes 4000000 | tf_op jit(solution)/shard_map/carried_other/pallas_call | solution.py:631
  89.2 1.7 %collective-permute-start.14 = (bf16[256,2048]{1,0:T(8,128)(2,1)}, bf16[256,2048]{1,0:T(8,128)(2,1)S(1)}, u32[]{:S(2)}, u32[]{:S(2)}) collective-permute-start(bf16[256,2048]{1,0:T(8,128)(2,1)} %carried_other.1), channel_id=1, source_target_pairs={{0,1},{1,0},{2,3},{3,2},{4,5},{5,4},{6,7},{7,6},{8,9},{9,8},{10,11... | collective-permute-start | bytes 3145736 | tf_op jit(solution)/shard_map/ppermute | solution.py:855
  90.9 0.0 collective-permute-done.18
  90.9 1.0 add.45
  91.9 0.1 collective-permute-start.20
  92.0 2.1 %collective-permute-start.21 = (bf16[32,512]{1,0:T(8,128)(2,1)S(1)}, bf16[32,512]{1,0:T(8,128)(2,1)S(1)}, u32[]{:S(2)}, u32[]{:S(2)}) collective-permute-start(bf16[32,512]{1,0:T(8,128)(2,1)S(1)} %get-tuple-element.97), channel_id=1, source_target_pairs={{0,4},{1,5},{2,6},{3,7},{4,0},{5,1},{6,2},{7,3},{8,12},{9,13},{10,... | collective-permute-start | bytes 98312 | tf_op jit(solution)/shard_map/ppermute | solution.py:806
  94.1 1.7 %collective-permute-start.22 = (bf16[32,512]{1,0:T(8,128)(2,1)S(1)}, bf16[32,512]{1,0:T(8,128)(2,1)S(1)}, u32[]{:S(2)}, u32[]{:S(2)}) collective-permute-start(bf16[32,512]{1,0:T(8,128)(2,1)S(1)} %get-tuple-element.96), channel_id=1, source_target_pairs={{0,6},{1,7},{2,4},{3,5},{4,2},{5,3},{6,0},{7,1},{8,14},{9,15},{10,... | collective-permute-start | bytes 98312 | tf_op jit(solution)/shard_map/ppermute | solution.py:806
  95.8 3.8 %carried_own.1.whole = bf16[256,4096]{1,0:T(8,128)(2,1)} custom-call(s32[8]{0:T(128)S(1)} %stack.36.s_ref, f32[512,2048]{1,0:T(8,128)} %get-tuple-element.71.local, bf16[512,512]{1,0:T(8,128)(2,1)S(1)} %get-tuple-element.51.bcc.c_rows, bf16[512,128]{1,0:T(8,128)(2,1)S(1)} %get-tuple-element.72.wc3, bf16[256,512]{1,0:T(8,128)(2,1)S(1)} %get-tuple-element.73.r0, ...), custom_call_target="tpu_custom_call" | custom-call | flops 1000000000 | bytes 4000000 | tf_op jit(solution)/shard_map/carried_own/pallas_call | solution.py:631
  99.7 0.0 collective-permute-done.20
  99.8 0.1 reshape.87
  99.8 0.1 select_bitcast_fusion
  99.9 0.9 collective-permute-start.23
  100.8 1.6 %put_group.1 = bf16[256,4096]{1,0:T(8,128)(2,1)} custom-call(s32[8]{0:T(128)S(1)} %stack.36.s_ref, bf16[256,2048]{1,0:T(8,128)(2,1)S(1)} %collective-permute-done.14.part, bf16[256,4096]{1,0:T(8,128)(2,1)} %carried_own.1.whole), custom_call_target="tpu_custom_call", output_to_operand_aliasing={{}: (2, {})} | custom-call | bytes 2000000 | tf_op jit(solution)/shard_map/put_group/pallas_call | solution.py:656
  102.5 0.8 maximum_select_fusion
  (39 shorter events, 0.2 us)
Async XLA Ops:
  0.6 20.9 %copy-start = (bf16[4,2,512]{2,1,0:T(2,128)(2,1)S(1)}, bf16[4,2,512]{2,1,0:T(2,128)(2,1)}, u32[]{:S(2)}) copy-start(bf16[4,2,512]{2,1,0:T(2,128)(2,1)} %param.20) | copy-start | bytes 24580
  1.4 17.4 %copy-start.1 = (s32[1,3]{1,0:T(1,128)S(1)}, s32[1,3]{1,0:T(1,128)}, u32[]{:S(2)}) copy-start(s32[1,3]{1,0:T(1,128)} %bounds.1) | copy-start | bytes 40
  1.4 20.2 %copy-start.4 = (f32[2,512]{1,0:T(2,128)S(1)}, f32[2,512]{1,0:T(2,128)}, u32[]{:S(2)}) copy-start(f32[2,512]{1,0:T(2,128)} %param.21) | copy-start | bytes 12292
  1.4 20.2 %copy-start.7 = (f32[64]{0:T(128)S(1)}, f32[64]{0:T(128)}, u32[]{:S(2)}) copy-start(f32[64]{0:T(128)} %param.23) | copy-start | bytes 772
  1.4 20.2 %copy-start.6 = (f32[64]{0:T(128)S(1)}, f32[64]{0:T(128)}, u32[]{:S(2)}) copy-start(f32[64]{0:T(128)} %param.22) | copy-start | bytes 772
  1.4 20.4 %copy-start.5 = (f32[64]{0:T(128)S(1)}, f32[64]{0:T(128)}, u32[]{:S(2)}) copy-start(f32[64]{0:T(128)} %param.24) | copy-start | bytes 772
  1.4 20.6 %copy-start.3 = (f32[4096]{0:T(1024)S(1)}, f32[4096]{0:T(1024)}, u32[]{:S(2)}) copy-start(f32[4096]{0:T(1024)} %param.19) | copy-start | bytes 49156
  1.4 21.9 %copy-start.2 = (bf16[4,4096]{1,0:T(4,128)(2,1)S(1)}, bf16[4,4096]{1,0:T(4,128)(2,1)}, u32[]{:S(2)}) copy-start(bf16[4,4096]{1,0:T(4,128)(2,1)} %wx.1) | copy-start | bytes 98308
  6.3 17.0 %collective-permute-start = (bf16[256,3072]{1,0:T(8,128)(2,1)}, bf16[256,3072]{1,0:T(8,128)(2,1)}, u32[]{:S(2)}, u32[]{:S(2)}) collective-permute-start(bf16[256,3072]{1,0:T(8,128)(2,1)} %get-tuple-element.46), channel_id=1, source_target_pairs={{0,1},{1,0},{2,3},{3,2},{4,5},{5,4},{6,7},{7,6},{8,9},{9,8},{10,11... | collective-permute-start | bytes 4718600 | tf_op jit(solution)/shard_map/ppermute | solution.py:787
  7.8 27.3 %collective-permute-start.3 = (bf16[16,3072]{1,0:T(8,128)(2,1)}, bf16[16,3072]{1,0:T(8,128)(2,1)S(1)}, u32[]{:S(2)}, u32[]{:S(2)}) collective-permute-start(bf16[16,3072]{1,0:T(8,128)(2,1)} %get-tuple-element.55), channel_id=1, source_target_pairs={{0,64},{1,65},{2,66},{3,67},{4,68},{5,69},{6,70},{7,71},{8,72},{9,... | collective-permute-start | bytes 294920 | tf_op jit(solution)/shard_map/ppermute | solution.py:799
  9.2 28.4 %collective-permute-start.5 = (bf16[16,3072]{1,0:T(8,128)(2,1)}, bf16[16,3072]{1,0:T(8,128)(2,1)S(1)}, u32[]{:S(2)}, u32[]{:S(2)}) collective-permute-start(bf16[16,3072]{1,0:T(8,128)(2,1)} %get-tuple-element.55), channel_id=1, source_target_pairs={{0,72},{1,73},{2,74},{3,75},{4,76},{5,77},{6,78},{7,79},{8,64},{9,... | collective-permute-start | bytes 294920 | tf_op jit(solution)/shard_map/ppermute | solution.py:799
  11.1 11.1 %collective-permute-start.1 = (bf16[16,3072]{1,0:T(8,128)(2,1)}, bf16[16,3072]{1,0:T(8,128)(2,1)S(1)}, u32[]{:S(2)}, u32[]{:S(2)}) collective-permute-start(bf16[16,3072]{1,0:T(8,128)(2,1)} %get-tuple-element.47), channel_id=1, source_target_pairs={{1,2},{3,4},{5,6},{7,8},{9,10},{11,12},{13,14},{17,18},{19,20},{21... | collective-permute-start | bytes 294920 | tf_op jit(solution)/shard_map/ppermute | solution.py:789
  15.1 7.1 %collective-permute-start.2 = (bf16[16,3072]{1,0:T(8,128)(2,1)}, bf16[16,3072]{1,0:T(8,128)(2,1)S(1)}, u32[]{:S(2)}, u32[]{:S(2)}) collective-permute-start(bf16[16,3072]{1,0:T(8,128)(2,1)} %get-tuple-element.48), channel_id=1, source_target_pairs={{1,3},{3,5},{5,7},{7,9},{9,11},{11,13},{13,15},{17,19},{19,21},{21... | collective-permute-start | bytes 294920 | tf_op jit(solution)/shard_map/ppermute | solution.py:790
  22.2 13.3 %collective-permute-start.4 = (bf16[16,3072]{1,0:T(8,128)(2,1)}, bf16[16,3072]{1,0:T(8,128)(2,1)S(1)}, u32[]{:S(2)}, u32[]{:S(2)}) collective-permute-start(bf16[16,3072]{1,0:T(8,128)(2,1)} %get-tuple-element.56), channel_id=1, source_target_pairs={{0,65},{1,64},{2,67},{3,66},{4,69},{5,68},{6,71},{7,70},{8,73},{9,... | collective-permute-start | bytes 294920 | tf_op jit(solution)/shard_map/ppermute | solution.py:799
  22.3 15.3 %collective-permute-start.6 = (bf16[16,3072]{1,0:T(8,128)(2,1)}, bf16[16,3072]{1,0:T(8,128)(2,1)S(1)}, u32[]{:S(2)}, u32[]{:S(2)}) collective-permute-start(bf16[16,3072]{1,0:T(8,128)(2,1)} %get-tuple-element.56), channel_id=1, source_target_pairs={{0,73},{1,72},{2,75},{3,74},{4,77},{5,76},{6,79},{7,78},{8,65},{9,... | collective-permute-start | bytes 294920 | tf_op jit(solution)/shard_map/ppermute | solution.py:799
  33.7 18.1 %collective-permute-start.7 = (bf16[272,512]{1,0:T(8,128)(2,1)S(1)}, bf16[272,512]{1,0:T(8,128)(2,1)S(1)}, u32[]{:S(2)}, u32[]{:S(2)}) collective-permute-start(bf16[272,512]{1,0:T(8,128)(2,1)S(1)} %get-tuple-element.58), channel_id=1, source_target_pairs={{0,2},{1,3},{2,0},{3,1},{4,6},{5,7},{6,4},{7,5},{8,10},{9,11},{10,... | collective-permute-start | bytes 835592 | tf_op jit(solution)/shard_map/ppermute | solution.py:806
  35.1 17.7 %collective-permute-start.8 = (bf16[272,512]{1,0:T(8,128)(2,1)S(1)}, bf16[272,512]{1,0:T(8,128)(2,1)S(1)}, u32[]{:S(2)}, u32[]{:S(2)}) collective-permute-start(bf16[272,512]{1,0:T(8,128)(2,1)S(1)} %get-tuple-element.59), channel_id=1, source_target_pairs={{0,4},{1,5},{2,6},{3,7},{4,0},{5,1},{6,2},{7,3},{8,12},{9,13},{10,... | collective-permute-start | bytes 835592 | tf_op jit(solution)/shard_map/ppermute | solution.py:806
  35.5 17.3 %collective-permute-start.9 = (bf16[272,512]{1,0:T(8,128)(2,1)S(1)}, bf16[272,512]{1,0:T(8,128)(2,1)S(1)}, u32[]{:S(2)}, u32[]{:S(2)}) collective-permute-start(bf16[272,512]{1,0:T(8,128)(2,1)S(1)} %get-tuple-element.60), channel_id=1, source_target_pairs={{0,6},{1,7},{2,4},{3,5},{4,2},{5,3},{6,0},{7,1},{8,14},{9,15},{10,... | collective-permute-start | bytes 835592 | tf_op jit(solution)/shard_map/ppermute | solution.py:806
  48.9 20.1 %collective-permute-start.15 = (bf16[448,512]{1,0:T(8,128)(2,1)S(1)}, bf16[448,512]{1,0:T(8,128)(2,1)S(1)}, u32[]{:S(2)}, u32[]{:S(2)}) collective-permute-start(bf16[448,512]{1,0:T(8,128)(2,1)S(1)} %get-tuple-element.61), channel_id=1, source_target_pairs={{0,2},{1,3},{2,0},{3,1},{4,6},{5,7},{6,4},{7,5},{8,10},{9,11},{10,... | collective-permute-start | bytes 1376264 | tf_op jit(solution)/shard_map/ppermute | solution.py:806
  49.0 21.0 %collective-permute-start.16 = (bf16[448,512]{1,0:T(8,128)(2,1)S(1)}, bf16[448,512]{1,0:T(8,128)(2,1)S(1)}, u32[]{:S(2)}, u32[]{:S(2)}) collective-permute-start(bf16[448,512]{1,0:T(8,128)(2,1)S(1)} %get-tuple-element.78), channel_id=1, source_target_pairs={{0,4},{1,5},{2,6},{3,7},{4,0},{5,1},{6,2},{7,3},{8,12},{9,13},{10,... | collective-permute-start | bytes 1376264 | tf_op jit(solution)/shard_map/ppermute | solution.py:806
  51.8 18.2 %collective-permute-start.17 = (bf16[448,512]{1,0:T(8,128)(2,1)S(1)}, bf16[448,512]{1,0:T(8,128)(2,1)S(1)}, u32[]{:S(2)}, u32[]{:S(2)}) collective-permute-start(bf16[448,512]{1,0:T(8,128)(2,1)S(1)} %get-tuple-element.79), channel_id=1, source_target_pairs={{0,6},{1,7},{2,4},{3,5},{4,2},{5,3},{6,0},{7,1},{8,14},{9,15},{10,... | collective-permute-start | bytes 1376264 | tf_op jit(solution)/shard_map/ppermute | solution.py:806
  53.7 10.0 %collective-permute-start.10 = (bf16[256,512]{1,0:T(8,128)(2,1)S(1)}, bf16[256,512]{1,0:T(8,128)(2,1)S(1)}, u32[]{:S(2)}, u32[]{:S(2)}) collective-permute-start(bf16[256,512]{1,0:T(8,128)(2,1)S(1)} %half_total.1), channel_id=1, source_target_pairs={{0,8},{1,9},{2,10},{3,11},{4,12},{5,13},{6,14},{7,15},{16,24},{17,... | collective-permute-start | bytes 786440 | tf_op jit(solution)/shard_map/ppermute | solution.py:826
  64.8 8.6 %collective-permute-start.11 = (bf16[256,512]{1,0:T(8,128)(2,1)S(1)}, bf16[256,512]{1,0:T(8,128)(2,1)S(1)}, u32[]{:S(2)}, u32[]{:S(2)}) collective-permute-start(bf16[256,512]{1,0:T(8,128)(2,1)S(1)} %get-tuple-element.74), channel_id=1, source_target_pairs={{0,2},{1,3},{2,0},{3,1},{4,6},{5,7},{6,4},{7,5},{8,10},{9,11},{10,... | collective-permute-start | bytes 786440 | tf_op jit(solution)/shard_map/ppermute | solution.py:806
  64.9 16.6 %collective-permute-start.12 = (bf16[256,512]{1,0:T(8,128)(2,1)S(1)}, bf16[256,512]{1,0:T(8,128)(2,1)S(1)}, u32[]{:S(2)}, u32[]{:S(2)}) collective-permute-start(bf16[256,512]{1,0:T(8,128)(2,1)S(1)} %get-tuple-element.75), channel_id=1, source_target_pairs={{0,4},{1,5},{2,6},{3,7},{4,0},{5,1},{6,2},{7,3},{8,12},{9,13},{10,... | collective-permute-start | bytes 786440 | tf_op jit(solution)/shard_map/ppermute | solution.py:806
  69.0 16.3 %collective-permute-start.13 = (bf16[256,512]{1,0:T(8,128)(2,1)S(1)}, bf16[256,512]{1,0:T(8,128)(2,1)S(1)}, u32[]{:S(2)}, u32[]{:S(2)}) collective-permute-start(bf16[256,512]{1,0:T(8,128)(2,1)S(1)} %get-tuple-element.76), channel_id=1, source_target_pairs={{0,6},{1,7},{2,4},{3,5},{4,2},{5,3},{6,0},{7,1},{8,14},{9,15},{10,... | collective-permute-start | bytes 786440 | tf_op jit(solution)/shard_map/ppermute | solution.py:806
  73.4 17.5 %collective-permute-start.18 = (bf16[4,32,512]{2,1,0:T(8,128)(2,1)S(1)}, bf16[4,32,512]{2,1,0:T(8,128)(2,1)}, u32[]{:S(2)}, u32[]{:S(2)}) collective-permute-start(bf16[4,32,512]{2,1,0:T(8,128)(2,1)S(1)} %get-tuple-element.82), channel_id=1, source_target_pairs={{0,64},{1,65},{2,66},{3,67},{4,68},{5,69},{6,70},{7,71},{8,72},{9,... | collective-permute-start | bytes 393224 | tf_op jit(solution)/shard_map/ppermute | solution.py:856
  77.1 13.8 %collective-permute-start.19 = (bf16[4,32,512]{2,1,0:T(8,128)(2,1)S(1)}, bf16[4,32,512]{2,1,0:T(8,128)(2,1)}, u32[]{:S(2)}, u32[]{:S(2)}) collective-permute-start(bf16[4,32,512]{2,1,0:T(8,128)(2,1)S(1)} %get-tuple-element.83), channel_id=1, source_target_pairs={{0,72},{1,73},{2,74},{3,75},{4,76},{5,77},{6,78},{7,79},{8,64},{9,... | collective-permute-start | bytes 393224 | tf_op jit(solution)/shard_map/ppermute | solution.py:857
  89.2 11.6 %collective-permute-start.14 = (bf16[256,2048]{1,0:T(8,128)(2,1)}, bf16[256,2048]{1,0:T(8,128)(2,1)S(1)}, u32[]{:S(2)}, u32[]{:S(2)}) collective-permute-start(bf16[256,2048]{1,0:T(8,128)(2,1)} %carried_other.1), channel_id=1, source_target_pairs={{0,1},{1,0},{2,3},{3,2},{4,5},{5,4},{6,7},{7,6},{8,9},{9,8},{10,11... | collective-permute-start | bytes 3145736 | tf_op jit(solution)/shard_map/ppermute | solution.py:855
  91.9 7.8 %collective-permute-start.20 = (bf16[32,512]{1,0:T(8,128)(2,1)S(1)}, bf16[32,512]{1,0:T(8,128)(2,1)S(1)}, u32[]{:S(2)}, u32[]{:S(2)}) collective-permute-start(bf16[32,512]{1,0:T(8,128)(2,1)S(1)} %get-tuple-element.98), channel_id=1, source_target_pairs={{0,2},{1,3},{2,0},{3,1},{4,6},{5,7},{6,4},{7,5},{8,10},{9,11},{10,... | collective-permute-start | bytes 98312 | tf_op jit(solution)/shard_map/ppermute | solution.py:806
  92.0 7.7 %collective-permute-start.21 = (bf16[32,512]{1,0:T(8,128)(2,1)S(1)}, bf16[32,512]{1,0:T(8,128)(2,1)S(1)}, u32[]{:S(2)}, u32[]{:S(2)}) collective-permute-start(bf16[32,512]{1,0:T(8,128)(2,1)S(1)} %get-tuple-element.97), channel_id=1, source_target_pairs={{0,4},{1,5},{2,6},{3,7},{4,0},{5,1},{6,2},{7,3},{8,12},{9,13},{10,... | collective-permute-start | bytes 98312 | tf_op jit(solution)/shard_map/ppermute | solution.py:806
  94.1 5.6 %collective-permute-start.22 = (bf16[32,512]{1,0:T(8,128)(2,1)S(1)}, bf16[32,512]{1,0:T(8,128)(2,1)S(1)}, u32[]{:S(2)}, u32[]{:S(2)}) collective-permute-start(bf16[32,512]{1,0:T(8,128)(2,1)S(1)} %get-tuple-element.96), channel_id=1, source_target_pairs={{0,6},{1,7},{2,4},{3,5},{4,2},{5,3},{6,0},{7,1},{8,14},{9,15},{10,... | collective-permute-start | bytes 98312 | tf_op jit(solution)/shard_map/ppermute | solution.py:806
  99.9 2.6 %collective-permute-start.23 = (bf16[16,2048]{1,0:T(8,128)(2,1)S(1)}, bf16[16,2048]{1,0:T(8,128)(2,1)S(1)}, u32[]{:S(2)}, u32[]{:S(2)}) collective-permute-start(bf16[16,2048]{1,0:T(8,128)(2,1)S(1)} %select_n.156), channel_id=1, source_target_pairs={{0,1},{1,0},{2,3},{3,2},{4,5},{5,4},{6,7},{7,6},{8,9},{9,8},{10,11... | collective-permute-start | bytes 196616 | tf_op jit(solution)/shard_map/ppermute | solution.py:869

commit v5 on v4

--- a/solution.py
+++ b/solution.py
@@ -17,7 +17,7 @@
 CORES = 2
 RING = 4
 LANES = 128
-DEC = STATE + 48
+DEC = STATE + 32
 MSG = DEC + 144
 SCRATCH_B = 14
 REP = 32
@@ -324,9 +324,12 @@
         @pl.when(m == base + index)
         def _():
             out[0:STATE] = jnp.zeros((STATE, CHUNK), BF16)
-            out[STATE : STATE + 16] = rows_of(split3(keep[BLOCKS + 1 : BLOCKS + 2]), 16, CHUNK).astype(BF16)
-            out[STATE + 16 : STATE + 32] = cx[...]
-            out[STATE + 32 : STATE + 48] = cg[...]
+            row = lax.broadcasted_iota(jnp.int32, (16, CHUNK), 0)
+            tile = cx[...].astype(F32)
+            for part, value in enumerate(split3(keep[BLOCKS + 1 : BLOCKS + 2])):
+                tile = jnp.where(row == 9 + part, value, tile)
+            out[STATE : STATE + 16] = tile.astype(BF16)
+            out[STATE + 16 : STATE + 32] = cg[...]
             at = pl.multiple_of(chunk * CHUNK, CHUNK)
             out[DEC : DEC + 64] = dec_rows[:, pl.ds(at, CHUNK)].astype(BF16)
             out[DEC + 64 : DEC + 128] = dec_rows[:, GROUP_CH : GROUP_CH + 512].astype(BF16)
@@ -520,12 +523,12 @@
             @pl.when((local >= 0) & (local < CHIP_TOKENS - 1))
             def _():
                 fresh = pick(fs, which, slice(0, STATE))
-                reach = decay_rows(pick(fs, which, slice(STATE, STATE + 16)))
+                reach = decay_rows(pick(fs, which, slice(STATE, STATE + 16))[9:12])
                 final[q] = fresh + reach * state
 
         state = after
-    cache_x = sum(f[STATE + 16 : STATE + 32].astype(F32) for f in fs)
-    cache_g = sum(f[STATE + 32 : STATE + 48].astype(F32) for f in fs)
+    cache_x = sum(f[STATE : STATE + 16].astype(F32) for f in fs)
+    cache_g = sum(f[STATE + 16 : STATE + 32].astype(F32) for f in fs)
     spread = spread_matrix(z)
     for index, f in enumerate(fs):
         rows_f32[index, :, 0:CHUNK] = f[DEC : DEC + 64].astype(F32)
@@ -798,12 +801,17 @@
     def hop(value, flip):
         return lax.ppermute(value, both, [(i, ((i + count) % total) ^ flip) for i in range(total)])
 
-    dec_hops = [hop(d_own, 0), hop(d_other, 1), hop(d_own, CORES * RING), hop(d_other, CORES * RING + 1)]
-
     def z_swap(value, m):
         if m == 0:
             return value
         return lax.ppermute(value, "dp", [(i, i ^ (CORES * m)) for i in range(count)])
+
+    def z_swaps(values):
+        order = (0, 2, 1, 3)
+        moved = {m: z_swap(values[m], m) for m in order}
+        return [moved[m] for m in range(RING)]
+
+    dec_hops = [hop(d_own, 0), hop(d_other, 1), hop(d_own, CORES * RING), hop(d_other, CORES * RING + 1)]
 
     w_group = lax.dynamic_slice_in_dim(conv_w_bc, core * STATE, STATE, 2).reshape(CONV, 2 * STATE)
     b_group = lax.dynamic_slice_in_dim(conv_b_bc, core * STATE, STATE, 1).reshape(1, 2 * STATE)
@@ -815,17 +823,17 @@
     b_x = conv_b_x[None]
 
     *ls, xc, bcc, dtc, wc3, cx, cg = run_a(scalars, x_rows, recv, halo, conv_w_x, b_x, g_own, w_group, b_group, vecs)
-    sent_ls = [z_swap(part, m) for m, part in enumerate(ls)]
+    sent_ls = z_swaps(ls)
     *fs, local = run_b(scalars, xc, bcc, dtc, skip, cx, cg, dec_hops, 1, 3)
     ls = after(tuple(sent_ls), fs[0])
     state_shape = jax.ShapeDtypeStruct((STATE, CHUNK), BF16)
     half_total = whole_call(kernel_total, state_shape, "half_total", 10**6)(scalars, *ls)
     own_end, local = run_b(scalars, xc, bcc, dtc, skip, cx, cg, after(tuple(dec_hops), half_total), 0, 1, in_hbm(local))
-    fs = [z_swap(part, m) for m, part in enumerate([own_end, *fs])]
+    fs = z_swaps([own_end, *fs])
     local = in_hbm(local)
     start = lax.ppermute(half_total, "dp", [(i, i + CORES * RING) for i in range(CORES * RING)])
     starts = whole_call(kernel_starts, [state_shape] * RING, "chip_starts", 10**6)(scalars, *ls, start)
-    starts = [z_swap(part, m) for m, part in enumerate(starts)]
+    starts = z_swaps(starts)
 
     def own_columns(value):
         return lax.dynamic_slice_in_dim(value, core * GROUP_CH + z * CHUNK, CHUNK, 1)

time: 104 us -> 103 us (level)
  waiting for transfers between devices: 5.84 us -> 4.12 us
    ppermute x1, starting transfers between devices: 3.63 us -> 5.71 us  [on_device(): lax.ppermute(sent, both, [(i, (i + count) % total ^ CORES * RING) for i i...]
    ppermute x1, starting transfers between devices: 3.68 us -> 1.7 us  [on_device(): lax.ppermute(kept, both, [(i, (i + count) % total) for i in range(total)])]
    ppermute x12, waiting for transfers between devices: 5.81 us -> 4.09 us  [z_swap(): return lax.ppermute(value, 'dp', [(i, i ^ CORES * m) for i in range(count)])]
  transfers between devices with their start and end apart: 24 -> 24, of which waited for: 4 -> 2; matrix products, arithmetic and copies ran while one was open for 2% -> 2% of each run, Pallas kernels for 40% -> 41%
where the time goes in v5:
time: 103 us; the launch traced here: 102 us
  Pallas kernels  46.5 us (45%)
  starting transfers between devices  43.9 us (43%)
  waiting for transfers between devices  4.12 us (4%)
  between operations  3.14 us (3%)
  other arithmetic  2.63 us (3%)
  local copies, waits for them, and re-layouts  1.36 us (1%)
    pallas_call x2, Pallas kernels, run_b(): pl.pallas_call(functools.partial(kernel_b, base, count), grid_spec=pltpu....  16.7 us
    ppermute x12, starting transfers between devices, z_swap(): return lax.ppermute(value, 'dp', [(i, i ^ CORES * m) for i in range(count)])  15.7 us
    pallas_call x1, Pallas kernels, run_a(): pl.pallas_call(kernel_a, grid_spec=pltpu.PrefetchScalarGridSpec(num_scala...  10.3 us
    pallas_call x2, Pallas kernels, run_d(): pl.pallas_call(kernel_d, grid_spec=pltpu.PrefetchScalarGridSpec(num_scala...  7.72 us
    ppermute x1, starting transfers between devices, on_device(): lax.ppermute(sent, both, [(i, (i + count) % total ^ CORES * RING) for i i...  5.71 us
    pallas_call x1, Pallas kernels, run_pack(): pl.pallas_call(kernel_pack, grid_spec=pltpu.PrefetchScalarGridSpec(num_sc...  4.84 us
    ppermute x1, starting transfers between devices, on_device(): lax.ppermute(half_total, 'dp', [(i, i + CORES * RING) for i in range(CORE...  4.45 us
    ppermute x4, starting transfers between devices, hop(): lax.ppermute(value, both, [(i, (i + count) % total ^ flip) for i in range...  4.34 us
  transfers between devices with their start and end apart: 24, of which 2 were waited for; matrix products, arithmetic and copies ran while one was open for 2% of the time, Pallas kernels for 41%

profile of v5, /device:TPU:1, one launch (start us, length us, event | category | flops | bytes accessed | tf_op | source)
XLA Modules:
  0.0 101.7 jit_solution(17115607296424603922)
XLA Ops:
  0.6 0.0 copy-start
  0.7 0.7 pad_add_fusion.s_ref
  1.4 0.0 copy-start.5
  1.4 0.0 copy-start.2
  1.4 0.0 copy-start.3
  1.4 4.8 %pack.1 = (bf16[256,3072]{1,0:T(8,128)(2,1)}, bf16[16,3072]{1,0:T(8,128)(2,1)}, bf16[16,3072]{1,0:T(8,128)(2,1)}, bf16[256,1024]{1,0:T(8,128)(2,1)}, bf16[16,3072]{1,0:T(8,128)(2,1)}, /*index=5*/bf16[16,3072]{1,0:T(8,128)(2,1)}) custom-call(s32[5]{0:T(128)S(1)} %pad_add_fusion.s_ref, bf16[256,4096]{1,0:T(8,128)(2,1)} %bitcast.60, ...), custom_call_target="tpu_custom_call" | custom-call | flops 1000000 | bytes 4000000 | tf_op jit(solution)/shard_map/pack/pallas_call | solution.py:738
  6.3 1.5 %collective-permute-start = (bf16[256,3072]{1,0:T(8,128)(2,1)}, bf16[256,3072]{1,0:T(8,128)(2,1)}, u32[]{:S(2)}, u32[]{:S(2)}) collective-permute-start(bf16[256,3072]{1,0:T(8,128)(2,1)} %get-tuple-element.46), channel_id=1, source_target_pairs={{0,1},{1,0},{2,3},{3,2},{4,5},{5,4},{6,7},{7,6},{8,9},{9,8},{10,11... | collective-permute-start | bytes 4718600 | tf_op jit(solution)/shard_map/ppermute | solution.py:790
  7.8 1.4 %collective-permute-start.3 = (bf16[16,3072]{1,0:T(8,128)(2,1)}, bf16[16,3072]{1,0:T(8,128)(2,1)S(1)}, u32[]{:S(2)}, u32[]{:S(2)}) collective-permute-start(bf16[16,3072]{1,0:T(8,128)(2,1)} %get-tuple-element.55), channel_id=1, source_target_pairs={{0,64},{1,65},{2,66},{3,67},{4,68},{5,69},{6,70},{7,71},{8,72},{9,... | collective-permute-start | bytes 294920 | tf_op jit(solution)/shard_map/ppermute | solution.py:802
  9.2 1.9 %collective-permute-start.5 = (bf16[16,3072]{1,0:T(8,128)(2,1)}, bf16[16,3072]{1,0:T(8,128)(2,1)S(1)}, u32[]{:S(2)}, u32[]{:S(2)}) collective-permute-start(bf16[16,3072]{1,0:T(8,128)(2,1)} %get-tuple-element.55), channel_id=1, source_target_pairs={{0,72},{1,73},{2,74},{3,75},{4,76},{5,77},{6,78},{7,79},{8,64},{9,... | collective-permute-start | bytes 294920 | tf_op jit(solution)/shard_map/ppermute | solution.py:802
  11.1 4.1 %collective-permute-start.1 = (bf16[16,3072]{1,0:T(8,128)(2,1)}, bf16[16,3072]{1,0:T(8,128)(2,1)S(1)}, u32[]{:S(2)}, u32[]{:S(2)}) collective-permute-start(bf16[16,3072]{1,0:T(8,128)(2,1)} %get-tuple-element.47), channel_id=1, source_target_pairs={{1,2},{3,4},{5,6},{7,8},{9,10},{11,12},{13,14},{17,18},{19,20},{21... | collective-permute-start | bytes 294920 | tf_op jit(solution)/shard_map/ppermute | solution.py:792
  15.1 3.5 %collective-permute-start.2 = (bf16[16,3072]{1,0:T(8,128)(2,1)}, bf16[16,3072]{1,0:T(8,128)(2,1)S(1)}, u32[]{:S(2)}, u32[]{:S(2)}) collective-permute-start(bf16[16,3072]{1,0:T(8,128)(2,1)} %get-tuple-element.48), channel_id=1, source_target_pairs={{1,3},{3,5},{5,7},{7,9},{9,11},{11,13},{13,15},{17,19},{19,21},{21... | collective-permute-start | bytes 294920 | tf_op jit(solution)/shard_map/ppermute | solution.py:793
  18.8 0.7 fusion
  21.6 0.1 constant_dynamic-slice_fusion.2
  21.7 0.1 tile.10
  21.8 0.1 broadcast_in_dim.11
  21.9 0.1 broadcast_in_dim_reshape.3.skip
  22.0 0.1 stack.36.s_ref
  22.1 0.0 collective-permute-done.1
  22.1 0.1 collective-permute-start.4
  22.2 0.0 collective-permute-done.2
  22.2 1.0 collective-permute-start.6
  23.3 10.3 %conv_and_states.1 = (bf16[272,512]{1,0:T(8,128)(2,1)S(1)}, bf16[272,512]{1,0:T(8,128)(2,1)S(1)}, bf16[272,512]{1,0:T(8,128)(2,1)S(1)}, bf16[272,512]{1,0:T(8,12...) custom-call(s32[8]{0:T(128)S(1)} %stack.36.s_ref, ...), custom_call_target="tpu_custom_call" | custom-call | flops 6000000000 | bytes 8000000 | tf_op jit(solution)/shard_map/conv_and_states/pallas_call | solution.py:216
  33.6 1.4 %collective-permute-start.7 = (bf16[272,512]{1,0:T(8,128)(2,1)S(1)}, bf16[272,512]{1,0:T(8,128)(2,1)S(1)}, u32[]{:S(2)}, u32[]{:S(2)}) collective-permute-start(bf16[272,512]{1,0:T(8,128)(2,1)S(1)} %get-tuple-element.58), channel_id=1, source_target_pairs={{0,2},{1,3},{2,0},{3,1},{4,6},{5,7},{6,4},{7,5},{8,10},{9,11},{10,... | collective-permute-start | bytes 835592 | tf_op jit(solution)/shard_map/ppermute | solution.py:807
  35.0 0.0 collective-permute-done.3.near_same
  35.0 0.5 collective-permute-start.8
  35.5 0.0 collective-permute-done.4.near_cross
  35.5 2.0 %collective-permute-start.9 = (bf16[272,512]{1,0:T(8,128)(2,1)S(1)}, bf16[272,512]{1,0:T(8,128)(2,1)S(1)}, u32[]{:S(2)}, u32[]{:S(2)}) collective-permute-start(bf16[272,512]{1,0:T(8,128)(2,1)S(1)} %get-tuple-element.60), channel_id=1, source_target_pairs={{0,6},{1,7},{2,4},{3,5},{4,2},{5,3},{6,0},{7,1},{8,14},{9,15},{10,... | collective-permute-start | bytes 835592 | tf_op jit(solution)/shard_map/ppermute | solution.py:807
  37.5 0.0 collective-permute-done.5.far_same
  37.5 0.0 collective-permute-done.6.far_cross
  37.5 11.2 %output_within_chip_1.1 = (bf16[432,512]{1,0:T(8,128)(2,1)S(1)}, bf16[432,512]{1,0:T(8,128)(2,1)S(1)}, bf16[432,512]{1,0:T(8,128)(2,1)S(1)}, f32[512,2048]{1,0:T(8,128)}) custom-call(s32[8]{0:T(128)S(1)} %stack.36.s_ref, bf16[512,2048]{1,0:T(8,128)(2,1)S(1)} %get-tuple-element.50.xc_ref, bf16[512,512]{1,0:T(8,128)(2,1)S(1)} %get-tuple-element.51.bcc.c_rows, ...), custom_call_target="tpu_custom_call" | custom-call | flops 8999999488 | bytes 6000000 | tf_op jit(solution)/shard_map/output_within_chip_1/pallas_call | solution.py:426
  48.8 0.1 collective-permute-start.15
  48.8 1.7 %collective-permute-start.16 = (bf16[432,512]{1,0:T(8,128)(2,1)S(1)}, bf16[432,512]{1,0:T(8,128)(2,1)S(1)}, u32[]{:S(2)}, u32[]{:S(2)}) collective-permute-start(bf16[432,512]{1,0:T(8,128)(2,1)S(1)} %get-tuple-element.78), channel_id=1, source_target_pairs={{0,4},{1,5},{2,6},{3,7},{4,0},{5,1},{6,2},{7,3},{8,12},{9,13},{10,... | collective-permute-start | bytes 1327112 | tf_op jit(solution)/shard_map/ppermute | solution.py:807
  50.5 2.1 %collective-permute-start.17 = (bf16[432,512]{1,0:T(8,128)(2,1)S(1)}, bf16[432,512]{1,0:T(8,128)(2,1)S(1)}, u32[]{:S(2)}, u32[]{:S(2)}) collective-permute-start(bf16[432,512]{1,0:T(8,128)(2,1)S(1)} %get-tuple-element.79), channel_id=1, source_target_pairs={{0,6},{1,7},{2,4},{3,5},{4,2},{5,3},{6,0},{7,1},{8,14},{9,15},{10,... | collective-permute-start | bytes 1327112 | tf_op jit(solution)/shard_map/ppermute | solution.py:807
  52.6 0.1 dynamic-slice.3
  52.7 0.0 collective-permute-done.8.l2
  52.7 0.9 half_total.1
  53.6 4.4 %collective-permute-start.10 = (bf16[256,512]{1,0:T(8,128)(2,1)S(1)}, bf16[256,512]{1,0:T(8,128)(2,1)S(1)}, u32[]{:S(2)}, u32[]{:S(2)}) collective-permute-start(bf16[256,512]{1,0:T(8,128)(2,1)S(1)} %half_total.1), channel_id=1, source_target_pairs={{0,8},{1,9},{2,10},{3,11},{4,12},{5,13},{6,14},{7,15},{16,24},{17,... | collective-permute-start | bytes 786440 | tf_op jit(solution)/shard_map/ppermute | solution.py:834
  58.0 5.5 %output_within_chip_0.1 = (bf16[432,512]{1,0:T(8,128)(2,1)S(1)}, f32[512,2048]{1,0:T(8,128)}) custom-call(s32[8]{0:T(128)S(1)} %stack.36.s_ref, bf16[512,2048]{1,0:T(8,128)(2,1)S(1)} %get-tuple-element.50.xc_ref, bf16[512,512]{1,0:T(8,128)(2,1)S(1)} %get-tuple-element.51.bcc.c_rows, ...), custom_call_target="tpu_custom_call", output_to_operand_aliasing={{1}: (11, {})} | custom-call | flops 3000000000 | bytes 2000000 | tf_op jit(solution)/shard_map/output_within_chip_0/pallas_call | solution.py:426
  63.6 1.2 %chip_starts.1 = (bf16[256,512]{1,0:T(8,128)(2,1)S(1)}, bf16[256,512]{1,0:T(8,128)(2,1)S(1)}, bf16[256,512]{1,0:T(8,128)(2,1)S(1)}, bf16[256,512]{1,0:T(8,128)(2,1)S(1)}) custom-call(s32[8]{0:T(128)S(1)} %stack.36.s_ref, bf16[272,512]{1,0:T(8,128)(2,1)S(1)} %get-tuple-element.62.l0, bf16[272,512]{1,0:T(8,128)(2,1)S(1)} %collective-permute-done.7.l1, ...), custom_call_target="tpu_custom_call" | custom-call | flops 1000000 | bytes 3000000 | tf_op jit(solution)/shard_map/chip_starts/pallas_call | solution.py:484
  64.8 0.1 collective-permute-start.11
  64.9 2.4 %collective-permute-start.12 = (bf16[256,512]{1,0:T(8,128)(2,1)S(1)}, bf16[256,512]{1,0:T(8,128)(2,1)S(1)}, u32[]{:S(2)}, u32[]{:S(2)}) collective-permute-start(bf16[256,512]{1,0:T(8,128)(2,1)S(1)} %get-tuple-element.75), channel_id=1, source_target_pairs={{0,4},{1,5},{2,6},{3,7},{4,0},{5,1},{6,2},{7,3},{8,12},{9,13},{10,... | collective-permute-start | bytes 786440 | tf_op jit(solution)/shard_map/ppermute | solution.py:807
  67.3 0.0 collective-permute-done.15.f1
  67.3 1.4 %collective-permute-start.13 = (bf16[256,512]{1,0:T(8,128)(2,1)S(1)}, bf16[256,512]{1,0:T(8,128)(2,1)S(1)}, u32[]{:S(2)}, u32[]{:S(2)}) collective-permute-start(bf16[256,512]{1,0:T(8,128)(2,1)S(1)} %get-tuple-element.76), channel_id=1, source_target_pairs={{0,6},{1,7},{2,4},{3,5},{4,2},{5,3},{6,0},{7,1},{8,14},{9,15},{10,... | collective-permute-start | bytes 786440 | tf_op jit(solution)/shard_map/ppermute | solution.py:807
  68.7 0.0 collective-permute-done.16.f2
  68.7 0.0 collective-permute-done.17.f3
  68.7 3.2 %decode_rows.1 = (bf16[4,32,512]{2,1,0:T(8,128)(2,1)S(1)}, bf16[4,32,512]{2,1,0:T(8,128)(2,1)S(1)}) custom-call(s32[8]{0:T(128)S(1)} %stack.36.s_ref, bf16[272,512]{1,0:T(8,128)(2,1)S(1)} %get-tuple-element.62.l0, bf16[272,512]{1,0:T(8,128)(2,1)S(1)} %collective-permute-done.7.l1, bf16[272,512]{1,0:T(8,128)(2,1)S(1)} %collective-permute-done.8.l2, ...), custom_call_target="tpu_custom_call" | custom-call | flops 20000000000 | bytes 6000000 | tf_op jit(solution)/shard_map/decode_rows/pallas_call | solution.py:844
  71.9 1.3 %collective-permute-done.11.r1 = bf16[256,512]{1,0:T(8,128)(2,1)S(1)} collective-permute-done((bf16[256,512]{1,0:T(8,128)(2,1)S(1)}, bf16[256,512]{1,0:T(8,128)(2,1)S(1)}, u32[]{:S(2)}, u32[]{:S(2)}) %collective-permute-start.11) | collective-permute-done | bytes 262176 | tf_op jit(solution)/shard_map/ppermute | solution.py:807
  73.2 1.7 %collective-permute-start.18 = (bf16[4,32,512]{2,1,0:T(8,128)(2,1)S(1)}, bf16[4,32,512]{2,1,0:T(8,128)(2,1)}, u32[]{:S(2)}, u32[]{:S(2)}) collective-permute-start(bf16[4,32,512]{2,1,0:T(8,128)(2,1)S(1)} %get-tuple-element.82), channel_id=1, source_target_pairs={{0,64},{1,65},{2,66},{3,67},{4,68},{5,69},{6,70},{7,71},{8,72},{9,... | collective-permute-start | bytes 393224 | tf_op jit(solution)/shard_map/ppermute | solution.py:864
  74.9 5.7 %collective-permute-start.19 = (bf16[4,32,512]{2,1,0:T(8,128)(2,1)S(1)}, bf16[4,32,512]{2,1,0:T(8,128)(2,1)}, u32[]{:S(2)}, u32[]{:S(2)}) collective-permute-start(bf16[4,32,512]{2,1,0:T(8,128)(2,1)S(1)} %get-tuple-element.83), channel_id=1, source_target_pairs={{0,72},{1,73},{2,74},{3,75},{4,76},{5,77},{6,78},{7,79},{8,64},{9,... | collective-permute-start | bytes 393224 | tf_op jit(solution)/shard_map/ppermute | solution.py:865
  80.6 2.8 %collective-permute-done.13.r3 = bf16[256,512]{1,0:T(8,128)(2,1)S(1)} collective-permute-done((bf16[256,512]{1,0:T(8,128)(2,1)S(1)}, bf16[256,512]{1,0:T(8,128)(2,1)S(1)}, u32[]{:S(2)}, u32[]{:S(2)}) %collective-permute-start.13) | collective-permute-done | bytes 262176 | tf_op jit(solution)/shard_map/ppermute | solution.py:807
  83.4 3.9 %carried_other.1 = bf16[256,2048]{1,0:T(8,128)(2,1)} custom-call(s32[8]{0:T(128)S(1)} %stack.36.s_ref, f32[512,2048]{1,0:T(8,128)} %get-tuple-element.71.local, bf16[512,512]{1,0:T(8,128)(2,1)S(1)} %get-tuple-element.51.bcc.c_rows, bf16[512,128]{1,0:T(8,128)(2,1)S(1)} %get-tuple-element.72.wc3, bf16[256,512]{1,0:T(8,128)(2,1)S(1)} %get-tuple-element.73.r0, ...), custom_call_target="tpu_custom_call" | custom-call | flops 1000000000 | bytes 4000000 | tf_op jit(solution)/shard_map/carried_other/pallas_call | solution.py:634
  87.3 1.7 %collective-permute-start.14 = (bf16[256,2048]{1,0:T(8,128)(2,1)}, bf16[256,2048]{1,0:T(8,128)(2,1)S(1)}, u32[]{:S(2)}, u32[]{:S(2)}) collective-permute-start(bf16[256,2048]{1,0:T(8,128)(2,1)} %carried_other.1), channel_id=1, source_target_pairs={{0,1},{1,0},{2,3},{3,2},{4,5},{5,4},{6,7},{7,6},{8,9},{9,8},{10,11... | collective-permute-start | bytes 3145736 | tf_op jit(solution)/shard_map/ppermute | solution.py:863
  88.9 1.0 add.45
  90.0 0.1 collective-permute-start.20
  90.1 3.2 %collective-permute-start.21 = (bf16[32,512]{1,0:T(8,128)(2,1)S(1)}, bf16[32,512]{1,0:T(8,128)(2,1)S(1)}, u32[]{:S(2)}, u32[]{:S(2)}) collective-permute-start(bf16[32,512]{1,0:T(8,128)(2,1)S(1)} %get-tuple-element.97), channel_id=1, source_target_pairs={{0,4},{1,5},{2,6},{3,7},{4,0},{5,1},{6,2},{7,3},{8,12},{9,13},{10,... | collective-permute-start | bytes 98312 | tf_op jit(solution)/shard_map/ppermute | solution.py:807
  93.3 0.6 collective-permute-start.22
  93.9 3.8 %carried_own.1.whole = bf16[256,4096]{1,0:T(8,128)(2,1)} custom-call(s32[8]{0:T(128)S(1)} %stack.36.s_ref, f32[512,2048]{1,0:T(8,128)} %get-tuple-element.71.local, bf16[512,512]{1,0:T(8,128)(2,1)S(1)} %get-tuple-element.51.bcc.c_rows, bf16[512,128]{1,0:T(8,128)(2,1)S(1)} %get-tuple-element.72.wc3, bf16[256,512]{1,0:T(8,128)(2,1)S(1)} %get-tuple-element.73.r0, ...), custom_call_target="tpu_custom_call" | custom-call | flops 1000000000 | bytes 4000000 | tf_op jit(solution)/shard_map/carried_own/pallas_call | solution.py:634
  97.8 0.0 collective-permute-done.20
  97.8 0.1 reshape.87
  97.9 0.1 select_bitcast_fusion
  98.0 1.3 %collective-permute-start.23 = (bf16[16,2048]{1,0:T(8,128)(2,1)S(1)}, bf16[16,2048]{1,0:T(8,128)(2,1)S(1)}, u32[]{:S(2)}, u32[]{:S(2)}) collective-permute-start(bf16[16,2048]{1,0:T(8,128)(2,1)S(1)} %select_n.156), channel_id=1, source_target_pairs={{0,1},{1,0},{2,3},{3,2},{4,5},{5,4},{6,7},{7,6},{8,9},{9,8},{10,11... | collective-permute-start | bytes 196616 | tf_op jit(solution)/shard_map/ppermute | solution.py:877
  99.3 0.0 collective-permute-done.14.part
  99.3 1.6 %put_group.1 = bf16[256,4096]{1,0:T(8,128)(2,1)} custom-call(s32[8]{0:T(128)S(1)} %stack.36.s_ref, bf16[256,2048]{1,0:T(8,128)(2,1)S(1)} %collective-permute-done.14.part, bf16[256,4096]{1,0:T(8,128)(2,1)} %carried_own.1.whole), custom_call_target="tpu_custom_call", output_to_operand_aliasing={{}: (2, {})} | custom-call | bytes 2000000 | tf_op jit(solution)/shard_map/put_group/pallas_call | solution.py:659
  100.9 0.8 maximum_select_fusion
  (39 shorter events, 0.2 us)
Async XLA Ops:
  0.6 20.9 %copy-start = (bf16[4,2,512]{2,1,0:T(2,128)(2,1)S(1)}, bf16[4,2,512]{2,1,0:T(2,128)(2,1)}, u32[]{:S(2)}) copy-start(bf16[4,2,512]{2,1,0:T(2,128)(2,1)} %param.20) | copy-start | bytes 24580
  1.4 17.4 %copy-start.1 = (s32[1,3]{1,0:T(1,128)S(1)}, s32[1,3]{1,0:T(1,128)}, u32[]{:S(2)}) copy-start(s32[1,3]{1,0:T(1,128)} %bounds.1) | copy-start | bytes 40
  1.4 20.2 %copy-start.4 = (f32[2,512]{1,0:T(2,128)S(1)}, f32[2,512]{1,0:T(2,128)}, u32[]{:S(2)}) copy-start(f32[2,512]{1,0:T(2,128)} %param.21) | copy-start | bytes 12292
  1.4 20.2 %copy-start.7 = (f32[64]{0:T(128)S(1)}, f32[64]{0:T(128)}, u32[]{:S(2)}) copy-start(f32[64]{0:T(128)} %param.23) | copy-start | bytes 772
  1.4 20.2 %copy-start.6 = (f32[64]{0:T(128)S(1)}, f32[64]{0:T(128)}, u32[]{:S(2)}) copy-start(f32[64]{0:T(128)} %param.22) | copy-start | bytes 772
  1.4 20.4 %copy-start.5 = (f32[64]{0:T(128)S(1)}, f32[64]{0:T(128)}, u32[]{:S(2)}) copy-start(f32[64]{0:T(128)} %param.24) | copy-start | bytes 772
  1.4 21.8 %copy-start.2 = (bf16[4,4096]{1,0:T(4,128)(2,1)S(1)}, bf16[4,4096]{1,0:T(4,128)(2,1)}, u32[]{:S(2)}) copy-start(bf16[4,4096]{1,0:T(4,128)(2,1)} %wx.1) | copy-start | bytes 98308
  1.4 21.8 %copy-start.3 = (f32[4096]{0:T(1024)S(1)}, f32[4096]{0:T(1024)}, u32[]{:S(2)}) copy-start(f32[4096]{0:T(1024)} %param.19) | copy-start | bytes 49156
  6.3 16.9 %collective-permute-start = (bf16[256,3072]{1,0:T(8,128)(2,1)}, bf16[256,3072]{1,0:T(8,128)(2,1)}, u32[]{:S(2)}, u32[]{:S(2)}) collective-permute-start(bf16[256,3072]{1,0:T(8,128)(2,1)} %get-tuple-element.46), channel_id=1, source_target_pairs={{0,1},{1,0},{2,3},{3,2},{4,5},{5,4},{6,7},{7,6},{8,9},{9,8},{10,11... | collective-permute-start | bytes 4718600 | tf_op jit(solution)/shard_map/ppermute | solution.py:790
  7.8 27.2 %collective-permute-start.3 = (bf16[16,3072]{1,0:T(8,128)(2,1)}, bf16[16,3072]{1,0:T(8,128)(2,1)S(1)}, u32[]{:S(2)}, u32[]{:S(2)}) collective-permute-start(bf16[16,3072]{1,0:T(8,128)(2,1)} %get-tuple-element.55), channel_id=1, source_target_pairs={{0,64},{1,65},{2,66},{3,67},{4,68},{5,69},{6,70},{7,71},{8,72},{9,... | collective-permute-start | bytes 294920 | tf_op jit(solution)/shard_map/ppermute | solution.py:802
  9.2 28.3 %collective-permute-start.5 = (bf16[16,3072]{1,0:T(8,128)(2,1)}, bf16[16,3072]{1,0:T(8,128)(2,1)S(1)}, u32[]{:S(2)}, u32[]{:S(2)}) collective-permute-start(bf16[16,3072]{1,0:T(8,128)(2,1)} %get-tuple-element.55), channel_id=1, source_target_pairs={{0,72},{1,73},{2,74},{3,75},{4,76},{5,77},{6,78},{7,79},{8,64},{9,... | collective-permute-start | bytes 294920 | tf_op jit(solution)/shard_map/ppermute | solution.py:802
  11.1 11.0 %collective-permute-start.1 = (bf16[16,3072]{1,0:T(8,128)(2,1)}, bf16[16,3072]{1,0:T(8,128)(2,1)S(1)}, u32[]{:S(2)}, u32[]{:S(2)}) collective-permute-start(bf16[16,3072]{1,0:T(8,128)(2,1)} %get-tuple-element.47), channel_id=1, source_target_pairs={{1,2},{3,4},{5,6},{7,8},{9,10},{11,12},{13,14},{17,18},{19,20},{21... | collective-permute-start | bytes 294920 | tf_op jit(solution)/shard_map/ppermute | solution.py:792
  15.1 7.1 %collective-permute-start.2 = (bf16[16,3072]{1,0:T(8,128)(2,1)}, bf16[16,3072]{1,0:T(8,128)(2,1)S(1)}, u32[]{:S(2)}, u32[]{:S(2)}) collective-permute-start(bf16[16,3072]{1,0:T(8,128)(2,1)} %get-tuple-element.48), channel_id=1, source_target_pairs={{1,3},{3,5},{5,7},{7,9},{9,11},{11,13},{13,15},{17,19},{19,21},{21... | collective-permute-start | bytes 294920 | tf_op jit(solution)/shard_map/ppermute | solution.py:793
  22.1 13.4 %collective-permute-start.4 = (bf16[16,3072]{1,0:T(8,128)(2,1)}, bf16[16,3072]{1,0:T(8,128)(2,1)S(1)}, u32[]{:S(2)}, u32[]{:S(2)}) collective-permute-start(bf16[16,3072]{1,0:T(8,128)(2,1)} %get-tuple-element.56), channel_id=1, source_target_pairs={{0,65},{1,64},{2,67},{3,66},{4,69},{5,68},{6,71},{7,70},{8,73},{9,... | collective-permute-start | bytes 294920 | tf_op jit(solution)/shard_map/ppermute | solution.py:802
  22.2 15.3 %collective-permute-start.6 = (bf16[16,3072]{1,0:T(8,128)(2,1)}, bf16[16,3072]{1,0:T(8,128)(2,1)S(1)}, u32[]{:S(2)}, u32[]{:S(2)}) collective-permute-start(bf16[16,3072]{1,0:T(8,128)(2,1)} %get-tuple-element.56), channel_id=1, source_target_pairs={{0,73},{1,72},{2,75},{3,74},{4,77},{5,76},{6,79},{7,78},{8,65},{9,... | collective-permute-start | bytes 294920 | tf_op jit(solution)/shard_map/ppermute | solution.py:802
  33.6 17.0 %collective-permute-start.7 = (bf16[272,512]{1,0:T(8,128)(2,1)S(1)}, bf16[272,512]{1,0:T(8,128)(2,1)S(1)}, u32[]{:S(2)}, u32[]{:S(2)}) collective-permute-start(bf16[272,512]{1,0:T(8,128)(2,1)S(1)} %get-tuple-element.58), channel_id=1, source_target_pairs={{0,2},{1,3},{2,0},{3,1},{4,6},{5,7},{6,4},{7,5},{8,10},{9,11},{10,... | collective-permute-start | bytes 835592 | tf_op jit(solution)/shard_map/ppermute | solution.py:807
  35.0 17.7 %collective-permute-start.8 = (bf16[272,512]{1,0:T(8,128)(2,1)S(1)}, bf16[272,512]{1,0:T(8,128)(2,1)S(1)}, u32[]{:S(2)}, u32[]{:S(2)}) collective-permute-start(bf16[272,512]{1,0:T(8,128)(2,1)S(1)} %get-tuple-element.59), channel_id=1, source_target_pairs={{0,4},{1,5},{2,6},{3,7},{4,0},{5,1},{6,2},{7,3},{8,12},{9,13},{10,... | collective-permute-start | bytes 835592 | tf_op jit(solution)/shard_map/ppermute | solution.py:807
  35.5 17.2 %collective-permute-start.9 = (bf16[272,512]{1,0:T(8,128)(2,1)S(1)}, bf16[272,512]{1,0:T(8,128)(2,1)S(1)}, u32[]{:S(2)}, u32[]{:S(2)}) collective-permute-start(bf16[272,512]{1,0:T(8,128)(2,1)S(1)} %get-tuple-element.60), channel_id=1, source_target_pairs={{0,6},{1,7},{2,4},{3,5},{4,2},{5,3},{6,0},{7,1},{8,14},{9,15},{10,... | collective-permute-start | bytes 835592 | tf_op jit(solution)/shard_map/ppermute | solution.py:807
  48.8 18.5 %collective-permute-start.15 = (bf16[432,512]{1,0:T(8,128)(2,1)S(1)}, bf16[432,512]{1,0:T(8,128)(2,1)S(1)}, u32[]{:S(2)}, u32[]{:S(2)}) collective-permute-start(bf16[432,512]{1,0:T(8,128)(2,1)S(1)} %get-tuple-element.61), channel_id=1, source_target_pairs={{0,2},{1,3},{2,0},{3,1},{4,6},{5,7},{6,4},{7,5},{8,10},{9,11},{10,... | collective-permute-start | bytes 1327112 | tf_op jit(solution)/shard_map/ppermute | solution.py:807
  48.8 19.9 %collective-permute-start.16 = (bf16[432,512]{1,0:T(8,128)(2,1)S(1)}, bf16[432,512]{1,0:T(8,128)(2,1)S(1)}, u32[]{:S(2)}, u32[]{:S(2)}) collective-permute-start(bf16[432,512]{1,0:T(8,128)(2,1)S(1)} %get-tuple-element.78), channel_id=1, source_target_pairs={{0,4},{1,5},{2,6},{3,7},{4,0},{5,1},{6,2},{7,3},{8,12},{9,13},{10,... | collective-permute-start | bytes 1327112 | tf_op jit(solution)/shard_map/ppermute | solution.py:807
  50.5 18.2 %collective-permute-start.17 = (bf16[432,512]{1,0:T(8,128)(2,1)S(1)}, bf16[432,512]{1,0:T(8,128)(2,1)S(1)}, u32[]{:S(2)}, u32[]{:S(2)}) collective-permute-start(bf16[432,512]{1,0:T(8,128)(2,1)S(1)} %get-tuple-element.79), channel_id=1, source_target_pairs={{0,6},{1,7},{2,4},{3,5},{4,2},{5,3},{6,0},{7,1},{8,14},{9,15},{10,... | collective-permute-start | bytes 1327112 | tf_op jit(solution)/shard_map/ppermute | solution.py:807
  53.6 10.0 %collective-permute-start.10 = (bf16[256,512]{1,0:T(8,128)(2,1)S(1)}, bf16[256,512]{1,0:T(8,128)(2,1)S(1)}, u32[]{:S(2)}, u32[]{:S(2)}) collective-permute-start(bf16[256,512]{1,0:T(8,128)(2,1)S(1)} %half_total.1), channel_id=1, source_target_pairs={{0,8},{1,9},{2,10},{3,11},{4,12},{5,13},{6,14},{7,15},{16,24},{17,... | collective-permute-start | bytes 786440 | tf_op jit(solution)/shard_map/ppermute | solution.py:834
  64.8 8.5 %collective-permute-start.11 = (bf16[256,512]{1,0:T(8,128)(2,1)S(1)}, bf16[256,512]{1,0:T(8,128)(2,1)S(1)}, u32[]{:S(2)}, u32[]{:S(2)}) collective-permute-start(bf16[256,512]{1,0:T(8,128)(2,1)S(1)} %get-tuple-element.74), channel_id=1, source_target_pairs={{0,2},{1,3},{2,0},{3,1},{4,6},{5,7},{6,4},{7,5},{8,10},{9,11},{10,... | collective-permute-start | bytes 786440 | tf_op jit(solution)/shard_map/ppermute | solution.py:807
  64.9 15.8 %collective-permute-start.12 = (bf16[256,512]{1,0:T(8,128)(2,1)S(1)}, bf16[256,512]{1,0:T(8,128)(2,1)S(1)}, u32[]{:S(2)}, u32[]{:S(2)}) collective-permute-start(bf16[256,512]{1,0:T(8,128)(2,1)S(1)} %get-tuple-element.75), channel_id=1, source_target_pairs={{0,4},{1,5},{2,6},{3,7},{4,0},{5,1},{6,2},{7,3},{8,12},{9,13},{10,... | collective-permute-start | bytes 786440 | tf_op jit(solution)/shard_map/ppermute | solution.py:807
  67.3 16.1 %collective-permute-start.13 = (bf16[256,512]{1,0:T(8,128)(2,1)S(1)}, bf16[256,512]{1,0:T(8,128)(2,1)S(1)}, u32[]{:S(2)}, u32[]{:S(2)}) collective-permute-start(bf16[256,512]{1,0:T(8,128)(2,1)S(1)} %get-tuple-element.76), channel_id=1, source_target_pairs={{0,6},{1,7},{2,4},{3,5},{4,2},{5,3},{6,0},{7,1},{8,14},{9,15},{10,... | collective-permute-start | bytes 786440 | tf_op jit(solution)/shard_map/ppermute | solution.py:807
  73.2 15.7 %collective-permute-start.18 = (bf16[4,32,512]{2,1,0:T(8,128)(2,1)S(1)}, bf16[4,32,512]{2,1,0:T(8,128)(2,1)}, u32[]{:S(2)}, u32[]{:S(2)}) collective-permute-start(bf16[4,32,512]{2,1,0:T(8,128)(2,1)S(1)} %get-tuple-element.82), channel_id=1, source_target_pairs={{0,64},{1,65},{2,66},{3,67},{4,68},{5,69},{6,70},{7,71},{8,72},{9,... | collective-permute-start | bytes 393224 | tf_op jit(solution)/shard_map/ppermute | solution.py:864
  74.9 14.0 %collective-permute-start.19 = (bf16[4,32,512]{2,1,0:T(8,128)(2,1)S(1)}, bf16[4,32,512]{2,1,0:T(8,128)(2,1)}, u32[]{:S(2)}, u32[]{:S(2)}) collective-permute-start(bf16[4,32,512]{2,1,0:T(8,128)(2,1)S(1)} %get-tuple-element.83), channel_id=1, source_target_pairs={{0,72},{1,73},{2,74},{3,75},{4,76},{5,77},{6,78},{7,79},{8,64},{9,... | collective-permute-start | bytes 393224 | tf_op jit(solution)/shard_map/ppermute | solution.py:865
  87.3 12.0 %collective-permute-start.14 = (bf16[256,2048]{1,0:T(8,128)(2,1)}, bf16[256,2048]{1,0:T(8,128)(2,1)S(1)}, u32[]{:S(2)}, u32[]{:S(2)}) collective-permute-start(bf16[256,2048]{1,0:T(8,128)(2,1)} %carried_other.1), channel_id=1, source_target_pairs={{0,1},{1,0},{2,3},{3,2},{4,5},{5,4},{6,7},{7,6},{8,9},{9,8},{10,11... | collective-permute-start | bytes 3145736 | tf_op jit(solution)/shard_map/ppermute | solution.py:863
  90.0 7.8 %collective-permute-start.20 = (bf16[32,512]{1,0:T(8,128)(2,1)S(1)}, bf16[32,512]{1,0:T(8,128)(2,1)S(1)}, u32[]{:S(2)}, u32[]{:S(2)}) collective-permute-start(bf16[32,512]{1,0:T(8,128)(2,1)S(1)} %get-tuple-element.98), channel_id=1, source_target_pairs={{0,2},{1,3},{2,0},{3,1},{4,6},{5,7},{6,4},{7,5},{8,10},{9,11},{10,... | collective-permute-start | bytes 98312 | tf_op jit(solution)/shard_map/ppermute | solution.py:807
  90.1 7.7 %collective-permute-start.21 = (bf16[32,512]{1,0:T(8,128)(2,1)S(1)}, bf16[32,512]{1,0:T(8,128)(2,1)S(1)}, u32[]{:S(2)}, u32[]{:S(2)}) collective-permute-start(bf16[32,512]{1,0:T(8,128)(2,1)S(1)} %get-tuple-element.97), channel_id=1, source_target_pairs={{0,4},{1,5},{2,6},{3,7},{4,0},{5,1},{6,2},{7,3},{8,12},{9,13},{10,... | collective-permute-start | bytes 98312 | tf_op jit(solution)/shard_map/ppermute | solution.py:807
  93.3 4.5 %collective-permute-start.22 = (bf16[32,512]{1,0:T(8,128)(2,1)S(1)}, bf16[32,512]{1,0:T(8,128)(2,1)S(1)}, u32[]{:S(2)}, u32[]{:S(2)}) collective-permute-start(bf16[32,512]{1,0:T(8,128)(2,1)S(1)} %get-tuple-element.96), channel_id=1, source_target_pairs={{0,6},{1,7},{2,4},{3,5},{4,2},{5,3},{6,0},{7,1},{8,14},{9,15},{10,... | collective-permute-start | bytes 98312 | tf_op jit(solution)/shard_map/ppermute | solution.py:807
  98.0 2.9 %collective-permute-start.23 = (bf16[16,2048]{1,0:T(8,128)(2,1)S(1)}, bf16[16,2048]{1,0:T(8,128)(2,1)S(1)}, u32[]{:S(2)}, u32[]{:S(2)}) collective-permute-start(bf16[16,2048]{1,0:T(8,128)(2,1)S(1)} %select_n.156), channel_id=1, source_target_pairs={{0,1},{1,0},{2,3},{3,2},{4,5},{5,4},{6,7},{7,6},{8,9},{9,8},{10,11... | collective-permute-start | bytes 196616 | tf_op jit(solution)/shard_map/ppermute | solution.py:877

commit v6 on v5

--- a/solution.py
+++ b/solution.py
@@ -861,10 +861,10 @@
     kept, sent = after(tuple(decode(lengths.astype(jnp.int32))), starts[1])
     other_rows = run_d(scalars, local, bcc, wc3, starts, False)
     other_group = lax.ppermute(other_rows, "dp", [(i, i ^ 1) for i in range(count)])
+    crossed = lax.ppermute(sent, both, [(i, ((i + count) % total) ^ (CORES * RING)) for i in range(total)])
     straight = lax.ppermute(kept, both, [(i, (i + count) % total) for i in range(total)])
-    crossed = lax.ppermute(sent, both, [(i, ((i + count) % total) ^ (CORES * RING)) for i in range(total)])
     answers = after(straight + crossed, other_rows)
-    answers = [z_swap(answers[m], m) for m in range(RING)]
+    answers = z_swaps([answers[m] for m in range(RING)])
     own_group = run_d(scalars, local, bcc, wc3, starts, True)
     answers = after(tuple(answers), own_group)
     columns = [

time: 103 us -> 103 us (level)
  transfers between devices with their start and end apart: 24 -> 24, of which waited for: 2 -> 4; matrix products, arithmetic and copies ran while one was open for 2% -> 2% of each run, Pallas kernels for 41% -> 41%
where the time goes in v6:
time: 103 us; the launch traced here: 102 us
  Pallas kernels  46.5 us (45%)
  starting transfers between devices  43.8 us (43%)
  waiting for transfers between devices  5 us (5%)
  between operations  3.14 us (3%)
  other arithmetic  2.63 us (3%)
  local copies, waits for them, and re-layouts  1.36 us (1%)
    pallas_call x2, Pallas kernels, run_b(): pl.pallas_call(functools.partial(kernel_b, base, count), grid_spec=pltpu....  16.7 us
    ppermute x12, starting transfers between devices, z_swap(): return lax.ppermute(value, 'dp', [(i, i ^ CORES * m) for i in range(count)])  15.9 us
    pallas_call x1, Pallas kernels, run_a(): pl.pallas_call(kernel_a, grid_spec=pltpu.PrefetchScalarGridSpec(num_scala...  10.3 us
    pallas_call x2, Pallas kernels, run_d(): pl.pallas_call(kernel_d, grid_spec=pltpu.PrefetchScalarGridSpec(num_scala...  7.72 us
    ppermute x1, starting transfers between devices, on_device(): lax.ppermute(sent, both, [(i, (i + count) % total ^ CORES * RING) for i i...  5.71 us
    ppermute x12, waiting for transfers between devices, z_swap(): return lax.ppermute(value, 'dp', [(i, i ^ CORES * m) for i in range(count)])  4.97 us
    pallas_call x1, Pallas kernels, run_pack(): pl.pallas_call(kernel_pack, grid_spec=pltpu.PrefetchScalarGridSpec(num_sc...  4.84 us
    ppermute x1, starting transfers between devices, on_device(): lax.ppermute(half_total, 'dp', [(i, i + CORES * RING) for i in range(CORE...  4.45 us
  transfers between devices with their start and end apart: 24, of which 4 were waited for; matrix products, arithmetic and copies ran while one was open for 2% of the time, Pallas kernels for 41%

profile of v6, /device:TPU:1, one launch (start us, length us, event | category | flops | bytes accessed | tf_op | source)
XLA Modules:
  0.0 102.5 jit_solution(17115607296424603922)
XLA Ops:
  0.6 0.0 copy-start
  0.7 0.7 pad_add_fusion.s_ref
  1.4 0.0 copy-start.5
  1.4 0.0 copy-start.2
  1.4 0.0 copy-start.3
  1.4 4.8 %pack.1 = (bf16[256,3072]{1,0:T(8,128)(2,1)}, bf16[16,3072]{1,0:T(8,128)(2,1)}, bf16[16,3072]{1,0:T(8,128)(2,1)}, bf16[256,1024]{1,0:T(8,128)(2,1)}, bf16[16,3072]{1,0:T(8,128)(2,1)}, /*index=5*/bf16[16,3072]{1,0:T(8,128)(2,1)}) custom-call(s32[5]{0:T(128)S(1)} %pad_add_fusion.s_ref, bf16[256,4096]{1,0:T(8,128)(2,1)} %bitcast.60, ...), custom_call_target="tpu_custom_call" | custom-call | flops 1000000 | bytes 4000000 | tf_op jit(solution)/shard_map/pack/pallas_call | solution.py:738
  6.3 1.5 %collective-permute-start = (bf16[256,3072]{1,0:T(8,128)(2,1)}, bf16[256,3072]{1,0:T(8,128)(2,1)}, u32[]{:S(2)}, u32[]{:S(2)}) collective-permute-start(bf16[256,3072]{1,0:T(8,128)(2,1)} %get-tuple-element.46), channel_id=1, source_target_pairs={{0,1},{1,0},{2,3},{3,2},{4,5},{5,4},{6,7},{7,6},{8,9},{9,8},{10,11... | collective-permute-start | bytes 4718600 | tf_op jit(solution)/shard_map/ppermute | solution.py:790
  7.8 1.4 %collective-permute-start.3 = (bf16[16,3072]{1,0:T(8,128)(2,1)}, bf16[16,3072]{1,0:T(8,128)(2,1)S(1)}, u32[]{:S(2)}, u32[]{:S(2)}) collective-permute-start(bf16[16,3072]{1,0:T(8,128)(2,1)} %get-tuple-element.55), channel_id=1, source_target_pairs={{0,64},{1,65},{2,66},{3,67},{4,68},{5,69},{6,70},{7,71},{8,72},{9,... | collective-permute-start | bytes 294920 | tf_op jit(solution)/shard_map/ppermute | solution.py:802
  9.2 1.9 %collective-permute-start.5 = (bf16[16,3072]{1,0:T(8,128)(2,1)}, bf16[16,3072]{1,0:T(8,128)(2,1)S(1)}, u32[]{:S(2)}, u32[]{:S(2)}) collective-permute-start(bf16[16,3072]{1,0:T(8,128)(2,1)} %get-tuple-element.55), channel_id=1, source_target_pairs={{0,72},{1,73},{2,74},{3,75},{4,76},{5,77},{6,78},{7,79},{8,64},{9,... | collective-permute-start | bytes 294920 | tf_op jit(solution)/shard_map/ppermute | solution.py:802
  11.1 4.1 %collective-permute-start.1 = (bf16[16,3072]{1,0:T(8,128)(2,1)}, bf16[16,3072]{1,0:T(8,128)(2,1)S(1)}, u32[]{:S(2)}, u32[]{:S(2)}) collective-permute-start(bf16[16,3072]{1,0:T(8,128)(2,1)} %get-tuple-element.47), channel_id=1, source_target_pairs={{1,2},{3,4},{5,6},{7,8},{9,10},{11,12},{13,14},{17,18},{19,20},{21... | collective-permute-start | bytes 294920 | tf_op jit(solution)/shard_map/ppermute | solution.py:792
  15.1 3.5 %collective-permute-start.2 = (bf16[16,3072]{1,0:T(8,128)(2,1)}, bf16[16,3072]{1,0:T(8,128)(2,1)S(1)}, u32[]{:S(2)}, u32[]{:S(2)}) collective-permute-start(bf16[16,3072]{1,0:T(8,128)(2,1)} %get-tuple-element.48), channel_id=1, source_target_pairs={{1,3},{3,5},{5,7},{7,9},{9,11},{11,13},{13,15},{17,19},{19,21},{21... | collective-permute-start | bytes 294920 | tf_op jit(solution)/shard_map/ppermute | solution.py:793
  18.8 0.7 fusion
  21.6 0.1 constant_dynamic-slice_fusion.2
  21.7 0.1 tile.10
  21.8 0.1 broadcast_in_dim.11
  21.9 0.1 broadcast_in_dim_reshape.3.skip
  22.0 0.1 stack.36.s_ref
  22.1 0.0 collective-permute-done.1
  22.1 0.1 collective-permute-start.4
  22.2 1.0 collective-permute-start.6
  23.2 0.0 collective-permute-done.x_rec.g_rec
  23.3 10.3 %conv_and_states.1 = (bf16[272,512]{1,0:T(8,128)(2,1)S(1)}, bf16[272,512]{1,0:T(8,128)(2,1)S(1)}, bf16[272,512]{1,0:T(8,128)(2,1)S(1)}, bf16[272,512]{1,0:T(8,12...) custom-call(s32[8]{0:T(128)S(1)} %stack.36.s_ref, ...), custom_call_target="tpu_custom_call" | custom-call | flops 6000000000 | bytes 8000000 | tf_op jit(solution)/shard_map/conv_and_states/pallas_call | solution.py:216
  33.6 1.4 %collective-permute-start.7 = (bf16[272,512]{1,0:T(8,128)(2,1)S(1)}, bf16[272,512]{1,0:T(8,128)(2,1)S(1)}, u32[]{:S(2)}, u32[]{:S(2)}) collective-permute-start(bf16[272,512]{1,0:T(8,128)(2,1)S(1)} %get-tuple-element.58), channel_id=1, source_target_pairs={{0,2},{1,3},{2,0},{3,1},{4,6},{5,7},{6,4},{7,5},{8,10},{9,11},{10,... | collective-permute-start | bytes 835592 | tf_op jit(solution)/shard_map/ppermute | solution.py:807
  35.0 0.4 collective-permute-start.8
  35.4 0.0 collective-permute-done.4.near_cross
  35.4 2.1 %collective-permute-start.9 = (bf16[272,512]{1,0:T(8,128)(2,1)S(1)}, bf16[272,512]{1,0:T(8,128)(2,1)S(1)}, u32[]{:S(2)}, u32[]{:S(2)}) collective-permute-start(bf16[272,512]{1,0:T(8,128)(2,1)S(1)} %get-tuple-element.60), channel_id=1, source_target_pairs={{0,6},{1,7},{2,4},{3,5},{4,2},{5,3},{6,0},{7,1},{8,14},{9,15},{10,... | collective-permute-start | bytes 835592 | tf_op jit(solution)/shard_map/ppermute | solution.py:807
  37.5 11.2 %output_within_chip_1.1 = (bf16[432,512]{1,0:T(8,128)(2,1)S(1)}, bf16[432,512]{1,0:T(8,128)(2,1)S(1)}, bf16[432,512]{1,0:T(8,128)(2,1)S(1)}, f32[512,2048]{1,0:T(8,128)}) custom-call(s32[8]{0:T(128)S(1)} %stack.36.s_ref, bf16[512,2048]{1,0:T(8,128)(2,1)S(1)} %get-tuple-element.50.xc_ref, bf16[512,512]{1,0:T(8,128)(2,1)S(1)} %get-tuple-element.51.bcc.c_rows, ...), custom_call_target="tpu_custom_call" | custom-call | flops 8999999488 | bytes 6000000 | tf_op jit(solution)/shard_map/output_within_chip_1/pallas_call | solution.py:426
  48.8 0.1 collective-permute-start.15
  48.8 2.8 %collective-permute-start.16 = (bf16[432,512]{1,0:T(8,128)(2,1)S(1)}, bf16[432,512]{1,0:T(8,128)(2,1)S(1)}, u32[]{:S(2)}, u32[]{:S(2)}) collective-permute-start(bf16[432,512]{1,0:T(8,128)(2,1)S(1)} %get-tuple-element.78), channel_id=1, source_target_pairs={{0,4},{1,5},{2,6},{3,7},{4,0},{5,1},{6,2},{7,3},{8,12},{9,13},{10,... | collective-permute-start | bytes 1327112 | tf_op jit(solution)/shard_map/ppermute | solution.py:807
  51.7 0.0 collective-permute-done.7.l1
  51.7 0.9 collective-permute-start.17
  52.6 0.1 dynamic-slice.3
  52.7 0.0 collective-permute-done.8.l2
  52.7 0.0 collective-permute-done.9.l3
  52.7 0.9 half_total.1
  53.6 4.4 %collective-permute-start.10 = (bf16[256,512]{1,0:T(8,128)(2,1)S(1)}, bf16[256,512]{1,0:T(8,128)(2,1)S(1)}, u32[]{:S(2)}, u32[]{:S(2)}) collective-permute-start(bf16[256,512]{1,0:T(8,128)(2,1)S(1)} %half_total.1), channel_id=1, source_target_pairs={{0,8},{1,9},{2,10},{3,11},{4,12},{5,13},{6,14},{7,15},{16,24},{17,... | collective-permute-start | bytes 786440 | tf_op jit(solution)/shard_map/ppermute | solution.py:834
  58.0 5.5 %output_within_chip_0.1 = (bf16[432,512]{1,0:T(8,128)(2,1)S(1)}, f32[512,2048]{1,0:T(8,128)}) custom-call(s32[8]{0:T(128)S(1)} %stack.36.s_ref, bf16[512,2048]{1,0:T(8,128)(2,1)S(1)} %get-tuple-element.50.xc_ref, bf16[512,512]{1,0:T(8,128)(2,1)S(1)} %get-tuple-element.51.bcc.c_rows, ...), custom_call_target="tpu_custom_call", output_to_operand_aliasing={{1}: (11, {})} | custom-call | flops 3000000000 | bytes 2000000 | tf_op jit(solution)/shard_map/output_within_chip_0/pallas_call | solution.py:426
  63.6 0.0 collective-permute-done.10.start
  63.6 1.2 %chip_starts.1 = (bf16[256,512]{1,0:T(8,128)(2,1)S(1)}, bf16[256,512]{1,0:T(8,128)(2,1)S(1)}, bf16[256,512]{1,0:T(8,128)(2,1)S(1)}, bf16[256,512]{1,0:T(8,128)(2,1)S(1)}) custom-call(s32[8]{0:T(128)S(1)} %stack.36.s_ref, bf16[272,512]{1,0:T(8,128)(2,1)S(1)} %get-tuple-element.62.l0, bf16[272,512]{1,0:T(8,128)(2,1)S(1)} %collective-permute-done.7.l1, ...), custom_call_target="tpu_custom_call" | custom-call | flops 1000000 | bytes 3000000 | tf_op jit(solution)/shard_map/chip_starts/pallas_call | solution.py:484
  64.8 0.1 collective-permute-start.11
  64.9 4.1 %collective-permute-start.12 = (bf16[256,512]{1,0:T(8,128)(2,1)S(1)}, bf16[256,512]{1,0:T(8,128)(2,1)S(1)}, u32[]{:S(2)}, u32[]{:S(2)}) collective-permute-start(bf16[256,512]{1,0:T(8,128)(2,1)S(1)} %get-tuple-element.75), channel_id=1, source_target_pairs={{0,4},{1,5},{2,6},{3,7},{4,0},{5,1},{6,2},{7,3},{8,12},{9,13},{10,... | collective-permute-start | bytes 786440 | tf_op jit(solution)/shard_map/ppermute | solution.py:807
  69.0 0.0 collective-permute-done.15.f1
  69.0 0.0 collective-permute-start.13
  69.0 0.1 collective-permute-done.16.f2
  69.1 3.2 %decode_rows.1 = (bf16[4,32,512]{2,1,0:T(8,128)(2,1)S(1)}, bf16[4,32,512]{2,1,0:T(8,128)(2,1)S(1)}) custom-call(s32[8]{0:T(128)S(1)} %stack.36.s_ref, bf16[272,512]{1,0:T(8,128)(2,1)S(1)} %get-tuple-element.62.l0, bf16[272,512]{1,0:T(8,128)(2,1)S(1)} %collective-permute-done.7.l1, bf16[272,512]{1,0:T(8,128)(2,1)S(1)} %collective-permute-done.8.l2, ...), custom_call_target="tpu_custom_call" | custom-call | flops 20000000000 | bytes 6000000 | tf_op jit(solution)/shard_map/decode_rows/pallas_call | solution.py:844
  72.3 0.9 collective-permute-done.11.r1
  73.2 1.7 %collective-permute-start.18 = (bf16[4,32,512]{2,1,0:T(8,128)(2,1)S(1)}, bf16[4,32,512]{2,1,0:T(8,128)(2,1)}, u32[]{:S(2)}, u32[]{:S(2)}) collective-permute-start(bf16[4,32,512]{2,1,0:T(8,128)(2,1)S(1)} %get-tuple-element.82), channel_id=1, source_target_pairs={{0,64},{1,65},{2,66},{3,67},{4,68},{5,69},{6,70},{7,71},{8,72},{9,... | collective-permute-start | bytes 393224 | tf_op jit(solution)/shard_map/ppermute | solution.py:865
  74.9 5.7 %collective-permute-start.19 = (bf16[4,32,512]{2,1,0:T(8,128)(2,1)S(1)}, bf16[4,32,512]{2,1,0:T(8,128)(2,1)}, u32[]{:S(2)}, u32[]{:S(2)}) collective-permute-start(bf16[4,32,512]{2,1,0:T(8,128)(2,1)S(1)} %get-tuple-element.83), channel_id=1, source_target_pairs={{0,72},{1,73},{2,74},{3,75},{4,76},{5,77},{6,78},{7,79},{8,64},{9,... | collective-permute-start | bytes 393224 | tf_op jit(solution)/shard_map/ppermute | solution.py:864
  80.6 0.9 collective-permute-done.12.r2
  81.6 3.0 %collective-permute-done.13.r3 = bf16[256,512]{1,0:T(8,128)(2,1)S(1)} collective-permute-done((bf16[256,512]{1,0:T(8,128)(2,1)S(1)}, bf16[256,512]{1,0:T(8,128)(2,1)S(1)}, u32[]{:S(2)}, u32[]{:S(2)}) %collective-permute-start.13) | collective-permute-done | bytes 262176 | tf_op jit(solution)/shard_map/ppermute | solution.py:807
  84.5 3.9 %carried_other.1 = bf16[256,2048]{1,0:T(8,128)(2,1)} custom-call(s32[8]{0:T(128)S(1)} %stack.36.s_ref, f32[512,2048]{1,0:T(8,128)} %get-tuple-element.71.local, bf16[512,512]{1,0:T(8,128)(2,1)S(1)} %get-tuple-element.51.bcc.c_rows, bf16[512,128]{1,0:T(8,128)(2,1)S(1)} %get-tuple-element.72.wc3, bf16[256,512]{1,0:T(8,128)(2,1)S(1)} %get-tuple-element.73.r0, ...), custom_call_target="tpu_custom_call" | custom-call | flops 1000000000 | bytes 4000000 | tf_op jit(solution)/shard_map/carried_other/pallas_call | solution.py:634
  88.4 1.7 %collective-permute-start.14 = (bf16[256,2048]{1,0:T(8,128)(2,1)}, bf16[256,2048]{1,0:T(8,128)(2,1)S(1)}, u32[]{:S(2)}, u32[]{:S(2)}) collective-permute-start(bf16[256,2048]{1,0:T(8,128)(2,1)} %carried_other.1), channel_id=1, source_target_pairs={{0,1},{1,0},{2,3},{3,2},{4,5},{5,4},{6,7},{7,6},{8,9},{9,8},{10,11... | collective-permute-start | bytes 3145736 | tf_op jit(solution)/shard_map/ppermute | solution.py:863
  90.1 0.0 collective-permute-done.18
  90.1 0.0 collective-permute-done.19
  90.1 1.0 add.45
  91.1 0.1 collective-permute-start.20
  91.2 2.1 %collective-permute-start.21 = (bf16[32,512]{1,0:T(8,128)(2,1)S(1)}, bf16[32,512]{1,0:T(8,128)(2,1)S(1)}, u32[]{:S(2)}, u32[]{:S(2)}) collective-permute-start(bf16[32,512]{1,0:T(8,128)(2,1)S(1)} %get-tuple-element.97), channel_id=1, source_target_pairs={{0,4},{1,5},{2,6},{3,7},{4,0},{5,1},{6,2},{7,3},{8,12},{9,13},{10,... | collective-permute-start | bytes 98312 | tf_op jit(solution)/shard_map/ppermute | solution.py:807
  93.3 1.8 %collective-permute-start.22 = (bf16[32,512]{1,0:T(8,128)(2,1)S(1)}, bf16[32,512]{1,0:T(8,128)(2,1)S(1)}, u32[]{:S(2)}, u32[]{:S(2)}) collective-permute-start(bf16[32,512]{1,0:T(8,128)(2,1)S(1)} %get-tuple-element.96), channel_id=1, source_target_pairs={{0,6},{1,7},{2,4},{3,5},{4,2},{5,3},{6,0},{7,1},{8,14},{9,15},{10,... | collective-permute-start | bytes 98312 | tf_op jit(solution)/shard_map/ppermute | solution.py:807
  95.1 3.8 %carried_own.1.whole = bf16[256,4096]{1,0:T(8,128)(2,1)} custom-call(s32[8]{0:T(128)S(1)} %stack.36.s_ref, f32[512,2048]{1,0:T(8,128)} %get-tuple-element.71.local, bf16[512,512]{1,0:T(8,128)(2,1)S(1)} %get-tuple-element.51.bcc.c_rows, bf16[512,128]{1,0:T(8,128)(2,1)S(1)} %get-tuple-element.72.wc3, bf16[256,512]{1,0:T(8,128)(2,1)S(1)} %get-tuple-element.73.r0, ...), custom_call_target="tpu_custom_call" | custom-call | flops 1000000000 | bytes 4000000 | tf_op jit(solution)/shard_map/carried_own/pallas_call | solution.py:634
  99.0 0.1 reshape.87
  99.0 0.1 select_bitcast_fusion
  99.1 0.9 collective-permute-start.23
  100.0 1.6 %put_group.1 = bf16[256,4096]{1,0:T(8,128)(2,1)} custom-call(s32[8]{0:T(128)S(1)} %stack.36.s_ref, bf16[256,2048]{1,0:T(8,128)(2,1)S(1)} %collective-permute-done.14.part, bf16[256,4096]{1,0:T(8,128)(2,1)} %carried_own.1.whole), custom_call_target="tpu_custom_call", output_to_operand_aliasing={{}: (2, {})} | custom-call | bytes 2000000 | tf_op jit(solution)/shard_map/put_group/pallas_call | solution.py:659
  101.7 0.8 maximum_select_fusion
  (39 shorter events, 0.2 us)
Async XLA Ops:
  0.6 20.9 %copy-start = (bf16[4,2,512]{2,1,0:T(2,128)(2,1)S(1)}, bf16[4,2,512]{2,1,0:T(2,128)(2,1)}, u32[]{:S(2)}) copy-start(bf16[4,2,512]{2,1,0:T(2,128)(2,1)} %param.20) | copy-start | bytes 24580
  1.4 17.4 %copy-start.1 = (s32[1,3]{1,0:T(1,128)S(1)}, s32[1,3]{1,0:T(1,128)}, u32[]{:S(2)}) copy-start(s32[1,3]{1,0:T(1,128)} %bounds.1) | copy-start | bytes 40
  1.4 20.2 %copy-start.4 = (f32[2,512]{1,0:T(2,128)S(1)}, f32[2,512]{1,0:T(2,128)}, u32[]{:S(2)}) copy-start(f32[2,512]{1,0:T(2,128)} %param.21) | copy-start | bytes 12292
  1.4 20.2 %copy-start.7 = (f32[64]{0:T(128)S(1)}, f32[64]{0:T(128)}, u32[]{:S(2)}) copy-start(f32[64]{0:T(128)} %param.23) | copy-start | bytes 772
  1.4 20.2 %copy-start.6 = (f32[64]{0:T(128)S(1)}, f32[64]{0:T(128)}, u32[]{:S(2)}) copy-start(f32[64]{0:T(128)} %param.22) | copy-start | bytes 772
  1.4 20.4 %copy-start.5 = (f32[64]{0:T(128)S(1)}, f32[64]{0:T(128)}, u32[]{:S(2)}) copy-start(f32[64]{0:T(128)} %param.24) | copy-start | bytes 772
  1.4 21.8 %copy-start.2 = (bf16[4,4096]{1,0:T(4,128)(2,1)S(1)}, bf16[4,4096]{1,0:T(4,128)(2,1)}, u32[]{:S(2)}) copy-start(bf16[4,4096]{1,0:T(4,128)(2,1)} %wx.1) | copy-start | bytes 98308
  1.4 21.8 %copy-start.3 = (f32[4096]{0:T(1024)S(1)}, f32[4096]{0:T(1024)}, u32[]{:S(2)}) copy-start(f32[4096]{0:T(1024)} %param.19) | copy-start | bytes 49156
  6.3 16.9 %collective-permute-start = (bf16[256,3072]{1,0:T(8,128)(2,1)}, bf16[256,3072]{1,0:T(8,128)(2,1)}, u32[]{:S(2)}, u32[]{:S(2)}) collective-permute-start(bf16[256,3072]{1,0:T(8,128)(2,1)} %get-tuple-element.46), channel_id=1, source_target_pairs={{0,1},{1,0},{2,3},{3,2},{4,5},{5,4},{6,7},{7,6},{8,9},{9,8},{10,11... | collective-permute-start | bytes 4718600 | tf_op jit(solution)/shard_map/ppermute | solution.py:790
  7.8 27.2 %collective-permute-start.3 = (bf16[16,3072]{1,0:T(8,128)(2,1)}, bf16[16,3072]{1,0:T(8,128)(2,1)S(1)}, u32[]{:S(2)}, u32[]{:S(2)}) collective-permute-start(bf16[16,3072]{1,0:T(8,128)(2,1)} %get-tuple-element.55), channel_id=1, source_target_pairs={{0,64},{1,65},{2,66},{3,67},{4,68},{5,69},{6,70},{7,71},{8,72},{9,... | collective-permute-start | bytes 294920 | tf_op jit(solution)/shard_map/ppermute | solution.py:802
  9.2 28.3 %collective-permute-start.5 = (bf16[16,3072]{1,0:T(8,128)(2,1)}, bf16[16,3072]{1,0:T(8,128)(2,1)S(1)}, u32[]{:S(2)}, u32[]{:S(2)}) collective-permute-start(bf16[16,3072]{1,0:T(8,128)(2,1)} %get-tuple-element.55), channel_id=1, source_target_pairs={{0,72},{1,73},{2,74},{3,75},{4,76},{5,77},{6,78},{7,79},{8,64},{9,... | collective-permute-start | bytes 294920 | tf_op jit(solution)/shard_map/ppermute | solution.py:802
  11.1 11.0 %collective-permute-start.1 = (bf16[16,3072]{1,0:T(8,128)(2,1)}, bf16[16,3072]{1,0:T(8,128)(2,1)S(1)}, u32[]{:S(2)}, u32[]{:S(2)}) collective-permute-start(bf16[16,3072]{1,0:T(8,128)(2,1)} %get-tuple-element.47), channel_id=1, source_target_pairs={{1,2},{3,4},{5,6},{7,8},{9,10},{11,12},{13,14},{17,18},{19,20},{21... | collective-permute-start | bytes 294920 | tf_op jit(solution)/shard_map/ppermute | solution.py:792
  15.1 7.1 %collective-permute-start.2 = (bf16[16,3072]{1,0:T(8,128)(2,1)}, bf16[16,3072]{1,0:T(8,128)(2,1)S(1)}, u32[]{:S(2)}, u32[]{:S(2)}) collective-permute-start(bf16[16,3072]{1,0:T(8,128)(2,1)} %get-tuple-element.48), channel_id=1, source_target_pairs={{1,3},{3,5},{5,7},{7,9},{9,11},{11,13},{13,15},{17,19},{19,21},{21... | collective-permute-start | bytes 294920 | tf_op jit(solution)/shard_map/ppermute | solution.py:793
  22.1 13.3 %collective-permute-start.4 = (bf16[16,3072]{1,0:T(8,128)(2,1)}, bf16[16,3072]{1,0:T(8,128)(2,1)S(1)}, u32[]{:S(2)}, u32[]{:S(2)}) collective-permute-start(bf16[16,3072]{1,0:T(8,128)(2,1)} %get-tuple-element.56), channel_id=1, source_target_pairs={{0,65},{1,64},{2,67},{3,66},{4,69},{5,68},{6,71},{7,70},{8,73},{9,... | collective-permute-start | bytes 294920 | tf_op jit(solution)/shard_map/ppermute | solution.py:802
  22.2 15.3 %collective-permute-start.6 = (bf16[16,3072]{1,0:T(8,128)(2,1)}, bf16[16,3072]{1,0:T(8,128)(2,1)S(1)}, u32[]{:S(2)}, u32[]{:S(2)}) collective-permute-start(bf16[16,3072]{1,0:T(8,128)(2,1)} %get-tuple-element.56), channel_id=1, source_target_pairs={{0,73},{1,72},{2,75},{3,74},{4,77},{5,76},{6,79},{7,78},{8,65},{9,... | collective-permute-start | bytes 294920 | tf_op jit(solution)/shard_map/ppermute | solution.py:802
  33.6 18.1 %collective-permute-start.7 = (bf16[272,512]{1,0:T(8,128)(2,1)S(1)}, bf16[272,512]{1,0:T(8,128)(2,1)S(1)}, u32[]{:S(2)}, u32[]{:S(2)}) collective-permute-start(bf16[272,512]{1,0:T(8,128)(2,1)S(1)} %get-tuple-element.58), channel_id=1, source_target_pairs={{0,2},{1,3},{2,0},{3,1},{4,6},{5,7},{6,4},{7,5},{8,10},{9,11},{10,... | collective-permute-start | bytes 835592 | tf_op jit(solution)/shard_map/ppermute | solution.py:807
  35.0 17.7 %collective-permute-start.8 = (bf16[272,512]{1,0:T(8,128)(2,1)S(1)}, bf16[272,512]{1,0:T(8,128)(2,1)S(1)}, u32[]{:S(2)}, u32[]{:S(2)}) collective-permute-start(bf16[272,512]{1,0:T(8,128)(2,1)S(1)} %get-tuple-element.59), channel_id=1, source_target_pairs={{0,4},{1,5},{2,6},{3,7},{4,0},{5,1},{6,2},{7,3},{8,12},{9,13},{10,... | collective-permute-start | bytes 835592 | tf_op jit(solution)/shard_map/ppermute | solution.py:807
  35.4 17.3 %collective-permute-start.9 = (bf16[272,512]{1,0:T(8,128)(2,1)S(1)}, bf16[272,512]{1,0:T(8,128)(2,1)S(1)}, u32[]{:S(2)}, u32[]{:S(2)}) collective-permute-start(bf16[272,512]{1,0:T(8,128)(2,1)S(1)} %get-tuple-element.60), channel_id=1, source_target_pairs={{0,6},{1,7},{2,4},{3,5},{4,2},{5,3},{6,0},{7,1},{8,14},{9,15},{10,... | collective-permute-start | bytes 835592 | tf_op jit(solution)/shard_map/ppermute | solution.py:807
  48.8 20.2 %collective-permute-start.15 = (bf16[432,512]{1,0:T(8,128)(2,1)S(1)}, bf16[432,512]{1,0:T(8,128)(2,1)S(1)}, u32[]{:S(2)}, u32[]{:S(2)}) collective-permute-start(bf16[432,512]{1,0:T(8,128)(2,1)S(1)} %get-tuple-element.61), channel_id=1, source_target_pairs={{0,2},{1,3},{2,0},{3,1},{4,6},{5,7},{6,4},{7,5},{8,10},{9,11},{10,... | collective-permute-start | bytes 1327112 | tf_op jit(solution)/shard_map/ppermute | solution.py:807
  48.8 20.2 %collective-permute-start.16 = (bf16[432,512]{1,0:T(8,128)(2,1)S(1)}, bf16[432,512]{1,0:T(8,128)(2,1)S(1)}, u32[]{:S(2)}, u32[]{:S(2)}) collective-permute-start(bf16[432,512]{1,0:T(8,128)(2,1)S(1)} %get-tuple-element.78), channel_id=1, source_target_pairs={{0,4},{1,5},{2,6},{3,7},{4,0},{5,1},{6,2},{7,3},{8,12},{9,13},{10,... | collective-permute-start | bytes 1327112 | tf_op jit(solution)/shard_map/ppermute | solution.py:807
  51.7 17.4 %collective-permute-start.17 = (bf16[432,512]{1,0:T(8,128)(2,1)S(1)}, bf16[432,512]{1,0:T(8,128)(2,1)S(1)}, u32[]{:S(2)}, u32[]{:S(2)}) collective-permute-start(bf16[432,512]{1,0:T(8,128)(2,1)S(1)} %get-tuple-element.79), channel_id=1, source_target_pairs={{0,6},{1,7},{2,4},{3,5},{4,2},{5,3},{6,0},{7,1},{8,14},{9,15},{10,... | collective-permute-start | bytes 1327112 | tf_op jit(solution)/shard_map/ppermute | solution.py:807
  53.6 10.0 %collective-permute-start.10 = (bf16[256,512]{1,0:T(8,128)(2,1)S(1)}, bf16[256,512]{1,0:T(8,128)(2,1)S(1)}, u32[]{:S(2)}, u32[]{:S(2)}) collective-permute-start(bf16[256,512]{1,0:T(8,128)(2,1)S(1)} %half_total.1), channel_id=1, source_target_pairs={{0,8},{1,9},{2,10},{3,11},{4,12},{5,13},{6,14},{7,15},{16,24},{17,... | collective-permute-start | bytes 786440 | tf_op jit(solution)/shard_map/ppermute | solution.py:834
  64.8 8.5 %collective-permute-start.11 = (bf16[256,512]{1,0:T(8,128)(2,1)S(1)}, bf16[256,512]{1,0:T(8,128)(2,1)S(1)}, u32[]{:S(2)}, u32[]{:S(2)}) collective-permute-start(bf16[256,512]{1,0:T(8,128)(2,1)S(1)} %get-tuple-element.74), channel_id=1, source_target_pairs={{0,2},{1,3},{2,0},{3,1},{4,6},{5,7},{6,4},{7,5},{8,10},{9,11},{10,... | collective-permute-start | bytes 786440 | tf_op jit(solution)/shard_map/ppermute | solution.py:807
  64.9 16.7 %collective-permute-start.12 = (bf16[256,512]{1,0:T(8,128)(2,1)S(1)}, bf16[256,512]{1,0:T(8,128)(2,1)S(1)}, u32[]{:S(2)}, u32[]{:S(2)}) collective-permute-start(bf16[256,512]{1,0:T(8,128)(2,1)S(1)} %get-tuple-element.75), channel_id=1, source_target_pairs={{0,4},{1,5},{2,6},{3,7},{4,0},{5,1},{6,2},{7,3},{8,12},{9,13},{10,... | collective-permute-start | bytes 786440 | tf_op jit(solution)/shard_map/ppermute | solution.py:807
  69.0 15.6 %collective-permute-start.13 = (bf16[256,512]{1,0:T(8,128)(2,1)S(1)}, bf16[256,512]{1,0:T(8,128)(2,1)S(1)}, u32[]{:S(2)}, u32[]{:S(2)}) collective-permute-start(bf16[256,512]{1,0:T(8,128)(2,1)S(1)} %get-tuple-element.76), channel_id=1, source_target_pairs={{0,6},{1,7},{2,4},{3,5},{4,2},{5,3},{6,0},{7,1},{8,14},{9,15},{10,... | collective-permute-start | bytes 786440 | tf_op jit(solution)/shard_map/ppermute | solution.py:807
  73.2 16.9 %collective-permute-start.18 = (bf16[4,32,512]{2,1,0:T(8,128)(2,1)S(1)}, bf16[4,32,512]{2,1,0:T(8,128)(2,1)}, u32[]{:S(2)}, u32[]{:S(2)}) collective-permute-start(bf16[4,32,512]{2,1,0:T(8,128)(2,1)S(1)} %get-tuple-element.82), channel_id=1, source_target_pairs={{0,64},{1,65},{2,66},{3,67},{4,68},{5,69},{6,70},{7,71},{8,72},{9,... | collective-permute-start | bytes 393224 | tf_op jit(solution)/shard_map/ppermute | solution.py:865
  74.9 15.2 %collective-permute-start.19 = (bf16[4,32,512]{2,1,0:T(8,128)(2,1)S(1)}, bf16[4,32,512]{2,1,0:T(8,128)(2,1)}, u32[]{:S(2)}, u32[]{:S(2)}) collective-permute-start(bf16[4,32,512]{2,1,0:T(8,128)(2,1)S(1)} %get-tuple-element.83), channel_id=1, source_target_pairs={{0,72},{1,73},{2,74},{3,75},{4,76},{5,77},{6,78},{7,79},{8,64},{9,... | collective-permute-start | bytes 393224 | tf_op jit(solution)/shard_map/ppermute | solution.py:864
  88.4 11.6 %collective-permute-start.14 = (bf16[256,2048]{1,0:T(8,128)(2,1)}, bf16[256,2048]{1,0:T(8,128)(2,1)S(1)}, u32[]{:S(2)}, u32[]{:S(2)}) collective-permute-start(bf16[256,2048]{1,0:T(8,128)(2,1)} %carried_other.1), channel_id=1, source_target_pairs={{0,1},{1,0},{2,3},{3,2},{4,5},{5,4},{6,7},{7,6},{8,9},{9,8},{10,11... | collective-permute-start | bytes 3145736 | tf_op jit(solution)/shard_map/ppermute | solution.py:863
  91.1 7.8 %collective-permute-start.20 = (bf16[32,512]{1,0:T(8,128)(2,1)S(1)}, bf16[32,512]{1,0:T(8,128)(2,1)S(1)}, u32[]{:S(2)}, u32[]{:S(2)}) collective-permute-start(bf16[32,512]{1,0:T(8,128)(2,1)S(1)} %get-tuple-element.98), channel_id=1, source_target_pairs={{0,2},{1,3},{2,0},{3,1},{4,6},{5,7},{6,4},{7,5},{8,10},{9,11},{10,... | collective-permute-start | bytes 98312 | tf_op jit(solution)/shard_map/ppermute | solution.py:807
  91.2 7.7 %collective-permute-start.21 = (bf16[32,512]{1,0:T(8,128)(2,1)S(1)}, bf16[32,512]{1,0:T(8,128)(2,1)S(1)}, u32[]{:S(2)}, u32[]{:S(2)}) collective-permute-start(bf16[32,512]{1,0:T(8,128)(2,1)S(1)} %get-tuple-element.97), channel_id=1, source_target_pairs={{0,4},{1,5},{2,6},{3,7},{4,0},{5,1},{6,2},{7,3},{8,12},{9,13},{10,... | collective-permute-start | bytes 98312 | tf_op jit(solution)/shard_map/ppermute | solution.py:807
  93.3 5.6 %collective-permute-start.22 = (bf16[32,512]{1,0:T(8,128)(2,1)S(1)}, bf16[32,512]{1,0:T(8,128)(2,1)S(1)}, u32[]{:S(2)}, u32[]{:S(2)}) collective-permute-start(bf16[32,512]{1,0:T(8,128)(2,1)S(1)} %get-tuple-element.96), channel_id=1, source_target_pairs={{0,6},{1,7},{2,4},{3,5},{4,2},{5,3},{6,0},{7,1},{8,14},{9,15},{10,... | collective-permute-start | bytes 98312 | tf_op jit(solution)/shard_map/ppermute | solution.py:807
  99.1 2.6 %collective-permute-start.23 = (bf16[16,2048]{1,0:T(8,128)(2,1)S(1)}, bf16[16,2048]{1,0:T(8,128)(2,1)S(1)}, u32[]{:S(2)}, u32[]{:S(2)}) collective-permute-start(bf16[16,2048]{1,0:T(8,128)(2,1)S(1)} %select_n.156), channel_id=1, source_target_pairs={{0,1},{1,0},{2,3},{3,2},{4,5},{5,4},{6,7},{7,6},{8,9},{9,8},{10,11... | collective-permute-start | bytes 196616 | tf_op jit(solution)/shard_map/ppermute | solution.py:877
